TPU v7x, 32 devices: a whole 2x2x4 slice. The times are simulated.
32 devices in a mesh: oct: 32 (over z, y, x, core).
Axes of the slice: x: 2, y: 2, z: 4, core: 2. Of those that a mesh axis runs over, the one named last changes fastest.
Arguments:
- points: float32 [2048, 3, 128], P('oct'), may hold values from -6 to 6
- dens: float32 [2048, 32, 128], P('oct'), may hold values from -6 to 6
- surface: float32 [2048, 3, 152], P('oct'), may hold values from -6 to 6
- counts: int32 [2048], P('oct'), may hold values from 1 to 128, as said below
- ulist: int32 [2048, 27], P('oct'), may hold values from -1 to 2047, as said below
- vlist: int32 [256, 316], P('oct'), may hold values from -1 to 255, as said below
- up_inverse: float32 [152, 152], replicated, may hold values from -0.5 to 0.5
- down_inverse: float32 [152, 152], replicated, may hold values from -0.5 to 0.5
- shift_up: float32 [8, 152, 152], replicated, may hold values from -0.15625 to 0.15625
- shift_down: float32 [8, 152, 152], replicated, may hold values from -0.5 to 0.5
- coarse: float32 [8, 152, 152], replicated, may hold values from -0.25 to 0.25
- translate: bfloat16 [316, 152, 152], replicated, may hold values from -0.0390625 to 0.0390625
Outputs:
- potential: float32 [2048, 32, 128], P('oct')
Inputs may be any that keep to these rules, and one draw needn't show every extreme that they name: `counts`: each leaf has 1 to 128 stations in use; the first leaf of every slab of 64 leaves is full. `ulist`: slot 0 holds the leaf itself; slots 1 to 8 hold -1 or leaves of the next lower slab of 64 leaves, slots 9 to 17 -1 or leaves of the leaf's own slab, slots 18 to 26 -1 or leaves of the next upper slab. `vlist`: every id is -1 or a node of the same slab of 8 nodes or of an adjacent one.
All inputs are finite; a program needn't handle non-finite values.
Results may differ from a plain program's by a relative error of at most 0.0017.
Values may be sent and summed in bfloat16 or wider, within the bound.
No kernel may reach another device: no remote copies, remote signals or barrier semaphores. Data moves between devices by JAX's collectives and lax.ppermute only.
A program may use at most 192 MiB of HBM per device.

v0:
```python
import jax
import jax.numpy as jnp
from jax import lax
from jax.sharding import PartitionSpec as P

HIGHEST = lax.Precision.HIGHEST


def extended(value, sides, width):
    for axis, dim in sides:
        count, length = (lax.axis_size(axis), value.shape[dim])
        up = [(i, (i + 1) % count) for i in range(count - 1)]
        down = [(j, i) for i, j in up]
        last = lax.slice_in_dim(value, length - width, length, axis=dim)
        first = lax.slice_in_dim(value, 0, width, axis=dim)
        before = lax.ppermute(last, axis, up)
        after = lax.ppermute(first, axis, down)
        value = jnp.concatenate([before, value, after], axis=dim)
    return value


def swapped(value, axis, bit):
    mask = 2**bit
    pairs = [(source, source ^ mask) for source in range(lax.axis_size(axis))]
    return lax.ppermute(value, axis, pairs)


def kernel(left_pts, right_pts):
    total_sq = jnp.zeros((left_pts.shape[1], right_pts.shape[1]), jnp.float32)
    for coord_index in range(3):
        offset = left_pts[coord_index][:, None] - right_pts[coord_index][None, :]
        total_sq = total_sq + offset * offset
    return jnp.exp(-0.5 * total_sq)


def near_field(target_pts, target_ids, source_base, flat_sources, q_width):
    source_count = flat_sources.shape[0]
    p_width = target_pts.shape[2]
    coord_len = 3 * p_width
    local_ids = target_ids - source_base
    usable = (target_ids >= 0) & (local_ids >= 0) & (local_ids < source_count)
    safe_ids = jnp.clip(local_ids, 0, source_count - 1)

    def one_leaf(leaf_pts, leaf_ids, leaf_usable):
        picked = flat_sources[leaf_ids]
        slot_count = picked.shape[0]
        src_pts = picked[:, :coord_len].reshape(slot_count, 3, p_width)
        weights = jnp.where(leaf_usable[:, None], picked[:, coord_len:], 0.0).reshape(
            slot_count, q_width, p_width
        )
        kernels = jax.vmap(kernel, in_axes=(0, None))(src_pts, leaf_pts)
        partial_sums = jnp.einsum(
            "sqp,spt->sqt", weights, kernels, precision=HIGHEST, preferred_element_type=jnp.float32
        )
        return jnp.sum(partial_sums, axis=0)

    def block_fn(block):
        return jax.vmap(one_leaf)(block[0], block[1], block[2])

    leaf_count = target_pts.shape[0]
    blocked = (
        target_pts.reshape((leaf_count // 4, 4) + target_pts.shape[1:]),
        safe_ids.reshape(leaf_count // 4, 4, -1),
        usable.reshape(leaf_count // 4, 4, -1),
    )
    result = lax.map(block_fn, blocked)
    return result.reshape(leaf_count, q_width, p_width)


def local(
    points,
    dens,
    surface,
    counts,
    ulist,
    vlist,
    up_inverse,
    down_inverse,
    shift_up,
    shift_down,
    coarse,
    translate,
):
    leaf_count, q_width, p_width = dens.shape
    eq_width = surface.shape[2]
    node_count = vlist.shape[0]
    index = lax.axis_index("oct")
    slots = jnp.arange(p_width)
    mask = (slots[None, :] < counts[:, None]).astype(jnp.float32)[:, None, :]
    masked = dens * mask
    own_sources = jnp.concatenate(
        [points.reshape(leaf_count, 3 * p_width), masked.reshape(leaf_count, q_width * p_width)],
        axis=1,
    )
    up_kernel = jax.vmap(kernel)(points, surface)
    check = jnp.einsum("lqp,lpe->lqe", masked, up_kernel, precision=HIGHEST)
    leaf_eq = jnp.dot(
        check.reshape(-1, eq_width),
        up_inverse,
        precision=HIGHEST,
        preferred_element_type=jnp.float32,
    ).reshape(leaf_count, q_width, eq_width)
    node_eq = jnp.einsum(
        "ncqe,cef->nqf", leaf_eq.reshape(-1, 8, q_width, eq_width), shift_up, precision=HIGHEST
    )
    node_send = node_eq.astype(jnp.bfloat16).reshape(node_count, q_width * eq_width)
    slab_eq = jnp.einsum("cqe,cef->qf", node_eq, shift_up, precision=HIGHEST)
    cycle = extended(node_send, (("oct", 0),), node_count)
    bit_count = lax.axis_size("oct").bit_length() - 1
    slab_local = jnp.zeros((q_width, eq_width), jnp.float32)
    current = slab_eq
    for level_start in range(0, bit_count, 3):
        width_bits = min(3, bit_count - level_start)
        child_slot = jnp.right_shift(index, level_start) & 7
        current = jnp.dot(
            current, shift_up[child_slot], precision=HIGHEST, preferred_element_type=jnp.float32
        )
        for bit_number in range(level_start, level_start + width_bits):
            current = current + swapped(current, "oct", bit_number)
        slab_local = slab_local + jnp.dot(
            current, coarse[child_slot], precision=HIGHEST, preferred_element_type=jnp.float32
        )
    cycle_rows = 3 * node_count
    cycle_view = cycle.reshape(cycle_rows, q_width, eq_width)
    cycle_base = (index - 1) * node_count
    local_ids = vlist - cycle_base
    usable = (vlist >= 0) & (local_ids >= 0) & (local_ids < cycle_rows)
    row_ids = jnp.arange(cycle_rows)
    type_block = translate.shape[0] // 4
    far_node = jnp.zeros((node_count * q_width, eq_width), jnp.float32)
    for block_index in range(4):
        lower_type = block_index * type_block
        block_ids = local_ids[:, lower_type : lower_type + type_block]
        block_usable = usable[:, lower_type : lower_type + type_block]
        selector = (
            (block_ids[:, :, None] == row_ids[None, None, :]) & block_usable[:, :, None]
        ).astype(jnp.bfloat16)
        picked = jnp.einsum(
            "ntm,mqe->nqte", selector, cycle_view, preferred_element_type=jnp.float32
        ).astype(jnp.bfloat16)
        picked = picked.reshape(node_count * q_width, type_block * eq_width)
        block_table = translate[lower_type : lower_type + type_block].reshape(
            type_block * eq_width, eq_width
        )
        far_node = far_node + jnp.dot(picked, block_table, preferred_element_type=jnp.float32)
    far_node = far_node.reshape(node_count, q_width, eq_width)
    parent_part = jnp.einsum("qe,cef->cqf", slab_local, shift_down, precision=HIGHEST)
    node_local = far_node + parent_part
    leaf_local = jnp.einsum("nqe,cef->ncqf", node_local, shift_down, precision=HIGHEST).reshape(
        leaf_count, q_width, eq_width
    )
    leaf_down = jnp.dot(
        leaf_local.reshape(-1, eq_width),
        down_inverse,
        precision=HIGHEST,
        preferred_element_type=jnp.float32,
    ).reshape(leaf_count, q_width, eq_width)
    far_pot = jnp.einsum("lqe,lpe->lqp", leaf_down, up_kernel, precision=HIGHEST)
    sources = extended(own_sources, (("oct", 0),), leaf_count)
    near_total = near_field(points, ulist, (index - 1) * leaf_count, sources, q_width)
    return (far_pot + near_total) * mask


def solution(mesh):
    placed = (
        P("oct", None, None),
        P("oct", None, None),
        P("oct", None, None),
        P("oct"),
        P("oct", None),
        P("oct", None),
        P(),
        P(),
        P(),
        P(),
        P(),
        P(),
    )
    return jax.shard_map(
        local, mesh=mesh, in_specs=placed, out_specs=P("oct", None, None), check_vma=False
    )
```

profile of v0, /device:TPU:1, one launch (start us, length us, event | category | flops | bytes accessed | tf_op | source)
XLA Modules:
  0.0 815.8 jit_solution(15750481546014870883)
XLA Ops:
  4.2 14.7 %fusion.14 = f32[64,32,152]{2,1,0:T(8,128)S(1)} fusion(f32[64,32,128]{2,1,0:T(8,128)S(1)} %broadcast_multiply_fusion, f32[64,152]{1,0:T(8,128)S(1)} %get-tuple-element.67, f32[64,128]{1,0:T(8,128)S(1)} %get-tuple-element.70, f32[64,152]{1,0:T(8,128)S(1)} %get-tuple-element.68, f32[64,128]{1,0:T(8,128)S(1)} %get-tuple-element.71, ...), kind=kOutput, calls=%fused_computation.21 | convolution fusion | flops 489357312 | bytes 2508800 | tf_op jit(solution)/shard_map/lqp,lpe->lqe/dot_general | solution.py:96
  43.1 22.3 %fusion.90 = (bf16[79,152,152]{0,2,1:T(8,128)(2,1)}, bf16[79,152,152]{0,2,1:T(8,128)(2,1)}, bf16[79,152,152]{0,2,1:T(8,128)(2,1)}, bf16[79,152,152]{0,2,1:T(8,128)(2,1)}) fusion(bf16[316,152,152]{0,2,1:T(8,128)(2,1)} %param.25), kind=kLoop, calls=%fused_computation.118 | loop fusion | bytes 29203456 | tf_op jit(solution)/shard_map/slice | solution.py:142
  76.9 11.7 %copy.32 = bf16[79,152,152]{1,0,2:T(8,128)(2,1)} copy(bf16[79,152,152]{0,2,1:T(8,128)(2,1)} %get-tuple-element.64) | data formatting | bytes 7300864 | tf_op jit(solution)/shard_map/slice | solution.py:142
  88.5 10.6 %reshape.132 = bf16[12008,152]{0,1:T(8,128)(2,1)} reshape(bf16[79,152,152]{1,0,2:T(8,128)(2,1)} %copy.32) | data formatting | bytes 7300864 | tf_op jit(solution)/shard_map/reshape | solution.py:142
  99.2 11.6 %copy.35 = bf16[79,152,152]{1,0,2:T(8,128)(2,1)} copy(bf16[79,152,152]{0,2,1:T(8,128)(2,1)} %get-tuple-element.63) | data formatting | bytes 7300864 | tf_op jit(solution)/shard_map/slice | solution.py:142
  110.8 10.7 %reshape.134 = bf16[12008,152]{0,1:T(8,128)(2,1)} reshape(bf16[79,152,152]{1,0,2:T(8,128)(2,1)} %copy.35) | data formatting | bytes 7300864 | tf_op jit(solution)/shard_map/reshape | solution.py:142
  121.5 11.6 %copy.38 = bf16[79,152,152]{1,0,2:T(8,128)(2,1)} copy(bf16[79,152,152]{0,2,1:T(8,128)(2,1)} %get-tuple-element.65) | data formatting | bytes 7300864 | tf_op jit(solution)/shard_map/slice | solution.py:142
  133.1 10.6 %reshape.136 = bf16[12008,152]{0,1:T(8,128)(2,1)} reshape(bf16[79,152,152]{1,0,2:T(8,128)(2,1)} %copy.38) | data formatting | bytes 7300864 | tf_op jit(solution)/shard_map/reshape | solution.py:142
  143.8 11.6 %copy.41 = bf16[79,152,152]{1,0,2:T(8,128)(2,1)} copy(bf16[79,152,152]{0,2,1:T(8,128)(2,1)} %get-tuple-element.62) | data formatting | bytes 7300864 | tf_op jit(solution)/shard_map/slice | solution.py:142
  155.4 10.8 %reshape.138 = bf16[12008,152]{0,1:T(8,128)(2,1)} reshape(bf16[79,152,152]{1,0,2:T(8,128)(2,1)} %copy.41) | data formatting | bytes 7300864 | tf_op jit(solution)/shard_map/reshape | solution.py:142
  177.5 15.3 %copy.31 = bf16[8,32,79,152]{3,2,1,0:T(8,128)(2,1)} copy(bf16[8,32,79,152]{2,3,0,1:T(8,128)(2,1)} %convert_bitcast_fusion.3) | data formatting | bytes 12296192 | tf_op jit(solution)/shard_map/convert_element_type | solution.py:140
  192.9 16.7 %reshape.131 = bf16[256,12008]{1,0:T(8,128)(2,1)} reshape(bf16[8,32,79,152]{3,2,1,0:T(8,128)(2,1)} %copy.31) | data formatting | bytes 12296192 | tf_op jit(solution)/shard_map/reshape | solution.py:141
  215.1 15.3 %copy.34 = bf16[8,32,79,152]{3,2,1,0:T(8,128)(2,1)} copy(bf16[8,32,79,152]{2,3,0,1:T(8,128)(2,1)} %convert_bitcast_fusion.2) | data formatting | bytes 12296192 | tf_op jit(solution)/shard_map/convert_element_type | solution.py:140
  230.4 16.8 %reshape.133 = bf16[256,12008]{1,0:T(8,128)(2,1)} reshape(bf16[8,32,79,152]{3,2,1,0:T(8,128)(2,1)} %copy.34) | data formatting | bytes 12296192 | tf_op jit(solution)/shard_map/reshape | solution.py:141
  252.8 15.3 %copy.37 = bf16[8,32,79,152]{3,2,1,0:T(8,128)(2,1)} copy(bf16[8,32,79,152]{2,3,0,1:T(8,128)(2,1)} %convert_bitcast_fusion.1) | data formatting | bytes 12296192 | tf_op jit(solution)/shard_map/convert_element_type | solution.py:140
  268.2 16.7 %reshape.135 = bf16[256,12008]{1,0:T(8,128)(2,1)} reshape(bf16[8,32,79,152]{3,2,1,0:T(8,128)(2,1)} %copy.37) | data formatting | bytes 12296192 | tf_op jit(solution)/shard_map/reshape | solution.py:141
  290.4 15.3 %copy.40 = bf16[8,32,79,152]{3,2,1,0:T(8,128)(2,1)} copy(bf16[8,32,79,152]{2,3,0,1:T(8,128)(2,1)} %convert_bitcast_fusion) | data formatting | bytes 12296192 | tf_op jit(solution)/shard_map/convert_element_type | solution.py:140
  305.7 17.0 %reshape.137 = bf16[256,12008]{1,0:T(8,128)(2,1)} reshape(bf16[8,32,79,152]{3,2,1,0:T(8,128)(2,1)} %copy.40) | data formatting | bytes 12296192 | tf_op jit(solution)/shard_map/reshape | solution.py:141
  349.3 455.8 %while.10 = (s32[]{:T(128)}, f32[16,4,32,128]{3,2,1,0:T(8,128)}, pred[16,4,27]{2,1,0:T(4,128)(4,1)S(1)}, s32[16,4,27]{2,1,0:T(4,128)}, f32[192,4480]{1,0:T(8,128)S(1)}, /*index=5*/f32[16,4,3,128]{3,1,0,2:T(4,128)}, s32[]{:T(128)}) while((s32[]{:T(128)}, f32[16,4,32,128]{3,2,1,0:T(8,128)}, pred[16,4,27]{2,1,0:T(4,128)(4,1)S(1)}, ...), condition=%wide.region_1.2_spmd, body=%wide.region_0.1_spmd.sunk | while | flops 695846208 | bytes 18517436 | solution.py:66
  367.8 10.3 %fusion.122 = f32[16,4,32,128]{3,2,1,0:T(8,128)} fusion(f32[16,4,32,128]{3,2,1,0:T(8,128)} %get-tuple-element.139, s32[]{:T(128)} %get-tuple-element.138, f32[4,27,32,128]{3,2,1,0:T(8,128)} %reshape.183, f32[4,128]{1,0:T(4,128)S(1)} %get-tuple-element.125, f32[4,27,128]{2,1,0:T(8,128)S(1)} %copy.99, f32[4,128]{1,0:T(4,128)S(1)} %get-tuple-element.127, ...), kind=kOutput, calls=%fused_computation.7.clone.1 | convolution fusion | flops 695402496 | bytes 2007552 | tf_op jit(solution)/shard_map/while/body/eval_jaxpr/vmap(sqp,spt->sqt)/dot_general | solution.py:52
  396.3 10.3 %fusion.122 = f32[16,4,32,128]{3,2,1,0:T(8,128)} fusion(f32[16,4,32,128]{3,2,1,0:T(8,128)} %get-tuple-element.139, s32[]{:T(128)} %get-tuple-element.138, f32[4,27,32,128]{3,2,1,0:T(8,128)} %reshape.183, f32[4,128]{1,0:T(4,128)S(1)} %get-tuple-element.125, f32[4,27,128]{2,1,0:T(8,128)S(1)} %copy.99, f32[4,128]{1,0:T(4,128)S(1)} %get-tuple-element.127, ...), kind=kOutput, calls=%fused_computation.7.clone.1 | convolution fusion | flops 695402496 | bytes 2007552 | tf_op jit(solution)/shard_map/while/body/eval_jaxpr/vmap(sqp,spt->sqt)/dot_general | solution.py:52
  453.2 10.3 %fusion.122 = f32[16,4,32,128]{3,2,1,0:T(8,128)} fusion(f32[16,4,32,128]{3,2,1,0:T(8,128)} %get-tuple-element.139, s32[]{:T(128)} %get-tuple-element.138, f32[4,27,32,128]{3,2,1,0:T(8,128)} %reshape.183, f32[4,128]{1,0:T(4,128)S(1)} %get-tuple-element.125, f32[4,27,128]{2,1,0:T(8,128)S(1)} %copy.99, f32[4,128]{1,0:T(4,128)S(1)} %get-tuple-element.127, ...), kind=kOutput, calls=%fused_computation.7.clone.1 | convolution fusion | flops 695402496 | bytes 2007552 | tf_op jit(solution)/shard_map/while/body/eval_jaxpr/vmap(sqp,spt->sqt)/dot_general | solution.py:52
  481.7 10.3 %fusion.122 = f32[16,4,32,128]{3,2,1,0:T(8,128)} fusion(f32[16,4,32,128]{3,2,1,0:T(8,128)} %get-tuple-element.139, s32[]{:T(128)} %get-tuple-element.138, f32[4,27,32,128]{3,2,1,0:T(8,128)} %reshape.183, f32[4,128]{1,0:T(4,128)S(1)} %get-tuple-element.125, f32[4,27,128]{2,1,0:T(8,128)S(1)} %copy.99, f32[4,128]{1,0:T(4,128)S(1)} %get-tuple-element.127, ...), kind=kOutput, calls=%fused_computation.7.clone.1 | convolution fusion | flops 695402496 | bytes 2007552 | tf_op jit(solution)/shard_map/while/body/eval_jaxpr/vmap(sqp,spt->sqt)/dot_general | solution.py:52
  510.1 10.3 %fusion.122 = f32[16,4,32,128]{3,2,1,0:T(8,128)} fusion(f32[16,4,32,128]{3,2,1,0:T(8,128)} %get-tuple-element.139, s32[]{:T(128)} %get-tuple-element.138, f32[4,27,32,128]{3,2,1,0:T(8,128)} %reshape.183, f32[4,128]{1,0:T(4,128)S(1)} %get-tuple-element.125, f32[4,27,128]{2,1,0:T(8,128)S(1)} %copy.99, f32[4,128]{1,0:T(4,128)S(1)} %get-tuple-element.127, ...), kind=kOutput, calls=%fused_computation.7.clone.1 | convolution fusion | flops 695402496 | bytes 2007552 | tf_op jit(solution)/shard_map/while/body/eval_jaxpr/vmap(sqp,spt->sqt)/dot_general | solution.py:52
  538.6 10.3 %fusion.122 = f32[16,4,32,128]{3,2,1,0:T(8,128)} fusion(f32[16,4,32,128]{3,2,1,0:T(8,128)} %get-tuple-element.139, s32[]{:T(128)} %get-tuple-element.138, f32[4,27,32,128]{3,2,1,0:T(8,128)} %reshape.183, f32[4,128]{1,0:T(4,128)S(1)} %get-tuple-element.125, f32[4,27,128]{2,1,0:T(8,128)S(1)} %copy.99, f32[4,128]{1,0:T(4,128)S(1)} %get-tuple-element.127, ...), kind=kOutput, calls=%fused_computation.7.clone.1 | convolution fusion | flops 695402496 | bytes 2007552 | tf_op jit(solution)/shard_map/while/body/eval_jaxpr/vmap(sqp,spt->sqt)/dot_general | solution.py:52
  595.5 10.3 %fusion.122 = f32[16,4,32,128]{3,2,1,0:T(8,128)} fusion(f32[16,4,32,128]{3,2,1,0:T(8,128)} %get-tuple-element.139, s32[]{:T(128)} %get-tuple-element.138, f32[4,27,32,128]{3,2,1,0:T(8,128)} %reshape.183, f32[4,128]{1,0:T(4,128)S(1)} %get-tuple-element.125, f32[4,27,128]{2,1,0:T(8,128)S(1)} %copy.99, f32[4,128]{1,0:T(4,128)S(1)} %get-tuple-element.127, ...), kind=kOutput, calls=%fused_computation.7.clone.1 | convolution fusion | flops 695402496 | bytes 2007552 | tf_op jit(solution)/shard_map/while/body/eval_jaxpr/vmap(sqp,spt->sqt)/dot_general | solution.py:52
  624.0 10.3 %fusion.122 = f32[16,4,32,128]{3,2,1,0:T(8,128)} fusion(f32[16,4,32,128]{3,2,1,0:T(8,128)} %get-tuple-element.139, s32[]{:T(128)} %get-tuple-element.138, f32[4,27,32,128]{3,2,1,0:T(8,128)} %reshape.183, f32[4,128]{1,0:T(4,128)S(1)} %get-tuple-element.125, f32[4,27,128]{2,1,0:T(8,128)S(1)} %copy.99, f32[4,128]{1,0:T(4,128)S(1)} %get-tuple-element.127, ...), kind=kOutput, calls=%fused_computation.7.clone.1 | convolution fusion | flops 695402496 | bytes 2007552 | tf_op jit(solution)/shard_map/while/body/eval_jaxpr/vmap(sqp,spt->sqt)/dot_general | solution.py:52
  652.5 10.3 %fusion.122 = f32[16,4,32,128]{3,2,1,0:T(8,128)} fusion(f32[16,4,32,128]{3,2,1,0:T(8,128)} %get-tuple-element.139, s32[]{:T(128)} %get-tuple-element.138, f32[4,27,32,128]{3,2,1,0:T(8,128)} %reshape.183, f32[4,128]{1,0:T(4,128)S(1)} %get-tuple-element.125, f32[4,27,128]{2,1,0:T(8,128)S(1)} %copy.99, f32[4,128]{1,0:T(4,128)S(1)} %get-tuple-element.127, ...), kind=kOutput, calls=%fused_computation.7.clone.1 | convolution fusion | flops 695402496 | bytes 2007552 | tf_op jit(solution)/shard_map/while/body/eval_jaxpr/vmap(sqp,spt->sqt)/dot_general | solution.py:52
  709.4 10.3 %fusion.122 = f32[16,4,32,128]{3,2,1,0:T(8,128)} fusion(f32[16,4,32,128]{3,2,1,0:T(8,128)} %get-tuple-element.139, s32[]{:T(128)} %get-tuple-element.138, f32[4,27,32,128]{3,2,1,0:T(8,128)} %reshape.183, f32[4,128]{1,0:T(4,128)S(1)} %get-tuple-element.125, f32[4,27,128]{2,1,0:T(8,128)S(1)} %copy.99, f32[4,128]{1,0:T(4,128)S(1)} %get-tuple-element.127, ...), kind=kOutput, calls=%fused_computation.7.clone.1 | convolution fusion | flops 695402496 | bytes 2007552 | tf_op jit(solution)/shard_map/while/body/eval_jaxpr/vmap(sqp,spt->sqt)/dot_general | solution.py:52
  737.9 10.3 %fusion.122 = f32[16,4,32,128]{3,2,1,0:T(8,128)} fusion(f32[16,4,32,128]{3,2,1,0:T(8,128)} %get-tuple-element.139, s32[]{:T(128)} %get-tuple-element.138, f32[4,27,32,128]{3,2,1,0:T(8,128)} %reshape.183, f32[4,128]{1,0:T(4,128)S(1)} %get-tuple-element.125, f32[4,27,128]{2,1,0:T(8,128)S(1)} %copy.99, f32[4,128]{1,0:T(4,128)S(1)} %get-tuple-element.127, ...), kind=kOutput, calls=%fused_computation.7.clone.1 | convolution fusion | flops 695402496 | bytes 2007552 | tf_op jit(solution)/shard_map/while/body/eval_jaxpr/vmap(sqp,spt->sqt)/dot_general | solution.py:52
  766.3 10.3 %fusion.122 = f32[16,4,32,128]{3,2,1,0:T(8,128)} fusion(f32[16,4,32,128]{3,2,1,0:T(8,128)} %get-tuple-element.139, s32[]{:T(128)} %get-tuple-element.138, f32[4,27,32,128]{3,2,1,0:T(8,128)} %reshape.183, f32[4,128]{1,0:T(4,128)S(1)} %get-tuple-element.125, f32[4,27,128]{2,1,0:T(8,128)S(1)} %copy.99, f32[4,128]{1,0:T(4,128)S(1)} %get-tuple-element.127, ...), kind=kOutput, calls=%fused_computation.7.clone.1 | convolution fusion | flops 695402496 | bytes 2007552 | tf_op jit(solution)/shard_map/while/body/eval_jaxpr/vmap(sqp,spt->sqt)/dot_general | solution.py:52
  794.8 10.3 %fusion.122 = f32[16,4,32,128]{3,2,1,0:T(8,128)} fusion(f32[16,4,32,128]{3,2,1,0:T(8,128)} %get-tuple-element.139, s32[]{:T(128)} %get-tuple-element.138, f32[4,27,32,128]{3,2,1,0:T(8,128)} %reshape.183, f32[4,128]{1,0:T(4,128)S(1)} %get-tuple-element.125, f32[4,27,128]{2,1,0:T(8,128)S(1)} %copy.99, f32[4,128]{1,0:T(4,128)S(1)} %get-tuple-element.127, ...), kind=kOutput, calls=%fused_computation.7.clone.1 | convolution fusion | flops 695402496 | bytes 2007552 | tf_op jit(solution)/shard_map/while/body/eval_jaxpr/vmap(sqp,spt->sqt)/dot_general | solution.py:52
  (386 shorter events, 425.1 us)
Async XLA Ops:
  0.0 341.3 %copy-start = (f32[8,152,152]{2,1,0:T(8,128)S(1)}, f32[8,152,152]{2,1,0:T(8,128)}, u32[]{:S(2)}) copy-start(f32[8,152,152]{2,1,0:T(8,128)} %param.23) | copy-start | bytes 2217988
  1.0 3.1 copy-start.12
  1.0 3.1 copy-start.14
  1.0 3.1 copy-start.15
  1.9 2.2 copy-start.17
  1.9 2.2 copy-start.18
  1.9 2.2 copy-start.19
  4.2 14.7 %copy-start.7 = (f32[152,152]{1,0:T(8,128)S(1)}, f32[152,152]{1,0:T(8,128)}, u32[]{:S(2)}) copy-start(f32[152,152]{1,0:T(8,128)} %param.20) | copy-start | bytes 277252
  18.9 1.9 copy-start.5
  25.3 144.1 %collective-permute-start = (bf16[8,4864]{1,0:T(8,128)(2,1)}, bf16[8,4864]{1,0:T(8,128)(2,1)}, u32[]{:S(2)}, u32[]{:S(2)}) collective-permute-start(bf16[8,4864]{1,0:T(8,128)(2,1)} %reshape.130), channel_id=1, source_target_pairs={{0,1},{1,2},{2,3},{3,4},{4,5},{5,6},{6,7},{7,8},{8,9},{9,10},{10,1... | collective-permute-start | bytes 233480 | tf_op jit(solution)/shard_map/ppermute | solution.py:16
  29.8 140.9 %collective-permute-start.1 = (bf16[8,4864]{1,0:T(8,128)(2,1)}, bf16[8,4864]{1,0:T(8,128)(2,1)}, u32[]{:S(2)}, u32[]{:S(2)}) collective-permute-start(bf16[8,4864]{1,0:T(8,128)(2,1)} %reshape.130), channel_id=1, source_target_pairs={{1,0},{2,1},{3,2},{4,3},{5,4},{6,5},{7,6},{8,7},{9,8},{10,9},{11,1... | collective-permute-start | bytes 233480 | tf_op jit(solution)/shard_map/ppermute | solution.py:17
  34.9 312.2 %collective-permute-start.7 = (f32[64,4480]{1,0:T(8,128)}, f32[64,4480]{1,0:T(8,128)}, u32[]{:S(2)}, u32[]{:S(2)}) collective-permute-start(f32[64,4480]{1,0:T(8,128)} %bitcast_dynamic-update-slice_fusion), channel_id=1, source_target_pairs={{0,1},{1,2},{2,3},{3,4},{4,5},{5,6},{6,7},{7,8},{8,9},{9,10},{10,1... | collective-permute-start | bytes 3440648 | tf_op jit(solution)/shard_map/ppermute | solution.py:16
  38.5 308.6 %collective-permute-start.8 = (f32[64,4480]{1,0:T(8,128)}, f32[64,4480]{1,0:T(8,128)}, u32[]{:S(2)}, u32[]{:S(2)}) collective-permute-start(f32[64,4480]{1,0:T(8,128)} %bitcast_dynamic-update-slice_fusion), channel_id=1, source_target_pairs={{1,0},{2,1},{3,2},{4,3},{5,4},{6,5},{7,6},{8,7},{9,8},{10,9},{11,1... | collective-permute-start | bytes 3440648 | tf_op jit(solution)/shard_map/ppermute | solution.py:17
  43.0 22.4 %collective-permute-start.2 = (f32[32,152]{1,0:T(8,128)S(1)}, f32[32,152]{1,0:T(8,128)S(1)}, u32[]{:S(2)}, u32[]{:S(2)}) collective-permute-start(f32[32,152]{1,0:T(8,128)S(1)} %fusion.53), channel_id=1, source_target_pairs={{0,1},{1,0},{2,3},{3,2},{4,5},{5,4},{6,7},{7,6},{8,9},{9,8},{10,11... | collective-permute-start | bytes 58376 | tf_op jit(solution)/shard_map/ppermute | solution.py:25
  43.1 22.3 %copy-start.16 = (s32[8,316]{1,0:T(8,128)S(1)}, s32[8,316]{1,0:T(8,128)}, u32[]{:S(2)}) copy-start(s32[8,316]{1,0:T(8,128)} %param.19) | copy-start | bytes 30340
  43.1 22.3 %copy-start.11 = (s32[64,27]{0,1:T(8,128)S(1)}, s32[64,27]{0,1:T(8,128)}, u32[]{:S(2)}) copy-start(s32[64,27]{0,1:T(8,128)} %param.18) | copy-start | bytes 20740
  65.4 3.5 collective-permute-start.3
  68.9 4.3 collective-permute-start.4
  73.4 93.6 %collective-permute-start.5 = (f32[32,152]{1,0:T(8,128)S(1)}, f32[32,152]{1,0:T(8,128)S(1)}, u32[]{:S(2)}, u32[]{:S(2)}) collective-permute-start(f32[32,152]{1,0:T(8,128)S(1)} %fusion.50), channel_id=1, source_target_pairs={{0,8},{1,9},{2,10},{3,11},{4,12},{5,13},{6,14},{7,15},{8,0},{9,1},... | collective-permute-start | bytes 58376 | tf_op jit(solution)/shard_map/ppermute | solution.py:25
  155.4 16.5 %copy-start.6 = (bf16[8,32,152]{2,1,0:T(8,128)(2,1)S(1)}, bf16[8,32,152]{2,1,0:T(8,128)(2,1)}, u32[]{:S(2)}) copy-start(bf16[8,32,152]{2,1,0:T(8,128)(2,1)} %get-tuple-element.80) | copy-start | bytes 233476
  167.1 172.0 %collective-permute-start.6 = (f32[32,152]{1,0:T(8,128)S(1)}, f32[32,152]{1,0:T(8,128)S(1)}, u32[]{:S(2)}, u32[]{:S(2)}) collective-permute-start(f32[32,152]{1,0:T(8,128)S(1)} %add.77), channel_id=1, source_target_pairs={{0,16},{1,17},{2,18},{3,19},{4,20},{5,21},{6,22},{7,23},{8,24},{9,... | collective-permute-start | bytes 58376 | tf_op jit(solution)/shard_map/ppermute | solution.py:25
  322.7 6.1 copy-start.2
  322.7 11.3 %slice-start = ((s8[6160384]{0:T(1024)(128)(4,1)}), s8[4194304]{0:T(1024)(128)(4,1)S(1)}, s32[]{:S(2)}) async-start(s8[6160384]{0:T(1024)(128)(4,1)} %bitcast.173), calls=%async_computation | async-start | bytes 8388608
  328.8 5.1 slice-start.1
  328.9 5.1 copy-start.3
  328.9 7.3 slice-start.2
  334.0 2.8 slice-start.3
  334.0 2.8 copy-start.4
  338.9 5.0 copy-start.8
  349.3 455.8 %copy-start.10 = (f32[64,128]{1,0:T(8,128)S(1)}, f32[64,128]{1,0:T(8,128)}, u32[]{:S(2)}) copy-start(f32[64,128]{1,0:T(8,128)} %copy-done.9) | copy-start | bytes 98308
  349.3 455.8 %copy-start.13 = (f32[64,152]{1,0:T(8,128)S(1)}, f32[64,152]{1,0:T(8,128)}, u32[]{:S(2)}) copy-start(f32[64,152]{1,0:T(8,128)} %copy-done.12) | copy-start | bytes 116740
  805.1 10.2 %copy-start.1 = (f32[8,152,152]{2,1,0:T(8,128)S(1)}, f32[8,152,152]{2,1,0:T(8,128)}, u32[]{:S(2)}) copy-start(f32[8,152,152]{2,1,0:T(8,128)} %param.23) | copy-start | bytes 2217988
  (1 other events, 1.5 us)
where the time goes:
time: 832 us; the launch traced here: 816 us
  local copies, waits for them, and re-layouts  479 us (58%)
  matrix products  242 us (29%)
  other arithmetic  66.6 us (8%)
  starting transfers between devices  23.5 us (3%)
    dot_general x16, matrix products, one_leaf(): jnp.einsum('sqp,spt->sqt', weights, kernels, precision=HIGHEST, preferred...  165 us
    gather x32, local copies, waits for them, and re-layouts, one_leaf(): picked = flat_sources[leaf_ids]  91.7 us
    slice x5, local copies, waits for them, and re-layouts, local(): translate[lower_type:lower_type + type_block]  68.8 us
    reshape x4, local copies, waits for them, and re-layouts, local(): picked = picked.reshape(node_count * q_width, type_block * eq_width)  67.2 us
    convert_element_type x4, local copies, waits for them, and re-layouts, local(): picked = jnp.einsum('ntm,mqe->nqte', selector, cycle_view, preferred_elem...  61.4 us
    select_n x16, other arithmetic, one_leaf(): jnp.where(leaf_usable[:, None], picked[:, coord_len:], 0.0)  51.2 us
    reshape x16, local copies, waits for them, and re-layouts, one_leaf(): jnp.where(leaf_usable[:, None], picked[:, coord_len:], 0.0)  47.2 us
    reshape x4, local copies, waits for them, and re-layouts, local(): translate[lower_type:lower_type + type_block]  42.8 us
  transfers between devices with their start and end apart: 9, of which 2 were waited for; matrix products, arithmetic and copies ran while one was open for 36% of the time, Pallas kernels for 0%

commit v1 on v0

v1 whole, which is shorter than its diff:
```python
import math

import jax
import jax.numpy as jnp
from jax import lax
from jax.experimental import pallas as pl
from jax.experimental.pallas import tpu as pltpu
from jax.sharding import PartitionSpec as P

F32 = jnp.float32
BF16 = jnp.bfloat16
HIGHEST = lax.Precision.HIGHEST
SCALE = math.sqrt(math.log2(math.e))
VMEM_LIMIT = 56 * 1024 * 1024
NT = (((1,), (1,)), ((), ()))
TN = (((0,), (0,)), ((), ()))
BLOCK = 256
UNROLL = 4
SOURCES = 32


def dot(left, right):
    return jnp.dot(left, right, preferred_element_type=F32)


def dot_nt(left, right):
    return lax.dot_general(left, right, NT, preferred_element_type=F32)


def dot_tn(left, right):
    return lax.dot_general(left, right, TN, preferred_element_type=F32)


def halves(value):
    high = value.astype(BF16)
    low = (value - high.astype(F32)).astype(BF16)
    return high, low


def dot3(left, right):
    left_high, left_low = halves(left)
    right_high, right_low = halves(right)
    return dot(left_high, right_high) + dot(left_high, right_low) + dot(left_low, right_high)


def iota(shape, dim):
    return lax.broadcasted_iota(jnp.int32, shape, dim)


def coords_of(ref, leaf):
    width = ref.shape[2]
    row = iota((8, width), 0)
    value = jnp.zeros((8, width), F32)
    for dim in range(3):
        line = jnp.broadcast_to(ref[dim, pl.ds(leaf, 1), :], (8, width))
        value = jnp.where(row == dim, line, value)
    return value


def pieces(coords):
    row = iota(coords.shape, 0)
    used = row < 3
    scaled = jnp.where(used, coords, 0.0) * SCALE
    high = scaled.astype(BF16).astype(F32)
    rest = scaled - high
    mid = rest.astype(BF16).astype(F32)
    low = (rest - mid).astype(BF16).astype(F32)
    norm = -0.5 * jnp.sum(scaled * scaled, axis=0, keepdims=True)
    norm_high = norm.astype(BF16).astype(F32)
    norm_rest = norm - norm_high
    norm_mid = norm_rest.astype(BF16).astype(F32)
    norm_low = norm_rest - norm_mid
    norms = jnp.where(row == 0, norm_high, jnp.where(row == 1, norm_mid, jnp.where(row == 2, norm_low, 0.0)))
    ones = jnp.where(used, 1.0, 0.0)
    return high, mid, low, norms, ones


def left_rows(parts):
    high, mid, low, norms, ones = parts
    return jnp.concatenate([high, high, mid, mid, high, low, ones, norms], axis=0)


def right_rows(parts):
    high, mid, low, norms, ones = parts
    return jnp.concatenate([high, mid, high, mid, low, high, norms, ones], axis=0)


def padded_left(parts):
    rows = left_rows(parts)
    return jnp.concatenate([jnp.zeros_like(rows), rows], axis=0).astype(BF16)


def packed_rows(weights, parts):
    weights_high = weights.astype(BF16).astype(F32)
    return jnp.concatenate([weights_high, weights - weights_high, right_rows(parts)], axis=0).astype(BF16)


def upward_kernel(
    points_ref, dens_ref, surface_ref, counts_ref, up_ref, shift_ref, pack_ref, target_ref, message_ref, send_ref,
    slab_ref, check_ref
):
    leaf_count, q_width, p_width = dens_ref.shape
    eq_width = surface_ref.shape[2]
    node_count = leaf_count // 8
    lane = iota((q_width, p_width), 1)
    row = iota((8, p_width), 0)

    def node_step(node, carry):
        for child in range(8):
            leaf = node * 8 + child
            count = counts_ref[leaf]
            weights = jnp.where(lane < count, dens_ref[leaf], 0.0)
            coords = coords_of(points_ref, leaf)
            message_ref[leaf, :q_width, :] = weights
            message_ref[leaf, q_width:, :] = jnp.where(row == 3, count.astype(F32), coords)
            parts = pieces(coords)
            rows = packed_rows(weights, parts)
            pack = rows.T
            pack_ref[leaf] = pack
            target_ref[leaf] = padded_left(parts).T
            values = jnp.exp2(dot(pack, padded_left(pieces(coords_of(surface_ref, leaf)))))
            values_high, values_low = halves(values)
            both = dot(rows[: 2 * q_width], values_high)
            check = both[:q_width] + both[q_width:] + dot(rows[:q_width], values_low)
            check_ref[child, pl.ds(pl.multiple_of(node * q_width, q_width), q_width), :] = check
        return carry

    lax.fori_loop(0, node_count, node_step, 0)

    def child_step(child, total):
        leaf_eq = dot3(check_ref[child], up_ref[...])
        return total + dot3(leaf_eq, shift_ref[child])

    node_eq = lax.fori_loop(0, 8, child_step, jnp.zeros((node_count * q_width, eq_width), F32))
    send_ref[: node_count * q_width, :] = node_eq.astype(BF16)
    slab_eq = jnp.zeros((q_width, eq_width), F32)
    for child in range(8):
        slab_eq = slab_eq + dot3(node_eq[child * q_width : (child + 1) * q_width], shift_ref[child])
    index = lax.axis_index("oct")
    slab = dot3(slab_eq, shift_ref[index & 7])
    slab_ref[...] = slab
    high, rest = halves(slab)
    low = (slab - high.astype(F32) - rest.astype(F32)).astype(BF16)
    for place, part in enumerate((high, rest, low)):
        start = node_count * q_width + place * q_width
        send_ref[start : start + q_width, :] = part


def far_kernel(lower_ref, own_ref, upper_ref, vlist_ref, table_hbm, out_ref, table_ref, wide_ref, total_ref, sems):
    node_count, type_count = vlist_ref.shape
    eq_width = own_ref.shape[1]
    q_width = out_ref.shape[0] // node_count
    lanes = node_count * q_width
    chunk = 8
    chunk_count = eq_width // chunk

    def copy_of(number):
        span = pl.ds(number * chunk, chunk)
        return pltpu.make_async_copy(table_hbm.at[span], table_ref.at[span], sems.at[number])

    for number in range(chunk_count):
        copy_of(number).start()

    index = lax.axis_index("oct")
    tile = 128 // q_width
    repeat = (iota((q_width, 128), 1) % q_width == iota((q_width, 128), 0)).astype(BF16)
    for part, source in enumerate((lower_ref, own_ref, upper_ref)):
        for node in range(node_count):
            spread = dot_tn(source[node * q_width : (node + 1) * q_width, :], repeat)
            wide_ref[pl.ds(part * node_count + node, eq_width, stride=SOURCES), :] = spread
    for place in range(3 * node_count, SOURCES):
        wide_ref[pl.ds(place, eq_width, stride=SOURCES), :] = jnp.zeros((eq_width, 128), F32)

    ids = vlist_ref[...]
    places = jnp.where(ids >= 0, ids - (index - 1) * node_count, -1).astype(F32).astype(BF16)
    spread = (iota((node_count, lanes), 1) // SOURCES == iota((node_count, lanes), 0)).astype(BF16)
    wanted = dot_tn(places, spread)
    chosen = (wanted == (iota((type_count, lanes), 1) % SOURCES).astype(F32)).astype(BF16)
    lane_node = iota((SOURCES, 128), 1) // q_width
    nothing = jnp.zeros((SOURCES, 128), F32)
    total_ref[...] = jnp.zeros_like(total_ref)

    def chunk_step(number, carry):
        copy_of(number).wait()
        total = jnp.zeros((eq_width, lanes), F32)
        for step in range(chunk):
            row = number * chunk + step
            summed = dot(table_ref[row], chosen)
            high = summed.astype(BF16).astype(F32)
            both = jnp.concatenate([high, summed - high], axis=0).astype(BF16)
            sent = wide_ref[pl.ds(pl.multiple_of(row * SOURCES, SOURCES), SOURCES), :]
            parts = [jnp.where(lane_node == place, sent, 0.0) for place in range(tile)]
            blocks = []
            for node in range(node_count):
                line = [parts[node % tile] if place == node // tile else nothing for place in range(node_count // tile)]
                blocks.append(jnp.concatenate(line, axis=1))
            product = dot(both, jnp.concatenate(blocks, axis=0).astype(BF16))
            total = total + product[:eq_width] + product[eq_width:]
        total_ref[...] += total
        return carry

    lax.fori_loop(0, chunk_count, chunk_step, 0)
    out_ref[...] = total_ref[...].T


def near_kernel(sides, ulist_ref, counts_ref, pack_ref, target_ref, out_ref, gather_ref, value_ref, total_ref, owner_ref):
    leaf_count, q_width, p_width = out_ref.shape
    slot_count = sum(end - first for first, end, _, _ in sides)
    index = lax.axis_index("oct")

    def gather(leaf, member, block):
        offset = block * BLOCK
        for first, end, slab, start in sides:
            base = (index + slab) * leaf_count - start
            for slot in range(first, end):
                leaf_id = ulist_ref[slot, leaf]
                place = jnp.where(leaf_id >= 0, leaf_id - base, start)
                length = jnp.where(leaf_id >= 0, jnp.bitwise_and(counts_ref[place] + 15, -16), 0)
                gather_ref[pl.ds(pl.multiple_of(offset, 16), p_width), :] = pack_ref[place]
                offset = offset + length
        gather_ref[pl.ds(pl.multiple_of(offset, 16), BLOCK), :] = jnp.zeros((BLOCK, 128), BF16)
        for number in range(-(-slot_count * p_width // BLOCK)):
            owner_ref[UNROLL + block + number] = member
        return lax.div(offset + (BLOCK - 1), BLOCK)

    for number in range(UNROLL):
        owner_ref[number] = 8

    def group_step(group, carry):
        block_count = lax.fori_loop(0, 8, lambda member, block: gather(group * 8 + member, member, block), 0)
        for number in range(2 * UNROLL):
            owner_ref[UNROLL + block_count + number] = 8
        total_ref[...] = jnp.zeros_like(total_ref)

        def sources_of(block):
            return gather_ref[pl.ds(pl.multiple_of(block * BLOCK, BLOCK), BLOCK), :]

        def blocks_step(step, inner):
            slot = jnp.bitwise_and(step, 1) * UNROLL
            for part in range(UNROLL):
                block = jnp.maximum(step - 1, 0) * UNROLL + part
                member = owner_ref[step * UNROLL + part]
                total_ref[member] += dot(value_ref[UNROLL - slot + part], sources_of(block))
            for part in range(UNROLL):
                block = step * UNROLL + part
                member = owner_ref[UNROLL + block]
                targets = target_ref[group * 8 + jnp.minimum(member, 7)]
                value_ref[slot + part] = jnp.exp2(dot_nt(targets, sources_of(block))).astype(BF16)
            return inner

        lax.fori_loop(0, lax.div(block_count + (2 * UNROLL - 1), UNROLL), blocks_step, 0)

        for member in range(8):
            turned = total_ref[member].T
            out_ref[group * 8 + member] = turned[:q_width] + turned[q_width : 2 * q_width]
        return carry

    lax.fori_loop(0, leaf_count // 8, group_step, 0)


def near_call(sides, ulist, counts, pack, targets, q_width, name):
    leaf_count, p_width = targets.shape[:2]
    slot_count = sum(end - first for first, end, _, _ in sides)
    member_blocks = -(-slot_count * p_width // BLOCK)
    vmem = pl.BlockSpec(memory_space=pltpu.VMEM)
    smem = pl.BlockSpec(memory_space=pltpu.SMEM)
    return pl.pallas_call(
        lambda *refs: near_kernel(sides, *refs),
        out_shape=jax.ShapeDtypeStruct((leaf_count, q_width, p_width), F32),
        in_specs=[smem, smem, vmem, vmem],
        out_specs=vmem,
        scratch_shapes=[
            pltpu.VMEM(((8 * member_blocks + 2 * UNROLL + 2) * BLOCK, 128), BF16),
            pltpu.VMEM((2 * UNROLL, p_width, BLOCK), BF16),
            pltpu.VMEM((9, p_width, 128), F32),
            pltpu.SMEM((9 * member_blocks + 4 * UNROLL,), jnp.int32),
        ],
        compiler_params=pltpu.CompilerParams(vmem_limit_bytes=VMEM_LIMIT),
        name=name,
    )(ulist, counts, pack, targets)


def pack_kernel(lower_ref, upper_ref, sum_ref, pair_ref, shift_ref, pack_ref, counts_ref, top_ref, next_ref):
    leaf_count, rows, p_width = lower_ref.shape
    q_width = rows - 8
    index = lax.axis_index("oct")
    top = sum_ref[...] + pair_ref[...]
    top_ref[...] = top
    next_ref[...] = dot3(top, shift_ref[jnp.right_shift(index, 3) & 7])
    lane = iota((1, p_width), 1)

    def pack_step(step, counts):
        lower_counts, upper_counts = counts
        for part in range(4):
            leaf = step * 4 + part
            for side, source in ((0, lower_ref), (1, upper_ref)):
                packed = packed_rows(source[leaf, :q_width, :], pieces(source[leaf, q_width:, :]))
                pack_ref[side * leaf_count + leaf] = packed.T
            lower_counts = jnp.where(lane == leaf, lower_ref[leaf, q_width + 3 : q_width + 4, :], lower_counts)
            upper_counts = jnp.where(lane == leaf, upper_ref[leaf, q_width + 3 : q_width + 4, :], upper_counts)
        return lower_counts, upper_counts

    nothing = jnp.zeros((1, p_width), F32)
    lower_counts, upper_counts = lax.fori_loop(0, leaf_count // 4, pack_step, (nothing, nothing))
    counts_ref[0:1, :] = lower_counts.astype(jnp.int32)
    counts_ref[1:2, :] = upper_counts.astype(jnp.int32)


def final_kernel(
    level_count, pack_ref, surface_ref, counts_ref, own_near_ref, side_near_ref, far_ref, coarse_ref, shift_ref,
    down_ref, *rest
):
    top_refs, (out_ref, node_ref, down_leaf_ref) = rest[:level_count], rest[level_count:]
    leaf_count, q_width, p_width = out_ref.shape
    eq_width = far_ref.shape[1]
    node_count = leaf_count // 8
    index = lax.axis_index("oct")
    slab_local = jnp.zeros((q_width, eq_width), F32)
    for level, top_ref in enumerate(top_refs):
        slab_local = slab_local + dot3(top_ref[...], coarse_ref[jnp.right_shift(index, 3 * level) & 7])
    for node in range(node_count):
        rows = slice(node * q_width, (node + 1) * q_width)
        node_ref[rows, :] = far_ref[rows, :] + dot3(slab_local, shift_ref[node])

    def child_step(child, carry):
        down_leaf_ref[child] = dot3(dot3(node_ref[...], shift_ref[child]), down_ref[...])
        return carry

    lax.fori_loop(0, 8, child_step, 0)
    lane = iota((q_width, p_width), 1)

    def node_step(node, carry):
        for child in range(8):
            leaf = node * 8 + child
            values = jnp.exp2(dot(pack_ref[leaf], padded_left(pieces(coords_of(surface_ref, leaf)))))
            values_high, values_low = halves(values)
            down = down_leaf_ref[child, pl.ds(pl.multiple_of(node * q_width, q_width), q_width), :]
            down_high = down.astype(BF16).astype(F32)
            empty = jnp.zeros((128 - 2 * q_width, eq_width), F32)
            down_rows = jnp.concatenate([down_high, down - down_high, empty], axis=0).astype(BF16)
            down_first = jnp.concatenate([down_high, jnp.zeros_like(down_high), empty], axis=0).astype(BF16)
            turned = (dot_nt(values_high, down_rows) + dot_nt(values_low, down_first)).T
            summed = turned[:q_width] + turned[q_width : 2 * q_width] + own_near_ref[leaf] + side_near_ref[leaf]
            out_ref[leaf] = jnp.where(lane < counts_ref[leaf], summed, 0.0)
        return carry

    lax.fori_loop(0, node_count, node_step, 0)


def shifted(value, size):
    up = [(i, i + 1) for i in range(size - 1)]
    down = [(j, i) for i, j in up]
    return lax.ppermute(value, "oct", up), lax.ppermute(value, "oct", down)


def swapped(value, size, bit):
    return lax.ppermute(value, "oct", [(source, source ^ (1 << bit)) for source in range(size)])


def local(
    points,
    dens,
    surface,
    counts,
    ulist,
    vlist,
    up_inverse,
    down_inverse,
    shift_up,
    shift_down,
    coarse,
    translate,
):
    leaf_count, q_width, p_width = dens.shape
    eq_width = surface.shape[2]
    node_count, type_count = vlist.shape
    node_rows = node_count * q_width
    size = lax.axis_size("oct")
    bits = size.bit_length() - 1
    index = lax.axis_index("oct")
    vmem = pl.BlockSpec(memory_space=pltpu.VMEM)
    smem = pl.BlockSpec(memory_space=pltpu.SMEM)
    hbm = pl.BlockSpec(memory_space=pl.ANY)
    params = pltpu.CompilerParams(vmem_limit_bytes=VMEM_LIMIT)
    points = jnp.transpose(points, (1, 0, 2))
    surface = jnp.transpose(surface, (1, 0, 2))
    ulist = ulist.T
    table = jnp.transpose(translate, (1, 2, 0))

    pack, targets, message, send, slab = pl.pallas_call(
        upward_kernel,
        out_shape=(
            jax.ShapeDtypeStruct((leaf_count, p_width, 128), BF16),
            jax.ShapeDtypeStruct((leaf_count, p_width, 128), BF16),
            jax.ShapeDtypeStruct((leaf_count, q_width + 8, p_width), F32),
            jax.ShapeDtypeStruct((node_rows + 3 * q_width, eq_width), BF16),
            jax.ShapeDtypeStruct((q_width, eq_width), F32),
        ),
        in_specs=[vmem, vmem, vmem, smem, vmem, vmem],
        out_specs=(vmem,) * 5,
        scratch_shapes=[pltpu.VMEM((8, node_rows, eq_width), F32)],
        compiler_params=params,
        name="upward",
    )(points, dens, surface, counts, up_inverse, shift_up)

    send_lower, send_upper = shifted(send, size)
    lower, upper = shifted(message, size)

    partner = jnp.where(index & 1 == 1, send_lower[node_rows:], send_upper[node_rows:]).astype(F32)
    total = slab + (partner[:q_width] + partner[q_width : 2 * q_width] + partner[2 * q_width :])
    total = total + swapped(total, size, 1)
    pair = swapped(total, size, 2)

    near_own = near_call(
        ((0, 1, 0, 0), (9, 18, 0, 0)), ulist, counts, pack, targets, q_width, "near_own"
    )

    far_node = pl.pallas_call(
        far_kernel,
        out_shape=jax.ShapeDtypeStruct((node_rows, eq_width), F32),
        in_specs=[vmem, vmem, vmem, vmem, hbm],
        out_specs=vmem,
        scratch_shapes=[
            pltpu.VMEM((eq_width, eq_width, type_count), BF16),
            pltpu.VMEM((eq_width * SOURCES, 128), F32),
            pltpu.VMEM((eq_width, node_rows), F32),
            pltpu.SemaphoreType.DMA((eq_width // 8,)),
        ],
        compiler_params=params,
        name="far",
    )(send_lower, send, send_upper, vlist, table)

    side_pack, side_counts, top, current = pl.pallas_call(
        pack_kernel,
        out_shape=(
            jax.ShapeDtypeStruct((2 * leaf_count, p_width, 128), BF16),
            jax.ShapeDtypeStruct((2, p_width), jnp.int32),
            jax.ShapeDtypeStruct((q_width, eq_width), F32),
            jax.ShapeDtypeStruct((q_width, eq_width), F32),
        ),
        in_specs=[vmem] * 5,
        out_specs=(vmem,) * 4,
        compiler_params=params,
        name="pack",
    )(lower, upper, total, pair, shift_up)

    tops = [top]
    for level in range(3, bits, 3):
        if level > 3:
            current = jnp.dot(current, shift_up[jnp.right_shift(index, level) & 7], precision=HIGHEST)
        for bit in range(level, min(level + 3, bits)):
            current = current + swapped(current, size, bit)
        tops.append(current)

    side_counts = side_counts[:, :leaf_count].reshape(-1)
    near_side = near_call(
        ((1, 9, -1, 0), (18, 27, 1, leaf_count)), ulist, side_counts, side_pack, targets, q_width, "near_side"
    )

    return pl.pallas_call(
        lambda *refs: final_kernel(len(tops), *refs),
        out_shape=jax.ShapeDtypeStruct((leaf_count, q_width, p_width), F32),
        in_specs=[vmem, vmem, smem] + [vmem] * (6 + len(tops)),
        out_specs=vmem,
        scratch_shapes=[
            pltpu.VMEM((node_rows, eq_width), F32),
            pltpu.VMEM((8, node_rows, eq_width), F32),
        ],
        compiler_params=params,
        name="final",
    )(pack, surface, counts, near_own, near_side, far_node, coarse, shift_down, down_inverse, *tops)


def solution(mesh):
    placed = (
        P("oct", None, None),
        P("oct", None, None),
        P("oct", None, None),
        P("oct"),
        P("oct", None),
        P("oct", None),
        P(),
        P(),
        P(),
        P(),
        P(),
        P(),
    )
    return jax.shard_map(
        local, mesh=mesh, in_specs=placed, out_specs=P("oct", None, None), check_vma=False
    )
```

time: 832 us -> 202 us (0.24)
  the two profiles are of different devices: /device:TPU:1 before, /device:TPU:4 now
where the time goes in v1:
time: 202 us; the launch traced here: 199 us
  Pallas kernels  143 us (71%)
  waiting for transfers between devices  33.8 us (17%)
  starting transfers between devices  17.1 us (8%)
  local copies, waits for them, and re-layouts  2.77 us (1%)
  other arithmetic  2.22 us (1%)
    pallas_call x2, Pallas kernels, near_call(): pl.pallas_call(lambda *refs: near_kernel(sides, *refs), out_shape=jax.Sha...  61 us
    pallas_call x1, Pallas kernels, local(): pl.pallas_call(far_kernel, out_shape=jax.ShapeDtypeStruct((node_rows, eq_...  44.4 us
    ppermute x4, waiting for transfers between devices, shifted(): return (lax.ppermute(value, 'oct', up), lax.ppermute(value, 'oct', down))  23.6 us
    pallas_call x1, Pallas kernels, local(): pl.pallas_call(lambda *refs: final_kernel(len(tops), *refs), out_shape=ja...  18.2 us
    pallas_call x1, Pallas kernels, local(): pl.pallas_call(upward_kernel, out_shape=(jax.ShapeDtypeStruct((leaf_count...  13.4 us
    ppermute x4, starting transfers between devices, shifted(): return (lax.ppermute(value, 'oct', up), lax.ppermute(value, 'oct', down))  12.9 us
    ppermute x4, waiting for transfers between devices, swapped(): lax.ppermute(value, 'oct', [(source, source ^ 1 << bit) for source in ran...  10.2 us
    pallas_call x1, Pallas kernels, local(): pl.pallas_call(pack_kernel, out_shape=(jax.ShapeDtypeStruct((2 * leaf_cou...  6.4 us
  transfers between devices with their start and end apart: 8, of which 5 were waited for; matrix products, arithmetic and copies ran while one was open for 1% of the time, Pallas kernels for 53%

profile of v1, /device:TPU:4, one launch (start us, length us, event | category | flops | bytes accessed | tf_op | source)
XLA Modules:
  0.0 199.4 jit_solution(16722860315229377057)
XLA Ops:
  0.0 13.4 %upward.1 = (bf16[64,128,128]{2,1,0:T(8,128)(2,1)}, bf16[64,128,128]{2,1,0:T(8,128)(2,1)}, f32[64,40,128]{2,1,0:T(8,128)}, bf16[352,152]{1,0:T(8,128)(2,1)}, f32[32,152]{1,0:T(8,128)}) custom-call(f32[3,64,128]{2,1,0:T(8,128)} %bitcast.8, f32[64,32,128]{2,1,0:T(8,128)} %dens_ref.1, f32[3,64,152]{2,1,0:T(8,128)} %bitcast.6, s32[64]{0:T(128)} %refs_2_.1, ...), custom_call_target="tpu_custom_call" | custom-call | tf_op jit(solution)/shard_map/upward/pallas_call | solution.py:390
  13.4 1.9 collective-permute-start
  15.3 4.5 %collective-permute-start.1 = (f32[64,40,128]{2,1,0:T(8,128)}, f32[64,40,128]{2,1,0:T(8,128)S(1)}, u32[]{:S(2)}, u32[]{:S(2)}) collective-permute-start(f32[64,40,128]{2,1,0:T(8,128)} %get-tuple-element.16), channel_id=1, source_target_pairs={{1,0},{2,1},{3,2},{4,3},{5,4},{6,5},{7,6},{8,7},{9,8},{10,9},{11,1... | collective-permute-start | bytes 3932168 | tf_op jit(solution)/shard_map/ppermute | solution.py:353
  19.9 1.9 collective-permute-start.2
  21.8 4.5 %collective-permute-start.3 = (bf16[352,152]{1,0:T(8,128)(2,1)}, bf16[352,152]{1,0:T(8,128)(2,1)S(1)}, u32[]{:S(2)}, u32[]{:S(2)}) collective-permute-start(bf16[352,152]{1,0:T(8,128)(2,1)} %get-tuple-element.18.own_ref), channel_id=1, source_target_pairs={{1,0},{2,1},{3,2},{4,3},{5,4},{6,5},{7,6},{8,7},{9,8},{10,9},{11,1... | collective-permute-start | bytes 321032 | tf_op jit(solution)/shard_map/ppermute | solution.py:353
  26.4 22.2 %collective-permute-done.2.lower_ref = bf16[352,152]{1,0:T(8,128)(2,1)S(1)} collective-permute-done((bf16[352,152]{1,0:T(8,128)(2,1)}, bf16[352,152]{1,0:T(8,128)(2,1)S(1)}, u32[]{:S(2)}, u32[]{:S(2)}) %collective-permute-start.2) | collective-permute-done | bytes 107040 | tf_op jit(solution)/shard_map/ppermute | solution.py:353
  48.5 1.4 collective-permute-done.3.upper_ref
  49.9 0.8 fusion.1
  50.8 0.1 collective-permute-start.4
  50.8 3.9 %collective-permute-done.4 = f32[32,152]{1,0:T(8,128)S(1)} collective-permute-done((f32[32,152]{1,0:T(8,128)S(1)}, f32[32,152]{1,0:T(8,128)S(1)}, u32[]{:S(2)}, u32[]{:S(2)}) %collective-permute-start.4) | collective-permute-done | bytes 19488 | tf_op jit(solution)/shard_map/ppermute | solution.py:357
  54.8 0.6 collective-permute-start.5
  55.3 3.4 %collective-permute-done.5.pair_ref = f32[32,152]{1,0:T(8,128)S(1)} collective-permute-done((f32[32,152]{1,0:T(8,128)S(1)}, f32[32,152]{1,0:T(8,128)S(1)}, u32[]{:S(2)}, u32[]{:S(2)}) %collective-permute-start.5) | collective-permute-done | bytes 19488 | tf_op jit(solution)/shard_map/ppermute | solution.py:357
  58.7 0.0 collective-permute-done.lower_ref
  58.7 0.0 collective-permute-done.1.upper_ref
  58.8 0.0 copy-done.4
  58.8 0.6 copy-done.5
  59.3 0.5 copy-done
  59.9 1.0 copy-done.1
  60.9 6.4 %pack.1 = (bf16[128,128,128]{2,1,0:T(8,128)(2,1)}, s32[2,128]{1,0:T(2,128)}, f32[32,152]{1,0:T(8,128)}, f32[32,152]{1,0:T(8,128)}) custom-call(f32[64,40,128]{2,1,0:T(8,128)} %copy-done, f32[64,40,128]{2,1,0:T(8,128)} %copy-done.1, f32[32,152]{1,0:T(8,128)} %copy-done.4, f32[32,152]{1,0:T(8,128)} %copy-done.5, f32[8,152,152]{2,1,0:T(8,128)} %shift_ref.3), custom_call_target="tpu_custom_call" | custom-call | tf_op jit(solution)/shard_map/pack/pallas_call | solution.py:433
  67.3 0.0 copy-done.3
  67.3 1.3 collective-permute-start.6
  68.6 2.9 %collective-permute-done.6 = f32[32,152]{1,0:T(8,128)S(1)} collective-permute-done((f32[32,152]{1,0:T(8,128)}, f32[32,152]{1,0:T(8,128)S(1)}, u32[]{:S(2)}, u32[]{:S(2)}) %collective-permute-start.6) | collective-permute-done | bytes 19488 | tf_op jit(solution)/shard_map/ppermute | solution.py:357
  71.5 0.8 add.22
  72.3 2.2 %collective-permute-start.7 = (f32[32,152]{1,0:T(8,128)S(1)}, f32[32,152]{1,0:T(8,128)S(1)}, u32[]{:S(2)}, u32[]{:S(2)}) collective-permute-start(f32[32,152]{1,0:T(8,128)S(1)} %add.22), channel_id=1, source_target_pairs={{0,16},{1,17},{2,18},{3,19},{4,20},{5,21},{6,22},{7,23},{8,24},{9,... | collective-permute-start | bytes 58376 | tf_op jit(solution)/shard_map/ppermute | solution.py:357
  74.5 27.6 %near_own.1.refs_3_ = f32[64,32,128]{2,1,0:T(8,128)} custom-call(s32[27,64]{1,0:T(8,128)} %bitcast.9, s32[64]{0:T(128)} %refs_2_.1, bf16[64,128,128]{2,1,0:T(8,128)(2,1)} %get-tuple-element.14.refs_2_.refs_0_, bf16[64,128,128]{2,1,0:T(8,128)(2,1)} %get-tuple-element.15.refs_3_), custom_call_target="tpu_custom_call" | custom-call | tf_op jit(solution)/shard_map/near_own/pallas_call | solution.py:267
  102.1 44.4 %far.1.refs_5_ = f32[256,152]{1,0:T(8,128)} custom-call(bf16[352,152]{1,0:T(8,128)(2,1)} %copy-done.2, bf16[352,152]{1,0:T(8,128)(2,1)} %get-tuple-element.18.own_ref, bf16[352,152]{1,0:T(8,128)(2,1)} %copy-done.3, s32[8,316]{1,0:T(8,128)} %vlist_ref.1, bf16[152,152,316]{2,1,0:T(8,128)(2,1)} %bitcast.5), custom_call_target="tpu_custom_call" | custom-call | tf_op jit(solution)/shard_map/far/pallas_call | solution.py:418
  146.5 0.0 copy-done.6
  146.5 0.6 reshape.3.refs_1_
  147.1 33.5 %near_side.1.refs_4_ = f32[64,32,128]{2,1,0:T(8,128)} custom-call(s32[27,64]{1,0:T(8,128)} %bitcast.10, s32[128]{0:T(128)} %reshape.3.refs_1_, bf16[128,128,128]{2,1,0:T(8,128)(2,1)} %get-tuple-element.20.refs_2_, bf16[64,128,128]{2,1,0:T(8,128)(2,1)} %get-tuple-element.15.refs_3_), custom_call_target="tpu_custom_call" | custom-call | tf_op jit(solution)/shard_map/near_side/pallas_call | solution.py:267
  180.6 0.0 collective-permute-done.7
  180.6 0.6 add.23.refs_10_
  181.2 18.2 %final.1 = f32[64,32,128]{2,1,0:T(8,128)} custom-call(bf16[64,128,128]{2,1,0:T(8,128)(2,1)} %get-tuple-element.14.refs_2_.refs_0_, f32[3,64,152]{2,1,0:T(8,128)} %bitcast.7, s32[64]{0:T(128)} %refs_2_.1, f32[64,32,128]{2,1,0:T(8,128)} %near_own.1.refs_3_, f32[64,32,128]{2,1,0:T(8,128)} %near_side.1.refs_4_, f32[256,152]{1,0:T(8,128)} %far.1.refs_5_, ...), custom_call_target="tpu_custom_call" | custom-call | tf_op jit(solution)/shard_map/final/pallas_call | solution.py:460
  (10 shorter events, 0.0 us)
Async XLA Ops:
  13.4 45.3 %collective-permute-start = (f32[64,40,128]{2,1,0:T(8,128)}, f32[64,40,128]{2,1,0:T(8,128)S(1)}, u32[]{:S(2)}, u32[]{:S(2)}) collective-permute-start(f32[64,40,128]{2,1,0:T(8,128)} %get-tuple-element.16), channel_id=1, source_target_pairs={{0,1},{1,2},{2,3},{3,4},{4,5},{5,6},{6,7},{7,8},{8,9},{9,10},{10,1... | collective-permute-start | bytes 3932168 | tf_op jit(solution)/shard_map/ppermute | solution.py:353
  15.3 43.4 %collective-permute-start.1 = (f32[64,40,128]{2,1,0:T(8,128)}, f32[64,40,128]{2,1,0:T(8,128)S(1)}, u32[]{:S(2)}, u32[]{:S(2)}) collective-permute-start(f32[64,40,128]{2,1,0:T(8,128)} %get-tuple-element.16), channel_id=1, source_target_pairs={{1,0},{2,1},{3,2},{4,3},{5,4},{6,5},{7,6},{8,7},{9,8},{10,9},{11,1... | collective-permute-start | bytes 3932168 | tf_op jit(solution)/shard_map/ppermute | solution.py:353
  19.9 28.7 %collective-permute-start.2 = (bf16[352,152]{1,0:T(8,128)(2,1)}, bf16[352,152]{1,0:T(8,128)(2,1)S(1)}, u32[]{:S(2)}, u32[]{:S(2)}) collective-permute-start(bf16[352,152]{1,0:T(8,128)(2,1)} %get-tuple-element.18.own_ref), channel_id=1, source_target_pairs={{0,1},{1,2},{2,3},{3,4},{4,5},{5,6},{6,7},{7,8},{8,9},{9,10},{10,1... | collective-permute-start | bytes 321032 | tf_op jit(solution)/shard_map/ppermute | solution.py:353
  21.8 28.1 %collective-permute-start.3 = (bf16[352,152]{1,0:T(8,128)(2,1)}, bf16[352,152]{1,0:T(8,128)(2,1)S(1)}, u32[]{:S(2)}, u32[]{:S(2)}) collective-permute-start(bf16[352,152]{1,0:T(8,128)(2,1)} %get-tuple-element.18.own_ref), channel_id=1, source_target_pairs={{1,0},{2,1},{3,2},{4,3},{5,4},{6,5},{7,6},{8,7},{9,8},{10,9},{11,1... | collective-permute-start | bytes 321032 | tf_op jit(solution)/shard_map/ppermute | solution.py:353
  48.5 18.8 %copy-start.2 = (bf16[352,152]{1,0:T(8,128)(2,1)}, bf16[352,152]{1,0:T(8,128)(2,1)S(1)}, u32[]{:S(2)}) copy-start(bf16[352,152]{1,0:T(8,128)(2,1)S(1)} %collective-permute-done.2.lower_ref) | copy-start | bytes 321028
  49.9 17.4 %copy-start.3 = (bf16[352,152]{1,0:T(8,128)(2,1)}, bf16[352,152]{1,0:T(8,128)(2,1)S(1)}, u32[]{:S(2)}) copy-start(bf16[352,152]{1,0:T(8,128)(2,1)S(1)} %collective-permute-done.3.upper_ref) | copy-start | bytes 321028
  50.8 4.0 %collective-permute-start.4 = (f32[32,152]{1,0:T(8,128)S(1)}, f32[32,152]{1,0:T(8,128)S(1)}, u32[]{:S(2)}, u32[]{:S(2)}) collective-permute-start(f32[32,152]{1,0:T(8,128)S(1)} %fusion.1), channel_id=1, source_target_pairs={{0,2},{1,3},{2,0},{3,1},{4,6},{5,7},{6,4},{7,5},{8,10},{9,11},{10,... | collective-permute-start | bytes 58376 | tf_op jit(solution)/shard_map/ppermute | solution.py:357
  54.8 4.0 %copy-start.4 = (f32[32,152]{1,0:T(8,128)}, f32[32,152]{1,0:T(8,128)S(1)}, u32[]{:S(2)}) copy-start(f32[32,152]{1,0:T(8,128)S(1)} %add.21.sum_ref) | copy-start | bytes 58372
  54.8 4.0 %collective-permute-start.5 = (f32[32,152]{1,0:T(8,128)S(1)}, f32[32,152]{1,0:T(8,128)S(1)}, u32[]{:S(2)}, u32[]{:S(2)}) collective-permute-start(f32[32,152]{1,0:T(8,128)S(1)} %add.21.sum_ref), channel_id=1, source_target_pairs={{0,4},{1,5},{2,6},{3,7},{4,0},{5,1},{6,2},{7,3},{8,12},{9,13},{10,... | collective-permute-start | bytes 58376 | tf_op jit(solution)/shard_map/ppermute | solution.py:357
  58.7 0.6 copy-start.5
  58.7 1.1 copy-start
  59.9 1.0 copy-start.1
  67.3 4.2 %collective-permute-start.6 = (f32[32,152]{1,0:T(8,128)}, f32[32,152]{1,0:T(8,128)S(1)}, u32[]{:S(2)}, u32[]{:S(2)}) collective-permute-start(f32[32,152]{1,0:T(8,128)} %get-tuple-element.22), channel_id=1, source_target_pairs={{0,8},{1,9},{2,10},{3,11},{4,12},{5,13},{6,14},{7,15},{8,0},{9,1},... | collective-permute-start | bytes 58376 | tf_op jit(solution)/shard_map/ppermute | solution.py:357
  72.3 108.3 %collective-permute-start.7 = (f32[32,152]{1,0:T(8,128)S(1)}, f32[32,152]{1,0:T(8,128)S(1)}, u32[]{:S(2)}, u32[]{:S(2)}) collective-permute-start(f32[32,152]{1,0:T(8,128)S(1)} %add.22), channel_id=1, source_target_pairs={{0,16},{1,17},{2,18},{3,19},{4,20},{5,21},{6,22},{7,23},{8,24},{9,... | collective-permute-start | bytes 58376 | tf_op jit(solution)/shard_map/ppermute | solution.py:357
  102.1 44.4 %copy-start.6 = (s32[2,128]{1,0:T(2,128)S(1)}, s32[2,128]{1,0:T(2,128)}, u32[]{:S(2)}) copy-start(s32[2,128]{1,0:T(2,128)} %get-tuple-element.19) | copy-start | bytes 3076

commit v2 on v1

--- a/solution.py
+++ b/solution.py
@@ -146,23 +146,34 @@
         send_ref[start : start + q_width, :] = part
 
 
-def far_kernel(lower_ref, own_ref, upper_ref, vlist_ref, table_hbm, out_ref, table_ref, wide_ref, total_ref, sems):
+def far_kernel(
+    lower_ref, own_ref, upper_ref, vlist_ref, table_hbm, out_ref, table_ref, tail_ref, wide_ref, total_ref, sems
+):
     node_count, type_count = vlist_ref.shape
     eq_width = own_ref.shape[1]
     q_width = out_ref.shape[0] // node_count
     lanes = node_count * q_width
+    tile = 128 // q_width
     chunk = 8
+    chunk_rows = chunk * eq_width
     chunk_count = eq_width // chunk
-
-    def copy_of(number):
-        span = pl.ds(number * chunk, chunk)
-        return pltpu.make_async_copy(table_hbm.at[span], table_ref.at[span], sems.at[number])
+    full = type_count // 128
+
+    def copies_of(number):
+        span = pl.ds(number * chunk_rows, chunk_rows)
+        copies = []
+        for part in range(full):
+            source = table_hbm.at[span, pl.ds(part * 128, 128)]
+            copies.append(pltpu.make_async_copy(source, table_ref.at[part, span], sems.at[number, part]))
+        source = table_hbm.at[span, pl.ds(full * 128, type_count - full * 128)]
+        copies.append(pltpu.make_async_copy(source, tail_ref.at[span], sems.at[number, full]))
+        return copies
 
     for number in range(chunk_count):
-        copy_of(number).start()
+        for copy in copies_of(number):
+            copy.start()
 
     index = lax.axis_index("oct")
-    tile = 128 // q_width
     repeat = (iota((q_width, 128), 1) % q_width == iota((q_width, 128), 0)).astype(BF16)
     for part, source in enumerate((lower_ref, own_ref, upper_ref)):
         for node in range(node_count):
@@ -175,109 +186,120 @@
     places = jnp.where(ids >= 0, ids - (index - 1) * node_count, -1).astype(F32).astype(BF16)
     spread = (iota((node_count, lanes), 1) // SOURCES == iota((node_count, lanes), 0)).astype(BF16)
     wanted = dot_tn(places, spread)
-    chosen = (wanted == (iota((type_count, lanes), 1) % SOURCES).astype(F32)).astype(BF16)
+    chosen = (wanted == (iota((type_count, lanes), 1) % SOURCES).astype(F32)).astype(F32)
+    chosen_full = chosen[: full * 128].astype(BF16)
+    chosen_tail = chosen[full * 128 :].astype(BF16)
     lane_node = iota((SOURCES, 128), 1) // q_width
     nothing = jnp.zeros((SOURCES, 128), F32)
     total_ref[...] = jnp.zeros_like(total_ref)
 
     def chunk_step(number, carry):
-        copy_of(number).wait()
-        total = jnp.zeros((eq_width, lanes), F32)
+        for copy in copies_of(number):
+            copy.wait()
+        span = pl.ds(pl.multiple_of(number * chunk_rows, chunk_rows), chunk_rows)
+        left = jnp.concatenate([table_ref[part, span, :] for part in range(full)], axis=1)
+        summed = dot(left, chosen_full) + dot(tail_ref[span, :], chosen_tail)
+        lefts, rights = [], []
         for step in range(chunk):
+            value = summed[step * eq_width : (step + 1) * eq_width]
+            high = value.astype(BF16).astype(F32)
+            lefts.append(jnp.concatenate([high, value - high], axis=0).astype(BF16))
             row = number * chunk + step
-            summed = dot(table_ref[row], chosen)
-            high = summed.astype(BF16).astype(F32)
-            both = jnp.concatenate([high, summed - high], axis=0).astype(BF16)
             sent = wide_ref[pl.ds(pl.multiple_of(row * SOURCES, SOURCES), SOURCES), :]
             parts = [jnp.where(lane_node == place, sent, 0.0) for place in range(tile)]
-            blocks = []
             for node in range(node_count):
                 line = [parts[node % tile] if place == node // tile else nothing for place in range(node_count // tile)]
-                blocks.append(jnp.concatenate(line, axis=1))
-            product = dot(both, jnp.concatenate(blocks, axis=0).astype(BF16))
-            total = total + product[:eq_width] + product[eq_width:]
-        total_ref[...] += total
+                rights.append(jnp.concatenate(line, axis=1))
+        product = dot(jnp.concatenate(lefts, axis=1), jnp.concatenate(rights, axis=0).astype(BF16))
+        total_ref[...] += product[:eq_width] + product[eq_width:]
         return carry
 
     lax.fori_loop(0, chunk_count, chunk_step, 0)
     out_ref[...] = total_ref[...].T
 
 
-def near_kernel(sides, ulist_ref, counts_ref, pack_ref, target_ref, out_ref, gather_ref, value_ref, total_ref, owner_ref):
+def near_kernel(
+    ulist_ref, counts_ref, side_counts_ref, own_pack_ref, side_pack_ref, target_ref, out_ref, first_ref, second_ref,
+    value_ref, total_ref, owner_ref
+):
     leaf_count, q_width, p_width = out_ref.shape
-    slot_count = sum(end - first for first, end, _, _ in sides)
+    slot_count = ulist_ref.shape[0]
+    member_blocks = -(-slot_count * p_width // BLOCK)
+    spare_block = 8 * member_blocks + 10 * UNROLL
+    group_count = leaf_count // 8
     index = lax.axis_index("oct")
-
-    def gather(leaf, member, block):
+    buffers = (first_ref, second_ref)
+
+    def source_of(slot, leaf):
+        leaf_id = ulist_ref[slot, leaf]
+        side = 0 if slot == 0 else (-1 if slot < 9 else (0 if slot < 18 else 1))
+        place = jnp.where(leaf_id >= 0, leaf_id - (index + side) * leaf_count, 0)
+        if side == 0:
+            count, pack = counts_ref[place], own_pack_ref[place]
+        else:
+            half = (side + 1) // 2
+            count, pack = side_counts_ref[half, place], side_pack_ref[half * leaf_count + place]
+        return jnp.where(leaf_id >= 0, jnp.bitwise_and(count + 15, -16), 0), pack
+
+    def gather(half, leaf, member, block):
+        gather_ref = buffers[half]
         offset = block * BLOCK
-        for first, end, slab, start in sides:
-            base = (index + slab) * leaf_count - start
-            for slot in range(first, end):
-                leaf_id = ulist_ref[slot, leaf]
-                place = jnp.where(leaf_id >= 0, leaf_id - base, start)
-                length = jnp.where(leaf_id >= 0, jnp.bitwise_and(counts_ref[place] + 15, -16), 0)
-                gather_ref[pl.ds(pl.multiple_of(offset, 16), p_width), :] = pack_ref[place]
-                offset = offset + length
+        for slot in range(slot_count):
+            length, pack = source_of(slot, leaf)
+            gather_ref[pl.ds(pl.multiple_of(offset, 16), p_width), :] = pack
+            offset = offset + length
         gather_ref[pl.ds(pl.multiple_of(offset, 16), BLOCK), :] = jnp.zeros((BLOCK, 128), BF16)
-        for number in range(-(-slot_count * p_width // BLOCK)):
-            owner_ref[UNROLL + block + number] = member
-        return lax.div(offset + (BLOCK - 1), BLOCK)
-
-    for number in range(UNROLL):
-        owner_ref[number] = 8
-
-    def group_step(group, carry):
-        block_count = lax.fori_loop(0, 8, lambda member, block: gather(group * 8 + member, member, block), 0)
-        for number in range(2 * UNROLL):
-            owner_ref[UNROLL + block_count + number] = 8
+        for number in range(member_blocks):
+            owner_ref[half, UNROLL + block + number] = member
+        return lax.shift_right_logical(offset + (BLOCK - 1), BLOCK.bit_length() - 1)
+
+    for half in range(2):
+        for number in range(UNROLL):
+            owner_ref[half, number] = 8
+
+    first_count = lax.fori_loop(0, 8, lambda member, block: gather(0, member, member, block), 0)
+
+    def group_step(group, half, block_count):
+        for number in range(10 * UNROLL):
+            owner_ref[half, UNROLL + block_count + number] = 8
         total_ref[...] = jnp.zeros_like(total_ref)
+        later = jnp.minimum(group + 1, group_count - 1)
 
         def sources_of(block):
-            return gather_ref[pl.ds(pl.multiple_of(block * BLOCK, BLOCK), BLOCK), :]
-
-        def blocks_step(step, inner):
+            return buffers[half][pl.ds(pl.multiple_of(block * BLOCK, BLOCK), BLOCK), :]
+
+        def blocks_step(step, later_block):
             slot = jnp.bitwise_and(step, 1) * UNROLL
             for part in range(UNROLL):
                 block = jnp.maximum(step - 1, 0) * UNROLL + part
-                member = owner_ref[step * UNROLL + part]
-                total_ref[member] += dot(value_ref[UNROLL - slot + part], sources_of(block))
+                member = owner_ref[half, step * UNROLL + part]
+                values = jnp.concatenate([value_ref[UNROLL - slot + part, side] for side in range(2)], axis=1)
+                total_ref[member] += dot(values, sources_of(block))
             for part in range(UNROLL):
                 block = step * UNROLL + part
-                member = owner_ref[UNROLL + block]
+                member = owner_ref[half, UNROLL + block]
                 targets = target_ref[group * 8 + jnp.minimum(member, 7)]
-                value_ref[slot + part] = jnp.exp2(dot_nt(targets, sources_of(block))).astype(BF16)
-            return inner
-
-        lax.fori_loop(0, lax.div(block_count + (2 * UNROLL - 1), UNROLL), blocks_step, 0)
+                values = jnp.exp2(dot_nt(targets, sources_of(block))).astype(BF16)
+                for side in range(2):
+                    value_ref[slot + part, side] = values[:, side * 128 : (side + 1) * 128]
+            live = step < 8
+            member = jnp.minimum(step, 7)
+            place = jnp.where(live, later_block, spare_block)
+            following = gather(1 - half, later * 8 + member, member, place)
+            return jnp.where(live, following, later_block)
+
+        steps = jnp.maximum(lax.div(block_count + (2 * UNROLL - 1), UNROLL), 8)
+        later_count = lax.fori_loop(0, steps, blocks_step, 0)
 
         for member in range(8):
             turned = total_ref[member].T
             out_ref[group * 8 + member] = turned[:q_width] + turned[q_width : 2 * q_width]
-        return carry
-
-    lax.fori_loop(0, leaf_count // 8, group_step, 0)
-
-
-def near_call(sides, ulist, counts, pack, targets, q_width, name):
-    leaf_count, p_width = targets.shape[:2]
-    slot_count = sum(end - first for first, end, _, _ in sides)
-    member_blocks = -(-slot_count * p_width // BLOCK)
-    vmem = pl.BlockSpec(memory_space=pltpu.VMEM)
-    smem = pl.BlockSpec(memory_space=pltpu.SMEM)
-    return pl.pallas_call(
-        lambda *refs: near_kernel(sides, *refs),
-        out_shape=jax.ShapeDtypeStruct((leaf_count, q_width, p_width), F32),
-        in_specs=[smem, smem, vmem, vmem],
-        out_specs=vmem,
-        scratch_shapes=[
-            pltpu.VMEM(((8 * member_blocks + 2 * UNROLL + 2) * BLOCK, 128), BF16),
-            pltpu.VMEM((2 * UNROLL, p_width, BLOCK), BF16),
-            pltpu.VMEM((9, p_width, 128), F32),
-            pltpu.SMEM((9 * member_blocks + 4 * UNROLL,), jnp.int32),
-        ],
-        compiler_params=pltpu.CompilerParams(vmem_limit_bytes=VMEM_LIMIT),
-        name=name,
-    )(ulist, counts, pack, targets)
+        return later_count
+
+    def pair_step(pair, block_count):
+        return group_step(2 * pair + 1, 1, group_step(2 * pair, 0, block_count))
+
+    lax.fori_loop(0, group_count // 2, pair_step, first_count)
 
 
 def pack_kernel(lower_ref, upper_ref, sum_ref, pair_ref, shift_ref, pack_ref, counts_ref, top_ref, next_ref):
@@ -307,7 +329,7 @@
 
 
 def final_kernel(
-    level_count, pack_ref, surface_ref, counts_ref, own_near_ref, side_near_ref, far_ref, coarse_ref, shift_ref,
+    level_count, pack_ref, surface_ref, counts_ref, near_ref, far_ref, coarse_ref, shift_ref,
     down_ref, *rest
 ):
     top_refs, (out_ref, node_ref, down_leaf_ref) = rest[:level_count], rest[level_count:]
@@ -336,11 +358,10 @@
             values_high, values_low = halves(values)
             down = down_leaf_ref[child, pl.ds(pl.multiple_of(node * q_width, q_width), q_width), :]
             down_high = down.astype(BF16).astype(F32)
-            empty = jnp.zeros((128 - 2 * q_width, eq_width), F32)
-            down_rows = jnp.concatenate([down_high, down - down_high, empty], axis=0).astype(BF16)
-            down_first = jnp.concatenate([down_high, jnp.zeros_like(down_high), empty], axis=0).astype(BF16)
+            down_rows = jnp.concatenate([down_high, down - down_high], axis=0).astype(BF16)
+            down_first = jnp.concatenate([down_high, jnp.zeros_like(down_high)], axis=0).astype(BF16)
             turned = (dot_nt(values_high, down_rows) + dot_nt(values_low, down_first)).T
-            summed = turned[:q_width] + turned[q_width : 2 * q_width] + own_near_ref[leaf] + side_near_ref[leaf]
+            summed = turned[:q_width] + turned[q_width : 2 * q_width] + near_ref[leaf]
             out_ref[leaf] = jnp.where(lane < counts_ref[leaf], summed, 0.0)
         return carry
 
@@ -404,31 +425,32 @@
     )(points, dens, surface, counts, up_inverse, shift_up)
 
     send_lower, send_upper = shifted(send, size)
-    lower, upper = shifted(message, size)
-
     partner = jnp.where(index & 1 == 1, send_lower[node_rows:], send_upper[node_rows:]).astype(F32)
     total = slab + (partner[:q_width] + partner[q_width : 2 * q_width] + partner[2 * q_width :])
+    message, total = lax.optimization_barrier((message, total))
+    lower, upper = shifted(message, size)
     total = total + swapped(total, size, 1)
     pair = swapped(total, size, 2)
-
-    near_own = near_call(
-        ((0, 1, 0, 0), (9, 18, 0, 0)), ulist, counts, pack, targets, q_width, "near_own"
-    )
-
+    send_lower, total = lax.optimization_barrier((send_lower, total))
+
+    table = table.reshape(eq_width * eq_width, type_count)
     far_node = pl.pallas_call(
         far_kernel,
         out_shape=jax.ShapeDtypeStruct((node_rows, eq_width), F32),
         in_specs=[vmem, vmem, vmem, vmem, hbm],
         out_specs=vmem,
         scratch_shapes=[
-            pltpu.VMEM((eq_width, eq_width, type_count), BF16),
+            pltpu.VMEM((type_count // 128, eq_width * eq_width, 128), BF16),
+            pltpu.VMEM((eq_width * eq_width, type_count % 128), BF16),
             pltpu.VMEM((eq_width * SOURCES, 128), F32),
             pltpu.VMEM((eq_width, node_rows), F32),
-            pltpu.SemaphoreType.DMA((eq_width // 8,)),
+            pltpu.SemaphoreType.DMA((eq_width // 8, type_count // 128 + 1)),
         ],
         compiler_params=params,
+        cost_estimate=pl.CostEstimate(flops=2 * 10**10, bytes_accessed=18 * 10**6, transcendentals=0),
         name="far",
     )(send_lower, send, send_upper, vlist, table)
+    far_node, lower, upper = lax.optimization_barrier((far_node, lower, upper))
 
     side_pack, side_counts, top, current = pl.pallas_call(
         pack_kernel,
@@ -452,15 +474,29 @@
             current = current + swapped(current, size, bit)
         tops.append(current)
 
-    side_counts = side_counts[:, :leaf_count].reshape(-1)
-    near_side = near_call(
-        ((1, 9, -1, 0), (18, 27, 1, leaf_count)), ulist, side_counts, side_pack, targets, q_width, "near_side"
-    )
+    member_blocks = -(-ulist.shape[0] * p_width // BLOCK)
+    gather_rows = (9 * member_blocks + 10 * UNROLL + 2) * BLOCK
+    near = pl.pallas_call(
+        near_kernel,
+        out_shape=jax.ShapeDtypeStruct((leaf_count, q_width, p_width), F32),
+        in_specs=[smem, smem, smem, vmem, vmem, vmem],
+        out_specs=vmem,
+        scratch_shapes=[
+            pltpu.VMEM((gather_rows, 128), BF16),
+            pltpu.VMEM((gather_rows, 128), BF16),
+            pltpu.VMEM((2 * UNROLL, 2, p_width, 128), BF16),
+            pltpu.VMEM((9, p_width, 128), F32),
+            pltpu.SMEM((2, 9 * member_blocks + 12 * UNROLL), jnp.int32),
+        ],
+        compiler_params=params,
+        cost_estimate=pl.CostEstimate(flops=3 * 10**10, bytes_accessed=10**7, transcendentals=0),
+        name="near",
+    )(ulist, counts, side_counts, pack, side_pack, targets)
 
     return pl.pallas_call(
         lambda *refs: final_kernel(len(tops), *refs),
         out_shape=jax.ShapeDtypeStruct((leaf_count, q_width, p_width), F32),
-        in_specs=[vmem, vmem, smem] + [vmem] * (6 + len(tops)),
+        in_specs=[vmem, vmem, smem] + [vmem] * (5 + len(tops)),
         out_specs=vmem,
         scratch_shapes=[
             pltpu.VMEM((node_rows, eq_width), F32),
@@ -468,7 +504,7 @@
         ],
         compiler_params=params,
         name="final",
-    )(pack, surface, counts, near_own, near_side, far_node, coarse, shift_down, down_inverse, *tops)
+    )(pack, surface, counts, near, far_node, coarse, shift_down, down_inverse, *tops)
 
 
 def solution(mesh):

time: 202 us -> 161 us (0.80)
  the two profiles are of different devices: /device:TPU:4 before, /device:TPU:1 now
where the time goes in v2:
time: 161 us; the launch traced here: 159 us
  Pallas kernels  129 us (80%)
  starting transfers between devices  18.8 us (12%)
  waiting for transfers between devices  6.12 us (4%)
  other arithmetic  2.21 us (1%)
  local copies, waits for them, and re-layouts  2.14 us (1%)
    pallas_call x1, Pallas kernels, local(): pl.pallas_call(near_kernel, out_shape=jax.ShapeDtypeStruct((leaf_count, q...  63.7 us
    pallas_call x1, Pallas kernels, local(): pl.pallas_call(far_kernel, out_shape=jax.ShapeDtypeStruct((node_rows, eq_...  28 us
    pallas_call x1, Pallas kernels, local(): pl.pallas_call(lambda *refs: final_kernel(len(tops), *refs), out_shape=ja...  17.8 us
    pallas_call x1, Pallas kernels, local(): pl.pallas_call(upward_kernel, out_shape=(jax.ShapeDtypeStruct((leaf_count...  13.4 us
    ppermute x4, starting transfers between devices, shifted(): return (lax.ppermute(value, 'oct', up), lax.ppermute(value, 'oct', down))  12.8 us
    pallas_call x1, Pallas kernels, local(): pl.pallas_call(pack_kernel, out_shape=(jax.ShapeDtypeStruct((2 * leaf_cou...  6.38 us
    ppermute x4, starting transfers between devices, swapped(): lax.ppermute(value, 'oct', [(source, source ^ 1 << bit) for source in ran...  5.96 us
    ppermute x4, waiting for transfers between devices, shifted(): return (lax.ppermute(value, 'oct', up), lax.ppermute(value, 'oct', down))  4.6 us
  transfers between devices with their start and end apart: 8, of which 3 were waited for; matrix products, arithmetic and copies ran while one was open for 0% of the time, Pallas kernels for 58%

profile of v2, /device:TPU:1, one launch (start us, length us, event | category | flops | bytes accessed | tf_op | source)
XLA Modules:
  0.0 158.7 jit_solution(14840159840951472744)
XLA Ops:
  0.0 13.4 %upward.1 = (bf16[64,128,128]{2,1,0:T(8,128)(2,1)}, bf16[64,128,128]{2,1,0:T(8,128)(2,1)}, f32[64,40,128]{2,1,0:T(8,128)}, bf16[352,152]{1,0:T(8,128)(2,1)}, f32[32,152]{1,0:T(8,128)}) custom-call(f32[3,64,128]{2,1,0:T(8,128)} %bitcast.8, f32[64,32,128]{2,1,0:T(8,128)} %dens_ref.1, f32[3,64,152]{2,1,0:T(8,128)} %bitcast.6, s32[64]{0:T(128)} %refs_2_.1, ...), custom_call_target="tpu_custom_call" | custom-call | tf_op jit(solution)/shard_map/upward/pallas_call | solution.py:411
  13.4 2.0 %collective-permute-start.1 = (bf16[352,152]{1,0:T(8,128)(2,1)}, bf16[352,152]{1,0:T(8,128)(2,1)S(1)}, u32[]{:S(2)}, u32[]{:S(2)}) collective-permute-start(bf16[352,152]{1,0:T(8,128)(2,1)} %get-tuple-element.22.own_ref), channel_id=1, source_target_pairs={{1,0},{2,1},{3,2},{4,3},{5,4},{6,5},{7,6},{8,7},{9,8},{10,9},{11,1... | collective-permute-start | bytes 321032 | tf_op jit(solution)/shard_map/ppermute | solution.py:374
  15.4 4.5 %collective-permute-start = (bf16[352,152]{1,0:T(8,128)(2,1)}, bf16[352,152]{1,0:T(8,128)(2,1)S(1)}, u32[]{:S(2)}, u32[]{:S(2)}) collective-permute-start(bf16[352,152]{1,0:T(8,128)(2,1)} %get-tuple-element.22.own_ref), channel_id=1, source_target_pairs={{0,1},{1,2},{2,3},{3,4},{4,5},{5,6},{6,7},{7,8},{8,9},{9,10},{10,1... | collective-permute-start | bytes 321032 | tf_op jit(solution)/shard_map/ppermute | solution.py:374
  19.9 1.4 collective-permute-done.1.upper_ref
  21.3 3.2 %collective-permute-done.lower_ref = bf16[352,152]{1,0:T(8,128)(2,1)S(1)} collective-permute-done((bf16[352,152]{1,0:T(8,128)(2,1)}, bf16[352,152]{1,0:T(8,128)(2,1)S(1)}, u32[]{:S(2)}, u32[]{:S(2)}) %collective-permute-start) | collective-permute-done | bytes 107040 | tf_op jit(solution)/shard_map/ppermute | solution.py:374
  24.5 0.8 fusion.1
  25.3 0.3 collective-permute-start.2
  25.6 4.5 %collective-permute-start.4 = (f32[64,40,128]{2,1,0:T(8,128)}, f32[64,40,128]{2,1,0:T(8,128)S(1)}, u32[]{:S(2)}, u32[]{:S(2)}) collective-permute-start(f32[64,40,128]{2,1,0:T(8,128)} %get-tuple-element.27), channel_id=1, source_target_pairs={{1,0},{2,1},{3,2},{4,3},{5,4},{6,5},{7,6},{8,7},{9,8},{10,9},{11,1... | collective-permute-start | bytes 3932168 | tf_op jit(solution)/shard_map/ppermute | solution.py:374
  30.0 1.9 %collective-permute-start.3 = (f32[64,40,128]{2,1,0:T(8,128)}, f32[64,40,128]{2,1,0:T(8,128)S(1)}, u32[]{:S(2)}, u32[]{:S(2)}) collective-permute-start(f32[64,40,128]{2,1,0:T(8,128)} %get-tuple-element.27), channel_id=1, source_target_pairs={{0,1},{1,2},{2,3},{3,4},{4,5},{5,6},{6,7},{7,8},{8,9},{9,10},{10,1... | collective-permute-start | bytes 3932168 | tf_op jit(solution)/shard_map/ppermute | solution.py:374
  32.0 0.0 collective-permute-done.2
  32.0 0.0 copy-start.2
  32.0 1.4 collective-permute-start.5
  33.4 0.0 copy-done.4
  33.4 0.0 copy-done.5
  33.4 28.0 %far.1.refs_4_ = f32[256,152]{1,0:T(8,128)} custom-call(bf16[352,152]{1,0:T(8,128)(2,1)} %copy-done.5, bf16[352,152]{1,0:T(8,128)(2,1)} %get-tuple-element.22.own_ref, bf16[352,152]{1,0:T(8,128)(2,1)} %copy-done.4, s32[8,316]{1,0:T(8,128)} %vlist_ref.1, bf16[23104,316]{1,0:T(8,128)(2,1)} %bitcast.9), custom_call_target="tpu_custom_call" | custom-call | flops 20000000000 | bytes 18000000 | tf_op jit(solution)/shard_map/far/pallas_call | solution.py:437
  61.4 0.0 copy-done.2
  61.4 0.0 collective-permute-done.4.upper_ref
  61.4 0.0 copy-start
  61.4 0.0 collective-permute-done.3.lower_ref
  61.4 0.0 collective-permute-done.5.pair_ref
  61.4 1.1 copy-done
  62.5 0.4 copy-done.1
  62.9 0.6 copy-done.3
  63.6 6.4 %pack.1 = (bf16[128,128,128]{2,1,0:T(8,128)(2,1)}, s32[2,128]{1,0:T(2,128)}, f32[32,152]{1,0:T(8,128)}, f32[32,152]{1,0:T(8,128)}) custom-call(f32[64,40,128]{2,1,0:T(8,128)} %copy-done.1, f32[64,40,128]{2,1,0:T(8,128)} %copy-done, f32[32,152]{1,0:T(8,128)} %copy-done.2, f32[32,152]{1,0:T(8,128)} %copy-done.3, f32[8,152,152]{2,1,0:T(8,128)} %shift_ref.3), custom_call_target="tpu_custom_call" | custom-call | tf_op jit(solution)/shard_map/pack/pallas_call | solution.py:455
  69.9 1.9 %collective-permute-start.6 = (f32[32,152]{1,0:T(8,128)}, f32[32,152]{1,0:T(8,128)S(1)}, u32[]{:S(2)}, u32[]{:S(2)}) collective-permute-start(f32[32,152]{1,0:T(8,128)} %get-tuple-element.36), channel_id=1, source_target_pairs={{0,8},{1,9},{2,10},{3,11},{4,12},{5,13},{6,14},{7,15},{8,0},{9,1},... | collective-permute-start | bytes 58376 | tf_op jit(solution)/shard_map/ppermute | solution.py:378
  71.8 1.5 collective-permute-done.6
  73.3 0.8 add.22
  74.1 2.5 %collective-permute-start.7 = (f32[32,152]{1,0:T(8,128)S(1)}, f32[32,152]{1,0:T(8,128)S(1)}, u32[]{:S(2)}, u32[]{:S(2)}) collective-permute-start(f32[32,152]{1,0:T(8,128)S(1)} %add.22), channel_id=1, source_target_pairs={{0,16},{1,17},{2,18},{3,19},{4,20},{5,21},{6,22},{7,23},{8,24},{9,... | collective-permute-start | bytes 58376 | tf_op jit(solution)/shard_map/ppermute | solution.py:378
  76.6 63.7 %near.1.refs_3_ = f32[64,32,128]{2,1,0:T(8,128)} custom-call(s32[27,64]{1,0:T(8,128)} %bitcast.10, s32[64]{0:T(128)} %refs_2_.1, s32[2,128]{1,0:T(2,128)} %get-tuple-element.31.side_counts_ref, bf16[64,128,128]{2,1,0:T(8,128)(2,1)} %get-tuple-element.21.own_pack_ref.refs_0_, bf16[128,128,128]{2,1,0:T(8,128)(2,1)} %get-tuple-element.32.side_pack_ref, ...), custom_call_target="tpu_custom_call" | custom-call | flops 30000001024 | bytes 10000000 | tf_op jit(solution)/shard_map/near/pallas_call | solution.py:479
  140.3 0.0 collective-permute-done.7
  140.3 0.6 add.23.refs_9_
  140.9 17.8 %final.1 = f32[64,32,128]{2,1,0:T(8,128)} custom-call(bf16[64,128,128]{2,1,0:T(8,128)(2,1)} %get-tuple-element.21.own_pack_ref.refs_0_, f32[3,64,152]{2,1,0:T(8,128)} %bitcast.7, s32[64]{0:T(128)} %refs_2_.1, f32[64,32,128]{2,1,0:T(8,128)} %near.1.refs_3_, f32[256,152]{1,0:T(8,128)} %far.1.refs_4_, f32[8,152,152]{2,1,0:T(8,128)} %refs_5_.1, ...), custom_call_target="tpu_custom_call" | custom-call | tf_op jit(solution)/shard_map/final/pallas_call | solution.py:496
  (6 shorter events, 0.0 us)
Async XLA Ops:
  13.4 7.9 %collective-permute-start.1 = (bf16[352,152]{1,0:T(8,128)(2,1)}, bf16[352,152]{1,0:T(8,128)(2,1)S(1)}, u32[]{:S(2)}, u32[]{:S(2)}) collective-permute-start(bf16[352,152]{1,0:T(8,128)(2,1)} %get-tuple-element.22.own_ref), channel_id=1, source_target_pairs={{1,0},{2,1},{3,2},{4,3},{5,4},{6,5},{7,6},{8,7},{9,8},{10,9},{11,1... | collective-permute-start | bytes 321032 | tf_op jit(solution)/shard_map/ppermute | solution.py:374
  15.4 9.1 %collective-permute-start = (bf16[352,152]{1,0:T(8,128)(2,1)}, bf16[352,152]{1,0:T(8,128)(2,1)S(1)}, u32[]{:S(2)}, u32[]{:S(2)}) collective-permute-start(bf16[352,152]{1,0:T(8,128)(2,1)} %get-tuple-element.22.own_ref), channel_id=1, source_target_pairs={{0,1},{1,2},{2,3},{3,4},{4,5},{5,6},{6,7},{7,8},{8,9},{9,10},{10,1... | collective-permute-start | bytes 321032 | tf_op jit(solution)/shard_map/ppermute | solution.py:374
  21.3 12.1 %copy-start.4 = (bf16[352,152]{1,0:T(8,128)(2,1)}, bf16[352,152]{1,0:T(8,128)(2,1)S(1)}, u32[]{:S(2)}) copy-start(bf16[352,152]{1,0:T(8,128)(2,1)S(1)} %collective-permute-done.1.upper_ref) | copy-start | bytes 321028
  24.5 8.9 %copy-start.5 = (bf16[352,152]{1,0:T(8,128)(2,1)}, bf16[352,152]{1,0:T(8,128)(2,1)S(1)}, u32[]{:S(2)}) copy-start(bf16[352,152]{1,0:T(8,128)(2,1)S(1)} %collective-permute-done.lower_ref) | copy-start | bytes 321028
  25.3 6.7 %collective-permute-start.2 = (f32[32,152]{1,0:T(8,128)S(1)}, f32[32,152]{1,0:T(8,128)S(1)}, u32[]{:S(2)}, u32[]{:S(2)}) collective-permute-start(f32[32,152]{1,0:T(8,128)S(1)} %fusion.1), channel_id=1, source_target_pairs={{0,2},{1,3},{2,0},{3,1},{4,6},{5,7},{6,4},{7,5},{8,10},{9,11},{10,... | collective-permute-start | bytes 58376 | tf_op jit(solution)/shard_map/ppermute | solution.py:378
  25.6 35.8 %collective-permute-start.4 = (f32[64,40,128]{2,1,0:T(8,128)}, f32[64,40,128]{2,1,0:T(8,128)S(1)}, u32[]{:S(2)}, u32[]{:S(2)}) collective-permute-start(f32[64,40,128]{2,1,0:T(8,128)} %get-tuple-element.27), channel_id=1, source_target_pairs={{1,0},{2,1},{3,2},{4,3},{5,4},{6,5},{7,6},{8,7},{9,8},{10,9},{11,1... | collective-permute-start | bytes 3932168 | tf_op jit(solution)/shard_map/ppermute | solution.py:374
  30.0 31.4 %collective-permute-start.3 = (f32[64,40,128]{2,1,0:T(8,128)}, f32[64,40,128]{2,1,0:T(8,128)S(1)}, u32[]{:S(2)}, u32[]{:S(2)}) collective-permute-start(f32[64,40,128]{2,1,0:T(8,128)} %get-tuple-element.27), channel_id=1, source_target_pairs={{0,1},{1,2},{2,3},{3,4},{4,5},{5,6},{6,7},{7,8},{8,9},{9,10},{10,1... | collective-permute-start | bytes 3932168 | tf_op jit(solution)/shard_map/ppermute | solution.py:374
  32.0 29.4 %copy-start.2 = (f32[32,152]{1,0:T(8,128)}, f32[32,152]{1,0:T(8,128)S(1)}, u32[]{:S(2)}) copy-start(f32[32,152]{1,0:T(8,128)S(1)} %add.21.sum_ref) | copy-start | bytes 58372
  32.0 29.4 %collective-permute-start.5 = (f32[32,152]{1,0:T(8,128)S(1)}, f32[32,152]{1,0:T(8,128)S(1)}, u32[]{:S(2)}, u32[]{:S(2)}) collective-permute-start(f32[32,152]{1,0:T(8,128)S(1)} %add.21.sum_ref), channel_id=1, source_target_pairs={{0,4},{1,5},{2,6},{3,7},{4,0},{5,1},{6,2},{7,3},{8,12},{9,13},{10,... | collective-permute-start | bytes 58376 | tf_op jit(solution)/shard_map/ppermute | solution.py:378
  61.4 1.1 copy-start
  61.4 1.5 copy-start.1
  62.9 0.6 copy-start.3
  69.9 3.4 %collective-permute-start.6 = (f32[32,152]{1,0:T(8,128)}, f32[32,152]{1,0:T(8,128)S(1)}, u32[]{:S(2)}, u32[]{:S(2)}) collective-permute-start(f32[32,152]{1,0:T(8,128)} %get-tuple-element.36), channel_id=1, source_target_pairs={{0,8},{1,9},{2,10},{3,11},{4,12},{5,13},{6,14},{7,15},{8,0},{9,1},... | collective-permute-start | bytes 58376 | tf_op jit(solution)/shard_map/ppermute | solution.py:378
  74.1 66.2 %collective-permute-start.7 = (f32[32,152]{1,0:T(8,128)S(1)}, f32[32,152]{1,0:T(8,128)S(1)}, u32[]{:S(2)}, u32[]{:S(2)}) collective-permute-start(f32[32,152]{1,0:T(8,128)S(1)} %add.22), channel_id=1, source_target_pairs={{0,16},{1,17},{2,18},{3,19},{4,20},{5,21},{6,22},{7,23},{8,24},{9,... | collective-permute-start | bytes 58376 | tf_op jit(solution)/shard_map/ppermute | solution.py:378

commit v3 on v2

--- a/solution.py
+++ b/solution.py
@@ -11,11 +11,11 @@
 BF16 = jnp.bfloat16
 HIGHEST = lax.Precision.HIGHEST
 SCALE = math.sqrt(math.log2(math.e))
-VMEM_LIMIT = 56 * 1024 * 1024
 NT = (((1,), (1,)), ((), ()))
 TN = (((0,), (0,)), ((), ()))
 BLOCK = 256
 UNROLL = 4
+PIECE = 32
 SOURCES = 32
 
 
@@ -41,6 +41,10 @@
     left_high, left_low = halves(left)
     right_high, right_low = halves(right)
     return dot(left_high, right_high) + dot(left_high, right_low) + dot(left_low, right_high)
+
+
+def grant(mebibytes):
+    return pltpu.CompilerParams(vmem_limit_bytes=mebibytes * 1024 * 1024)
 
 
 def iota(shape, dim):
@@ -75,24 +79,33 @@
     return high, mid, low, norms, ones
 
 
-def left_rows(parts):
-    high, mid, low, norms, ones = parts
-    return jnp.concatenate([high, high, mid, mid, high, low, ones, norms], axis=0)
-
-
-def right_rows(parts):
-    high, mid, low, norms, ones = parts
-    return jnp.concatenate([high, mid, high, mid, low, high, norms, ones], axis=0)
-
-
-def padded_left(parts):
-    rows = left_rows(parts)
-    return jnp.concatenate([jnp.zeros_like(rows), rows], axis=0).astype(BF16)
-
-
-def packed_rows(weights, parts):
-    weights_high = weights.astype(BF16).astype(F32)
-    return jnp.concatenate([weights_high, weights - weights_high, right_rows(parts)], axis=0).astype(BF16)
+LEFT = (0, 0, 1, 1, 0, 2, 4, 3)
+RIGHT = (0, 1, 0, 1, 2, 0, 3, 4)
+
+
+def selector(order):
+    row = iota((32, 40), 0)
+    column = iota((32, 40), 1)
+    picked = jnp.zeros((32, 40), F32)
+    for group, piece in enumerate(order):
+        shift = 8 * piece - 3 * group
+        inside = (row >= 3 * group) & (row < 3 * group + 3)
+        picked = jnp.where(inside & (column == row + shift), 1.0, picked)
+    return picked.astype(BF16)
+
+
+def stacked(coords):
+    return jnp.concatenate(pieces(coords), axis=0).astype(BF16)
+
+
+def weight_rows(weights):
+    high = weights.astype(BF16).astype(F32)
+    return high, weights - high
+
+
+def kernel_rows(surface_ref, leaf, right, select_left):
+    left = dot(select_left, stacked(coords_of(surface_ref, leaf))).astype(BF16)
+    return halves(jnp.exp2(dot_tn(left, right.astype(BF16))))
 
 
 def upward_kernel(
@@ -104,6 +117,8 @@
     node_count = leaf_count // 8
     lane = iota((q_width, p_width), 1)
     row = iota((8, p_width), 0)
+    column = iota((p_width, 128), 1)
+    select_left, select_right = selector(LEFT), selector(RIGHT)
 
     def node_step(node, carry):
         for child in range(8):
@@ -113,15 +128,16 @@
             coords = coords_of(points_ref, leaf)
             message_ref[leaf, :q_width, :] = weights
             message_ref[leaf, q_width:, :] = jnp.where(row == 3, count.astype(F32), coords)
-            parts = pieces(coords)
-            rows = packed_rows(weights, parts)
-            pack = rows.T
-            pack_ref[leaf] = pack
-            target_ref[leaf] = padded_left(parts).T
-            values = jnp.exp2(dot(pack, padded_left(pieces(coords_of(surface_ref, leaf)))))
-            values_high, values_low = halves(values)
-            both = dot(rows[: 2 * q_width], values_high)
-            check = both[:q_width] + both[q_width:] + dot(rows[:q_width], values_low)
+            base = stacked(coords)
+            left, right = dot(select_left, base), dot(select_right, base)
+            high, low = weight_rows(weights)
+            turned = jnp.concatenate([high, low, right, left], axis=0).T
+            pack_ref[leaf] = turned.astype(BF16)
+            moved = pltpu.roll(turned, 96, 1)
+            target_ref[leaf] = jnp.where((column >= 64) & (column < 96), moved, 0.0).astype(BF16)
+            values_high, values_low = kernel_rows(surface_ref, leaf, right, select_left)
+            both = dot_nt(jnp.concatenate([high, low], axis=0).astype(BF16), values_high)
+            check = both[:q_width] + both[q_width:] + dot_nt(high.astype(BF16), values_low)
             check_ref[child, pl.ds(pl.multiple_of(node * q_width, q_width), q_width), :] = check
         return carry
 
@@ -219,81 +235,115 @@
 
 
 def near_kernel(
-    ulist_ref, counts_ref, side_counts_ref, own_pack_ref, side_pack_ref, target_ref, out_ref, first_ref, second_ref,
-    value_ref, total_ref, owner_ref
+    ulist_ref, counts_ref, pack_ref, target_ref, out_ref, value_ref, total_ref, first_list, second_list, owner_ref,
+    order_ref
 ):
     leaf_count, q_width, p_width = out_ref.shape
     slot_count = ulist_ref.shape[0]
+    leaf_pieces = p_width // PIECE
+    block_pieces = BLOCK // PIECE
     member_blocks = -(-slot_count * p_width // BLOCK)
     spare_block = 8 * member_blocks + 10 * UNROLL
+    zero_piece = 3 * leaf_count * leaf_pieces
     group_count = leaf_count // 8
     index = lax.axis_index("oct")
-    buffers = (first_ref, second_ref)
-
-    def source_of(slot, leaf):
-        leaf_id = ulist_ref[slot, leaf]
-        side = 0 if slot == 0 else (-1 if slot < 9 else (0 if slot < 18 else 1))
-        place = jnp.where(leaf_id >= 0, leaf_id - (index + side) * leaf_count, 0)
-        if side == 0:
-            count, pack = counts_ref[place], own_pack_ref[place]
-        else:
-            half = (side + 1) // 2
-            count, pack = side_counts_ref[half, place], side_pack_ref[half * leaf_count + place]
-        return jnp.where(leaf_id >= 0, jnp.bitwise_and(count + 15, -16), 0), pack
-
-    def gather(half, leaf, member, block):
-        gather_ref = buffers[half]
-        offset = block * BLOCK
+    lists = (first_list, second_list)
+
+    def class_of(leaf):
+        return lax.shift_right_logical(counts_ref[1, leaf] - 1, 5)
+
+    def tally(leaf, totals):
+        own = class_of(leaf)
+        return tuple(total + (own == number).astype(jnp.int32) for number, total in enumerate(totals))
+
+    zero = jnp.int32(0)
+    totals = lax.fori_loop(0, leaf_count, tally, (zero,) * 4)
+
+    def assign(leaf, places):
+        own = class_of(leaf)
+        place = places[0]
+        for number in range(1, 4):
+            place = jnp.where(own == number, places[number], place)
+        order_ref[place] = leaf
+        return tuple(value + (own == number).astype(jnp.int32) for number, value in enumerate(places))
+
+    starts = (zero, totals[0], totals[0] + totals[1], totals[0] + totals[1] + totals[2])
+    lax.fori_loop(0, leaf_count, assign, starts)
+
+    def enlist(half, leaf, member, block):
+        list_ref = lists[half]
+        place = block * block_pieces
         for slot in range(slot_count):
-            length, pack = source_of(slot, leaf)
-            gather_ref[pl.ds(pl.multiple_of(offset, 16), p_width), :] = pack
-            offset = offset + length
-        gather_ref[pl.ds(pl.multiple_of(offset, 16), BLOCK), :] = jnp.zeros((BLOCK, 128), BF16)
+            side = 1 if slot == 0 else (0 if slot < 9 else (1 if slot < 18 else 2))
+            leaf_id = ulist_ref[slot, leaf]
+            near = jnp.where(leaf_id >= 0, leaf_id - (index + (side - 1)) * leaf_count, 0)
+            length = lax.shift_right_logical(counts_ref[side, near] + (PIECE - 1), PIECE.bit_length() - 1)
+            piece = (near + side * leaf_count) * leaf_pieces
+            for number in range(leaf_pieces):
+                list_ref[place + number] = piece + number
+            place = place + jnp.where(leaf_id >= 0, length, 0)
+        for number in range(block_pieces):
+            list_ref[place + number] = zero_piece
         for number in range(member_blocks):
             owner_ref[half, UNROLL + block + number] = member
-        return lax.shift_right_logical(offset + (BLOCK - 1), BLOCK.bit_length() - 1)
+        return lax.shift_right_logical(place + (block_pieces - 1), block_pieces.bit_length() - 1)
 
     for half in range(2):
         for number in range(UNROLL):
             owner_ref[half, number] = 8
 
-    first_count = lax.fori_loop(0, 8, lambda member, block: gather(0, member, member, block), 0)
+        def clear(number, carry, half=half):
+            lists[half][number] = zero_piece
+            return carry
+
+        lax.fori_loop(0, lists[half].shape[0], clear, 0)
+
+    first_count = lax.fori_loop(0, 8, lambda member, block: enlist(0, order_ref[member], member, block), 0)
 
     def group_step(group, half, block_count):
         for number in range(10 * UNROLL):
             owner_ref[half, UNROLL + block_count + number] = 8
         total_ref[...] = jnp.zeros_like(total_ref)
-        later = jnp.minimum(group + 1, group_count - 1)
+        later = jnp.minimum(group + 1, group_count - 1) * 8
 
         def sources_of(block):
-            return buffers[half][pl.ds(pl.multiple_of(block * BLOCK, BLOCK), BLOCK), :]
-
-        def blocks_step(step, later_block):
-            slot = jnp.bitwise_and(step, 1) * UNROLL
-            for part in range(UNROLL):
-                block = jnp.maximum(step - 1, 0) * UNROLL + part
-                member = owner_ref[half, step * UNROLL + part]
-                values = jnp.concatenate([value_ref[UNROLL - slot + part, side] for side in range(2)], axis=1)
-                total_ref[member] += dot(values, sources_of(block))
-            for part in range(UNROLL):
-                block = step * UNROLL + part
-                member = owner_ref[half, UNROLL + block]
-                targets = target_ref[group * 8 + jnp.minimum(member, 7)]
-                values = jnp.exp2(dot_nt(targets, sources_of(block))).astype(BF16)
-                for side in range(2):
-                    value_ref[slot + part, side] = values[:, side * 128 : (side + 1) * 128]
-            live = step < 8
-            member = jnp.minimum(step, 7)
-            place = jnp.where(live, later_block, spare_block)
-            following = gather(1 - half, later * 8 + member, member, place)
-            return jnp.where(live, following, later_block)
-
-        steps = jnp.maximum(lax.div(block_count + (2 * UNROLL - 1), UNROLL), 8)
-        later_count = lax.fori_loop(0, steps, blocks_step, 0)
+            rows = []
+            for number in range(block_pieces):
+                piece = lists[half][block * block_pieces + number]
+                rows.append(pack_ref[pl.ds(pl.multiple_of(piece * PIECE, PIECE), PIECE), :])
+            return jnp.concatenate(rows, axis=0)
+
+        def run(rows):
+            def blocks_step(step, later_block):
+                slot = jnp.bitwise_and(step, 1) * UNROLL
+                for part in range(UNROLL):
+                    block = jnp.maximum(step - 1, 0) * UNROLL + part
+                    member = owner_ref[half, step * UNROLL + part]
+                    values = [value_ref[UNROLL - slot + part, side, :rows] for side in range(2)]
+                    total_ref[member, :rows] += dot(jnp.concatenate(values, axis=1), sources_of(block))
+                for part in range(UNROLL):
+                    block = step * UNROLL + part
+                    member = owner_ref[half, UNROLL + block]
+                    leaf = order_ref[group * 8 + jnp.minimum(member, 7)]
+                    targets = target_ref[leaf, :rows]
+                    values = jnp.exp2(dot_nt(targets, sources_of(block))).astype(BF16)
+                    for side in range(2):
+                        value_ref[slot + part, side, :rows] = values[:, side * 128 : (side + 1) * 128]
+                live = step < 8
+                member = jnp.minimum(step, 7)
+                place = jnp.where(live, later_block, spare_block)
+                following = enlist(1 - half, order_ref[later + member], member, place)
+                return jnp.where(live, following, later_block)
+
+            steps = jnp.maximum(lax.div(block_count + (2 * UNROLL - 1), UNROLL), 8)
+            return lax.fori_loop(0, steps, blocks_step, 0)
+
+        largest = class_of(order_ref[group * 8 + 7])
+        later_count = lax.switch(largest, [lambda rows=rows: run(rows) for rows in (32, 64, 96, 128)])
 
         for member in range(8):
-            turned = total_ref[member].T
-            out_ref[group * 8 + member] = turned[:q_width] + turned[q_width : 2 * q_width]
+            turned = total_ref[member, :, : 2 * q_width].T
+            out_ref[order_ref[group * 8 + member]] = turned[:q_width] + turned[q_width:]
         return later_count
 
     def pair_step(pair, block_count):
@@ -302,41 +352,52 @@
     lax.fori_loop(0, group_count // 2, pair_step, first_count)
 
 
-def pack_kernel(lower_ref, upper_ref, sum_ref, pair_ref, shift_ref, pack_ref, counts_ref, top_ref, next_ref):
+def pack_kernel(
+    lower_ref, upper_ref, own_ref, own_counts_ref, sum_ref, pair_ref, shift_ref, pack_ref, counts_ref, top_ref, next_ref
+):
     leaf_count, rows, p_width = lower_ref.shape
     q_width = rows - 8
+    leaf_rows = leaf_count * p_width
     index = lax.axis_index("oct")
     top = sum_ref[...] + pair_ref[...]
     top_ref[...] = top
     next_ref[...] = dot3(top, shift_ref[jnp.right_shift(index, 3) & 7])
     lane = iota((1, p_width), 1)
+    select_right = selector(RIGHT)
+    blank = jnp.zeros((p_width - 2 * q_width - 32, p_width), F32)
+    pack_ref[leaf_rows : 2 * leaf_rows, :] = own_ref[...].reshape(leaf_rows, 128)
+    pack_ref[3 * leaf_rows :, :] = jnp.zeros((PIECE, 128), BF16)
 
     def pack_step(step, counts):
-        lower_counts, upper_counts = counts
+        side_counts = list(counts)
         for part in range(4):
             leaf = step * 4 + part
-            for side, source in ((0, lower_ref), (1, upper_ref)):
-                packed = packed_rows(source[leaf, :q_width, :], pieces(source[leaf, q_width:, :]))
-                pack_ref[side * leaf_count + leaf] = packed.T
-            lower_counts = jnp.where(lane == leaf, lower_ref[leaf, q_width + 3 : q_width + 4, :], lower_counts)
-            upper_counts = jnp.where(lane == leaf, upper_ref[leaf, q_width + 3 : q_width + 4, :], upper_counts)
-        return lower_counts, upper_counts
+            for side, source in ((0, lower_ref), (2, upper_ref)):
+                high, low = weight_rows(source[leaf, :q_width, :])
+                tail = source[leaf, q_width:, :]
+                right = dot(select_right, stacked(tail))
+                packed = jnp.concatenate([high, low, right, blank], axis=0).T.astype(BF16)
+                start = pl.multiple_of(side * leaf_rows + leaf * p_width, p_width)
+                pack_ref[pl.ds(start, p_width), :] = packed
+                side_counts[side // 2] = jnp.where(lane == leaf, tail[3:4], side_counts[side // 2])
+        return tuple(side_counts)
 
     nothing = jnp.zeros((1, p_width), F32)
     lower_counts, upper_counts = lax.fori_loop(0, leaf_count // 4, pack_step, (nothing, nothing))
     counts_ref[0:1, :] = lower_counts.astype(jnp.int32)
-    counts_ref[1:2, :] = upper_counts.astype(jnp.int32)
+    counts_ref[1:2, :leaf_count] = own_counts_ref[...]
+    counts_ref[2:3, :] = upper_counts.astype(jnp.int32)
 
 
 def final_kernel(
-    level_count, pack_ref, surface_ref, counts_ref, near_ref, far_ref, coarse_ref, shift_ref,
-    down_ref, *rest
+    level_count, points_ref, surface_ref, counts_ref, near_ref, far_ref, coarse_ref, shift_ref, down_ref, *rest
 ):
     top_refs, (out_ref, node_ref, down_leaf_ref) = rest[:level_count], rest[level_count:]
     leaf_count, q_width, p_width = out_ref.shape
     eq_width = far_ref.shape[1]
     node_count = leaf_count // 8
     index = lax.axis_index("oct")
+    select_left, select_right = selector(LEFT), selector(RIGHT)
     slab_local = jnp.zeros((q_width, eq_width), F32)
     for level, top_ref in enumerate(top_refs):
         slab_local = slab_local + dot3(top_ref[...], coarse_ref[jnp.right_shift(index, 3 * level) & 7])
@@ -354,15 +415,13 @@
     def node_step(node, carry):
         for child in range(8):
             leaf = node * 8 + child
-            values = jnp.exp2(dot(pack_ref[leaf], padded_left(pieces(coords_of(surface_ref, leaf)))))
-            values_high, values_low = halves(values)
+            right = dot(select_right, stacked(coords_of(points_ref, leaf)))
+            values_high, values_low = kernel_rows(surface_ref, leaf, right, select_left)
             down = down_leaf_ref[child, pl.ds(pl.multiple_of(node * q_width, q_width), q_width), :]
-            down_high = down.astype(BF16).astype(F32)
-            down_rows = jnp.concatenate([down_high, down - down_high], axis=0).astype(BF16)
-            down_first = jnp.concatenate([down_high, jnp.zeros_like(down_high)], axis=0).astype(BF16)
-            turned = (dot_nt(values_high, down_rows) + dot_nt(values_low, down_first)).T
-            summed = turned[:q_width] + turned[q_width : 2 * q_width] + near_ref[leaf]
-            out_ref[leaf] = jnp.where(lane < counts_ref[leaf], summed, 0.0)
+            high, low = weight_rows(down)
+            both = dot(jnp.concatenate([high, low], axis=0).astype(BF16), values_high)
+            far = both[:q_width] + both[q_width:] + dot(high.astype(BF16), values_low)
+            out_ref[leaf] = jnp.where(lane < counts_ref[leaf], far + near_ref[leaf], 0.0)
         return carry
 
     lax.fori_loop(0, node_count, node_step, 0)
@@ -402,7 +461,6 @@
     vmem = pl.BlockSpec(memory_space=pltpu.VMEM)
     smem = pl.BlockSpec(memory_space=pltpu.SMEM)
     hbm = pl.BlockSpec(memory_space=pl.ANY)
-    params = pltpu.CompilerParams(vmem_limit_bytes=VMEM_LIMIT)
     points = jnp.transpose(points, (1, 0, 2))
     surface = jnp.transpose(surface, (1, 0, 2))
     ulist = ulist.T
@@ -420,7 +478,7 @@
         in_specs=[vmem, vmem, vmem, smem, vmem, vmem],
         out_specs=(vmem,) * 5,
         scratch_shapes=[pltpu.VMEM((8, node_rows, eq_width), F32)],
-        compiler_params=params,
+        compiler_params=grant(24),
         name="upward",
     )(points, dens, surface, counts, up_inverse, shift_up)
 
@@ -446,25 +504,25 @@
             pltpu.VMEM((eq_width, node_rows), F32),
             pltpu.SemaphoreType.DMA((eq_width // 8, type_count // 128 + 1)),
         ],
-        compiler_params=params,
+        compiler_params=grant(36),
         cost_estimate=pl.CostEstimate(flops=2 * 10**10, bytes_accessed=18 * 10**6, transcendentals=0),
         name="far",
     )(send_lower, send, send_upper, vlist, table)
     far_node, lower, upper = lax.optimization_barrier((far_node, lower, upper))
 
-    side_pack, side_counts, top, current = pl.pallas_call(
+    all_pack, all_counts, top, current = pl.pallas_call(
         pack_kernel,
         out_shape=(
-            jax.ShapeDtypeStruct((2 * leaf_count, p_width, 128), BF16),
-            jax.ShapeDtypeStruct((2, p_width), jnp.int32),
+            jax.ShapeDtypeStruct((3 * leaf_count * p_width + PIECE, 128), BF16),
+            jax.ShapeDtypeStruct((3, p_width), jnp.int32),
             jax.ShapeDtypeStruct((q_width, eq_width), F32),
             jax.ShapeDtypeStruct((q_width, eq_width), F32),
         ),
-        in_specs=[vmem] * 5,
+        in_specs=[vmem] * 7,
         out_specs=(vmem,) * 4,
-        compiler_params=params,
+        compiler_params=grant(20),
         name="pack",
-    )(lower, upper, total, pair, shift_up)
+    )(lower, upper, pack, counts.reshape(1, leaf_count), total, pair, shift_up)
 
     tops = [top]
     for level in range(3, bits, 3):
@@ -475,23 +533,24 @@
         tops.append(current)
 
     member_blocks = -(-ulist.shape[0] * p_width // BLOCK)
-    gather_rows = (9 * member_blocks + 10 * UNROLL + 2) * BLOCK
+    list_blocks = 9 * member_blocks + 10 * UNROLL + 2
     near = pl.pallas_call(
         near_kernel,
         out_shape=jax.ShapeDtypeStruct((leaf_count, q_width, p_width), F32),
-        in_specs=[smem, smem, smem, vmem, vmem, vmem],
+        in_specs=[smem, smem, vmem, vmem],
         out_specs=vmem,
         scratch_shapes=[
-            pltpu.VMEM((gather_rows, 128), BF16),
-            pltpu.VMEM((gather_rows, 128), BF16),
             pltpu.VMEM((2 * UNROLL, 2, p_width, 128), BF16),
             pltpu.VMEM((9, p_width, 128), F32),
-            pltpu.SMEM((2, 9 * member_blocks + 12 * UNROLL), jnp.int32),
+            pltpu.SMEM((list_blocks * (BLOCK // PIECE),), jnp.int32),
+            pltpu.SMEM((list_blocks * (BLOCK // PIECE),), jnp.int32),
+            pltpu.SMEM((2, list_blocks + 2 * UNROLL), jnp.int32),
+            pltpu.SMEM((leaf_count,), jnp.int32),
         ],
-        compiler_params=params,
+        compiler_params=grant(24),
         cost_estimate=pl.CostEstimate(flops=3 * 10**10, bytes_accessed=10**7, transcendentals=0),
         name="near",
-    )(ulist, counts, side_counts, pack, side_pack, targets)
+    )(ulist, all_counts, all_pack, targets)
 
     return pl.pallas_call(
         lambda *refs: final_kernel(len(tops), *refs),
@@ -502,9 +561,9 @@
             pltpu.VMEM((node_rows, eq_width), F32),
             pltpu.VMEM((8, node_rows, eq_width), F32),
         ],
-        compiler_params=params,
+        compiler_params=grant(20),
         name="final",
-    )(pack, surface, counts, near, far_node, coarse, shift_down, down_inverse, *tops)
+    )(points, surface, counts, near, far_node, coarse, shift_down, down_inverse, *tops)
 
 
 def solution(mesh):

time: 161 us -> 224 us (1.39)
  Pallas kernels: 129 us -> 182 us
  local copies, waits for them, and re-layouts: 2.14 us -> 14.4 us
    pallas_call x1, Pallas kernels: 63.7 us -> 94.7 us  [local(): pl.pallas_call(near_kernel, out_shape=jax.ShapeDtypeStruct((leaf_count, q...]
    unnamed x12 -> x38, local copies, waits for them, and re-layouts: 2.14 us -> 14.4 us
    pallas_call x1, Pallas kernels: 17.8 us -> 30.1 us  [local(): pl.pallas_call(lambda *refs: final_kernel(len(tops), *refs), out_shape=ja...]
    pallas_call x1, Pallas kernels: 13.4 us -> 23.3 us  [local(): pl.pallas_call(upward_kernel, out_shape=(jax.ShapeDtypeStruct((leaf_count...]
  transfers between devices with their start and end apart: 8 -> 8, of which waited for: 3 -> 3; matrix products, arithmetic and copies ran while one was open for 0% -> 0% of each run, Pallas kernels for 58% -> 56%
where the time goes in v3:
time: 224 us; the launch traced here: 221 us
  Pallas kernels  182 us (81%)
  starting transfers between devices  18.9 us (8%)
  local copies, waits for them, and re-layouts  14.4 us (6%)
  waiting for transfers between devices  5.6 us (2%)
    pallas_call x1, Pallas kernels, local(): pl.pallas_call(near_kernel, out_shape=jax.ShapeDtypeStruct((leaf_count, q...  94.7 us
    pallas_call x1, Pallas kernels, local(): pl.pallas_call(lambda *refs: final_kernel(len(tops), *refs), out_shape=ja...  30.1 us
    pallas_call x1, Pallas kernels, local(): pl.pallas_call(far_kernel, out_shape=jax.ShapeDtypeStruct((node_rows, eq_...  29.4 us
    pallas_call x1, Pallas kernels, local(): pl.pallas_call(upward_kernel, out_shape=(jax.ShapeDtypeStruct((leaf_count...  23.3 us
    unnamed x38, local copies, waits for them, and re-layouts  14.4 us
    ppermute x4, starting transfers between devices, shifted(): return (lax.ppermute(value, 'oct', up), lax.ppermute(value, 'oct', down))  12.9 us
    ppermute x4, starting transfers between devices, swapped(): lax.ppermute(value, 'oct', [(source, source ^ 1 << bit) for source in ran...  6.02 us
    pallas_call x1, Pallas kernels, local(): pl.pallas_call(pack_kernel, out_shape=(jax.ShapeDtypeStruct((3 * leaf_cou...  4.59 us
  transfers between devices with their start and end apart: 8, of which 3 were waited for; matrix products, arithmetic and copies ran while one was open for 0% of the time, Pallas kernels for 56%

profile of v3, /device:TPU:1, one launch (start us, length us, event | category | flops | bytes accessed | tf_op | source)
XLA Modules:
  0.0 221.4 jit_solution(122363720385806042)
XLA Ops:
  0.0 1.3 copy-done
  1.3 1.2 copy-done.4
  2.5 0.9 copy-done.5
  3.4 0.9 copy-done.7
  4.3 0.9 copy-done.9
  5.3 0.7 copy-done.11
  5.9 23.3 %upward.1 = (bf16[64,128,128]{2,1,0:T(8,128)(2,1)S(1)}, bf16[64,128,128]{2,1,0:T(8,128)(2,1)S(1)}, f32[64,40,128]{2,1,0:T(8,128)S(1)}, bf16[352,152]{1,0:T(8,128)(2,1)S(1)}, f32[32,152]{1,0:T(8,128)S(1)}) custom-call(f32[3,64,128]{2,1,0:T(8,128)S(1)} %bitcast.9, f32[64,32,128]{2,1,0:T(8,128)S(1)} %copy-done.4, f32[3,64,152]{2,1,0:T(8,128)S(1)} %bitcast.7, ...), custom_call_target="tpu_custom_call" | custom-call | tf_op jit(solution)/shard_map/upward/pallas_call | solution.py:469
  29.2 1.3 copy-done.14
  30.6 1.1 copy-done.16
  31.6 2.0 collective-permute-start.1
  33.6 4.5 %collective-permute-start = (bf16[352,152]{1,0:T(8,128)(2,1)S(1)}, bf16[352,152]{1,0:T(8,128)(2,1)S(1)}, u32[]{:S(2)}, u32[]{:S(2)}) collective-permute-start(bf16[352,152]{1,0:T(8,128)(2,1)S(1)} %get-tuple-element.21.own_ref), channel_id=1, source_target_pairs={{0,1},{1,2},{2,3},{3,4},{4,5},{5,6},{6,7},{7,8},{8,9},{9,10},{10,1... | collective-permute-start | bytes 321032 | tf_op jit(solution)/shard_map/ppermute | solution.py:433
  38.1 1.2 collective-permute-done.1.upper_ref
  39.3 3.1 %collective-permute-done.lower_ref = bf16[352,152]{1,0:T(8,128)(2,1)S(1)} collective-permute-done((bf16[352,152]{1,0:T(8,128)(2,1)S(1)}, bf16[352,152]{1,0:T(8,128)(2,1)S(1)}, u32[]{:S(2)}, u32[]{:S(2)}) %collective-permute-start) | collective-permute-done | bytes 107040 | tf_op jit(solution)/shard_map/ppermute | solution.py:433
  42.4 0.3 collective-permute-start.2
  42.7 4.6 %collective-permute-start.4 = (f32[64,40,128]{2,1,0:T(8,128)}, f32[64,40,128]{2,1,0:T(8,128)S(1)}, u32[]{:S(2)}, u32[]{:S(2)}) collective-permute-start(f32[64,40,128]{2,1,0:T(8,128)} %copy-done.16), channel_id=1, source_target_pairs={{1,0},{2,1},{3,2},{4,3},{5,4},{6,5},{7,6},{8,7},{9,8},{10,9},{11,1... | collective-permute-start | bytes 3932168 | tf_op jit(solution)/shard_map/ppermute | solution.py:433
  47.2 1.9 collective-permute-start.3
  49.2 0.0 collective-permute-done.2
  49.2 1.3 collective-permute-start.5
  50.5 6.0 %copy-done.13 = bf16[316,152,152]{0,2,1:T(8,128)(2,1)S(1)} copy-done((bf16[316,152,152]{0,2,1:T(8,128)(2,1)S(1)}, bf16[316,152,152]{0,2,1:T(8,128)(2,1)}, u32[]{:S(2)}) %copy-start.13) | copy-done | bytes 14601752
  56.6 29.4 %far.1.refs_4_ = f32[256,152]{1,0:T(8,128)S(1)} custom-call(bf16[352,152]{1,0:T(8,128)(2,1)S(1)} %collective-permute-done.lower_ref, bf16[352,152]{1,0:T(8,128)(2,1)S(1)} %get-tuple-element.21.own_ref, bf16[352,152]{1,0:T(8,128)(2,1)S(1)} %collective-permute-done.1.upper_ref, s32[8,316]{1,0:T(8,128)S(1)} %copy-done.18, bf16[23104,316]{1,0:T(8,128)(2,1)S(1)} %bitcast.12), custom_call_target="tpu_custom_call" | custom-call | flops 20000000000 | bytes 18000000 | tf_op jit(solution)/shard_map/far/pallas_call | solution.py:495
  86.0 0.0 collective-permute-done.4.upper_ref
  86.0 0.0 collective-permute-done.5.pair_ref
  86.1 0.0 copy-start.17
  86.1 4.6 %pack.1 = (bf16[24608,128]{1,0:T(8,128)(2,1)S(1)}, s32[3,128]{1,0:T(4,128)S(1)}, f32[32,152]{1,0:T(8,128)S(1)}, f32[32,152]{1,0:T(8,128)S(1)}) custom-call(f32[64,40,128]{2,1,0:T(8,128)S(1)} %collective-permute-done.3.lower_ref, f32[64,40,128]{2,1,0:T(8,128)S(1)} %collective-permute-done.4.upper_ref, bf16[64,128,128]{2,1,0:T(8,128)(2,1)S(1)} %get-tuple-element.29.own_ref, ...), custom_call_target="tpu_custom_call" | custom-call | tf_op jit(solution)/shard_map/pack/pallas_call | solution.py:513
  90.7 1.9 collective-permute-start.6
  92.6 1.3 collective-permute-done.6
  94.0 2.5 %collective-permute-start.7 = (f32[32,152]{1,0:T(8,128)S(1)}, f32[32,152]{1,0:T(8,128)S(1)}, u32[]{:S(2)}, u32[]{:S(2)}) collective-permute-start(f32[32,152]{1,0:T(8,128)S(1)} %add.22), channel_id=1, source_target_pairs={{0,16},{1,17},{2,18},{3,19},{4,20},{5,21},{6,22},{7,23},{8,24},{9,... | collective-permute-start | bytes 58376 | tf_op jit(solution)/shard_map/ppermute | solution.py:437
  96.4 0.0 copy-start.6
  96.5 0.0 copy-start.8
  96.5 0.0 copy-start.10
  96.5 94.7 %near.1.refs_3_ = f32[64,32,128]{2,1,0:T(8,128)S(1)} custom-call(s32[27,64]{1,0:T(8,128)S(1)} %bitcast.13, s32[3,128]{1,0:T(4,128)S(1)} %get-tuple-element.31.counts_ref, bf16[24608,128]{1,0:T(8,128)(2,1)S(1)} %get-tuple-element.32.pack_ref, bf16[64,128,128]{2,1,0:T(8,128)(2,1)S(1)} %copy-done.15), custom_call_target="tpu_custom_call" | custom-call | flops 30000001024 | bytes 10000000 | tf_op jit(solution)/shard_map/near/pallas_call | solution.py:537
  191.3 30.1 %final.1 = f32[64,32,128]{2,1,0:T(8,128)} custom-call(f32[3,64,128]{2,1,0:T(8,128)S(1)} %bitcast.10, f32[3,64,152]{2,1,0:T(8,128)S(1)} %bitcast.8, s32[64]{0:T(128)S(1)} %copy-done.12, f32[64,32,128]{2,1,0:T(8,128)S(1)} %near.1.refs_3_, f32[256,152]{1,0:T(8,128)S(1)} %far.1.refs_4_, f32[8,152,152]{2,1,0:T(8,128)S(1)} %copy-done.2, ...), custom_call_target="tpu_custom_call" | custom-call | tf_op jit(solution)/shard_map/final/pallas_call | solution.py:555
  (32 shorter events, 0.1 us)
Async XLA Ops:
  0.0 1.3 copy-start
  1.3 1.2 copy-start.4
  2.5 0.9 copy-start.5
  3.4 0.9 copy-start.7
  4.3 0.9 copy-start.9
  5.3 0.7 copy-start.11
  5.9 44.6 %copy-start.18 = (s32[8,316]{1,0:T(8,128)S(1)}, s32[8,316]{1,0:T(8,128)}, u32[]{:S(2)}) copy-start(s32[8,316]{1,0:T(8,128)} %vlist_ref.1) | copy-start | bytes 30340
  29.2 1.3 copy-start.14
  30.6 1.1 copy-start.16
  31.6 7.7 %collective-permute-start.1 = (bf16[352,152]{1,0:T(8,128)(2,1)S(1)}, bf16[352,152]{1,0:T(8,128)(2,1)S(1)}, u32[]{:S(2)}, u32[]{:S(2)}) collective-permute-start(bf16[352,152]{1,0:T(8,128)(2,1)S(1)} %get-tuple-element.21.own_ref), channel_id=1, source_target_pairs={{1,0},{2,1},{3,2},{4,3},{5,4},{6,5},{7,6},{8,7},{9,8},{10,9},{11,1... | collective-permute-start | bytes 321032 | tf_op jit(solution)/shard_map/ppermute | solution.py:433
  33.6 8.8 %collective-permute-start = (bf16[352,152]{1,0:T(8,128)(2,1)S(1)}, bf16[352,152]{1,0:T(8,128)(2,1)S(1)}, u32[]{:S(2)}, u32[]{:S(2)}) collective-permute-start(bf16[352,152]{1,0:T(8,128)(2,1)S(1)} %get-tuple-element.21.own_ref), channel_id=1, source_target_pairs={{0,1},{1,2},{2,3},{3,4},{4,5},{5,6},{6,7},{7,8},{8,9},{9,10},{10,1... | collective-permute-start | bytes 321032 | tf_op jit(solution)/shard_map/ppermute | solution.py:433
  42.4 6.8 %collective-permute-start.2 = (f32[32,152]{1,0:T(8,128)S(1)}, f32[32,152]{1,0:T(8,128)S(1)}, u32[]{:S(2)}, u32[]{:S(2)}) collective-permute-start(f32[32,152]{1,0:T(8,128)S(1)} %fusion.1), channel_id=1, source_target_pairs={{0,2},{1,3},{2,0},{3,1},{4,6},{5,7},{6,4},{7,5},{8,10},{9,11},{10,... | collective-permute-start | bytes 58376 | tf_op jit(solution)/shard_map/ppermute | solution.py:437
  42.7 43.4 %collective-permute-start.4 = (f32[64,40,128]{2,1,0:T(8,128)}, f32[64,40,128]{2,1,0:T(8,128)S(1)}, u32[]{:S(2)}, u32[]{:S(2)}) collective-permute-start(f32[64,40,128]{2,1,0:T(8,128)} %copy-done.16), channel_id=1, source_target_pairs={{1,0},{2,1},{3,2},{4,3},{5,4},{6,5},{7,6},{8,7},{9,8},{10,9},{11,1... | collective-permute-start | bytes 3932168 | tf_op jit(solution)/shard_map/ppermute | solution.py:433
  47.2 38.8 %collective-permute-start.3 = (f32[64,40,128]{2,1,0:T(8,128)}, f32[64,40,128]{2,1,0:T(8,128)S(1)}, u32[]{:S(2)}, u32[]{:S(2)}) collective-permute-start(f32[64,40,128]{2,1,0:T(8,128)} %copy-done.16), channel_id=1, source_target_pairs={{0,1},{1,2},{2,3},{3,4},{4,5},{5,6},{6,7},{7,8},{8,9},{9,10},{10,1... | collective-permute-start | bytes 3932168 | tf_op jit(solution)/shard_map/ppermute | solution.py:433
  49.2 36.9 %collective-permute-start.5 = (f32[32,152]{1,0:T(8,128)S(1)}, f32[32,152]{1,0:T(8,128)S(1)}, u32[]{:S(2)}, u32[]{:S(2)}) collective-permute-start(f32[32,152]{1,0:T(8,128)S(1)} %add.21.sum_ref), channel_id=1, source_target_pairs={{0,4},{1,5},{2,6},{3,7},{4,0},{5,1},{6,2},{7,3},{8,12},{9,13},{10,... | collective-permute-start | bytes 58376 | tf_op jit(solution)/shard_map/ppermute | solution.py:437
  50.5 6.0 %copy-start.13 = (bf16[316,152,152]{0,2,1:T(8,128)(2,1)S(1)}, bf16[316,152,152]{0,2,1:T(8,128)(2,1)}, u32[]{:S(2)}) copy-start(bf16[316,152,152]{0,2,1:T(8,128)(2,1)} %param.23) | copy-start | bytes 43805188
  56.6 29.5 %copy-start.1 = (f32[8,152,152]{2,1,0:T(8,128)S(1)}, f32[8,152,152]{2,1,0:T(8,128)}, u32[]{:S(2)}) copy-start(f32[8,152,152]{2,1,0:T(8,128)} %shift_ref.3) | copy-start | bytes 2217988
  56.6 29.5 %copy-start.12 = (s32[64]{0:T(128)S(1)}, s32[64]{0:T(128)}, u32[]{:S(2)}) copy-start(s32[64]{0:T(128)} %refs_2_.1) | copy-start | bytes 772
  86.1 10.4 %copy-start.15 = (bf16[64,128,128]{2,1,0:T(8,128)(2,1)S(1)}, bf16[64,128,128]{2,1,0:T(8,128)(2,1)}, u32[]{:S(2)}) copy-start(bf16[64,128,128]{2,1,0:T(8,128)(2,1)} %copy-done.14) | copy-start | bytes 6291460
  86.1 10.3 %copy-start.17 = (s32[64,27]{0,1:T(8,128)S(1)}, s32[64,27]{0,1:T(8,128)}, u32[]{:S(2)}) copy-start(s32[64,27]{0,1:T(8,128)} %param.16) | copy-start | bytes 20740
  90.7 3.2 %collective-permute-start.6 = (f32[32,152]{1,0:T(8,128)S(1)}, f32[32,152]{1,0:T(8,128)S(1)}, u32[]{:S(2)}, u32[]{:S(2)}) collective-permute-start(f32[32,152]{1,0:T(8,128)S(1)} %get-tuple-element.36), channel_id=1, source_target_pairs={{0,8},{1,9},{2,10},{3,11},{4,12},{5,13},{6,14},{7,15},{8,0},{9,1},... | collective-permute-start | bytes 58376 | tf_op jit(solution)/shard_map/ppermute | solution.py:437
  94.0 97.3 %collective-permute-start.7 = (f32[32,152]{1,0:T(8,128)S(1)}, f32[32,152]{1,0:T(8,128)S(1)}, u32[]{:S(2)}, u32[]{:S(2)}) collective-permute-start(f32[32,152]{1,0:T(8,128)S(1)} %add.22), channel_id=1, source_target_pairs={{0,16},{1,17},{2,18},{3,19},{4,20},{5,21},{6,22},{7,23},{8,24},{9,... | collective-permute-start | bytes 58376 | tf_op jit(solution)/shard_map/ppermute | solution.py:437
  96.4 94.8 %copy-start.2 = (f32[8,152,152]{2,1,0:T(8,128)S(1)}, f32[8,152,152]{2,1,0:T(8,128)}, u32[]{:S(2)}) copy-start(f32[8,152,152]{2,1,0:T(8,128)} %refs_5_.1) | copy-start | bytes 2217988
  96.4 94.8 %copy-start.3 = (f32[8,152,152]{2,1,0:T(8,128)S(1)}, f32[8,152,152]{2,1,0:T(8,128)}, u32[]{:S(2)}) copy-start(f32[8,152,152]{2,1,0:T(8,128)} %refs_6_.1) | copy-start | bytes 2217988
  96.4 94.8 %copy-start.6 = (f32[64,3,152]{2,0,1:T(8,128)S(1)}, f32[64,3,152]{2,0,1:T(8,128)}, u32[]{:S(2)}) copy-start(f32[64,3,152]{2,0,1:T(8,128)} %param.14) | copy-start | bytes 350212
  96.5 94.8 %copy-start.8 = (f32[64,3,128]{2,0,1:T(8,128)S(1)}, f32[64,3,128]{2,0,1:T(8,128)}, u32[]{:S(2)}) copy-start(f32[64,3,128]{2,0,1:T(8,128)} %param.12) | copy-start | bytes 294916
  96.5 94.8 %copy-start.10 = (f32[152,152]{1,0:T(8,128)S(1)}, f32[152,152]{1,0:T(8,128)}, u32[]{:S(2)}) copy-start(f32[152,152]{1,0:T(8,128)} %refs_7_.1) | copy-start | bytes 277252

commit v4 on v2

--- a/solution.py
+++ b/solution.py
@@ -11,11 +11,12 @@
 BF16 = jnp.bfloat16
 HIGHEST = lax.Precision.HIGHEST
 SCALE = math.sqrt(math.log2(math.e))
-VMEM_LIMIT = 56 * 1024 * 1024
 NT = (((1,), (1,)), ((), ()))
 TN = (((0,), (0,)), ((), ()))
 BLOCK = 256
 UNROLL = 4
+GROUP = 16
+PLAN_SOURCE, PLAN_ORDER, PLAN_COUNT = 32, 62, 63
 SOURCES = 32
 
 
@@ -41,6 +42,10 @@
     left_high, left_low = halves(left)
     right_high, right_low = halves(right)
     return dot(left_high, right_high) + dot(left_high, right_low) + dot(left_low, right_high)
+
+
+def grant(mebibytes):
+    return pltpu.CompilerParams(vmem_limit_bytes=mebibytes * 1024 * 1024)
 
 
 def iota(shape, dim):
@@ -219,118 +224,147 @@
 
 
 def near_kernel(
-    ulist_ref, counts_ref, side_counts_ref, own_pack_ref, side_pack_ref, target_ref, out_ref, first_ref, second_ref,
-    value_ref, total_ref, owner_ref
+    plan_ref, own_pack_ref, side_pack_ref, target_ref, out_ref, gather_ref, value_ref, total_ref, owner_ref
 ):
     leaf_count, q_width, p_width = out_ref.shape
-    slot_count = ulist_ref.shape[0]
+    slot_count = 27
     member_blocks = -(-slot_count * p_width // BLOCK)
-    spare_block = 8 * member_blocks + 10 * UNROLL
-    group_count = leaf_count // 8
+    total_ref[...] = jnp.zeros_like(total_ref)
+    for number in range(UNROLL):
+        owner_ref[number] = leaf_count
+
+    def group_step(group, carry):
+        def gather(member, inner):
+            leaf = plan_ref[PLAN_ORDER, group * GROUP + member]
+            for slot in range(slot_count):
+                pack_ref = own_pack_ref if slot == 0 or 9 <= slot < 18 else side_pack_ref
+                source = pl.multiple_of(plan_ref[PLAN_SOURCE + slot, leaf], p_width)
+                offset = pl.multiple_of(plan_ref[slot, leaf], 16)
+                gather_ref[pl.ds(offset, p_width), :] = pack_ref[pl.ds(source, p_width), :]
+            offset = pl.multiple_of(plan_ref[slot_count, leaf], 16)
+            gather_ref[pl.ds(offset, BLOCK), :] = jnp.zeros((BLOCK, 128), BF16)
+            first = lax.shift_right_logical(plan_ref[0, leaf], 8)
+            for number in range(member_blocks):
+                owner_ref[UNROLL + first + number] = leaf
+            return inner
+
+        lax.fori_loop(0, GROUP, gather, 0)
+        last = plan_ref[PLAN_ORDER, group * GROUP + GROUP - 1]
+        block_count = lax.shift_right_logical(plan_ref[slot_count, last] + (BLOCK - 1), 8)
+        for number in range(2 * UNROLL):
+            owner_ref[UNROLL + block_count + number] = leaf_count
+
+        def sources_of(block):
+            return gather_ref[pl.ds(pl.multiple_of(block * BLOCK, BLOCK), BLOCK), :]
+
+        def run(rows):
+            def blocks_step(step, inner):
+                slot = jnp.bitwise_and(step, 1) * UNROLL
+                for part in range(UNROLL):
+                    block = jnp.maximum(step - 1, 0) * UNROLL + part
+                    leaf = owner_ref[step * UNROLL + part]
+                    values = [value_ref[UNROLL - slot + part, side, :rows] for side in range(2)]
+                    total_ref[leaf, :rows] += dot(jnp.concatenate(values, axis=1), sources_of(block))
+                for part in range(UNROLL):
+                    block = step * UNROLL + part
+                    leaf = jnp.minimum(owner_ref[UNROLL + block], leaf_count - 1)
+                    values = jnp.exp2(dot_nt(target_ref[leaf, :rows], sources_of(block))).astype(BF16)
+                    for side in range(2):
+                        value_ref[slot + part, side, :rows] = values[:, side * 128 : (side + 1) * 128]
+                return inner
+
+            lax.fori_loop(0, lax.div(block_count + (2 * UNROLL - 1), UNROLL), blocks_step, 0)
+
+        largest = plan_ref[PLAN_COUNT, last]
+        for low, rows in ((0, 32), (32, 64), (64, 96), (96, 128)):
+            pl.when((largest > low) & (largest <= rows))(lambda rows=rows: run(rows))
+        return carry
+
+    lax.fori_loop(0, leaf_count // GROUP, group_step, 0)
+
+    def turn_step(step, carry):
+        for part in range(8):
+            turned = total_ref[step * 8 + part, :, : 2 * q_width].T
+            out_ref[step * 8 + part] = turned[:q_width] + turned[q_width:]
+        return carry
+
+    lax.fori_loop(0, leaf_count // 8, turn_step, 0)
+
+
+def as_column(line):
+    width = line.shape[1]
+    wide = jnp.concatenate([line, jnp.zeros((1, 128 - width), F32)], axis=1) if width < 128 else line
+    return jnp.broadcast_to(wide, (128, 128)).T[:width, :width]
+
+
+def plan_of(ulist_ref, counts, plan_ref):
+    slot_count, leaf_count = ulist_ref.shape
     index = lax.axis_index("oct")
-    buffers = (first_ref, second_ref)
-
-    def source_of(slot, leaf):
-        leaf_id = ulist_ref[slot, leaf]
-        side = 0 if slot == 0 else (-1 if slot < 9 else (0 if slot < 18 else 1))
-        place = jnp.where(leaf_id >= 0, leaf_id - (index + side) * leaf_count, 0)
-        if side == 0:
-            count, pack = counts_ref[place], own_pack_ref[place]
-        else:
-            half = (side + 1) // 2
-            count, pack = side_counts_ref[half, place], side_pack_ref[half * leaf_count + place]
-        return jnp.where(leaf_id >= 0, jnp.bitwise_and(count + 15, -16), 0), pack
-
-    def gather(half, leaf, member, block):
-        gather_ref = buffers[half]
-        offset = block * BLOCK
-        for slot in range(slot_count):
-            length, pack = source_of(slot, leaf)
-            gather_ref[pl.ds(pl.multiple_of(offset, 16), p_width), :] = pack
-            offset = offset + length
-        gather_ref[pl.ds(pl.multiple_of(offset, 16), BLOCK), :] = jnp.zeros((BLOCK, 128), BF16)
-        for number in range(member_blocks):
-            owner_ref[half, UNROLL + block + number] = member
-        return lax.shift_right_logical(offset + (BLOCK - 1), BLOCK.bit_length() - 1)
-
-    for half in range(2):
-        for number in range(UNROLL):
-            owner_ref[half, number] = 8
-
-    first_count = lax.fori_loop(0, 8, lambda member, block: gather(0, member, member, block), 0)
-
-    def group_step(group, half, block_count):
-        for number in range(10 * UNROLL):
-            owner_ref[half, UNROLL + block_count + number] = 8
-        total_ref[...] = jnp.zeros_like(total_ref)
-        later = jnp.minimum(group + 1, group_count - 1)
-
-        def sources_of(block):
-            return buffers[half][pl.ds(pl.multiple_of(block * BLOCK, BLOCK), BLOCK), :]
-
-        def blocks_step(step, later_block):
-            slot = jnp.bitwise_and(step, 1) * UNROLL
-            for part in range(UNROLL):
-                block = jnp.maximum(step - 1, 0) * UNROLL + part
-                member = owner_ref[half, step * UNROLL + part]
-                values = jnp.concatenate([value_ref[UNROLL - slot + part, side] for side in range(2)], axis=1)
-                total_ref[member] += dot(values, sources_of(block))
-            for part in range(UNROLL):
-                block = step * UNROLL + part
-                member = owner_ref[half, UNROLL + block]
-                targets = target_ref[group * 8 + jnp.minimum(member, 7)]
-                values = jnp.exp2(dot_nt(targets, sources_of(block))).astype(BF16)
-                for side in range(2):
-                    value_ref[slot + part, side] = values[:, side * 128 : (side + 1) * 128]
-            live = step < 8
-            member = jnp.minimum(step, 7)
-            place = jnp.where(live, later_block, spare_block)
-            following = gather(1 - half, later * 8 + member, member, place)
-            return jnp.where(live, following, later_block)
-
-        steps = jnp.maximum(lax.div(block_count + (2 * UNROLL - 1), UNROLL), 8)
-        later_count = lax.fori_loop(0, steps, blocks_step, 0)
-
-        for member in range(8):
-            turned = total_ref[member].T
-            out_ref[group * 8 + member] = turned[:q_width] + turned[q_width : 2 * q_width]
-        return later_count
-
-    def pair_step(pair, block_count):
-        return group_step(2 * pair + 1, 1, group_step(2 * pair, 0, block_count))
-
-    lax.fori_loop(0, group_count // 2, pair_step, first_count)
-
-
-def pack_kernel(lower_ref, upper_ref, sum_ref, pair_ref, shift_ref, pack_ref, counts_ref, top_ref, next_ref):
+    shape = (leaf_count, leaf_count)
+    row, column = iota(shape, 0), iota(shape, 1)
+    tables = [as_column(line) for line in counts]
+    own = jnp.broadcast_to(counts[1], shape)
+    before = (tables[1] < own) | ((tables[1] == own) & (row < column))
+    rank = jnp.sum(jnp.where(before, 1.0, 0.0), axis=0, keepdims=True)
+    rank_column = as_column(rank).astype(jnp.int32)
+    rank_wide = jnp.broadcast_to(rank, shape).astype(jnp.int32)
+
+    offset = jnp.zeros((1, leaf_count), jnp.int32)
+    offsets = []
+    for slot in range(slot_count):
+        side = 1 if slot == 0 else (0 if slot < 9 else (1 if slot < 18 else 2))
+        ids = ulist_ref[slot : slot + 1, :]
+        place = jnp.where(ids >= 0, ids - (index + (side - 1)) * leaf_count, 0)
+        found = jnp.sum(jnp.where(row == place, tables[side], 0.0), axis=0, keepdims=True).astype(jnp.int32)
+        length = jnp.where(ids >= 0, jnp.bitwise_and(found + 15, -16), 0)
+        start = place + (leaf_count if side == 2 else 0)
+        plan_ref[PLAN_SOURCE + slot : PLAN_SOURCE + slot + 1, :] = start * 128
+        offsets.append(offset)
+        offset = offset + length
+    offsets.append(offset)
+    blocks = lax.shift_right_logical(offset + (BLOCK - 1), 8)
+    blocks_column = as_column(blocks.astype(F32))
+    group_shift = GROUP.bit_length() - 1
+    same = lax.shift_right_logical(rank_column, group_shift) == lax.shift_right_logical(rank_wide, group_shift)
+    first = jnp.sum(jnp.where(same & (rank_column < rank_wide), blocks_column, 0.0), axis=0, keepdims=True)
+    first = first.astype(jnp.int32) * BLOCK
+    for number, value in enumerate(offsets):
+        plan_ref[number : number + 1, :] = first + value
+    order = jnp.sum(jnp.where(rank_column == column, row.astype(F32), 0.0), axis=0, keepdims=True)
+    plan_ref[PLAN_ORDER : PLAN_ORDER + 1, :] = order.astype(jnp.int32)
+    plan_ref[PLAN_COUNT : PLAN_COUNT + 1, :] = counts[1].astype(jnp.int32)
+
+
+def pack_kernel(
+    lower_ref, upper_ref, ulist_ref, own_counts_ref, sum_ref, pair_ref, shift_ref, pack_ref, plan_ref, top_ref, next_ref
+):
     leaf_count, rows, p_width = lower_ref.shape
     q_width = rows - 8
     index = lax.axis_index("oct")
     top = sum_ref[...] + pair_ref[...]
     top_ref[...] = top
     next_ref[...] = dot3(top, shift_ref[jnp.right_shift(index, 3) & 7])
-    lane = iota((1, p_width), 1)
+    lane = iota((1, leaf_count), 1)
 
     def pack_step(step, counts):
-        lower_counts, upper_counts = counts
+        side_counts = list(counts)
         for part in range(4):
             leaf = step * 4 + part
-            for side, source in ((0, lower_ref), (1, upper_ref)):
-                packed = packed_rows(source[leaf, :q_width, :], pieces(source[leaf, q_width:, :]))
-                pack_ref[side * leaf_count + leaf] = packed.T
-            lower_counts = jnp.where(lane == leaf, lower_ref[leaf, q_width + 3 : q_width + 4, :], lower_counts)
-            upper_counts = jnp.where(lane == leaf, upper_ref[leaf, q_width + 3 : q_width + 4, :], upper_counts)
-        return lower_counts, upper_counts
-
-    nothing = jnp.zeros((1, p_width), F32)
+            for side, source in enumerate((lower_ref, upper_ref)):
+                tail = source[leaf, q_width:, :]
+                packed = packed_rows(source[leaf, :q_width, :], pieces(tail)).T
+                start = pl.multiple_of((side * leaf_count + leaf) * p_width, p_width)
+                pack_ref[pl.ds(start, p_width), :] = packed
+                side_counts[side] = jnp.where(lane == leaf, tail[3:4, :leaf_count], side_counts[side])
+        return tuple(side_counts)
+
+    nothing = jnp.zeros((1, leaf_count), F32)
     lower_counts, upper_counts = lax.fori_loop(0, leaf_count // 4, pack_step, (nothing, nothing))
-    counts_ref[0:1, :] = lower_counts.astype(jnp.int32)
-    counts_ref[1:2, :] = upper_counts.astype(jnp.int32)
+    plan_of(ulist_ref, (lower_counts, own_counts_ref[...].astype(F32), upper_counts), plan_ref)
 
 
 def final_kernel(
-    level_count, pack_ref, surface_ref, counts_ref, near_ref, far_ref, coarse_ref, shift_ref,
-    down_ref, *rest
+    level_count, plan_ref, pack_ref, surface_ref, near_ref, far_ref, coarse_ref, shift_ref, down_ref, *rest
 ):
     top_refs, (out_ref, node_ref, down_leaf_ref) = rest[:level_count], rest[level_count:]
     leaf_count, q_width, p_width = out_ref.shape
@@ -351,21 +385,32 @@
     lax.fori_loop(0, 8, child_step, 0)
     lane = iota((q_width, p_width), 1)
 
-    def node_step(node, carry):
-        for child in range(8):
-            leaf = node * 8 + child
-            values = jnp.exp2(dot(pack_ref[leaf], padded_left(pieces(coords_of(surface_ref, leaf)))))
-            values_high, values_low = halves(values)
-            down = down_leaf_ref[child, pl.ds(pl.multiple_of(node * q_width, q_width), q_width), :]
-            down_high = down.astype(BF16).astype(F32)
-            down_rows = jnp.concatenate([down_high, down - down_high], axis=0).astype(BF16)
-            down_first = jnp.concatenate([down_high, jnp.zeros_like(down_high)], axis=0).astype(BF16)
-            turned = (dot_nt(values_high, down_rows) + dot_nt(values_low, down_first)).T
-            summed = turned[:q_width] + turned[q_width : 2 * q_width] + near_ref[leaf]
-            out_ref[leaf] = jnp.where(lane < counts_ref[leaf], summed, 0.0)
+    def leaves_step(step, carry):
+        def run(rows):
+            for part in range(8):
+                leaf = plan_ref[PLAN_ORDER, step * 8 + part]
+                child = jnp.bitwise_and(leaf, 7)
+                node_row = pl.multiple_of(lax.shift_right_logical(leaf, 3) * q_width, q_width)
+                own = pack_ref[pl.ds(pl.multiple_of(leaf * p_width, p_width), rows), :]
+                values = jnp.exp2(dot(own, padded_left(pieces(coords_of(surface_ref, leaf)))))
+                values_high, values_low = halves(values)
+                down = down_leaf_ref[child, pl.ds(node_row, q_width), :]
+                down_high = down.astype(BF16).astype(F32)
+                down_rows = jnp.concatenate([down_high, down - down_high], axis=0).astype(BF16)
+                down_first = jnp.concatenate([down_high, jnp.zeros_like(down_high)], axis=0).astype(BF16)
+                far = dot_nt(values_high, down_rows) + dot_nt(values_low, down_first)
+                if rows < p_width:
+                    far = jnp.concatenate([far, jnp.zeros((p_width - rows, 2 * q_width), F32)], axis=0)
+                turned = far.T
+                summed = turned[:q_width] + turned[q_width:] + near_ref[leaf]
+                out_ref[leaf] = jnp.where(lane < plan_ref[PLAN_COUNT, leaf], summed, 0.0)
+
+        largest = plan_ref[PLAN_COUNT, plan_ref[PLAN_ORDER, step * 8 + 7]]
+        for low, rows in ((0, 32), (32, 64), (64, 96), (96, 128)):
+            pl.when((largest > low) & (largest <= rows))(lambda rows=rows: run(rows))
         return carry
 
-    lax.fori_loop(0, node_count, node_step, 0)
+    lax.fori_loop(0, node_count, leaves_step, 0)
 
 
 def shifted(value, size):
@@ -402,7 +447,7 @@
     vmem = pl.BlockSpec(memory_space=pltpu.VMEM)
     smem = pl.BlockSpec(memory_space=pltpu.SMEM)
     hbm = pl.BlockSpec(memory_space=pl.ANY)
-    params = pltpu.CompilerParams(vmem_limit_bytes=VMEM_LIMIT)
+    params = grant(56)
     points = jnp.transpose(points, (1, 0, 2))
     surface = jnp.transpose(surface, (1, 0, 2))
     ulist = ulist.T
@@ -452,19 +497,19 @@
     )(send_lower, send, send_upper, vlist, table)
     far_node, lower, upper = lax.optimization_barrier((far_node, lower, upper))
 
-    side_pack, side_counts, top, current = pl.pallas_call(
+    side_pack, plan, top, current = pl.pallas_call(
         pack_kernel,
         out_shape=(
-            jax.ShapeDtypeStruct((2 * leaf_count, p_width, 128), BF16),
-            jax.ShapeDtypeStruct((2, p_width), jnp.int32),
+            jax.ShapeDtypeStruct((2 * leaf_count * p_width, 128), BF16),
+            jax.ShapeDtypeStruct((64, leaf_count), jnp.int32),
             jax.ShapeDtypeStruct((q_width, eq_width), F32),
             jax.ShapeDtypeStruct((q_width, eq_width), F32),
         ),
-        in_specs=[vmem] * 5,
+        in_specs=[vmem] * 7,
         out_specs=(vmem,) * 4,
         compiler_params=params,
         name="pack",
-    )(lower, upper, total, pair, shift_up)
+    )(lower, upper, ulist, counts.reshape(1, leaf_count), total, pair, shift_up)
 
     tops = [top]
     for level in range(3, bits, 3):
@@ -474,29 +519,28 @@
             current = current + swapped(current, size, bit)
         tops.append(current)
 
-    member_blocks = -(-ulist.shape[0] * p_width // BLOCK)
-    gather_rows = (9 * member_blocks + 10 * UNROLL + 2) * BLOCK
+    pack = pack.reshape(leaf_count * p_width, 128)
+    group_blocks = GROUP * -(-ulist.shape[0] * p_width // BLOCK)
     near = pl.pallas_call(
         near_kernel,
         out_shape=jax.ShapeDtypeStruct((leaf_count, q_width, p_width), F32),
-        in_specs=[smem, smem, smem, vmem, vmem, vmem],
+        in_specs=[smem, vmem, vmem, vmem],
         out_specs=vmem,
         scratch_shapes=[
-            pltpu.VMEM((gather_rows, 128), BF16),
-            pltpu.VMEM((gather_rows, 128), BF16),
+            pltpu.VMEM(((group_blocks + 2 * UNROLL + 2) * BLOCK, 128), BF16),
             pltpu.VMEM((2 * UNROLL, 2, p_width, 128), BF16),
-            pltpu.VMEM((9, p_width, 128), F32),
-            pltpu.SMEM((2, 9 * member_blocks + 12 * UNROLL), jnp.int32),
+            pltpu.VMEM((leaf_count + 1, p_width, 128), F32),
+            pltpu.SMEM((group_blocks + 4 * UNROLL,), jnp.int32),
         ],
         compiler_params=params,
         cost_estimate=pl.CostEstimate(flops=3 * 10**10, bytes_accessed=10**7, transcendentals=0),
         name="near",
-    )(ulist, counts, side_counts, pack, side_pack, targets)
+    )(plan, pack, side_pack, targets)
 
     return pl.pallas_call(
         lambda *refs: final_kernel(len(tops), *refs),
         out_shape=jax.ShapeDtypeStruct((leaf_count, q_width, p_width), F32),
-        in_specs=[vmem, vmem, smem] + [vmem] * (5 + len(tops)),
+        in_specs=[smem] + [vmem] * (7 + len(tops)),
         out_specs=vmem,
         scratch_shapes=[
             pltpu.VMEM((node_rows, eq_width), F32),
@@ -504,7 +548,7 @@
         ],
         compiler_params=params,
         name="final",
-    )(pack, surface, counts, near, far_node, coarse, shift_down, down_inverse, *tops)
+    )(plan, pack, surface, near, far_node, coarse, shift_down, down_inverse, *tops)
 
 
 def solution(mesh):

time: 161 us -> 143 us (0.89)
  Pallas kernels: 129 us -> 112 us
    pallas_call x1, Pallas kernels: 63.7 us -> 46.2 us  [local(): pl.pallas_call(near_kernel, out_shape=jax.ShapeDtypeStruct((leaf_count, q...]
  transfers between devices with their start and end apart: 8 -> 8, of which waited for: 3 -> 3; matrix products, arithmetic and copies ran while one was open for 0% -> 0% of each run, Pallas kernels for 58% -> 53%
where the time goes in v4:
time: 143 us; the launch traced here: 140 us
  Pallas kernels  112 us (78%)
  starting transfers between devices  18.8 us (13%)
  waiting for transfers between devices  6.12 us (4%)
  other arithmetic  2.21 us (2%)
  local copies, waits for them, and re-layouts  1.52 us (1%)
    pallas_call x1, Pallas kernels, local(): pl.pallas_call(near_kernel, out_shape=jax.ShapeDtypeStruct((leaf_count, q...  46.2 us
    pallas_call x1, Pallas kernels, local(): pl.pallas_call(far_kernel, out_shape=jax.ShapeDtypeStruct((node_rows, eq_...  28 us
    pallas_call x1, Pallas kernels, local(): pl.pallas_call(lambda *refs: final_kernel(len(tops), *refs), out_shape=ja...  17.6 us
    pallas_call x1, Pallas kernels, local(): pl.pallas_call(upward_kernel, out_shape=(jax.ShapeDtypeStruct((leaf_count...  13.4 us
    ppermute x4, starting transfers between devices, shifted(): return (lax.ppermute(value, 'oct', up), lax.ppermute(value, 'oct', down))  12.8 us
    pallas_call x1, Pallas kernels, local(): pl.pallas_call(pack_kernel, out_shape=(jax.ShapeDtypeStruct((2 * leaf_cou...  6.47 us
    ppermute x4, starting transfers between devices, swapped(): lax.ppermute(value, 'oct', [(source, source ^ 1 << bit) for source in ran...  5.96 us
    ppermute x4, waiting for transfers between devices, shifted(): return (lax.ppermute(value, 'oct', up), lax.ppermute(value, 'oct', down))  4.6 us
  transfers between devices with their start and end apart: 8, of which 3 were waited for; matrix products, arithmetic and copies ran while one was open for 0% of the time, Pallas kernels for 53%

profile of v4, /device:TPU:1, one launch (start us, length us, event | category | flops | bytes accessed | tf_op | source)
XLA Modules:
  0.0 140.4 jit_solution(15530040960481779732)
XLA Ops:
  0.0 13.4 %upward.1 = (bf16[64,128,128]{2,1,0:T(8,128)(2,1)}, bf16[64,128,128]{2,1,0:T(8,128)(2,1)}, f32[64,40,128]{2,1,0:T(8,128)}, bf16[352,152]{1,0:T(8,128)(2,1)}, f32[32,152]{1,0:T(8,128)}) custom-call(f32[3,64,128]{2,1,0:T(8,128)} %bitcast.12, f32[64,32,128]{2,1,0:T(8,128)} %dens_ref.1, f32[3,64,152]{2,1,0:T(8,128)} %bitcast.10, s32[64]{0:T(128)} %counts_ref.1, ...), custom_call_target="tpu_custom_call" | custom-call | tf_op jit(solution)/shard_map/upward/pallas_call | solution.py:456
  13.4 2.0 %collective-permute-start.1 = (bf16[352,152]{1,0:T(8,128)(2,1)}, bf16[352,152]{1,0:T(8,128)(2,1)S(1)}, u32[]{:S(2)}, u32[]{:S(2)}) collective-permute-start(bf16[352,152]{1,0:T(8,128)(2,1)} %get-tuple-element.21.own_ref), channel_id=1, source_target_pairs={{1,0},{2,1},{3,2},{4,3},{5,4},{6,5},{7,6},{8,7},{9,8},{10,9},{11,1... | collective-permute-start | bytes 321032 | tf_op jit(solution)/shard_map/ppermute | solution.py:419
  15.4 4.5 %collective-permute-start = (bf16[352,152]{1,0:T(8,128)(2,1)}, bf16[352,152]{1,0:T(8,128)(2,1)S(1)}, u32[]{:S(2)}, u32[]{:S(2)}) collective-permute-start(bf16[352,152]{1,0:T(8,128)(2,1)} %get-tuple-element.21.own_ref), channel_id=1, source_target_pairs={{0,1},{1,2},{2,3},{3,4},{4,5},{5,6},{6,7},{7,8},{8,9},{9,10},{10,1... | collective-permute-start | bytes 321032 | tf_op jit(solution)/shard_map/ppermute | solution.py:419
  19.9 1.4 %collective-permute-done.1.upper_ref = bf16[352,152]{1,0:T(8,128)(2,1)S(1)} collective-permute-done((bf16[352,152]{1,0:T(8,128)(2,1)}, bf16[352,152]{1,0:T(8,128)(2,1)S(1)}, u32[]{:S(2)}, u32[]{:S(2)}) %collective-permute-start.1) | collective-permute-done | bytes 107040 | tf_op jit(solution)/shard_map/ppermute | solution.py:419
  21.3 3.2 %collective-permute-done.lower_ref = bf16[352,152]{1,0:T(8,128)(2,1)S(1)} collective-permute-done((bf16[352,152]{1,0:T(8,128)(2,1)}, bf16[352,152]{1,0:T(8,128)(2,1)S(1)}, u32[]{:S(2)}, u32[]{:S(2)}) %collective-permute-start) | collective-permute-done | bytes 107040 | tf_op jit(solution)/shard_map/ppermute | solution.py:419
  24.5 0.8 fusion.1
  25.3 0.3 collective-permute-start.2
  25.6 4.5 %collective-permute-start.4 = (f32[64,40,128]{2,1,0:T(8,128)}, f32[64,40,128]{2,1,0:T(8,128)S(1)}, u32[]{:S(2)}, u32[]{:S(2)}) collective-permute-start(f32[64,40,128]{2,1,0:T(8,128)} %get-tuple-element.26), channel_id=1, source_target_pairs={{1,0},{2,1},{3,2},{4,3},{5,4},{6,5},{7,6},{8,7},{9,8},{10,9},{11,1... | collective-permute-start | bytes 3932168 | tf_op jit(solution)/shard_map/ppermute | solution.py:419
  30.0 1.9 %collective-permute-start.3 = (f32[64,40,128]{2,1,0:T(8,128)}, f32[64,40,128]{2,1,0:T(8,128)S(1)}, u32[]{:S(2)}, u32[]{:S(2)}) collective-permute-start(f32[64,40,128]{2,1,0:T(8,128)} %get-tuple-element.26), channel_id=1, source_target_pairs={{0,1},{1,2},{2,3},{3,4},{4,5},{5,6},{6,7},{7,8},{8,9},{9,10},{10,1... | collective-permute-start | bytes 3932168 | tf_op jit(solution)/shard_map/ppermute | solution.py:419
  32.0 0.0 collective-permute-done.2
  32.0 0.0 copy-start.2
  32.0 1.4 collective-permute-start.5
  33.4 0.0 copy-done.4
  33.4 0.0 copy-done.5
  33.4 28.0 %far.1.refs_4_ = f32[256,152]{1,0:T(8,128)} custom-call(bf16[352,152]{1,0:T(8,128)(2,1)} %copy-done.5, bf16[352,152]{1,0:T(8,128)(2,1)} %get-tuple-element.21.own_ref, bf16[352,152]{1,0:T(8,128)(2,1)} %copy-done.4, s32[8,316]{1,0:T(8,128)} %vlist_ref.1, bf16[23104,316]{1,0:T(8,128)(2,1)} %bitcast.15), custom_call_target="tpu_custom_call" | custom-call | flops 20000000000 | bytes 18000000 | tf_op jit(solution)/shard_map/far/pallas_call | solution.py:482
  61.4 0.0 copy-done.2
  61.4 0.0 collective-permute-done.4.upper_ref
  61.4 0.0 copy-start
  61.4 0.0 collective-permute-done.3.lower_ref
  61.4 0.0 collective-permute-done.5.pair_ref
  61.4 0.0 copy-start.3
  61.4 1.1 copy-done
  62.5 0.4 copy-done.1
  62.9 6.5 %pack.1 = (bf16[16384,128]{1,0:T(8,128)(2,1)}, s32[64,64]{1,0:T(8,128)}, f32[32,152]{1,0:T(8,128)}, f32[32,152]{1,0:T(8,128)}) custom-call(f32[64,40,128]{2,1,0:T(8,128)} %copy-done.1, f32[64,40,128]{2,1,0:T(8,128)} %copy-done, s32[27,64]{1,0:T(8,128)} %bitcast.13, s32[1,64]{1,0:T(1,128)} %bitcast.14, f32[32,152]{1,0:T(8,128)} %copy-done.2, ...), custom_call_target="tpu_custom_call" | custom-call | tf_op jit(solution)/shard_map/pack/pallas_call | solution.py:500
  69.4 1.9 %collective-permute-start.6 = (f32[32,152]{1,0:T(8,128)}, f32[32,152]{1,0:T(8,128)S(1)}, u32[]{:S(2)}, u32[]{:S(2)}) collective-permute-start(f32[32,152]{1,0:T(8,128)} %get-tuple-element.36), channel_id=1, source_target_pairs={{0,8},{1,9},{2,10},{3,11},{4,12},{5,13},{6,14},{7,15},{8,0},{9,1},... | collective-permute-start | bytes 58376 | tf_op jit(solution)/shard_map/ppermute | solution.py:423
  71.3 1.5 %collective-permute-done.6 = f32[32,152]{1,0:T(8,128)S(1)} collective-permute-done((f32[32,152]{1,0:T(8,128)}, f32[32,152]{1,0:T(8,128)S(1)}, u32[]{:S(2)}, u32[]{:S(2)}) %collective-permute-start.6) | collective-permute-done | bytes 19488 | tf_op jit(solution)/shard_map/ppermute | solution.py:423
  72.8 0.8 add.22
  73.5 2.5 %collective-permute-start.7 = (f32[32,152]{1,0:T(8,128)S(1)}, f32[32,152]{1,0:T(8,128)S(1)}, u32[]{:S(2)}, u32[]{:S(2)}) collective-permute-start(f32[32,152]{1,0:T(8,128)S(1)} %add.22), channel_id=1, source_target_pairs={{0,16},{1,17},{2,18},{3,19},{4,20},{5,21},{6,22},{7,23},{8,24},{9,... | collective-permute-start | bytes 58376 | tf_op jit(solution)/shard_map/ppermute | solution.py:423
  76.0 46.2 %near.1.refs_3_ = f32[64,32,128]{2,1,0:T(8,128)} custom-call(s32[64,64]{1,0:T(8,128)} %get-tuple-element.30.plan_ref.refs_0_, bf16[8192,128]{1,0:T(8,128)(2,1)} %bitcast.8, bf16[16384,128]{1,0:T(8,128)(2,1)} %get-tuple-element.32.side_pack_ref, bf16[64,128,128]{2,1,0:T(8,128)(2,1)} %get-tuple-element.33.target_ref), custom_call_target="tpu_custom_call" | custom-call | flops 30000001024 | bytes 10000000 | tf_op jit(solution)/shard_map/near/pallas_call | solution.py:524
  122.2 0.0 collective-permute-done.7
  122.2 0.6 add.23.refs_9_
  122.8 17.6 %final.1 = f32[64,32,128]{2,1,0:T(8,128)} custom-call(s32[64,64]{1,0:T(8,128)} %get-tuple-element.30.plan_ref.refs_0_, bf16[8192,128]{1,0:T(8,128)(2,1)} %bitcast.9, f32[3,64,152]{2,1,0:T(8,128)} %bitcast.11, f32[64,32,128]{2,1,0:T(8,128)} %near.1.refs_3_, f32[256,152]{1,0:T(8,128)} %far.1.refs_4_, f32[8,152,152]{2,1,0:T(8,128)} %refs_5_.1, ...), custom_call_target="tpu_custom_call" | custom-call | tf_op jit(solution)/shard_map/final/pallas_call | solution.py:540
  (6 shorter events, 0.0 us)
Async XLA Ops:
  13.4 7.9 %collective-permute-start.1 = (bf16[352,152]{1,0:T(8,128)(2,1)}, bf16[352,152]{1,0:T(8,128)(2,1)S(1)}, u32[]{:S(2)}, u32[]{:S(2)}) collective-permute-start(bf16[352,152]{1,0:T(8,128)(2,1)} %get-tuple-element.21.own_ref), channel_id=1, source_target_pairs={{1,0},{2,1},{3,2},{4,3},{5,4},{6,5},{7,6},{8,7},{9,8},{10,9},{11,1... | collective-permute-start | bytes 321032 | tf_op jit(solution)/shard_map/ppermute | solution.py:419
  15.4 9.1 %collective-permute-start = (bf16[352,152]{1,0:T(8,128)(2,1)}, bf16[352,152]{1,0:T(8,128)(2,1)S(1)}, u32[]{:S(2)}, u32[]{:S(2)}) collective-permute-start(bf16[352,152]{1,0:T(8,128)(2,1)} %get-tuple-element.21.own_ref), channel_id=1, source_target_pairs={{0,1},{1,2},{2,3},{3,4},{4,5},{5,6},{6,7},{7,8},{8,9},{9,10},{10,1... | collective-permute-start | bytes 321032 | tf_op jit(solution)/shard_map/ppermute | solution.py:419
  21.3 12.1 %copy-start.4 = (bf16[352,152]{1,0:T(8,128)(2,1)}, bf16[352,152]{1,0:T(8,128)(2,1)S(1)}, u32[]{:S(2)}) copy-start(bf16[352,152]{1,0:T(8,128)(2,1)S(1)} %collective-permute-done.1.upper_ref) | copy-start | bytes 321028
  24.5 8.9 %copy-start.5 = (bf16[352,152]{1,0:T(8,128)(2,1)}, bf16[352,152]{1,0:T(8,128)(2,1)S(1)}, u32[]{:S(2)}) copy-start(bf16[352,152]{1,0:T(8,128)(2,1)S(1)} %collective-permute-done.lower_ref) | copy-start | bytes 321028
  25.3 6.7 %collective-permute-start.2 = (f32[32,152]{1,0:T(8,128)S(1)}, f32[32,152]{1,0:T(8,128)S(1)}, u32[]{:S(2)}, u32[]{:S(2)}) collective-permute-start(f32[32,152]{1,0:T(8,128)S(1)} %fusion.1), channel_id=1, source_target_pairs={{0,2},{1,3},{2,0},{3,1},{4,6},{5,7},{6,4},{7,5},{8,10},{9,11},{10,... | collective-permute-start | bytes 58376 | tf_op jit(solution)/shard_map/ppermute | solution.py:423
  25.6 35.8 %collective-permute-start.4 = (f32[64,40,128]{2,1,0:T(8,128)}, f32[64,40,128]{2,1,0:T(8,128)S(1)}, u32[]{:S(2)}, u32[]{:S(2)}) collective-permute-start(f32[64,40,128]{2,1,0:T(8,128)} %get-tuple-element.26), channel_id=1, source_target_pairs={{1,0},{2,1},{3,2},{4,3},{5,4},{6,5},{7,6},{8,7},{9,8},{10,9},{11,1... | collective-permute-start | bytes 3932168 | tf_op jit(solution)/shard_map/ppermute | solution.py:419
  30.0 31.4 %collective-permute-start.3 = (f32[64,40,128]{2,1,0:T(8,128)}, f32[64,40,128]{2,1,0:T(8,128)S(1)}, u32[]{:S(2)}, u32[]{:S(2)}) collective-permute-start(f32[64,40,128]{2,1,0:T(8,128)} %get-tuple-element.26), channel_id=1, source_target_pairs={{0,1},{1,2},{2,3},{3,4},{4,5},{5,6},{6,7},{7,8},{8,9},{9,10},{10,1... | collective-permute-start | bytes 3932168 | tf_op jit(solution)/shard_map/ppermute | solution.py:419
  32.0 29.4 %copy-start.2 = (f32[32,152]{1,0:T(8,128)}, f32[32,152]{1,0:T(8,128)S(1)}, u32[]{:S(2)}) copy-start(f32[32,152]{1,0:T(8,128)S(1)} %add.21.sum_ref) | copy-start | bytes 58372
  32.0 29.4 %collective-permute-start.5 = (f32[32,152]{1,0:T(8,128)S(1)}, f32[32,152]{1,0:T(8,128)S(1)}, u32[]{:S(2)}, u32[]{:S(2)}) collective-permute-start(f32[32,152]{1,0:T(8,128)S(1)} %add.21.sum_ref), channel_id=1, source_target_pairs={{0,4},{1,5},{2,6},{3,7},{4,0},{5,1},{6,2},{7,3},{8,12},{9,13},{10,... | collective-permute-start | bytes 58376 | tf_op jit(solution)/shard_map/ppermute | solution.py:423
  61.4 1.1 copy-start
  61.4 1.5 %copy-start.1 = (f32[64,40,128]{2,1,0:T(8,128)}, f32[64,40,128]{2,1,0:T(8,128)S(1)}, u32[]{:S(2)}) copy-start(f32[64,40,128]{2,1,0:T(8,128)S(1)} %collective-permute-done.3.lower_ref) | copy-start | bytes 3932164
  61.4 1.5 %copy-start.3 = (f32[32,152]{1,0:T(8,128)}, f32[32,152]{1,0:T(8,128)S(1)}, u32[]{:S(2)}) copy-start(f32[32,152]{1,0:T(8,128)S(1)} %collective-permute-done.5.pair_ref) | copy-start | bytes 58372
  69.4 3.4 %collective-permute-start.6 = (f32[32,152]{1,0:T(8,128)}, f32[32,152]{1,0:T(8,128)S(1)}, u32[]{:S(2)}, u32[]{:S(2)}) collective-permute-start(f32[32,152]{1,0:T(8,128)} %get-tuple-element.36), channel_id=1, source_target_pairs={{0,8},{1,9},{2,10},{3,11},{4,12},{5,13},{6,14},{7,15},{8,0},{9,1},... | collective-permute-start | bytes 58376 | tf_op jit(solution)/shard_map/ppermute | solution.py:423
  73.5 48.7 %collective-permute-start.7 = (f32[32,152]{1,0:T(8,128)S(1)}, f32[32,152]{1,0:T(8,128)S(1)}, u32[]{:S(2)}, u32[]{:S(2)}) collective-permute-start(f32[32,152]{1,0:T(8,128)S(1)} %add.22), channel_id=1, source_target_pairs={{0,16},{1,17},{2,18},{3,19},{4,20},{5,21},{6,22},{7,23},{8,24},{9,... | collective-permute-start | bytes 58376 | tf_op jit(solution)/shard_map/ppermute | solution.py:423

commit v5 on v4

--- a/solution.py
+++ b/solution.py
@@ -15,8 +15,9 @@
 TN = (((0,), (0,)), ((), ()))
 BLOCK = 256
 UNROLL = 4
-GROUP = 16
-PLAN_SOURCE, PLAN_ORDER, PLAN_COUNT = 32, 62, 63
+PIECE = 64
+CLASS_ROWS = (32, 64, 96, 128)
+PLAN_PLACES, PLAN_CLASS, PLAN_ORDER, PLAN_COUNT = 56, 60, 61, 62
 SOURCES = 32
 
 
@@ -80,29 +81,38 @@
     return high, mid, low, norms, ones
 
 
+def paired(first, second):
+    return first + pltpu.roll(second, 4, 0)
+
+
 def left_rows(parts):
     high, mid, low, norms, ones = parts
-    return jnp.concatenate([high, high, mid, mid, high, low, ones, norms], axis=0)
+    return jnp.concatenate([paired(high, high), paired(mid, mid), paired(high, low), paired(ones, norms)], axis=0)
 
 
 def right_rows(parts):
     high, mid, low, norms, ones = parts
-    return jnp.concatenate([high, mid, high, mid, low, high, norms, ones], axis=0)
-
-
-def padded_left(parts):
-    rows = left_rows(parts)
-    return jnp.concatenate([jnp.zeros_like(rows), rows], axis=0).astype(BF16)
-
-
-def packed_rows(weights, parts):
-    weights_high = weights.astype(BF16).astype(F32)
-    return jnp.concatenate([weights_high, weights - weights_high, right_rows(parts)], axis=0).astype(BF16)
+    both = paired(high, mid)
+    return jnp.concatenate([both, both, paired(low, high), paired(norms, ones)], axis=0)
+
+
+def weight_rows(weights):
+    high = weights.astype(BF16).astype(F32)
+    return [high, weights - high]
+
+
+def put_features(feature_ref, leaf, rows):
+    lower = iota(rows.shape, 1) < PIECE
+    for half in range(2):
+        alone = jnp.where(lower == (half == 0), rows, 0.0)
+        span = pl.ds(pl.multiple_of((2 * leaf + half) * 32, 32), 32)
+        feature_ref[half, span, :] = alone.astype(BF16)
+        feature_ref[1 - half, span, :] = pltpu.roll(alone, PIECE, 1).astype(BF16)
 
 
 def upward_kernel(
-    points_ref, dens_ref, surface_ref, counts_ref, up_ref, shift_ref, pack_ref, target_ref, message_ref, send_ref,
-    slab_ref, check_ref
+    points_ref, dens_ref, surface_ref, counts_ref, up_ref, shift_ref, pack_ref, feature_ref, turned_ref,
+    message_ref, send_ref, slab_ref, check_ref
 ):
     leaf_count, q_width, p_width = dens_ref.shape
     eq_width = surface_ref.shape[2]
@@ -119,24 +129,26 @@
             message_ref[leaf, :q_width, :] = weights
             message_ref[leaf, q_width:, :] = jnp.where(row == 3, count.astype(F32), coords)
             parts = pieces(coords)
-            rows = packed_rows(weights, parts)
-            pack = rows.T
-            pack_ref[leaf] = pack
-            target_ref[leaf] = padded_left(parts).T
-            values = jnp.exp2(dot(pack, padded_left(pieces(coords_of(surface_ref, leaf)))))
-            values_high, values_low = halves(values)
-            both = dot(rows[: 2 * q_width], values_high)
+            weight_parts = weight_rows(weights)
+            right = right_rows(parts)
+            pack = jnp.concatenate([left_rows(parts)] + weight_parts + [right], axis=0).astype(BF16).T
+            pack_ref[pl.ds(pl.multiple_of(leaf * p_width, p_width), p_width), :] = pack
+            put_features(feature_ref, leaf, right)
+            surface = left_rows(pieces(coords_of(surface_ref, leaf)))
+            turned_ref[leaf] = surface.astype(BF16).T
+            wide = jnp.concatenate([jnp.zeros((96, eq_width), F32), surface], axis=0).astype(BF16)
+            values_high, values_low = halves(jnp.exp2(dot(pack, wide)))
+            rows = jnp.concatenate(weight_parts, axis=0).astype(BF16)
+            both = dot(rows, values_high)
             check = both[:q_width] + both[q_width:] + dot(rows[:q_width], values_low)
             check_ref[child, pl.ds(pl.multiple_of(node * q_width, q_width), q_width), :] = check
         return carry
 
     lax.fori_loop(0, node_count, node_step, 0)
 
-    def child_step(child, total):
-        leaf_eq = dot3(check_ref[child], up_ref[...])
-        return total + dot3(leaf_eq, shift_ref[child])
-
-    node_eq = lax.fori_loop(0, 8, child_step, jnp.zeros((node_count * q_width, eq_width), F32))
+    node_eq = jnp.zeros((node_count * q_width, eq_width), F32)
+    for child in range(8):
+        node_eq = node_eq + dot3(dot3(check_ref[child], up_ref[...]), shift_ref[child])
     send_ref[: node_count * q_width, :] = node_eq.astype(BF16)
     slab_eq = jnp.zeros((q_width, eq_width), F32)
     for child in range(8):
@@ -224,68 +236,74 @@
 
 
 def near_kernel(
-    plan_ref, own_pack_ref, side_pack_ref, target_ref, out_ref, gather_ref, value_ref, total_ref, owner_ref
+    plan_ref, item_ref, own_hbm, side_hbm, own_feature_hbm, side_feature_hbm, out_ref, pack_ref, feature_ref,
+    value_ref, total_ref, sems
 ):
     leaf_count, q_width, p_width = out_ref.shape
-    slot_count = 27
-    member_blocks = -(-slot_count * p_width // BLOCK)
+    own_rows, side_rows = own_hbm.shape[0], side_hbm.shape[0]
+    own_lines, side_lines = own_feature_hbm.shape[1], side_feature_hbm.shape[1]
+    copies = [
+        (own_hbm, pack_ref.at[pl.ds(0, own_rows)]),
+        (side_hbm, pack_ref.at[pl.ds(own_rows, side_rows)]),
+        (own_feature_hbm, feature_ref.at[:, pl.ds(0, own_lines)]),
+        (side_feature_hbm, feature_ref.at[:, pl.ds(own_lines, side_lines)]),
+    ]
+    copies = [pltpu.make_async_copy(source, target, sems.at[n]) for n, (source, target) in enumerate(copies)]
+    for copy in copies:
+        copy.start()
+    pack_ref[own_rows + side_rows :, :] = jnp.zeros((PIECE, 128), BF16)
+    feature_ref[:, own_lines + side_lines :, :] = jnp.zeros((2, 32, 128), BF16)
     total_ref[...] = jnp.zeros_like(total_ref)
-    for number in range(UNROLL):
-        owner_ref[number] = leaf_count
-
-    def group_step(group, carry):
-        def gather(member, inner):
-            leaf = plan_ref[PLAN_ORDER, group * GROUP + member]
-            for slot in range(slot_count):
-                pack_ref = own_pack_ref if slot == 0 or 9 <= slot < 18 else side_pack_ref
-                source = pl.multiple_of(plan_ref[PLAN_SOURCE + slot, leaf], p_width)
-                offset = pl.multiple_of(plan_ref[slot, leaf], 16)
-                gather_ref[pl.ds(offset, p_width), :] = pack_ref[pl.ds(source, p_width), :]
-            offset = pl.multiple_of(plan_ref[slot_count, leaf], 16)
-            gather_ref[pl.ds(offset, BLOCK), :] = jnp.zeros((BLOCK, 128), BF16)
-            first = lax.shift_right_logical(plan_ref[0, leaf], 8)
-            for number in range(member_blocks):
-                owner_ref[UNROLL + first + number] = leaf
-            return inner
-
-        lax.fori_loop(0, GROUP, gather, 0)
-        last = plan_ref[PLAN_ORDER, group * GROUP + GROUP - 1]
-        block_count = lax.shift_right_logical(plan_ref[slot_count, last] + (BLOCK - 1), 8)
-        for number in range(2 * UNROLL):
-            owner_ref[UNROLL + block_count + number] = leaf_count
-
-        def sources_of(block):
-            return gather_ref[pl.ds(pl.multiple_of(block * BLOCK, BLOCK), BLOCK), :]
-
-        def run(rows):
-            def blocks_step(step, inner):
-                slot = jnp.bitwise_and(step, 1) * UNROLL
-                for part in range(UNROLL):
-                    block = jnp.maximum(step - 1, 0) * UNROLL + part
-                    leaf = owner_ref[step * UNROLL + part]
-                    values = [value_ref[UNROLL - slot + part, side, :rows] for side in range(2)]
-                    total_ref[leaf, :rows] += dot(jnp.concatenate(values, axis=1), sources_of(block))
-                for part in range(UNROLL):
-                    block = step * UNROLL + part
-                    leaf = jnp.minimum(owner_ref[UNROLL + block], leaf_count - 1)
-                    values = jnp.exp2(dot_nt(target_ref[leaf, :rows], sources_of(block))).astype(BF16)
-                    for side in range(2):
-                        value_ref[slot + part, side, :rows] = values[:, side * 128 : (side + 1) * 128]
-                return inner
-
-            lax.fori_loop(0, lax.div(block_count + (2 * UNROLL - 1), UNROLL), blocks_step, 0)
-
-        largest = plan_ref[PLAN_COUNT, last]
-        for low, rows in ((0, 32), (32, 64), (64, 96), (96, 128)):
-            pl.when((largest > low) & (largest <= rows))(lambda rows=rows: run(rows))
-        return carry
-
-    lax.fori_loop(0, leaf_count // GROUP, group_step, 0)
+    for copy in copies:
+        copy.wait()
+    step_lanes = 128 // UNROLL
+    shift = step_lanes.bit_length() - 1
+
+    def item_of(step, part):
+        line = lax.shift_right_logical(step, shift)
+        lane = jnp.bitwise_and(step, step_lanes - 1) * UNROLL + part
+        return item_ref[line, lane], item_ref[8 + line, lane]
+
+    def sources_of(leaf, place):
+        rows = []
+        for number in range(BLOCK // PIECE):
+            start = pl.multiple_of(plan_ref[place + number, leaf] * 2, PIECE)
+            rows.append(pack_ref[pl.ds(start, PIECE), :])
+        return jnp.concatenate(rows, axis=0)
+
+    def features_of(leaf, place):
+        tiles = []
+        for tile in range(BLOCK // 128):
+            starts = [pl.multiple_of(plan_ref[place + 2 * tile + half, leaf], 32) for half in range(2)]
+            halves_of = [feature_ref[half, pl.ds(start, 32), :] for half, start in enumerate(starts)]
+            tiles.append(halves_of[0] + halves_of[1])
+        return jnp.concatenate(tiles, axis=1)
+
+    def run(rows, first, count):
+        def blocks_step(step, carry):
+            slot = jnp.bitwise_and(step, 1) * UNROLL
+            for part in range(UNROLL):
+                leaf, place = item_of(step - 1, part)
+                values = [value_ref[UNROLL - slot + part, side, :rows] for side in range(2)]
+                total_ref[leaf, :rows] += dot(jnp.concatenate(values, axis=1), sources_of(leaf, place))
+            for part in range(UNROLL):
+                leaf, place = item_of(step, part)
+                start = pl.multiple_of(jnp.minimum(leaf, leaf_count - 1) * p_width, p_width)
+                targets = pack_ref[pl.ds(start, rows), :][:, :32]
+                values = jnp.exp2(dot(targets, features_of(leaf, place))).astype(BF16)
+                for side in range(2):
+                    value_ref[slot + part, side, :rows] = values[:, side * 128 : (side + 1) * 128]
+            return carry
+
+        lax.fori_loop(first, first + count, blocks_step, 0)
+
+    for number, rows in enumerate(CLASS_ROWS):
+        run(rows, plan_ref[PLAN_CLASS, 2 * number], plan_ref[PLAN_CLASS, 2 * number + 1])
 
     def turn_step(step, carry):
         for part in range(8):
-            turned = total_ref[step * 8 + part, :, : 2 * q_width].T
-            out_ref[step * 8 + part] = turned[:q_width] + turned[q_width:]
+            turned = total_ref[step * 8 + part].T
+            out_ref[step * 8 + part] = turned[32 : 32 + q_width] + turned[32 + q_width : 32 + 2 * q_width]
         return carry
 
     lax.fori_loop(0, leaf_count // 8, turn_step, 0)
@@ -297,7 +315,7 @@
     return jnp.broadcast_to(wide, (128, 128)).T[:width, :width]
 
 
-def plan_of(ulist_ref, counts, plan_ref):
+def plan_of(ulist_ref, counts, plan_ref, item_ref):
     slot_count, leaf_count = ulist_ref.shape
     index = lax.axis_index("oct")
     shape = (leaf_count, leaf_count)
@@ -309,34 +327,66 @@
     rank_column = as_column(rank).astype(jnp.int32)
     rank_wide = jnp.broadcast_to(rank, shape).astype(jnp.int32)
 
+    block_pieces = BLOCK // PIECE
+    zero_row = 3 * leaf_count * 64
+    place_shape = (PLAN_PLACES, leaf_count)
+    place_row = iota(place_shape, 0)
+    listed = jnp.full(place_shape, zero_row, jnp.int32)
     offset = jnp.zeros((1, leaf_count), jnp.int32)
-    offsets = []
     for slot in range(slot_count):
         side = 1 if slot == 0 else (0 if slot < 9 else (1 if slot < 18 else 2))
         ids = ulist_ref[slot : slot + 1, :]
         place = jnp.where(ids >= 0, ids - (index + (side - 1)) * leaf_count, 0)
         found = jnp.sum(jnp.where(row == place, tables[side], 0.0), axis=0, keepdims=True).astype(jnp.int32)
-        length = jnp.where(ids >= 0, jnp.bitwise_and(found + 15, -16), 0)
-        start = place + (leaf_count if side == 2 else 0)
-        plan_ref[PLAN_SOURCE + slot : PLAN_SOURCE + slot + 1, :] = start * 128
-        offsets.append(offset)
+        length = lax.shift_right_logical(found + (PIECE - 1), PIECE.bit_length() - 1)
+        length = jnp.where(ids >= 0, length, 0)
+        start = (place + (1, 0, 2)[side] * leaf_count) * 64
+        inside = (place_row >= offset) & (place_row < offset + length)
+        listed = jnp.where(inside, start + (place_row - offset) * 32, listed)
         offset = offset + length
-    offsets.append(offset)
-    blocks = lax.shift_right_logical(offset + (BLOCK - 1), 8)
+    plan_ref[:PLAN_PLACES, :leaf_count] = listed
+    plan_ref[:PLAN_PLACES, leaf_count:] = jnp.full((PLAN_PLACES, 128 - leaf_count), zero_row, jnp.int32)
+
+    blocks = lax.shift_right_logical(offset + (block_pieces - 1), block_pieces.bit_length() - 1)
     blocks_column = as_column(blocks.astype(F32))
-    group_shift = GROUP.bit_length() - 1
-    same = lax.shift_right_logical(rank_column, group_shift) == lax.shift_right_logical(rank_wide, group_shift)
-    first = jnp.sum(jnp.where(same & (rank_column < rank_wide), blocks_column, 0.0), axis=0, keepdims=True)
-    first = first.astype(jnp.int32) * BLOCK
-    for number, value in enumerate(offsets):
-        plan_ref[number : number + 1, :] = first + value
+    own_class = lax.shift_right_logical(counts[1].astype(jnp.int32) - 1, 5)
+    class_column = as_column(own_class.astype(F32)).astype(jnp.int32)
+    earlier = (class_column == jnp.broadcast_to(own_class, shape)) & (rank_column < rank_wide)
+    first = jnp.sum(jnp.where(earlier, blocks_column, 0.0), axis=0, keepdims=True).astype(jnp.int32)
+    lane = iota((1, 128), 1)
+    steps_line = jnp.zeros((1, 128), jnp.int32)
+    start = jnp.ones((1, 1), jnp.int32)
+    for number in range(len(CLASS_ROWS)):
+        inside = jnp.where(own_class == number, blocks.astype(F32), 0.0)
+        items = jnp.sum(inside, axis=1, keepdims=True).astype(jnp.int32)
+        steps = lax.shift_right_logical(items + (2 * UNROLL - 1), UNROLL.bit_length() - 1)
+        steps = jnp.where(items > 0, steps, 0)
+        first = first + jnp.where(own_class == number, start * UNROLL, 0)
+        steps_line = jnp.where(lane == 2 * number, start, jnp.where(lane == 2 * number + 1, steps, steps_line))
+        start = start + steps
+    plan_ref[PLAN_CLASS : PLAN_CLASS + 1, :] = steps_line
+
+    first_column = as_column(first.astype(F32))
+    wide = (leaf_count, 128)
+    first_wide = jnp.concatenate([first_column] * (128 // leaf_count), axis=1).astype(jnp.int32)
+    blocks_wide = jnp.concatenate([blocks_column] * (128 // leaf_count), axis=1).astype(jnp.int32)
+    leaf_row = iota(wide, 0).astype(F32)
+    for line in range(8):
+        after = iota(wide, 1) + 128 * line - first_wide
+        inside = (after >= 0) & (after < blocks_wide)
+        leaf = jnp.sum(jnp.where(inside, leaf_row - leaf_count, 0.0), axis=0, keepdims=True)
+        place = jnp.sum(jnp.where(inside, (after * block_pieces).astype(F32), 0.0), axis=0, keepdims=True)
+        item_ref[line : line + 1, :] = leaf.astype(jnp.int32) + leaf_count
+        item_ref[8 + line : 9 + line, :] = place.astype(jnp.int32)
+
     order = jnp.sum(jnp.where(rank_column == column, row.astype(F32), 0.0), axis=0, keepdims=True)
-    plan_ref[PLAN_ORDER : PLAN_ORDER + 1, :] = order.astype(jnp.int32)
-    plan_ref[PLAN_COUNT : PLAN_COUNT + 1, :] = counts[1].astype(jnp.int32)
+    plan_ref[PLAN_ORDER : PLAN_ORDER + 1, :leaf_count] = order.astype(jnp.int32)
+    plan_ref[PLAN_COUNT : PLAN_COUNT + 1, :leaf_count] = counts[1].astype(jnp.int32)
 
 
 def pack_kernel(
-    lower_ref, upper_ref, ulist_ref, own_counts_ref, sum_ref, pair_ref, shift_ref, pack_ref, plan_ref, top_ref, next_ref
+    lower_ref, upper_ref, ulist_ref, own_counts_ref, sum_ref, pair_ref, shift_ref, pack_ref, feature_ref, plan_ref,
+    item_ref, top_ref, next_ref
 ):
     leaf_count, rows, p_width = lower_ref.shape
     q_width = rows - 8
@@ -345,6 +395,7 @@
     top_ref[...] = top
     next_ref[...] = dot3(top, shift_ref[jnp.right_shift(index, 3) & 7])
     lane = iota((1, leaf_count), 1)
+    blank = jnp.zeros((32, p_width), F32)
 
     def pack_step(step, counts):
         side_counts = list(counts)
@@ -352,19 +403,21 @@
             leaf = step * 4 + part
             for side, source in enumerate((lower_ref, upper_ref)):
                 tail = source[leaf, q_width:, :]
-                packed = packed_rows(source[leaf, :q_width, :], pieces(tail)).T
-                start = pl.multiple_of((side * leaf_count + leaf) * p_width, p_width)
-                pack_ref[pl.ds(start, p_width), :] = packed
+                place = side * leaf_count + leaf
+                weights = weight_rows(source[leaf, :q_width, :])
+                packed = jnp.concatenate([blank] + weights + [blank], axis=0).astype(BF16).T
+                pack_ref[pl.ds(pl.multiple_of(place * p_width, p_width), p_width), :] = packed
+                put_features(feature_ref, place, right_rows(pieces(tail)))
                 side_counts[side] = jnp.where(lane == leaf, tail[3:4, :leaf_count], side_counts[side])
         return tuple(side_counts)
 
     nothing = jnp.zeros((1, leaf_count), F32)
     lower_counts, upper_counts = lax.fori_loop(0, leaf_count // 4, pack_step, (nothing, nothing))
-    plan_of(ulist_ref, (lower_counts, own_counts_ref[...].astype(F32), upper_counts), plan_ref)
+    plan_of(ulist_ref, (lower_counts, own_counts_ref[...].astype(F32), upper_counts), plan_ref, item_ref)
 
 
 def final_kernel(
-    level_count, plan_ref, pack_ref, surface_ref, near_ref, far_ref, coarse_ref, shift_ref, down_ref, *rest
+    level_count, counts_ref, feature_ref, turned_ref, near_ref, far_ref, coarse_ref, shift_ref, down_ref, *rest
 ):
     top_refs, (out_ref, node_ref, down_leaf_ref) = rest[:level_count], rest[level_count:]
     leaf_count, q_width, p_width = out_ref.shape
@@ -378,39 +431,23 @@
         rows = slice(node * q_width, (node + 1) * q_width)
         node_ref[rows, :] = far_ref[rows, :] + dot3(slab_local, shift_ref[node])
 
-    def child_step(child, carry):
+    for child in range(8):
         down_leaf_ref[child] = dot3(dot3(node_ref[...], shift_ref[child]), down_ref[...])
+    lane = iota((q_width, p_width), 1)
+
+    def node_step(node, carry):
+        for child in range(8):
+            leaf = node * 8 + child
+            starts = [pl.multiple_of((2 * leaf + half) * 32, 32) for half in range(2)]
+            features = feature_ref[0, pl.ds(starts[0], 32), :] + feature_ref[1, pl.ds(starts[1], 32), :]
+            values_high, values_low = halves(jnp.exp2(dot(turned_ref[leaf], features)))
+            down = weight_rows(down_leaf_ref[child, pl.ds(pl.multiple_of(node * q_width, q_width), q_width), :])
+            both = dot(jnp.concatenate(down, axis=0).astype(BF16), values_high)
+            far = both[:q_width] + both[q_width:] + dot(down[0].astype(BF16), values_low)
+            out_ref[leaf] = jnp.where(lane < counts_ref[leaf], far + near_ref[leaf], 0.0)
         return carry
 
-    lax.fori_loop(0, 8, child_step, 0)
-    lane = iota((q_width, p_width), 1)
-
-    def leaves_step(step, carry):
-        def run(rows):
-            for part in range(8):
-                leaf = plan_ref[PLAN_ORDER, step * 8 + part]
-                child = jnp.bitwise_and(leaf, 7)
-                node_row = pl.multiple_of(lax.shift_right_logical(leaf, 3) * q_width, q_width)
-                own = pack_ref[pl.ds(pl.multiple_of(leaf * p_width, p_width), rows), :]
-                values = jnp.exp2(dot(own, padded_left(pieces(coords_of(surface_ref, leaf)))))
-                values_high, values_low = halves(values)
-                down = down_leaf_ref[child, pl.ds(node_row, q_width), :]
-                down_high = down.astype(BF16).astype(F32)
-                down_rows = jnp.concatenate([down_high, down - down_high], axis=0).astype(BF16)
-                down_first = jnp.concatenate([down_high, jnp.zeros_like(down_high)], axis=0).astype(BF16)
-                far = dot_nt(values_high, down_rows) + dot_nt(values_low, down_first)
-                if rows < p_width:
-                    far = jnp.concatenate([far, jnp.zeros((p_width - rows, 2 * q_width), F32)], axis=0)
-                turned = far.T
-                summed = turned[:q_width] + turned[q_width:] + near_ref[leaf]
-                out_ref[leaf] = jnp.where(lane < plan_ref[PLAN_COUNT, leaf], summed, 0.0)
-
-        largest = plan_ref[PLAN_COUNT, plan_ref[PLAN_ORDER, step * 8 + 7]]
-        for low, rows in ((0, 32), (32, 64), (64, 96), (96, 128)):
-            pl.when((largest > low) & (largest <= rows))(lambda rows=rows: run(rows))
-        return carry
-
-    lax.fori_loop(0, node_count, leaves_step, 0)
+    lax.fori_loop(0, node_count, node_step, 0)
 
 
 def shifted(value, size):
@@ -453,17 +490,18 @@
     ulist = ulist.T
     table = jnp.transpose(translate, (1, 2, 0))
 
-    pack, targets, message, send, slab = pl.pallas_call(
+    pack, features, turned, message, send, slab = pl.pallas_call(
         upward_kernel,
         out_shape=(
-            jax.ShapeDtypeStruct((leaf_count, p_width, 128), BF16),
-            jax.ShapeDtypeStruct((leaf_count, p_width, 128), BF16),
+            jax.ShapeDtypeStruct((leaf_count * p_width, 128), BF16),
+            jax.ShapeDtypeStruct((2, leaf_count * 64, p_width), BF16),
+            jax.ShapeDtypeStruct((leaf_count, eq_width, 32), BF16),
             jax.ShapeDtypeStruct((leaf_count, q_width + 8, p_width), F32),
             jax.ShapeDtypeStruct((node_rows + 3 * q_width, eq_width), BF16),
             jax.ShapeDtypeStruct((q_width, eq_width), F32),
         ),
         in_specs=[vmem, vmem, vmem, smem, vmem, vmem],
-        out_specs=(vmem,) * 5,
+        out_specs=(vmem,) * 6,
         scratch_shapes=[pltpu.VMEM((8, node_rows, eq_width), F32)],
         compiler_params=params,
         name="upward",
@@ -497,16 +535,18 @@
     )(send_lower, send, send_upper, vlist, table)
     far_node, lower, upper = lax.optimization_barrier((far_node, lower, upper))
 
-    side_pack, plan, top, current = pl.pallas_call(
+    side_pack, side_features, plan, items, top, current = pl.pallas_call(
         pack_kernel,
         out_shape=(
             jax.ShapeDtypeStruct((2 * leaf_count * p_width, 128), BF16),
-            jax.ShapeDtypeStruct((64, leaf_count), jnp.int32),
+            jax.ShapeDtypeStruct((2, 2 * leaf_count * 64, p_width), BF16),
+            jax.ShapeDtypeStruct((64, 128), jnp.int32),
+            jax.ShapeDtypeStruct((16, 128), jnp.int32),
             jax.ShapeDtypeStruct((q_width, eq_width), F32),
             jax.ShapeDtypeStruct((q_width, eq_width), F32),
         ),
         in_specs=[vmem] * 7,
-        out_specs=(vmem,) * 4,
+        out_specs=(vmem,) * 6,
         compiler_params=params,
         name="pack",
     )(lower, upper, ulist, counts.reshape(1, leaf_count), total, pair, shift_up)
@@ -519,23 +559,22 @@
             current = current + swapped(current, size, bit)
         tops.append(current)
 
-    pack = pack.reshape(leaf_count * p_width, 128)
-    group_blocks = GROUP * -(-ulist.shape[0] * p_width // BLOCK)
     near = pl.pallas_call(
         near_kernel,
         out_shape=jax.ShapeDtypeStruct((leaf_count, q_width, p_width), F32),
-        in_specs=[smem, vmem, vmem, vmem],
+        in_specs=[smem, smem, hbm, hbm, hbm, hbm],
         out_specs=vmem,
         scratch_shapes=[
-            pltpu.VMEM(((group_blocks + 2 * UNROLL + 2) * BLOCK, 128), BF16),
+            pltpu.VMEM((3 * leaf_count * p_width + PIECE, 128), BF16),
+            pltpu.VMEM((2, 3 * leaf_count * 64 + 32, 128), BF16),
             pltpu.VMEM((2 * UNROLL, 2, p_width, 128), BF16),
             pltpu.VMEM((leaf_count + 1, p_width, 128), F32),
-            pltpu.SMEM((group_blocks + 4 * UNROLL,), jnp.int32),
+            pltpu.SemaphoreType.DMA((4,)),
         ],
         compiler_params=params,
         cost_estimate=pl.CostEstimate(flops=3 * 10**10, bytes_accessed=10**7, transcendentals=0),
         name="near",
-    )(plan, pack, side_pack, targets)
+    )(plan, items, pack, side_pack, features, side_features)
 
     return pl.pallas_call(
         lambda *refs: final_kernel(len(tops), *refs),
@@ -548,7 +587,7 @@
         ],
         compiler_params=params,
         name="final",
-    )(plan, pack, surface, near, far_node, coarse, shift_down, down_inverse, *tops)
+    )(counts, features, turned, near, far_node, coarse, shift_down, down_inverse, *tops)
 
 
 def solution(mesh):

time: 143 us -> 144 us (level)
  the two profiles are of different devices: /device:TPU:1 before, /device:TPU:4 now
where the time goes in v5:
time: 144 us; the launch traced here: 143 us
  Pallas kernels  114 us (79%)
  starting transfers between devices  16.6 us (12%)
  waiting for transfers between devices  8.13 us (6%)
  other arithmetic  2.21 us (2%)
  local copies, waits for them, and re-layouts  1.44 us (1%)
    pallas_call x1, Pallas kernels, local(): pl.pallas_call(near_kernel, out_shape=jax.ShapeDtypeStruct((leaf_count, q...  48.5 us
    pallas_call x1, Pallas kernels, local(): pl.pallas_call(far_kernel, out_shape=jax.ShapeDtypeStruct((node_rows, eq_...  28 us
    pallas_call x1, Pallas kernels, local(): pl.pallas_call(lambda *refs: final_kernel(len(tops), *refs), out_shape=ja...  18.5 us
    pallas_call x1, Pallas kernels, local(): pl.pallas_call(upward_kernel, out_shape=(jax.ShapeDtypeStruct((leaf_count...  10.2 us
    ppermute x4, starting transfers between devices, shifted(): return (lax.ppermute(value, 'oct', up), lax.ppermute(value, 'oct', down))  9.12 us
    pallas_call x1, Pallas kernels, local(): pl.pallas_call(pack_kernel, out_shape=(jax.ShapeDtypeStruct((2 * leaf_cou...  8.77 us
    ppermute x4, starting transfers between devices, swapped(): lax.ppermute(value, 'oct', [(source, source ^ 1 << bit) for source in ran...  7.47 us
    ppermute x4, waiting for transfers between devices, shifted(): return (lax.ppermute(value, 'oct', up), lax.ppermute(value, 'oct', down))  5.99 us
  transfers between devices with their start and end apart: 8, of which 3 were waited for; matrix products, arithmetic and copies ran while one was open for 0% of the time, Pallas kernels for 54%

profile of v5, /device:TPU:4, one launch (start us, length us, event | category | flops | bytes accessed | tf_op | source)
XLA Modules:
  0.0 142.5 jit_solution(443270180416661390)
XLA Ops:
  0.0 10.2 %upward.1 = (bf16[8192,128]{1,0:T(8,128)(2,1)}, bf16[2,4096,128]{2,1,0:T(8,128)(2,1)}, bf16[64,152,32]{2,1,0:T(8,128)(2,1)}, f32[64,40,128]{2,1,0:T(8,128)}, bf1...) custom-call(f32[3,64,128]{2,1,0:T(8,128)} %bitcast.8, f32[64,32,128]{2,1,0:T(8,128)} %dens_ref.1, f32[3,64,152]{2,1,0:T(8,128)} %bitcast.7, ...), custom_call_target="tpu_custom_call" | custom-call | tf_op jit(solution)/shard_map/upward/pallas_call | solution.py:493
  10.2 2.8 %collective-permute-start.1 = (bf16[352,152]{1,0:T(8,128)(2,1)}, bf16[352,152]{1,0:T(8,128)(2,1)S(1)}, u32[]{:S(2)}, u32[]{:S(2)}) collective-permute-start(bf16[352,152]{1,0:T(8,128)(2,1)} %get-tuple-element.26.own_ref), channel_id=1, source_target_pairs={{1,0},{2,1},{3,2},{4,3},{5,4},{6,5},{7,6},{8,7},{9,8},{10,9},{11,1... | collective-permute-start | bytes 321032 | tf_op jit(solution)/shard_map/ppermute | solution.py:456
  13.0 1.9 %collective-permute-start = (bf16[352,152]{1,0:T(8,128)(2,1)}, bf16[352,152]{1,0:T(8,128)(2,1)S(1)}, u32[]{:S(2)}, u32[]{:S(2)}) collective-permute-start(bf16[352,152]{1,0:T(8,128)(2,1)} %get-tuple-element.26.own_ref), channel_id=1, source_target_pairs={{0,1},{1,2},{2,3},{3,4},{4,5},{5,6},{6,7},{7,8},{8,9},{9,10},{10,1... | collective-permute-start | bytes 321032 | tf_op jit(solution)/shard_map/ppermute | solution.py:456
  14.9 1.4 collective-permute-done.1.upper_ref
  16.3 4.6 %collective-permute-done.lower_ref = bf16[352,152]{1,0:T(8,128)(2,1)S(1)} collective-permute-done((bf16[352,152]{1,0:T(8,128)(2,1)}, bf16[352,152]{1,0:T(8,128)(2,1)S(1)}, u32[]{:S(2)}, u32[]{:S(2)}) %collective-permute-start) | collective-permute-done | bytes 107040 | tf_op jit(solution)/shard_map/ppermute | solution.py:456
  20.9 0.8 fusion.1
  21.8 0.1 collective-permute-start.2
  21.8 2.5 %collective-permute-start.4 = (f32[64,40,128]{2,1,0:T(8,128)}, f32[64,40,128]{2,1,0:T(8,128)S(1)}, u32[]{:S(2)}, u32[]{:S(2)}) collective-permute-start(f32[64,40,128]{2,1,0:T(8,128)} %get-tuple-element.31), channel_id=1, source_target_pairs={{1,0},{2,1},{3,2},{4,3},{5,4},{6,5},{7,6},{8,7},{9,8},{10,9},{11,1... | collective-permute-start | bytes 3932168 | tf_op jit(solution)/shard_map/ppermute | solution.py:456
  24.4 1.9 %collective-permute-start.3 = (f32[64,40,128]{2,1,0:T(8,128)}, f32[64,40,128]{2,1,0:T(8,128)S(1)}, u32[]{:S(2)}, u32[]{:S(2)}) collective-permute-start(f32[64,40,128]{2,1,0:T(8,128)} %get-tuple-element.31), channel_id=1, source_target_pairs={{0,1},{1,2},{2,3},{3,4},{4,5},{5,6},{6,7},{7,8},{8,9},{9,10},{10,1... | collective-permute-start | bytes 3932168 | tf_op jit(solution)/shard_map/ppermute | solution.py:456
  26.3 0.0 collective-permute-done.2
  26.3 0.0 copy-start.2
  26.3 2.1 %collective-permute-start.5 = (f32[32,152]{1,0:T(8,128)S(1)}, f32[32,152]{1,0:T(8,128)S(1)}, u32[]{:S(2)}, u32[]{:S(2)}) collective-permute-start(f32[32,152]{1,0:T(8,128)S(1)} %add.21.sum_ref), channel_id=1, source_target_pairs={{0,4},{1,5},{2,6},{3,7},{4,0},{5,1},{6,2},{7,3},{8,12},{9,13},{10,... | collective-permute-start | bytes 58376 | tf_op jit(solution)/shard_map/ppermute | solution.py:460
  28.4 0.0 copy-done.4
  28.4 0.0 copy-done.5
  28.4 28.0 %far.1.refs_4_ = f32[256,152]{1,0:T(8,128)} custom-call(bf16[352,152]{1,0:T(8,128)(2,1)} %copy-done.5, bf16[352,152]{1,0:T(8,128)(2,1)} %get-tuple-element.26.own_ref, bf16[352,152]{1,0:T(8,128)(2,1)} %copy-done.4, s32[8,316]{1,0:T(8,128)} %vlist_ref.1, bf16[23104,316]{1,0:T(8,128)(2,1)} %bitcast.11), custom_call_target="tpu_custom_call" | custom-call | flops 20000000000 | bytes 18000000 | tf_op jit(solution)/shard_map/far/pallas_call | solution.py:520
  56.4 0.0 copy-done.2
  56.5 0.0 collective-permute-done.4.upper_ref
  56.5 0.0 collective-permute-done.3.lower_ref
  56.5 0.0 collective-permute-done.5.pair_ref
  56.5 0.0 copy-start.3
  56.5 1.0 copy-done
  57.5 0.4 copy-done.1
  57.9 0.0 copy-done.3
  57.9 8.8 %pack.1 = (bf16[16384,128]{1,0:T(8,128)(2,1)}, bf16[2,8192,128]{2,1,0:T(8,128)(2,1)}, s32[64,128]{1,0:T(8,128)}, s32[16,128]{1,0:T(8,128)}, f32[32,152]{1,0:T(8,128)}, /*index=5*/f32[32,152]{1,0:T(8,128)}) custom-call(f32[64,40,128]{2,1,0:T(8,128)} %copy-done.1, f32[64,40,128]{2,1,0:T(8,128)} %copy-done, s32[27,64]{1,0:T(8,128)} %bitcast.9, ...), custom_call_target="tpu_custom_call" | custom-call | tf_op jit(solution)/shard_map/pack/pallas_call | solution.py:538
  66.7 2.0 %collective-permute-start.6 = (f32[32,152]{1,0:T(8,128)}, f32[32,152]{1,0:T(8,128)S(1)}, u32[]{:S(2)}, u32[]{:S(2)}) collective-permute-start(f32[32,152]{1,0:T(8,128)} %get-tuple-element.42), channel_id=1, source_target_pairs={{0,8},{1,9},{2,10},{3,11},{4,12},{5,13},{6,14},{7,15},{8,0},{9,1},... | collective-permute-start | bytes 58376 | tf_op jit(solution)/shard_map/ppermute | solution.py:460
  68.7 2.1 %collective-permute-done.6 = f32[32,152]{1,0:T(8,128)S(1)} collective-permute-done((f32[32,152]{1,0:T(8,128)}, f32[32,152]{1,0:T(8,128)S(1)}, u32[]{:S(2)}, u32[]{:S(2)}) %collective-permute-start.6) | collective-permute-done | bytes 19488 | tf_op jit(solution)/shard_map/ppermute | solution.py:460
  70.8 0.8 add.22
  71.6 3.3 %collective-permute-start.7 = (f32[32,152]{1,0:T(8,128)S(1)}, f32[32,152]{1,0:T(8,128)S(1)}, u32[]{:S(2)}, u32[]{:S(2)}) collective-permute-start(f32[32,152]{1,0:T(8,128)S(1)} %add.22), channel_id=1, source_target_pairs={{0,16},{1,17},{2,18},{3,19},{4,20},{5,21},{6,22},{7,23},{8,24},{9,... | collective-permute-start | bytes 58376 | tf_op jit(solution)/shard_map/ppermute | solution.py:460
  74.9 48.5 %near.1.refs_3_ = f32[64,32,128]{2,1,0:T(8,128)} custom-call(s32[64,128]{1,0:T(8,128)} %get-tuple-element.35.plan_ref, s32[16,128]{1,0:T(8,128)} %get-tuple-element.36.item_ref, bf16[8192,128]{1,0:T(8,128)(2,1)} %get-tuple-element.37.own_hbm, bf16[16384,128]{1,0:T(8,128)(2,1)} %get-tuple-element.38.side_hbm, ...), custom_call_target="tpu_custom_call" | custom-call | flops 30000001024 | bytes 10000000 | tf_op jit(solution)/shard_map/near/pallas_call | solution.py:562
  123.4 0.0 collective-permute-done.7
  123.4 0.6 add.23.refs_9_
  124.0 18.5 %final.1 = f32[64,32,128]{2,1,0:T(8,128)} custom-call(s32[64]{0:T(128)} %refs_0_.1, bf16[2,4096,128]{2,1,0:T(8,128)(2,1)} %get-tuple-element.24.own_feature_hbm.refs_1_, bf16[64,152,32]{2,1,0:T(8,128)(2,1)} %get-tuple-element.25.refs_2_, f32[64,32,128]{2,1,0:T(8,128)} %near.1.refs_3_, f32[256,152]{1,0:T(8,128)} %far.1.refs_4_, f32[8,152,152]{2,1,0:T(8,128)} %refs_5_.1, ...), custom_call_target="tpu_custom_call" | custom-call | tf_op jit(solution)/shard_map/final/pallas_call | solution.py:579
  (6 shorter events, 0.0 us)
Async XLA Ops:
  10.2 6.1 %collective-permute-start.1 = (bf16[352,152]{1,0:T(8,128)(2,1)}, bf16[352,152]{1,0:T(8,128)(2,1)S(1)}, u32[]{:S(2)}, u32[]{:S(2)}) collective-permute-start(bf16[352,152]{1,0:T(8,128)(2,1)} %get-tuple-element.26.own_ref), channel_id=1, source_target_pairs={{1,0},{2,1},{3,2},{4,3},{5,4},{6,5},{7,6},{8,7},{9,8},{10,9},{11,1... | collective-permute-start | bytes 321032 | tf_op jit(solution)/shard_map/ppermute | solution.py:456
  13.0 7.9 %collective-permute-start = (bf16[352,152]{1,0:T(8,128)(2,1)}, bf16[352,152]{1,0:T(8,128)(2,1)S(1)}, u32[]{:S(2)}, u32[]{:S(2)}) collective-permute-start(bf16[352,152]{1,0:T(8,128)(2,1)} %get-tuple-element.26.own_ref), channel_id=1, source_target_pairs={{0,1},{1,2},{2,3},{3,4},{4,5},{5,6},{6,7},{7,8},{8,9},{9,10},{10,1... | collective-permute-start | bytes 321032 | tf_op jit(solution)/shard_map/ppermute | solution.py:456
  16.3 12.1 %copy-start.4 = (bf16[352,152]{1,0:T(8,128)(2,1)}, bf16[352,152]{1,0:T(8,128)(2,1)S(1)}, u32[]{:S(2)}) copy-start(bf16[352,152]{1,0:T(8,128)(2,1)S(1)} %collective-permute-done.1.upper_ref) | copy-start | bytes 321028
  20.9 7.5 %copy-start.5 = (bf16[352,152]{1,0:T(8,128)(2,1)}, bf16[352,152]{1,0:T(8,128)(2,1)S(1)}, u32[]{:S(2)}) copy-start(bf16[352,152]{1,0:T(8,128)(2,1)S(1)} %collective-permute-done.lower_ref) | copy-start | bytes 321028
  21.8 4.5 %collective-permute-start.2 = (f32[32,152]{1,0:T(8,128)S(1)}, f32[32,152]{1,0:T(8,128)S(1)}, u32[]{:S(2)}, u32[]{:S(2)}) collective-permute-start(f32[32,152]{1,0:T(8,128)S(1)} %fusion.1), channel_id=1, source_target_pairs={{0,2},{1,3},{2,0},{3,1},{4,6},{5,7},{6,4},{7,5},{8,10},{9,11},{10,... | collective-permute-start | bytes 58376 | tf_op jit(solution)/shard_map/ppermute | solution.py:460
  21.8 34.6 %collective-permute-start.4 = (f32[64,40,128]{2,1,0:T(8,128)}, f32[64,40,128]{2,1,0:T(8,128)S(1)}, u32[]{:S(2)}, u32[]{:S(2)}) collective-permute-start(f32[64,40,128]{2,1,0:T(8,128)} %get-tuple-element.31), channel_id=1, source_target_pairs={{1,0},{2,1},{3,2},{4,3},{5,4},{6,5},{7,6},{8,7},{9,8},{10,9},{11,1... | collective-permute-start | bytes 3932168 | tf_op jit(solution)/shard_map/ppermute | solution.py:456
  24.4 32.1 %collective-permute-start.3 = (f32[64,40,128]{2,1,0:T(8,128)}, f32[64,40,128]{2,1,0:T(8,128)S(1)}, u32[]{:S(2)}, u32[]{:S(2)}) collective-permute-start(f32[64,40,128]{2,1,0:T(8,128)} %get-tuple-element.31), channel_id=1, source_target_pairs={{0,1},{1,2},{2,3},{3,4},{4,5},{5,6},{6,7},{7,8},{8,9},{9,10},{10,1... | collective-permute-start | bytes 3932168 | tf_op jit(solution)/shard_map/ppermute | solution.py:456
  26.3 30.1 %copy-start.2 = (f32[32,152]{1,0:T(8,128)}, f32[32,152]{1,0:T(8,128)S(1)}, u32[]{:S(2)}) copy-start(f32[32,152]{1,0:T(8,128)S(1)} %add.21.sum_ref) | copy-start | bytes 58372
  26.3 30.2 %collective-permute-start.5 = (f32[32,152]{1,0:T(8,128)S(1)}, f32[32,152]{1,0:T(8,128)S(1)}, u32[]{:S(2)}, u32[]{:S(2)}) collective-permute-start(f32[32,152]{1,0:T(8,128)S(1)} %add.21.sum_ref), channel_id=1, source_target_pairs={{0,4},{1,5},{2,6},{3,7},{4,0},{5,1},{6,2},{7,3},{8,12},{9,13},{10,... | collective-permute-start | bytes 58376 | tf_op jit(solution)/shard_map/ppermute | solution.py:460
  56.5 1.1 copy-start
  56.5 1.4 %copy-start.1 = (f32[64,40,128]{2,1,0:T(8,128)}, f32[64,40,128]{2,1,0:T(8,128)S(1)}, u32[]{:S(2)}) copy-start(f32[64,40,128]{2,1,0:T(8,128)S(1)} %collective-permute-done.3.lower_ref) | copy-start | bytes 3932164
  56.5 1.4 %copy-start.3 = (f32[32,152]{1,0:T(8,128)}, f32[32,152]{1,0:T(8,128)S(1)}, u32[]{:S(2)}) copy-start(f32[32,152]{1,0:T(8,128)S(1)} %collective-permute-done.5.pair_ref) | copy-start | bytes 58372
  66.7 4.1 %collective-permute-start.6 = (f32[32,152]{1,0:T(8,128)}, f32[32,152]{1,0:T(8,128)S(1)}, u32[]{:S(2)}, u32[]{:S(2)}) collective-permute-start(f32[32,152]{1,0:T(8,128)} %get-tuple-element.42), channel_id=1, source_target_pairs={{0,8},{1,9},{2,10},{3,11},{4,12},{5,13},{6,14},{7,15},{8,0},{9,1},... | collective-permute-start | bytes 58376 | tf_op jit(solution)/shard_map/ppermute | solution.py:460
  71.6 51.8 %collective-permute-start.7 = (f32[32,152]{1,0:T(8,128)S(1)}, f32[32,152]{1,0:T(8,128)S(1)}, u32[]{:S(2)}, u32[]{:S(2)}) collective-permute-start(f32[32,152]{1,0:T(8,128)S(1)} %add.22), channel_id=1, source_target_pairs={{0,16},{1,17},{2,18},{3,19},{4,20},{5,21},{6,22},{7,23},{8,24},{9,... | collective-permute-start | bytes 58376 | tf_op jit(solution)/shard_map/ppermute | solution.py:460

commit v6 on v5

--- a/solution.py
+++ b/solution.py
@@ -19,6 +19,7 @@
 CLASS_ROWS = (32, 64, 96, 128)
 PLAN_PLACES, PLAN_CLASS, PLAN_ORDER, PLAN_COUNT = 56, 60, 61, 62
 SOURCES = 32
+CHUNK = 4
 
 
 def dot(left, right):
@@ -101,13 +102,20 @@
     return [high, weights - high]
 
 
-def put_features(feature_ref, leaf, rows):
+def feature_versions(rows):
     lower = iota(rows.shape, 1) < PIECE
+    versions = []
     for half in range(2):
         alone = jnp.where(lower == (half == 0), rows, 0.0)
+        versions.append((half, half, alone.astype(BF16)))
+        versions.append((half, 1 - half, pltpu.roll(alone, PIECE, 1).astype(BF16)))
+    return versions
+
+
+def put_features(feature_ref, leaf, versions):
+    for half, place, value in versions:
         span = pl.ds(pl.multiple_of((2 * leaf + half) * 32, 32), 32)
-        feature_ref[half, span, :] = alone.astype(BF16)
-        feature_ref[1 - half, span, :] = pltpu.roll(alone, PIECE, 1).astype(BF16)
+        feature_ref[place, span, :] = value
 
 
 def upward_kernel(
@@ -121,26 +129,34 @@
     row = iota((8, p_width), 0)
 
     def node_step(node, carry):
-        for child in range(8):
-            leaf = node * 8 + child
-            count = counts_ref[leaf]
-            weights = jnp.where(lane < count, dens_ref[leaf], 0.0)
-            coords = coords_of(points_ref, leaf)
-            message_ref[leaf, :q_width, :] = weights
-            message_ref[leaf, q_width:, :] = jnp.where(row == 3, count.astype(F32), coords)
-            parts = pieces(coords)
-            weight_parts = weight_rows(weights)
-            right = right_rows(parts)
-            pack = jnp.concatenate([left_rows(parts)] + weight_parts + [right], axis=0).astype(BF16).T
-            pack_ref[pl.ds(pl.multiple_of(leaf * p_width, p_width), p_width), :] = pack
-            put_features(feature_ref, leaf, right)
-            surface = left_rows(pieces(coords_of(surface_ref, leaf)))
-            turned_ref[leaf] = surface.astype(BF16).T
-            wide = jnp.concatenate([jnp.zeros((96, eq_width), F32), surface], axis=0).astype(BF16)
-            values_high, values_low = halves(jnp.exp2(dot(pack, wide)))
-            rows = jnp.concatenate(weight_parts, axis=0).astype(BF16)
-            both = dot(rows, values_high)
-            check = both[:q_width] + both[q_width:] + dot(rows[:q_width], values_low)
+        leaves = [node * 8 + child for child in range(8)]
+        counts = [counts_ref[leaf] for leaf in leaves]
+        weights = [jnp.where(lane < count, dens_ref[leaf], 0.0) for leaf, count in zip(leaves, counts)]
+        coords = [coords_of(points_ref, leaf) for leaf in leaves]
+        surfaces = [left_rows(pieces(coords_of(surface_ref, leaf))) for leaf in leaves]
+        parts = [pieces(value) for value in coords]
+        rights = [right_rows(value) for value in parts]
+        lists = [weight_rows(value) for value in weights]
+        packs = [
+            jnp.concatenate([left_rows(part)] + split + [right], axis=0).astype(BF16).T
+            for part, split, right in zip(parts, lists, rights)
+        ]
+        blank = jnp.zeros((96, eq_width), F32)
+        wides = [jnp.concatenate([blank, value], axis=0).astype(BF16) for value in surfaces]
+        exponents = [dot(pack, wide) for pack, wide in zip(packs, wides)]
+        values = [halves(jnp.exp2(value)) for value in exponents]
+        rows = [jnp.concatenate(split, axis=0).astype(BF16) for split in lists]
+        firsts = [dot(row, value[0]) for row, value in zip(rows, values)]
+        seconds = [dot(row[:q_width], value[1]) for row, value in zip(rows, values)]
+        turned = [value.astype(BF16).T for value in surfaces]
+        versions = [feature_versions(right) for right in rights]
+        for child, leaf in enumerate(leaves):
+            message_ref[leaf, :q_width, :] = weights[child]
+            message_ref[leaf, q_width:, :] = jnp.where(row == 3, counts[child].astype(F32), coords[child])
+            pack_ref[pl.ds(pl.multiple_of(leaf * p_width, p_width), p_width), :] = packs[child]
+            turned_ref[leaf] = turned[child]
+            put_features(feature_ref, leaf, versions[child])
+            check = firsts[child][:q_width] + firsts[child][q_width:] + seconds[child]
             check_ref[child, pl.ds(pl.multiple_of(node * q_width, q_width), q_width), :] = check
         return carry
 
@@ -164,14 +180,14 @@
 
 
 def far_kernel(
-    lower_ref, own_ref, upper_ref, vlist_ref, table_hbm, out_ref, table_ref, tail_ref, wide_ref, total_ref, sems
+    lower_ref, own_ref, upper_ref, vlist_ref, table_hbm, out_ref, table_ref, tail_ref, wide_ref, total_ref, first_ref, sems
 ):
     node_count, type_count = vlist_ref.shape
     eq_width = own_ref.shape[1]
     q_width = out_ref.shape[0] // node_count
     lanes = node_count * q_width
     tile = 128 // q_width
-    chunk = 8
+    chunk = CHUNK
     chunk_rows = chunk * eq_width
     chunk_count = eq_width // chunk
     full = type_count // 128
@@ -210,12 +226,15 @@
     nothing = jnp.zeros((SOURCES, 128), F32)
     total_ref[...] = jnp.zeros_like(total_ref)
 
-    def chunk_step(number, carry):
-        for copy in copies_of(number):
-            copy.wait()
+    def table_of(number):
         span = pl.ds(pl.multiple_of(number * chunk_rows, chunk_rows), chunk_rows)
         left = jnp.concatenate([table_ref[part, span, :] for part in range(full)], axis=1)
-        summed = dot(left, chosen_full) + dot(tail_ref[span, :], chosen_tail)
+        return left, tail_ref[span, :]
+
+    def first_product(left, tail):
+        return dot(left, chosen_full) + dot(tail, chosen_tail)
+
+    def second_product(number, summed):
         lefts, rights = [], []
         for step in range(chunk):
             value = summed[step * eq_width : (step + 1) * eq_width]
@@ -228,10 +247,31 @@
                 line = [parts[node % tile] if place == node // tile else nothing for place in range(node_count // tile)]
                 rights.append(jnp.concatenate(line, axis=1))
         product = dot(jnp.concatenate(lefts, axis=1), jnp.concatenate(rights, axis=0).astype(BF16))
-        total_ref[...] += product[:eq_width] + product[eq_width:]
+        return product[:eq_width] + product[eq_width:]
+
+    def wait_for(number):
+        for copy in copies_of(number):
+            copy.wait()
+
+    wait_for(0)
+    first_ref[...] = first_product(*table_of(0))
+
+    def pair_step(pair, carry):
+        number = 2 * pair
+        wait_for(number + 1)
+        pl.when(pair < chunk_count // 2 - 1)(lambda: wait_for(number + 2))
+        ahead = table_of(number + 1)
+        behind = table_of(jnp.minimum(number + 2, chunk_count - 1))
+        summed = first_ref[...]
+        middle = first_product(*ahead)
+        total = second_product(number, summed)
+        following = first_product(*behind)
+        total = total + second_product(number + 1, middle)
+        first_ref[...] = following
+        total_ref[...] += total
         return carry
 
-    lax.fori_loop(0, chunk_count, chunk_step, 0)
+    lax.fori_loop(0, chunk_count // 2, pair_step, 0)
     out_ref[...] = total_ref[...].T
 
 
@@ -282,17 +322,26 @@
     def run(rows, first, count):
         def blocks_step(step, carry):
             slot = jnp.bitwise_and(step, 1) * UNROLL
-            for part in range(UNROLL):
-                leaf, place = item_of(step - 1, part)
-                values = [value_ref[UNROLL - slot + part, side, :rows] for side in range(2)]
-                total_ref[leaf, :rows] += dot(jnp.concatenate(values, axis=1), sources_of(leaf, place))
-            for part in range(UNROLL):
-                leaf, place = item_of(step, part)
+            done = [item_of(step - 1, part) for part in range(UNROLL)]
+            items = [item_of(step, part) for part in range(UNROLL)]
+            features = [features_of(leaf, place) for leaf, place in items]
+            targets = []
+            for leaf, _ in items:
                 start = pl.multiple_of(jnp.minimum(leaf, leaf_count - 1) * p_width, p_width)
-                targets = pack_ref[pl.ds(start, rows), :][:, :32]
-                values = jnp.exp2(dot(targets, features_of(leaf, place))).astype(BF16)
+                targets.append(pack_ref[pl.ds(start, rows), :][:, :32])
+            sources = [sources_of(leaf, place) for leaf, place in done]
+            values = [
+                jnp.concatenate([value_ref[UNROLL - slot + part, side, :rows] for side in range(2)], axis=1)
+                for part in range(UNROLL)
+            ]
+            exponents = [dot(target, feature) for target, feature in zip(targets, features)]
+            products = [dot(value, source) for value, source in zip(values, sources)]
+            following = [jnp.exp2(value).astype(BF16) for value in exponents]
+            for part, value in enumerate(following):
                 for side in range(2):
-                    value_ref[slot + part, side, :rows] = values[:, side * 128 : (side + 1) * 128]
+                    value_ref[slot + part, side, :rows] = value[:, side * 128 : (side + 1) * 128]
+            for (leaf, _), product in zip(done, products):
+                total_ref[leaf, :rows] += product
             return carry
 
         lax.fori_loop(first, first + count, blocks_step, 0)
@@ -301,9 +350,9 @@
         run(rows, plan_ref[PLAN_CLASS, 2 * number], plan_ref[PLAN_CLASS, 2 * number + 1])
 
     def turn_step(step, carry):
-        for part in range(8):
-            turned = total_ref[step * 8 + part].T
-            out_ref[step * 8 + part] = turned[32 : 32 + q_width] + turned[32 + q_width : 32 + 2 * q_width]
+        turned = [total_ref[step * 8 + part].T for part in range(8)]
+        for part, value in enumerate(turned):
+            out_ref[step * 8 + part] = value[32 : 32 + q_width] + value[32 + q_width : 32 + 2 * q_width]
         return carry
 
     lax.fori_loop(0, leaf_count // 8, turn_step, 0)
@@ -399,16 +448,17 @@
 
     def pack_step(step, counts):
         side_counts = list(counts)
-        for part in range(4):
-            leaf = step * 4 + part
-            for side, source in enumerate((lower_ref, upper_ref)):
-                tail = source[leaf, q_width:, :]
-                place = side * leaf_count + leaf
-                weights = weight_rows(source[leaf, :q_width, :])
-                packed = jnp.concatenate([blank] + weights + [blank], axis=0).astype(BF16).T
-                pack_ref[pl.ds(pl.multiple_of(place * p_width, p_width), p_width), :] = packed
-                put_features(feature_ref, place, right_rows(pieces(tail)))
-                side_counts[side] = jnp.where(lane == leaf, tail[3:4, :leaf_count], side_counts[side])
+        chosen = [(step * 4 + part, side) for part in range(4) for side in range(2)]
+        sources = (lower_ref, upper_ref)
+        tails = [sources[side][leaf, q_width:, :] for leaf, side in chosen]
+        weights = [weight_rows(sources[side][leaf, :q_width, :]) for leaf, side in chosen]
+        packs = [jnp.concatenate([blank] + value + [blank], axis=0).astype(BF16).T for value in weights]
+        versions = [feature_versions(right_rows(pieces(tail))) for tail in tails]
+        for (leaf, side), tail, pack, version in zip(chosen, tails, packs, versions):
+            place = side * leaf_count + leaf
+            pack_ref[pl.ds(pl.multiple_of(place * p_width, p_width), p_width), :] = pack
+            put_features(feature_ref, place, version)
+            side_counts[side] = jnp.where(lane == leaf, tail[3:4, :leaf_count], side_counts[side])
         return tuple(side_counts)
 
     nothing = jnp.zeros((1, leaf_count), F32)
@@ -436,15 +486,22 @@
     lane = iota((q_width, p_width), 1)
 
     def node_step(node, carry):
-        for child in range(8):
-            leaf = node * 8 + child
+        leaves = [node * 8 + child for child in range(8)]
+        features = []
+        for leaf in leaves:
             starts = [pl.multiple_of((2 * leaf + half) * 32, 32) for half in range(2)]
-            features = feature_ref[0, pl.ds(starts[0], 32), :] + feature_ref[1, pl.ds(starts[1], 32), :]
-            values_high, values_low = halves(jnp.exp2(dot(turned_ref[leaf], features)))
-            down = weight_rows(down_leaf_ref[child, pl.ds(pl.multiple_of(node * q_width, q_width), q_width), :])
-            both = dot(jnp.concatenate(down, axis=0).astype(BF16), values_high)
-            far = both[:q_width] + both[q_width:] + dot(down[0].astype(BF16), values_low)
-            out_ref[leaf] = jnp.where(lane < counts_ref[leaf], far + near_ref[leaf], 0.0)
+            features.append(feature_ref[0, pl.ds(starts[0], 32), :] + feature_ref[1, pl.ds(starts[1], 32), :])
+        turned = [turned_ref[leaf] for leaf in leaves]
+        node_rows = pl.ds(pl.multiple_of(node * q_width, q_width), q_width)
+        downs = [weight_rows(down_leaf_ref[child, node_rows, :]) for child in range(8)]
+        nears = [near_ref[leaf] for leaf in leaves]
+        exponents = [dot(left, right) for left, right in zip(turned, features)]
+        values = [halves(jnp.exp2(value)) for value in exponents]
+        firsts = [dot(jnp.concatenate(down, axis=0).astype(BF16), value[0]) for down, value in zip(downs, values)]
+        seconds = [dot(down[0].astype(BF16), value[1]) for down, value in zip(downs, values)]
+        for child, leaf in enumerate(leaves):
+            far = firsts[child][:q_width] + firsts[child][q_width:] + seconds[child]
+            out_ref[leaf] = jnp.where(lane < counts_ref[leaf], far + nears[child], 0.0)
         return carry
 
     lax.fori_loop(0, node_count, node_step, 0)
@@ -527,7 +584,8 @@
             pltpu.VMEM((eq_width * eq_width, type_count % 128), BF16),
             pltpu.VMEM((eq_width * SOURCES, 128), F32),
             pltpu.VMEM((eq_width, node_rows), F32),
-            pltpu.SemaphoreType.DMA((eq_width // 8, type_count // 128 + 1)),
+            pltpu.VMEM((CHUNK * eq_width, node_rows), F32),
+            pltpu.SemaphoreType.DMA((eq_width // CHUNK, type_count // 128 + 1)),
         ],
         compiler_params=params,
         cost_estimate=pl.CostEstimate(flops=2 * 10**10, bytes_accessed=18 * 10**6, transcendentals=0),

time: 144 us -> 134 us (0.931)
  Pallas kernels: 114 us -> 98.2 us
  waiting for transfers between devices: 8.13 us -> 13.7 us
  starting transfers between devices: 16.6 us -> 18.1 us
    pallas_call x1, Pallas kernels: 18.5 us -> 10.8 us  [local(): pl.pallas_call(lambda *refs: final_kernel(len(tops), *refs), out_shape=ja...]
    pallas_call x1, Pallas kernels: 28 us -> 21 us  [local(): pl.pallas_call(far_kernel, out_shape=jax.ShapeDtypeStruct((node_rows, eq_...]
    ppermute x4, waiting for transfers between devices: 5.99 us -> 11.6 us  [shifted(): return (lax.ppermute(value, 'oct', up), lax.ppermute(value, 'oct', down))]
    ppermute x4, starting transfers between devices: 7.47 us -> 9 us  [swapped(): lax.ppermute(value, 'oct', [(source, source ^ 1 << bit) for source in ran...]
  transfers between devices with their start and end apart: 8 -> 8, of which waited for: 3 -> 5; matrix products, arithmetic and copies ran while one was open for 0% -> 0% of each run, Pallas kernels for 54% -> 52%
where the time goes in v6:
time: 134 us; the launch traced here: 133 us
  Pallas kernels  98.2 us (73%)
  starting transfers between devices  18.1 us (14%)
  waiting for transfers between devices  13.7 us (10%)
  other arithmetic  2.21 us (2%)
    pallas_call x1, Pallas kernels, local(): pl.pallas_call(near_kernel, out_shape=jax.ShapeDtypeStruct((leaf_count, q...  48 us
    pallas_call x1, Pallas kernels, local(): pl.pallas_call(far_kernel, out_shape=jax.ShapeDtypeStruct((node_rows, eq_...  21 us
    ppermute x4, waiting for transfers between devices, shifted(): return (lax.ppermute(value, 'oct', up), lax.ppermute(value, 'oct', down))  11.6 us
    pallas_call x1, Pallas kernels, local(): pl.pallas_call(lambda *refs: final_kernel(len(tops), *refs), out_shape=ja...  10.8 us
    pallas_call x1, Pallas kernels, local(): pl.pallas_call(upward_kernel, out_shape=(jax.ShapeDtypeStruct((leaf_count...  10.2 us
    ppermute x4, starting transfers between devices, shifted(): return (lax.ppermute(value, 'oct', up), lax.ppermute(value, 'oct', down))  9.13 us
    ppermute x4, starting transfers between devices, swapped(): lax.ppermute(value, 'oct', [(source, source ^ 1 << bit) for source in ran...  9 us
    pallas_call x1, Pallas kernels, local(): pl.pallas_call(pack_kernel, out_shape=(jax.ShapeDtypeStruct((2 * leaf_cou...  8.24 us
  transfers between devices with their start and end apart: 8, of which 5 were waited for; matrix products, arithmetic and copies ran while one was open for 0% of the time, Pallas kernels for 52%

profile of v6, /device:TPU:4, one launch (start us, length us, event | category | flops | bytes accessed | tf_op | source)
XLA Modules:
  0.0 133.4 jit_solution(9827655347532925542)
XLA Ops:
  0.0 10.2 %upward.1 = (bf16[8192,128]{1,0:T(8,128)(2,1)}, bf16[2,4096,128]{2,1,0:T(8,128)(2,1)}, bf16[64,152,32]{2,1,0:T(8,128)(2,1)}, f32[64,40,128]{2,1,0:T(8,128)}, bf1...) custom-call(f32[3,64,128]{2,1,0:T(8,128)} %bitcast.8, f32[64,32,128]{2,1,0:T(8,128)} %dens_ref.1, f32[3,64,152]{2,1,0:T(8,128)} %bitcast.7, ...), custom_call_target="tpu_custom_call" | custom-call | tf_op jit(solution)/shard_map/upward/pallas_call | solution.py:550
  10.2 2.8 %collective-permute-start.1 = (bf16[352,152]{1,0:T(8,128)(2,1)}, bf16[352,152]{1,0:T(8,128)(2,1)S(1)}, u32[]{:S(2)}, u32[]{:S(2)}) collective-permute-start(bf16[352,152]{1,0:T(8,128)(2,1)} %get-tuple-element.26.own_ref), channel_id=1, source_target_pairs={{1,0},{2,1},{3,2},{4,3},{5,4},{6,5},{7,6},{8,7},{9,8},{10,9},{11,1... | collective-permute-start | bytes 321032 | tf_op jit(solution)/shard_map/ppermute | solution.py:513
  13.0 1.9 %collective-permute-start = (bf16[352,152]{1,0:T(8,128)(2,1)}, bf16[352,152]{1,0:T(8,128)(2,1)S(1)}, u32[]{:S(2)}, u32[]{:S(2)}) collective-permute-start(bf16[352,152]{1,0:T(8,128)(2,1)} %get-tuple-element.26.own_ref), channel_id=1, source_target_pairs={{0,1},{1,2},{2,3},{3,4},{4,5},{5,6},{6,7},{7,8},{8,9},{9,10},{10,1... | collective-permute-start | bytes 321032 | tf_op jit(solution)/shard_map/ppermute | solution.py:513
  14.9 1.4 %collective-permute-done.1.upper_ref = bf16[352,152]{1,0:T(8,128)(2,1)S(1)} collective-permute-done((bf16[352,152]{1,0:T(8,128)(2,1)}, bf16[352,152]{1,0:T(8,128)(2,1)S(1)}, u32[]{:S(2)}, u32[]{:S(2)}) %collective-permute-start.1) | collective-permute-done | bytes 107040 | tf_op jit(solution)/shard_map/ppermute | solution.py:513
  16.3 0.0 copy-start.4
  16.3 4.6 %collective-permute-done.lower_ref = bf16[352,152]{1,0:T(8,128)(2,1)S(1)} collective-permute-done((bf16[352,152]{1,0:T(8,128)(2,1)}, bf16[352,152]{1,0:T(8,128)(2,1)S(1)}, u32[]{:S(2)}, u32[]{:S(2)}) %collective-permute-start) | collective-permute-done | bytes 107040 | tf_op jit(solution)/shard_map/ppermute | solution.py:513
  20.9 0.8 fusion.1
  21.7 0.1 collective-permute-start.2
  21.8 2.5 %collective-permute-start.4 = (f32[64,40,128]{2,1,0:T(8,128)}, f32[64,40,128]{2,1,0:T(8,128)S(1)}, u32[]{:S(2)}, u32[]{:S(2)}) collective-permute-start(f32[64,40,128]{2,1,0:T(8,128)} %get-tuple-element.31), channel_id=1, source_target_pairs={{1,0},{2,1},{3,2},{4,3},{5,4},{6,5},{7,6},{8,7},{9,8},{10,9},{11,1... | collective-permute-start | bytes 3932168 | tf_op jit(solution)/shard_map/ppermute | solution.py:513
  24.3 1.9 %collective-permute-start.3 = (f32[64,40,128]{2,1,0:T(8,128)}, f32[64,40,128]{2,1,0:T(8,128)S(1)}, u32[]{:S(2)}, u32[]{:S(2)}) collective-permute-start(f32[64,40,128]{2,1,0:T(8,128)} %get-tuple-element.31), channel_id=1, source_target_pairs={{0,1},{1,2},{2,3},{3,4},{4,5},{5,6},{6,7},{7,8},{8,9},{9,10},{10,1... | collective-permute-start | bytes 3932168 | tf_op jit(solution)/shard_map/ppermute | solution.py:513
  26.3 0.0 collective-permute-done.2
  26.3 0.0 copy-start.2
  26.3 2.1 %collective-permute-start.5 = (f32[32,152]{1,0:T(8,128)S(1)}, f32[32,152]{1,0:T(8,128)S(1)}, u32[]{:S(2)}, u32[]{:S(2)}) collective-permute-start(f32[32,152]{1,0:T(8,128)S(1)} %add.21.sum_ref), channel_id=1, source_target_pairs={{0,4},{1,5},{2,6},{3,7},{4,0},{5,1},{6,2},{7,3},{8,12},{9,13},{10,... | collective-permute-start | bytes 58376 | tf_op jit(solution)/shard_map/ppermute | solution.py:517
  28.4 0.0 copy-done.4
  28.4 0.0 copy-done.5
  28.4 21.0 %far.1.refs_4_ = f32[256,152]{1,0:T(8,128)} custom-call(bf16[352,152]{1,0:T(8,128)(2,1)} %copy-done.5, bf16[352,152]{1,0:T(8,128)(2,1)} %get-tuple-element.26.own_ref, bf16[352,152]{1,0:T(8,128)(2,1)} %copy-done.4, s32[8,316]{1,0:T(8,128)} %vlist_ref.1, bf16[23104,316]{1,0:T(8,128)(2,1)} %bitcast.11), custom_call_target="tpu_custom_call" | custom-call | flops 20000000000 | bytes 18000000 | tf_op jit(solution)/shard_map/far/pallas_call | solution.py:577
  49.5 0.0 copy-done.2
  49.5 1.5 %collective-permute-done.4.upper_ref = f32[64,40,128]{2,1,0:T(8,128)S(1)} collective-permute-done((f32[64,40,128]{2,1,0:T(8,128)}, f32[64,40,128]{2,1,0:T(8,128)S(1)}, u32[]{:S(2)}, u32[]{:S(2)}) %collective-permute-start.4) | collective-permute-done | bytes 1310752 | tf_op jit(solution)/shard_map/ppermute | solution.py:513
  51.0 4.1 %collective-permute-done.3.lower_ref = f32[64,40,128]{2,1,0:T(8,128)S(1)} collective-permute-done((f32[64,40,128]{2,1,0:T(8,128)}, f32[64,40,128]{2,1,0:T(8,128)S(1)}, u32[]{:S(2)}, u32[]{:S(2)}) %collective-permute-start.3) | collective-permute-done | bytes 1310752 | tf_op jit(solution)/shard_map/ppermute | solution.py:513
  55.1 0.0 collective-permute-done.5.pair_ref
  55.1 0.0 copy-done
  55.1 1.0 copy-done.1
  56.2 0.0 copy-done.3
  56.2 8.2 %pack.1 = (bf16[16384,128]{1,0:T(8,128)(2,1)}, bf16[2,8192,128]{2,1,0:T(8,128)(2,1)}, s32[64,128]{1,0:T(8,128)}, s32[16,128]{1,0:T(8,128)}, f32[32,152]{1,0:T(8,128)}, /*index=5*/f32[32,152]{1,0:T(8,128)}) custom-call(f32[64,40,128]{2,1,0:T(8,128)} %copy-done.1, f32[64,40,128]{2,1,0:T(8,128)} %copy-done, s32[27,64]{1,0:T(8,128)} %bitcast.9, ...), custom_call_target="tpu_custom_call" | custom-call | tf_op jit(solution)/shard_map/pack/pallas_call | solution.py:596
  64.4 3.8 %collective-permute-start.6 = (f32[32,152]{1,0:T(8,128)}, f32[32,152]{1,0:T(8,128)S(1)}, u32[]{:S(2)}, u32[]{:S(2)}) collective-permute-start(f32[32,152]{1,0:T(8,128)} %get-tuple-element.42), channel_id=1, source_target_pairs={{0,8},{1,9},{2,10},{3,11},{4,12},{5,13},{6,14},{7,15},{8,0},{9,1},... | collective-permute-start | bytes 58376 | tf_op jit(solution)/shard_map/ppermute | solution.py:517
  68.2 2.1 %collective-permute-done.6 = f32[32,152]{1,0:T(8,128)S(1)} collective-permute-done((f32[32,152]{1,0:T(8,128)}, f32[32,152]{1,0:T(8,128)S(1)}, u32[]{:S(2)}, u32[]{:S(2)}) %collective-permute-start.6) | collective-permute-done | bytes 19488 | tf_op jit(solution)/shard_map/ppermute | solution.py:517
  70.3 0.8 add.22
  71.0 3.0 %collective-permute-start.7 = (f32[32,152]{1,0:T(8,128)S(1)}, f32[32,152]{1,0:T(8,128)S(1)}, u32[]{:S(2)}, u32[]{:S(2)}) collective-permute-start(f32[32,152]{1,0:T(8,128)S(1)} %add.22), channel_id=1, source_target_pairs={{0,16},{1,17},{2,18},{3,19},{4,20},{5,21},{6,22},{7,23},{8,24},{9,... | collective-permute-start | bytes 58376 | tf_op jit(solution)/shard_map/ppermute | solution.py:517
  74.1 48.0 %near.1.refs_3_ = f32[64,32,128]{2,1,0:T(8,128)} custom-call(s32[64,128]{1,0:T(8,128)} %get-tuple-element.35.plan_ref, s32[16,128]{1,0:T(8,128)} %get-tuple-element.36.item_ref, bf16[8192,128]{1,0:T(8,128)(2,1)} %get-tuple-element.37.own_hbm, bf16[16384,128]{1,0:T(8,128)(2,1)} %get-tuple-element.38.side_hbm, ...), custom_call_target="tpu_custom_call" | custom-call | flops 30000001024 | bytes 10000000 | tf_op jit(solution)/shard_map/near/pallas_call | solution.py:620
  122.0 0.0 collective-permute-done.7
  122.0 0.6 add.23.refs_9_
  122.7 10.8 %final.1 = f32[64,32,128]{2,1,0:T(8,128)} custom-call(s32[64]{0:T(128)} %refs_0_.1, bf16[2,4096,128]{2,1,0:T(8,128)(2,1)} %get-tuple-element.24.own_feature_hbm.refs_1_, bf16[64,152,32]{2,1,0:T(8,128)(2,1)} %get-tuple-element.25.refs_2_, f32[64,32,128]{2,1,0:T(8,128)} %near.1.refs_3_, f32[256,152]{1,0:T(8,128)} %far.1.refs_4_, f32[8,152,152]{2,1,0:T(8,128)} %refs_5_.1, ...), custom_call_target="tpu_custom_call" | custom-call | tf_op jit(solution)/shard_map/final/pallas_call | solution.py:637
  (6 shorter events, 0.0 us)
Async XLA Ops:
  10.2 6.1 %collective-permute-start.1 = (bf16[352,152]{1,0:T(8,128)(2,1)}, bf16[352,152]{1,0:T(8,128)(2,1)S(1)}, u32[]{:S(2)}, u32[]{:S(2)}) collective-permute-start(bf16[352,152]{1,0:T(8,128)(2,1)} %get-tuple-element.26.own_ref), channel_id=1, source_target_pairs={{1,0},{2,1},{3,2},{4,3},{5,4},{6,5},{7,6},{8,7},{9,8},{10,9},{11,1... | collective-permute-start | bytes 321032 | tf_op jit(solution)/shard_map/ppermute | solution.py:513
  13.0 7.9 %collective-permute-start = (bf16[352,152]{1,0:T(8,128)(2,1)}, bf16[352,152]{1,0:T(8,128)(2,1)S(1)}, u32[]{:S(2)}, u32[]{:S(2)}) collective-permute-start(bf16[352,152]{1,0:T(8,128)(2,1)} %get-tuple-element.26.own_ref), channel_id=1, source_target_pairs={{0,1},{1,2},{2,3},{3,4},{4,5},{5,6},{6,7},{7,8},{8,9},{9,10},{10,1... | collective-permute-start | bytes 321032 | tf_op jit(solution)/shard_map/ppermute | solution.py:513
  16.3 12.1 %copy-start.4 = (bf16[352,152]{1,0:T(8,128)(2,1)}, bf16[352,152]{1,0:T(8,128)(2,1)S(1)}, u32[]{:S(2)}) copy-start(bf16[352,152]{1,0:T(8,128)(2,1)S(1)} %collective-permute-done.1.upper_ref) | copy-start | bytes 321028
  20.9 7.5 %copy-start.5 = (bf16[352,152]{1,0:T(8,128)(2,1)}, bf16[352,152]{1,0:T(8,128)(2,1)S(1)}, u32[]{:S(2)}) copy-start(bf16[352,152]{1,0:T(8,128)(2,1)S(1)} %collective-permute-done.lower_ref) | copy-start | bytes 321028
  21.7 4.5 %collective-permute-start.2 = (f32[32,152]{1,0:T(8,128)S(1)}, f32[32,152]{1,0:T(8,128)S(1)}, u32[]{:S(2)}, u32[]{:S(2)}) collective-permute-start(f32[32,152]{1,0:T(8,128)S(1)} %fusion.1), channel_id=1, source_target_pairs={{0,2},{1,3},{2,0},{3,1},{4,6},{5,7},{6,4},{7,5},{8,10},{9,11},{10,... | collective-permute-start | bytes 58376 | tf_op jit(solution)/shard_map/ppermute | solution.py:517
  21.8 29.1 %collective-permute-start.4 = (f32[64,40,128]{2,1,0:T(8,128)}, f32[64,40,128]{2,1,0:T(8,128)S(1)}, u32[]{:S(2)}, u32[]{:S(2)}) collective-permute-start(f32[64,40,128]{2,1,0:T(8,128)} %get-tuple-element.31), channel_id=1, source_target_pairs={{1,0},{2,1},{3,2},{4,3},{5,4},{6,5},{7,6},{8,7},{9,8},{10,9},{11,1... | collective-permute-start | bytes 3932168 | tf_op jit(solution)/shard_map/ppermute | solution.py:513
  24.3 30.8 %collective-permute-start.3 = (f32[64,40,128]{2,1,0:T(8,128)}, f32[64,40,128]{2,1,0:T(8,128)S(1)}, u32[]{:S(2)}, u32[]{:S(2)}) collective-permute-start(f32[64,40,128]{2,1,0:T(8,128)} %get-tuple-element.31), channel_id=1, source_target_pairs={{0,1},{1,2},{2,3},{3,4},{4,5},{5,6},{6,7},{7,8},{8,9},{9,10},{10,1... | collective-permute-start | bytes 3932168 | tf_op jit(solution)/shard_map/ppermute | solution.py:513
  26.3 23.2 %copy-start.2 = (f32[32,152]{1,0:T(8,128)}, f32[32,152]{1,0:T(8,128)S(1)}, u32[]{:S(2)}) copy-start(f32[32,152]{1,0:T(8,128)S(1)} %add.21.sum_ref) | copy-start | bytes 58372
  26.3 28.8 %collective-permute-start.5 = (f32[32,152]{1,0:T(8,128)S(1)}, f32[32,152]{1,0:T(8,128)S(1)}, u32[]{:S(2)}, u32[]{:S(2)}) collective-permute-start(f32[32,152]{1,0:T(8,128)S(1)} %add.21.sum_ref), channel_id=1, source_target_pairs={{0,4},{1,5},{2,6},{3,7},{4,0},{5,1},{6,2},{7,3},{8,12},{9,13},{10,... | collective-permute-start | bytes 58376 | tf_op jit(solution)/shard_map/ppermute | solution.py:517
  51.0 4.2 %copy-start = (f32[64,40,128]{2,1,0:T(8,128)}, f32[64,40,128]{2,1,0:T(8,128)S(1)}, u32[]{:S(2)}) copy-start(f32[64,40,128]{2,1,0:T(8,128)S(1)} %collective-permute-done.4.upper_ref) | copy-start | bytes 3932164
  55.1 1.1 copy-start.1
  55.1 1.1 copy-start.3
  64.4 5.9 %collective-permute-start.6 = (f32[32,152]{1,0:T(8,128)}, f32[32,152]{1,0:T(8,128)S(1)}, u32[]{:S(2)}, u32[]{:S(2)}) collective-permute-start(f32[32,152]{1,0:T(8,128)} %get-tuple-element.42), channel_id=1, source_target_pairs={{0,8},{1,9},{2,10},{3,11},{4,12},{5,13},{6,14},{7,15},{8,0},{9,1},... | collective-permute-start | bytes 58376 | tf_op jit(solution)/shard_map/ppermute | solution.py:517
  71.0 51.0 %collective-permute-start.7 = (f32[32,152]{1,0:T(8,128)S(1)}, f32[32,152]{1,0:T(8,128)S(1)}, u32[]{:S(2)}, u32[]{:S(2)}) collective-permute-start(f32[32,152]{1,0:T(8,128)S(1)} %add.22), channel_id=1, source_target_pairs={{0,16},{1,17},{2,18},{3,19},{4,20},{5,21},{6,22},{7,23},{8,24},{9,... | collective-permute-start | bytes 58376 | tf_op jit(solution)/shard_map/ppermute | solution.py:517

commit v7 on v6

--- a/solution.py
+++ b/solution.py
@@ -119,7 +119,7 @@
 
 
 def upward_kernel(
-    points_ref, dens_ref, surface_ref, counts_ref, up_ref, shift_ref, pack_ref, feature_ref, turned_ref,
+    level_count, points_ref, dens_ref, surface_ref, counts_ref, count_line_ref, up_ref, shift_ref, pack_ref, feature_ref, turned_ref,
     message_ref, send_ref, slab_ref, check_ref
 ):
     leaf_count, q_width, p_width = dens_ref.shape
@@ -170,17 +170,24 @@
     for child in range(8):
         slab_eq = slab_eq + dot3(node_eq[child * q_width : (child + 1) * q_width], shift_ref[child])
     index = lax.axis_index("oct")
-    slab = dot3(slab_eq, shift_ref[index & 7])
-    slab_ref[...] = slab
-    high, rest = halves(slab)
-    low = (slab - high.astype(F32) - rest.astype(F32)).astype(BF16)
-    for place, part in enumerate((high, rest, low)):
-        start = node_count * q_width + place * q_width
-        send_ref[start : start + q_width, :] = part
+    slab = slab_eq
+    start = node_count * q_width
+    for level in range(level_count):
+        slab = dot3(slab, shift_ref[jnp.right_shift(index, 3 * level) & 7])
+        slab_ref[level * q_width : (level + 1) * q_width, :] = slab
+        high, rest = halves(slab)
+        low = (slab - high.astype(F32) - rest.astype(F32)).astype(BF16)
+        for place, part in enumerate((high, rest, low)):
+            first = start + (place * level_count + level) * q_width
+            send_ref[first : first + q_width, :] = part
+    line = jnp.concatenate([count_line_ref[...].astype(F32), jnp.zeros((1, eq_width - leaf_count), F32)], axis=1)
+    start = start + 3 * level_count * q_width
+    send_ref[start : start + 16, :] = jnp.broadcast_to(line, (16, eq_width)).astype(BF16)
 
 
 def far_kernel(
-    lower_ref, own_ref, upper_ref, vlist_ref, table_hbm, out_ref, table_ref, tail_ref, wide_ref, total_ref, first_ref, sems
+    lower_ref, own_ref, upper_ref, vlist_ref, ulist_ref, table_hbm, out_ref, plan_ref, item_ref, table_ref, tail_ref,
+    wide_ref, total_ref, first_ref, sems
 ):
     node_count, type_count = vlist_ref.shape
     eq_width = own_ref.shape[1]
@@ -225,6 +232,11 @@
     lane_node = iota((SOURCES, 128), 1) // q_width
     nothing = jnp.zeros((SOURCES, 128), F32)
     total_ref[...] = jnp.zeros_like(total_ref)
+
+    leaf_count = ulist_ref.shape[1]
+    start = own_ref.shape[0] - 16
+    lines = [ref[start:, :].astype(F32)[:1, :leaf_count] for ref in (lower_ref, own_ref, upper_ref)]
+    plan_of(ulist_ref, lines, plan_ref, item_ref)
 
     def table_of(number):
         span = pl.ds(pl.multiple_of(number * chunk_rows, chunk_rows), chunk_rows)
@@ -276,26 +288,35 @@
 
 
 def near_kernel(
-    plan_ref, item_ref, own_hbm, side_hbm, own_feature_hbm, side_feature_hbm, out_ref, pack_ref, feature_ref,
-    value_ref, total_ref, sems
+    plan_ref, item_ref, own_hbm, own_feature_hbm, lower_ref, upper_ref, out_ref, pack_ref, feature_ref, value_ref,
+    total_ref, sems
 ):
     leaf_count, q_width, p_width = out_ref.shape
-    own_rows, side_rows = own_hbm.shape[0], side_hbm.shape[0]
-    own_lines, side_lines = own_feature_hbm.shape[1], side_feature_hbm.shape[1]
-    copies = [
-        (own_hbm, pack_ref.at[pl.ds(0, own_rows)]),
-        (side_hbm, pack_ref.at[pl.ds(own_rows, side_rows)]),
-        (own_feature_hbm, feature_ref.at[:, pl.ds(0, own_lines)]),
-        (side_feature_hbm, feature_ref.at[:, pl.ds(own_lines, side_lines)]),
-    ]
-    copies = [pltpu.make_async_copy(source, target, sems.at[n]) for n, (source, target) in enumerate(copies)]
-    for copy in copies:
-        copy.start()
-    pack_ref[own_rows + side_rows :, :] = jnp.zeros((PIECE, 128), BF16)
-    feature_ref[:, own_lines + side_lines :, :] = jnp.zeros((2, 32, 128), BF16)
+    own_rows, own_lines = own_hbm.shape[0], own_feature_hbm.shape[1]
+    own_copy = pltpu.make_async_copy(own_hbm, pack_ref.at[pl.ds(0, own_rows)], sems.at[0])
+    feature_copy = pltpu.make_async_copy(own_feature_hbm, feature_ref.at[:, pl.ds(0, own_lines)], sems.at[1])
+    own_copy.start()
+    feature_copy.start()
+    pack_ref[3 * own_rows :, :] = jnp.zeros((PIECE, 128), BF16)
+    feature_ref[:, 3 * own_lines :, :] = jnp.zeros((2, 32, 128), BF16)
     total_ref[...] = jnp.zeros_like(total_ref)
-    for copy in copies:
-        copy.wait()
+    blank = jnp.zeros((32, p_width), F32)
+
+    def pack_step(step, carry):
+        chosen = [(step * 4 + part, side) for part in range(4) for side in range(2)]
+        sources = (lower_ref, upper_ref)
+        weights = [weight_rows(sources[side][leaf, :q_width, :]) for leaf, side in chosen]
+        versions = [feature_versions(right_rows(pieces(sources[side][leaf, q_width:, :]))) for leaf, side in chosen]
+        packs = [jnp.concatenate([blank] + value + [blank], axis=0).astype(BF16).T for value in weights]
+        for (leaf, side), pack, version in zip(chosen, packs, versions):
+            place = (1 + side) * leaf_count + leaf
+            pack_ref[pl.ds(pl.multiple_of(place * p_width, p_width), p_width), :] = pack
+            put_features(feature_ref, place, version)
+        return carry
+
+    lax.fori_loop(0, leaf_count // 4, pack_step, 0)
+    own_copy.wait()
+    feature_copy.wait()
     step_lanes = 128 // UNROLL
     shift = step_lanes.bit_length() - 1
 
@@ -335,7 +356,11 @@
                 for part in range(UNROLL)
             ]
             exponents = [dot(target, feature) for target, feature in zip(targets, features)]
-            products = [dot(value, source) for value, source in zip(values, sources)]
+            products = []
+            for part in range(0, UNROLL, 2):
+                left = jnp.concatenate(values[part : part + 2], axis=0)
+                both = dot(left, jnp.concatenate(sources[part : part + 2], axis=1))
+                products += [both[:rows, :128], both[rows:, 128:]]
             following = [jnp.exp2(value).astype(BF16) for value in exponents]
             for part, value in enumerate(following):
                 for side in range(2):
@@ -433,39 +458,6 @@
     plan_ref[PLAN_COUNT : PLAN_COUNT + 1, :leaf_count] = counts[1].astype(jnp.int32)
 
 
-def pack_kernel(
-    lower_ref, upper_ref, ulist_ref, own_counts_ref, sum_ref, pair_ref, shift_ref, pack_ref, feature_ref, plan_ref,
-    item_ref, top_ref, next_ref
-):
-    leaf_count, rows, p_width = lower_ref.shape
-    q_width = rows - 8
-    index = lax.axis_index("oct")
-    top = sum_ref[...] + pair_ref[...]
-    top_ref[...] = top
-    next_ref[...] = dot3(top, shift_ref[jnp.right_shift(index, 3) & 7])
-    lane = iota((1, leaf_count), 1)
-    blank = jnp.zeros((32, p_width), F32)
-
-    def pack_step(step, counts):
-        side_counts = list(counts)
-        chosen = [(step * 4 + part, side) for part in range(4) for side in range(2)]
-        sources = (lower_ref, upper_ref)
-        tails = [sources[side][leaf, q_width:, :] for leaf, side in chosen]
-        weights = [weight_rows(sources[side][leaf, :q_width, :]) for leaf, side in chosen]
-        packs = [jnp.concatenate([blank] + value + [blank], axis=0).astype(BF16).T for value in weights]
-        versions = [feature_versions(right_rows(pieces(tail))) for tail in tails]
-        for (leaf, side), tail, pack, version in zip(chosen, tails, packs, versions):
-            place = side * leaf_count + leaf
-            pack_ref[pl.ds(pl.multiple_of(place * p_width, p_width), p_width), :] = pack
-            put_features(feature_ref, place, version)
-            side_counts[side] = jnp.where(lane == leaf, tail[3:4, :leaf_count], side_counts[side])
-        return tuple(side_counts)
-
-    nothing = jnp.zeros((1, leaf_count), F32)
-    lower_counts, upper_counts = lax.fori_loop(0, leaf_count // 4, pack_step, (nothing, nothing))
-    plan_of(ulist_ref, (lower_counts, own_counts_ref[...].astype(F32), upper_counts), plan_ref, item_ref)
-
-
 def final_kernel(
     level_count, counts_ref, feature_ref, turned_ref, near_ref, far_ref, coarse_ref, shift_ref, down_ref, *rest
 ):
@@ -476,7 +468,7 @@
     index = lax.axis_index("oct")
     slab_local = jnp.zeros((q_width, eq_width), F32)
     for level, top_ref in enumerate(top_refs):
-        slab_local = slab_local + dot3(top_ref[...], coarse_ref[jnp.right_shift(index, 3 * level) & 7])
+        slab_local = slab_local + dot3(top_ref[:q_width, :], coarse_ref[jnp.right_shift(index, 3 * level) & 7])
     for node in range(node_count):
         rows = slice(node * q_width, (node + 1) * q_width)
         node_ref[rows, :] = far_ref[rows, :] + dot3(slab_local, shift_ref[node])
@@ -497,10 +489,11 @@
         nears = [near_ref[leaf] for leaf in leaves]
         exponents = [dot(left, right) for left, right in zip(turned, features)]
         values = [halves(jnp.exp2(value)) for value in exponents]
-        firsts = [dot(jnp.concatenate(down, axis=0).astype(BF16), value[0]) for down, value in zip(downs, values)]
-        seconds = [dot(down[0].astype(BF16), value[1]) for down, value in zip(downs, values)]
+        lefts = [jnp.concatenate(down, axis=0).astype(BF16) for down in downs]
+        products = [dot(left, jnp.concatenate(value, axis=1)) for left, value in zip(lefts, values)]
         for child, leaf in enumerate(leaves):
-            far = firsts[child][:q_width] + firsts[child][q_width:] + seconds[child]
+            product = products[child]
+            far = product[:q_width, :p_width] + product[q_width:, :p_width] + product[:q_width, p_width:]
             out_ref[leaf] = jnp.where(lane < counts_ref[leaf], far + nears[child], 0.0)
         return carry
 
@@ -537,6 +530,8 @@
     node_rows = node_count * q_width
     size = lax.axis_size("oct")
     bits = size.bit_length() - 1
+    level_count = -(-bits // 3)
+    level_rows = level_count * q_width
     index = lax.axis_index("oct")
     vmem = pl.BlockSpec(memory_space=pltpu.VMEM)
     smem = pl.BlockSpec(memory_space=pltpu.SMEM)
@@ -548,37 +543,47 @@
     table = jnp.transpose(translate, (1, 2, 0))
 
     pack, features, turned, message, send, slab = pl.pallas_call(
-        upward_kernel,
+        lambda *refs: upward_kernel(level_count, *refs),
         out_shape=(
             jax.ShapeDtypeStruct((leaf_count * p_width, 128), BF16),
             jax.ShapeDtypeStruct((2, leaf_count * 64, p_width), BF16),
             jax.ShapeDtypeStruct((leaf_count, eq_width, 32), BF16),
             jax.ShapeDtypeStruct((leaf_count, q_width + 8, p_width), F32),
-            jax.ShapeDtypeStruct((node_rows + 3 * q_width, eq_width), BF16),
-            jax.ShapeDtypeStruct((q_width, eq_width), F32),
+            jax.ShapeDtypeStruct((node_rows + 3 * level_count * q_width + 16, eq_width), BF16),
+            jax.ShapeDtypeStruct((level_count * q_width, eq_width), F32),
         ),
-        in_specs=[vmem, vmem, vmem, smem, vmem, vmem],
+        in_specs=[vmem, vmem, vmem, smem, vmem, vmem, vmem],
         out_specs=(vmem,) * 6,
         scratch_shapes=[pltpu.VMEM((8, node_rows, eq_width), F32)],
         compiler_params=params,
         name="upward",
-    )(points, dens, surface, counts, up_inverse, shift_up)
+    )(points, dens, surface, counts, counts.reshape(1, leaf_count), up_inverse, shift_up)
 
     send_lower, send_upper = shifted(send, size)
-    partner = jnp.where(index & 1 == 1, send_lower[node_rows:], send_upper[node_rows:]).astype(F32)
-    total = slab + (partner[:q_width] + partner[q_width : 2 * q_width] + partner[2 * q_width :])
+    ends = slice(node_rows, node_rows + 3 * level_rows)
+    partner = jnp.where(index & 1 == 1, send_lower[ends], send_upper[ends]).astype(F32)
+    total = slab + (partner[:level_rows] + partner[level_rows : 2 * level_rows] + partner[2 * level_rows :])
     message, total = lax.optimization_barrier((message, total))
     lower, upper = shifted(message, size)
-    total = total + swapped(total, size, 1)
-    pair = swapped(total, size, 2)
-    send_lower, total = lax.optimization_barrier((send_lower, total))
+    tops = []
+    for level in range(level_count):
+        if level:
+            tops.append(total)
+            total = total[q_width:]
+        for bit in range(max(1, 3 * level), min(3 * level + 3, bits)):
+            total = total + swapped(total, size, bit)
+    tops.append(total)
 
     table = table.reshape(eq_width * eq_width, type_count)
-    far_node = pl.pallas_call(
+    far_node, plan, items = pl.pallas_call(
         far_kernel,
-        out_shape=jax.ShapeDtypeStruct((node_rows, eq_width), F32),
-        in_specs=[vmem, vmem, vmem, vmem, hbm],
-        out_specs=vmem,
+        out_shape=(
+            jax.ShapeDtypeStruct((node_rows, eq_width), F32),
+            jax.ShapeDtypeStruct((64, 128), jnp.int32),
+            jax.ShapeDtypeStruct((16, 128), jnp.int32),
+        ),
+        in_specs=[vmem, vmem, vmem, vmem, vmem, hbm],
+        out_specs=(vmem,) * 3,
         scratch_shapes=[
             pltpu.VMEM((type_count // 128, eq_width * eq_width, 128), BF16),
             pltpu.VMEM((eq_width * eq_width, type_count % 128), BF16),
@@ -590,49 +595,25 @@
         compiler_params=params,
         cost_estimate=pl.CostEstimate(flops=2 * 10**10, bytes_accessed=18 * 10**6, transcendentals=0),
         name="far",
-    )(send_lower, send, send_upper, vlist, table)
+    )(send_lower, send, send_upper, vlist, ulist, table)
     far_node, lower, upper = lax.optimization_barrier((far_node, lower, upper))
-
-    side_pack, side_features, plan, items, top, current = pl.pallas_call(
-        pack_kernel,
-        out_shape=(
-            jax.ShapeDtypeStruct((2 * leaf_count * p_width, 128), BF16),
-            jax.ShapeDtypeStruct((2, 2 * leaf_count * 64, p_width), BF16),
-            jax.ShapeDtypeStruct((64, 128), jnp.int32),
-            jax.ShapeDtypeStruct((16, 128), jnp.int32),
-            jax.ShapeDtypeStruct((q_width, eq_width), F32),
-            jax.ShapeDtypeStruct((q_width, eq_width), F32),
-        ),
-        in_specs=[vmem] * 7,
-        out_specs=(vmem,) * 6,
-        compiler_params=params,
-        name="pack",
-    )(lower, upper, ulist, counts.reshape(1, leaf_count), total, pair, shift_up)
-
-    tops = [top]
-    for level in range(3, bits, 3):
-        if level > 3:
-            current = jnp.dot(current, shift_up[jnp.right_shift(index, level) & 7], precision=HIGHEST)
-        for bit in range(level, min(level + 3, bits)):
-            current = current + swapped(current, size, bit)
-        tops.append(current)
 
     near = pl.pallas_call(
         near_kernel,
         out_shape=jax.ShapeDtypeStruct((leaf_count, q_width, p_width), F32),
-        in_specs=[smem, smem, hbm, hbm, hbm, hbm],
+        in_specs=[smem, smem, hbm, hbm, vmem, vmem],
         out_specs=vmem,
         scratch_shapes=[
             pltpu.VMEM((3 * leaf_count * p_width + PIECE, 128), BF16),
             pltpu.VMEM((2, 3 * leaf_count * 64 + 32, 128), BF16),
             pltpu.VMEM((2 * UNROLL, 2, p_width, 128), BF16),
             pltpu.VMEM((leaf_count + 1, p_width, 128), F32),
-            pltpu.SemaphoreType.DMA((4,)),
+            pltpu.SemaphoreType.DMA((2,)),
         ],
         compiler_params=params,
         cost_estimate=pl.CostEstimate(flops=3 * 10**10, bytes_accessed=10**7, transcendentals=0),
         name="near",
-    )(plan, items, pack, side_pack, features, side_features)
+    )(plan, items, pack, features, lower, upper)
 
     return pl.pallas_call(
         lambda *refs: final_kernel(len(tops), *refs),

time: 134 us -> 135 us (level)
  the two profiles are of different devices: /device:TPU:4 before, /device:TPU:1 now
where the time goes in v7:
time: 135 us; the launch traced here: 134 us
  Pallas kernels  98.2 us (73%)
  starting transfers between devices  20.3 us (15%)
  waiting for transfers between devices  13 us (10%)
  other arithmetic  1.61 us (1%)
    pallas_call x1, Pallas kernels, local(): pl.pallas_call(near_kernel, out_shape=jax.ShapeDtypeStruct((leaf_count, q...  55.4 us
    pallas_call x1, Pallas kernels, local(): pl.pallas_call(far_kernel, out_shape=(jax.ShapeDtypeStruct((node_rows, eq...  22.1 us
    ppermute x4, starting transfers between devices, shifted(): return (lax.ppermute(value, 'oct', up), lax.ppermute(value, 'oct', down))  11.8 us
    pallas_call x1, Pallas kernels, local(): pl.pallas_call(lambda *refs: upward_kernel(level_count, *refs), out_shape...  10.4 us
    pallas_call x1, Pallas kernels, local(): pl.pallas_call(lambda *refs: final_kernel(len(tops), *refs), out_shape=ja...  10.4 us
    ppermute x4, waiting for transfers between devices, shifted(): return (lax.ppermute(value, 'oct', up), lax.ppermute(value, 'oct', down))  9.49 us
    ppermute x4, starting transfers between devices, swapped(): lax.ppermute(value, 'oct', [(source, source ^ 1 << bit) for source in ran...  8.49 us
    ppermute x4, waiting for transfers between devices, swapped(): lax.ppermute(value, 'oct', [(source, source ^ 1 << bit) for source in ran...  3.54 us
  transfers between devices with their start and end apart: 8, of which 6 were waited for; matrix products, arithmetic and copies ran while one was open for 0% of the time, Pallas kernels for 16%

profile of v7, /device:TPU:1, one launch (start us, length us, event | category | flops | bytes accessed | tf_op | source)
XLA Modules:
  0.0 134.3 jit_solution(8647423233635427457)
XLA Ops:
  0.0 10.4 %upward.1 = (bf16[8192,128]{1,0:T(8,128)(2,1)}, bf16[2,4096,128]{2,1,0:T(8,128)(2,1)}, bf16[64,152,32]{2,1,0:T(8,128)(2,1)}, f32[64,40,128]{2,1,0:T(8,128)}, bf1...) custom-call(f32[3,64,128]{2,1,0:T(8,128)} %bitcast.8, f32[64,32,128]{2,1,0:T(8,128)} %refs_1_.1, f32[3,64,152]{2,1,0:T(8,128)} %bitcast.7, ...), custom_call_target="tpu_custom_call" | custom-call | tf_op jit(solution)/shard_map/upward/pallas_call | solution.py:545
  10.4 4.5 %collective-permute-start = (bf16[464,152]{1,0:T(8,128)(2,1)}, bf16[464,152]{1,0:T(8,128)(2,1)S(1)}, u32[]{:S(2)}, u32[]{:S(2)}) collective-permute-start(bf16[464,152]{1,0:T(8,128)(2,1)} %get-tuple-element.21.own_ref), channel_id=1, source_target_pairs={{0,1},{1,2},{2,3},{3,4},{4,5},{5,6},{6,7},{7,8},{8,9},{9,10},{10,1... | collective-permute-start | bytes 423176 | tf_op jit(solution)/shard_map/ppermute | solution.py:506
  14.9 1.9 %collective-permute-start.1 = (bf16[464,152]{1,0:T(8,128)(2,1)}, bf16[464,152]{1,0:T(8,128)(2,1)S(1)}, u32[]{:S(2)}, u32[]{:S(2)}) collective-permute-start(bf16[464,152]{1,0:T(8,128)(2,1)} %get-tuple-element.21.own_ref), channel_id=1, source_target_pairs={{1,0},{2,1},{3,2},{4,3},{5,4},{6,5},{7,6},{8,7},{9,8},{10,9},{11,1... | collective-permute-start | bytes 423176 | tf_op jit(solution)/shard_map/ppermute | solution.py:506
  16.8 1.4 %collective-permute-done.lower_ref = bf16[464,152]{1,0:T(8,128)(2,1)S(1)} collective-permute-done((bf16[464,152]{1,0:T(8,128)(2,1)}, bf16[464,152]{1,0:T(8,128)(2,1)S(1)}, u32[]{:S(2)}, u32[]{:S(2)}) %collective-permute-start) | collective-permute-done | bytes 141088 | tf_op jit(solution)/shard_map/ppermute | solution.py:506
  18.2 0.0 copy-start.1
  18.2 4.3 %collective-permute-done.1.upper_ref = bf16[464,152]{1,0:T(8,128)(2,1)S(1)} collective-permute-done((bf16[464,152]{1,0:T(8,128)(2,1)}, bf16[464,152]{1,0:T(8,128)(2,1)S(1)}, u32[]{:S(2)}, u32[]{:S(2)}) %collective-permute-start.1) | collective-permute-done | bytes 141088 | tf_op jit(solution)/shard_map/ppermute | solution.py:506
  22.5 0.0 copy-start.2
  22.6 0.9 fusion.1
  23.5 2.2 %collective-permute-start.4 = (f32[64,152]{1,0:T(8,128)S(1)}, f32[64,152]{1,0:T(8,128)S(1)}, u32[]{:S(2)}, u32[]{:S(2)}) collective-permute-start(f32[64,152]{1,0:T(8,128)S(1)} %fusion.1), channel_id=1, source_target_pairs={{0,2},{1,3},{2,0},{3,1},{4,6},{5,7},{6,4},{7,5},{8,10},{9,11},{10,... | collective-permute-start | bytes 116744 | tf_op jit(solution)/shard_map/ppermute | solution.py:510
  25.7 1.7 %collective-permute-done.4 = f32[64,152]{1,0:T(8,128)S(1)} collective-permute-done((f32[64,152]{1,0:T(8,128)S(1)}, f32[64,152]{1,0:T(8,128)S(1)}, u32[]{:S(2)}, u32[]{:S(2)}) %collective-permute-start.4) | collective-permute-done | bytes 38944 | tf_op jit(solution)/shard_map/ppermute | solution.py:510
  27.3 2.2 %collective-permute-start.5 = (f32[64,152]{1,0:T(8,128)S(1)}, f32[64,152]{1,0:T(8,128)S(1)}, u32[]{:S(2)}, u32[]{:S(2)}) collective-permute-start(f32[64,152]{1,0:T(8,128)S(1)} %add.24), channel_id=1, source_target_pairs={{0,4},{1,5},{2,6},{3,7},{4,0},{5,1},{6,2},{7,3},{8,12},{9,13},{10,... | collective-permute-start | bytes 116744 | tf_op jit(solution)/shard_map/ppermute | solution.py:510
  29.5 1.9 %collective-permute-done.5 = f32[64,152]{1,0:T(8,128)S(1)} collective-permute-done((f32[64,152]{1,0:T(8,128)S(1)}, f32[64,152]{1,0:T(8,128)S(1)}, u32[]{:S(2)}, u32[]{:S(2)}) %collective-permute-start.5) | collective-permute-done | bytes 38944 | tf_op jit(solution)/shard_map/ppermute | solution.py:510
  31.4 0.0 copy-start
  31.5 1.2 collective-permute-start.6
  32.7 3.3 %collective-permute-start.2 = (f32[64,40,128]{2,1,0:T(8,128)}, f32[64,40,128]{2,1,0:T(8,128)S(1)}, u32[]{:S(2)}, u32[]{:S(2)}) collective-permute-start(f32[64,40,128]{2,1,0:T(8,128)} %get-tuple-element.28), channel_id=1, source_target_pairs={{0,1},{1,2},{2,3},{3,4},{4,5},{5,6},{6,7},{7,8},{8,9},{9,10},{10,1... | collective-permute-start | bytes 3932168 | tf_op jit(solution)/shard_map/ppermute | solution.py:506
  36.0 2.0 %collective-permute-start.3 = (f32[64,40,128]{2,1,0:T(8,128)}, f32[64,40,128]{2,1,0:T(8,128)S(1)}, u32[]{:S(2)}, u32[]{:S(2)}) collective-permute-start(f32[64,40,128]{2,1,0:T(8,128)} %get-tuple-element.28), channel_id=1, source_target_pairs={{1,0},{2,1},{3,2},{4,3},{5,4},{6,5},{7,6},{8,7},{9,8},{10,9},{11,1... | collective-permute-start | bytes 3932168 | tf_op jit(solution)/shard_map/ppermute | solution.py:506
  38.0 0.0 collective-permute-done.6
  38.0 2.9 %collective-permute-start.7 = (f32[32,152]{1,0:T(8,128)S(1)}, f32[32,152]{1,0:T(8,128)S(1)}, u32[]{:S(2)}, u32[]{:S(2)}) collective-permute-start(f32[32,152]{1,0:T(8,128)S(1)} %slice_add_fusion.2), channel_id=1, source_target_pairs={{0,16},{1,17},{2,18},{3,19},{4,20},{5,21},{6,22},{7,23},{8,24},{9,... | collective-permute-start | bytes 58376 | tf_op jit(solution)/shard_map/ppermute | solution.py:510
  41.0 0.0 copy-done.1
  41.0 0.0 copy-done.2
  41.0 22.1 %far.1 = (f32[256,152]{1,0:T(8,128)}, s32[64,128]{1,0:T(8,128)}, s32[16,128]{1,0:T(8,128)}) custom-call(bf16[464,152]{1,0:T(8,128)(2,1)} %copy-done.1, bf16[464,152]{1,0:T(8,128)(2,1)} %get-tuple-element.21.own_ref, bf16[464,152]{1,0:T(8,128)(2,1)} %copy-done.2, s32[8,316]{1,0:T(8,128)} %vlist_ref.1, s32[27,64]{1,0:T(8,128)} %bitcast.11, ...), custom_call_target="tpu_custom_call" | custom-call | flops 20000000000 | bytes 18000000 | tf_op jit(solution)/shard_map/far/pallas_call | solution.py:578
  63.1 0.0 copy-done
  63.1 0.0 collective-permute-done.7
  63.1 0.6 add.27.refs_9_
  63.8 1.1 collective-permute-done.2.lower_ref
  64.9 0.0 copy-start.3
  64.9 2.6 %collective-permute-done.3.upper_ref = f32[64,40,128]{2,1,0:T(8,128)S(1)} collective-permute-done((f32[64,40,128]{2,1,0:T(8,128)}, f32[64,40,128]{2,1,0:T(8,128)S(1)}, u32[]{:S(2)}, u32[]{:S(2)}) %collective-permute-start.3) | collective-permute-done | bytes 1310752 | tf_op jit(solution)/shard_map/ppermute | solution.py:506
  67.5 0.0 copy-start.4
  67.5 0.0 copy-done.3
  67.5 1.1 copy-done.4
  68.6 55.4 %near.1.refs_3_ = f32[64,32,128]{2,1,0:T(8,128)} custom-call(s32[64,128]{1,0:T(8,128)} %get-tuple-element.22.plan_ref, s32[16,128]{1,0:T(8,128)} %get-tuple-element.23.item_ref, bf16[8192,128]{1,0:T(8,128)(2,1)} %get-tuple-element.24.own_hbm, bf16[2,4096,128]{2,1,0:T(8,128)(2,1)} %get-tuple-element.19.own_feature_hbm.refs_1_, f32[64,40,128]{2,1,0:T(8,128)} %copy-done.3, ...), custom_call_target="tpu_custom_call" | custom-call | flops 30000001024 | bytes 10000000 | tf_op jit(solution)/shard_map/near/pallas_call | solution.py:601
  124.0 10.4 %final.1 = f32[64,32,128]{2,1,0:T(8,128)} custom-call(s32[64]{0:T(128)} %refs_0_.1, bf16[2,4096,128]{2,1,0:T(8,128)(2,1)} %get-tuple-element.19.own_feature_hbm.refs_1_, bf16[64,152,32]{2,1,0:T(8,128)(2,1)} %get-tuple-element.20.refs_2_, f32[64,32,128]{2,1,0:T(8,128)} %near.1.refs_3_, f32[256,152]{1,0:T(8,128)} %get-tuple-element.31.refs_4_, ...), custom_call_target="tpu_custom_call" | custom-call | tf_op jit(solution)/shard_map/final/pallas_call | solution.py:618
  (5 shorter events, 0.0 us)
Async XLA Ops:
  10.4 7.9 %collective-permute-start = (bf16[464,152]{1,0:T(8,128)(2,1)}, bf16[464,152]{1,0:T(8,128)(2,1)S(1)}, u32[]{:S(2)}, u32[]{:S(2)}) collective-permute-start(bf16[464,152]{1,0:T(8,128)(2,1)} %get-tuple-element.21.own_ref), channel_id=1, source_target_pairs={{0,1},{1,2},{2,3},{3,4},{4,5},{5,6},{6,7},{7,8},{8,9},{9,10},{10,1... | collective-permute-start | bytes 423176 | tf_op jit(solution)/shard_map/ppermute | solution.py:506
  14.9 7.6 %collective-permute-start.1 = (bf16[464,152]{1,0:T(8,128)(2,1)}, bf16[464,152]{1,0:T(8,128)(2,1)S(1)}, u32[]{:S(2)}, u32[]{:S(2)}) collective-permute-start(bf16[464,152]{1,0:T(8,128)(2,1)} %get-tuple-element.21.own_ref), channel_id=1, source_target_pairs={{1,0},{2,1},{3,2},{4,3},{5,4},{6,5},{7,6},{8,7},{9,8},{10,9},{11,1... | collective-permute-start | bytes 423176 | tf_op jit(solution)/shard_map/ppermute | solution.py:506
  18.2 22.7 %copy-start.1 = (bf16[464,152]{1,0:T(8,128)(2,1)}, bf16[464,152]{1,0:T(8,128)(2,1)S(1)}, u32[]{:S(2)}) copy-start(bf16[464,152]{1,0:T(8,128)(2,1)S(1)} %collective-permute-done.lower_ref) | copy-start | bytes 423172
  22.5 18.4 %copy-start.2 = (bf16[464,152]{1,0:T(8,128)(2,1)}, bf16[464,152]{1,0:T(8,128)(2,1)S(1)}, u32[]{:S(2)}) copy-start(bf16[464,152]{1,0:T(8,128)(2,1)S(1)} %collective-permute-done.1.upper_ref) | copy-start | bytes 423172
  23.5 3.8 %collective-permute-start.4 = (f32[64,152]{1,0:T(8,128)S(1)}, f32[64,152]{1,0:T(8,128)S(1)}, u32[]{:S(2)}, u32[]{:S(2)}) collective-permute-start(f32[64,152]{1,0:T(8,128)S(1)} %fusion.1), channel_id=1, source_target_pairs={{0,2},{1,3},{2,0},{3,1},{4,6},{5,7},{6,4},{7,5},{8,10},{9,11},{10,... | collective-permute-start | bytes 116744 | tf_op jit(solution)/shard_map/ppermute | solution.py:510
  27.3 4.1 %collective-permute-start.5 = (f32[64,152]{1,0:T(8,128)S(1)}, f32[64,152]{1,0:T(8,128)S(1)}, u32[]{:S(2)}, u32[]{:S(2)}) collective-permute-start(f32[64,152]{1,0:T(8,128)S(1)} %add.24), channel_id=1, source_target_pairs={{0,4},{1,5},{2,6},{3,7},{4,0},{5,1},{6,2},{7,3},{8,12},{9,13},{10,... | collective-permute-start | bytes 116744 | tf_op jit(solution)/shard_map/ppermute | solution.py:510
  31.4 31.7 %copy-start = (f32[64,152]{1,0:T(8,128)}, f32[64,152]{1,0:T(8,128)S(1)}, u32[]{:S(2)}) copy-start(f32[64,152]{1,0:T(8,128)S(1)} %add.25.refs_8_) | copy-start | bytes 116740
  31.5 6.6 %collective-permute-start.6 = (f32[32,152]{1,0:T(8,128)S(1)}, f32[32,152]{1,0:T(8,128)S(1)}, u32[]{:S(2)}, u32[]{:S(2)}) collective-permute-start(f32[32,152]{1,0:T(8,128)S(1)} %slice.29), channel_id=1, source_target_pairs={{0,8},{1,9},{2,10},{3,11},{4,12},{5,13},{6,14},{7,15},{8,0},{9,1},... | collective-permute-start | bytes 58376 | tf_op jit(solution)/shard_map/ppermute | solution.py:510
  32.7 32.2 %collective-permute-start.2 = (f32[64,40,128]{2,1,0:T(8,128)}, f32[64,40,128]{2,1,0:T(8,128)S(1)}, u32[]{:S(2)}, u32[]{:S(2)}) collective-permute-start(f32[64,40,128]{2,1,0:T(8,128)} %get-tuple-element.28), channel_id=1, source_target_pairs={{0,1},{1,2},{2,3},{3,4},{4,5},{5,6},{6,7},{7,8},{8,9},{9,10},{10,1... | collective-permute-start | bytes 3932168 | tf_op jit(solution)/shard_map/ppermute | solution.py:506
  36.0 31.5 %collective-permute-start.3 = (f32[64,40,128]{2,1,0:T(8,128)}, f32[64,40,128]{2,1,0:T(8,128)S(1)}, u32[]{:S(2)}, u32[]{:S(2)}) collective-permute-start(f32[64,40,128]{2,1,0:T(8,128)} %get-tuple-element.28), channel_id=1, source_target_pairs={{1,0},{2,1},{3,2},{4,3},{5,4},{6,5},{7,6},{8,7},{9,8},{10,9},{11,1... | collective-permute-start | bytes 3932168 | tf_op jit(solution)/shard_map/ppermute | solution.py:506
  38.0 25.1 %collective-permute-start.7 = (f32[32,152]{1,0:T(8,128)S(1)}, f32[32,152]{1,0:T(8,128)S(1)}, u32[]{:S(2)}, u32[]{:S(2)}) collective-permute-start(f32[32,152]{1,0:T(8,128)S(1)} %slice_add_fusion.2), channel_id=1, source_target_pairs={{0,16},{1,17},{2,18},{3,19},{4,20},{5,21},{6,22},{7,23},{8,24},{9,... | collective-permute-start | bytes 58376 | tf_op jit(solution)/shard_map/ppermute | solution.py:510
  64.9 2.6 %copy-start.3 = (f32[64,40,128]{2,1,0:T(8,128)}, f32[64,40,128]{2,1,0:T(8,128)S(1)}, u32[]{:S(2)}) copy-start(f32[64,40,128]{2,1,0:T(8,128)S(1)} %collective-permute-done.2.lower_ref) | copy-start | bytes 3932164
  67.5 1.1 copy-start.4

commit v8 on v7

--- a/solution.py
+++ b/solution.py
@@ -14,10 +14,11 @@
 NT = (((1,), (1,)), ((), ()))
 TN = (((0,), (0,)), ((), ()))
 BLOCK = 256
-UNROLL = 4
+UNROLL = 8
+TOTALS = 4
 PIECE = 64
 CLASS_ROWS = (32, 64, 96, 128)
-PLAN_PLACES, PLAN_CLASS, PLAN_ORDER, PLAN_COUNT = 56, 60, 61, 62
+PLACES = 56
 SOURCES = 32
 CHUNK = 4
 
@@ -114,8 +115,11 @@
 
 def put_features(feature_ref, leaf, versions):
     for half, place, value in versions:
-        span = pl.ds(pl.multiple_of((2 * leaf + half) * 32, 32), 32)
-        feature_ref[place, span, :] = value
+        feature_ref[place, 2 * leaf + half] = value
+
+
+def put_pack(pack_ref, leaf, value):
+    pack_ref[pl.ds(2 * leaf, 2)] = value.reshape(2, PIECE, 128)
 
 
 def upward_kernel(
@@ -148,13 +152,14 @@
         rows = [jnp.concatenate(split, axis=0).astype(BF16) for split in lists]
         firsts = [dot(row, value[0]) for row, value in zip(rows, values)]
         seconds = [dot(row[:q_width], value[1]) for row, value in zip(rows, values)]
-        turned = [value.astype(BF16).T for value in surfaces]
+        fours = [jnp.concatenate(surfaces[first : first + 4], axis=0).astype(BF16).T for first in range(0, 8, 4)]
         versions = [feature_versions(right) for right in rights]
+        for number, four in enumerate(fours):
+            turned_ref[2 * node + number] = four
         for child, leaf in enumerate(leaves):
             message_ref[leaf, :q_width, :] = weights[child]
             message_ref[leaf, q_width:, :] = jnp.where(row == 3, counts[child].astype(F32), coords[child])
-            pack_ref[pl.ds(pl.multiple_of(leaf * p_width, p_width), p_width), :] = packs[child]
-            turned_ref[leaf] = turned[child]
+            put_pack(pack_ref, leaf, packs[child])
             put_features(feature_ref, leaf, versions[child])
             check = firsts[child][:q_width] + firsts[child][q_width:] + seconds[child]
             check_ref[child, pl.ds(pl.multiple_of(node * q_width, q_width), q_width), :] = check
@@ -180,14 +185,14 @@
         for place, part in enumerate((high, rest, low)):
             first = start + (place * level_count + level) * q_width
             send_ref[first : first + q_width, :] = part
+    start = start + 3 * level_count * q_width
     line = jnp.concatenate([count_line_ref[...].astype(F32), jnp.zeros((1, eq_width - leaf_count), F32)], axis=1)
-    start = start + 3 * level_count * q_width
     send_ref[start : start + 16, :] = jnp.broadcast_to(line, (16, eq_width)).astype(BF16)
 
 
 def far_kernel(
-    lower_ref, own_ref, upper_ref, vlist_ref, ulist_ref, table_hbm, out_ref, plan_ref, item_ref, table_ref, tail_ref,
-    wide_ref, total_ref, first_ref, sems
+    lower_ref, own_ref, upper_ref, vlist_ref, ulist_ref, table_hbm, out_ref, step_ref, piece_ref, item_ref, table_ref,
+    tail_ref, wide_ref, total_ref, first_ref, sems
 ):
     node_count, type_count = vlist_ref.shape
     eq_width = own_ref.shape[1]
@@ -236,7 +241,7 @@
     leaf_count = ulist_ref.shape[1]
     start = own_ref.shape[0] - 16
     lines = [ref[start:, :].astype(F32)[:1, :leaf_count] for ref in (lower_ref, own_ref, upper_ref)]
-    plan_of(ulist_ref, lines, plan_ref, item_ref)
+    plan_of(ulist_ref, lines, step_ref, piece_ref, item_ref)
 
     def table_of(number):
         span = pl.ds(pl.multiple_of(number * chunk_rows, chunk_rows), chunk_rows)
@@ -288,18 +293,21 @@
 
 
 def near_kernel(
-    plan_ref, item_ref, own_hbm, own_feature_hbm, lower_ref, upper_ref, out_ref, pack_ref, feature_ref, value_ref,
-    total_ref, sems
+    step_ref, piece_ref, item_ref, own_hbm, own_feature_hbm, lower_ref, upper_ref, out_ref, pack_ref, feature_ref, value_ref,
+    *rest
 ):
+    total_refs, sems = rest[:TOTALS], rest[TOTALS]
     leaf_count, q_width, p_width = out_ref.shape
-    own_rows, own_lines = own_hbm.shape[0], own_feature_hbm.shape[1]
-    own_copy = pltpu.make_async_copy(own_hbm, pack_ref.at[pl.ds(0, own_rows)], sems.at[0])
-    feature_copy = pltpu.make_async_copy(own_feature_hbm, feature_ref.at[:, pl.ds(0, own_lines)], sems.at[1])
+    own = pl.ds(0, 2 * leaf_count)
+    own_copy = pltpu.make_async_copy(own_hbm, pack_ref.at[own], sems.at[0])
+    feature_copy = pltpu.make_async_copy(own_feature_hbm, feature_ref.at[:, own], sems.at[1])
     own_copy.start()
     feature_copy.start()
-    pack_ref[3 * own_rows :, :] = jnp.zeros((PIECE, 128), BF16)
-    feature_ref[:, 3 * own_lines :, :] = jnp.zeros((2, 32, 128), BF16)
-    total_ref[...] = jnp.zeros_like(total_ref)
+    pack_ref[6 * leaf_count] = jnp.zeros((PIECE, 128), BF16)
+    for half in range(2):
+        feature_ref[half, 6 * leaf_count] = jnp.zeros((32, 128), BF16)
+    for total_ref in total_refs:
+        total_ref[...] = jnp.zeros_like(total_ref)
     blank = jnp.zeros((32, p_width), F32)
 
     def pack_step(step, carry):
@@ -310,47 +318,46 @@
         packs = [jnp.concatenate([blank] + value + [blank], axis=0).astype(BF16).T for value in weights]
         for (leaf, side), pack, version in zip(chosen, packs, versions):
             place = (1 + side) * leaf_count + leaf
-            pack_ref[pl.ds(pl.multiple_of(place * p_width, p_width), p_width), :] = pack
+            put_pack(pack_ref, place, pack)
             put_features(feature_ref, place, version)
         return carry
 
     lax.fori_loop(0, leaf_count // 4, pack_step, 0)
     own_copy.wait()
     feature_copy.wait()
-    step_lanes = 128 // UNROLL
-    shift = step_lanes.bit_length() - 1
-
-    def item_of(step, part):
-        line = lax.shift_right_logical(step, shift)
-        lane = jnp.bitwise_and(step, step_lanes - 1) * UNROLL + part
-        return item_ref[line, lane], item_ref[8 + line, lane]
-
-    def sources_of(leaf, place):
-        rows = []
-        for number in range(BLOCK // PIECE):
-            start = pl.multiple_of(plan_ref[place + number, leaf] * 2, PIECE)
-            rows.append(pack_ref[pl.ds(start, PIECE), :])
-        return jnp.concatenate(rows, axis=0)
-
-    def features_of(leaf, place):
+    block_pieces = BLOCK // PIECE
+
+    def items_of(step):
+        first = step * UNROLL
+        leaves = [item_ref[first + part] for part in range(UNROLL)]
+        first = first * block_pieces
+        pieces_of = [
+            [piece_ref[first + part * block_pieces + number] for number in range(block_pieces)] for part in range(UNROLL)
+        ]
+        return list(zip(leaves, pieces_of))
+
+    def sources_of(numbers):
+        return jnp.concatenate([pack_ref[number] for number in numbers], axis=0)
+
+    def features_of(numbers):
         tiles = []
         for tile in range(BLOCK // 128):
-            starts = [pl.multiple_of(plan_ref[place + 2 * tile + half, leaf], 32) for half in range(2)]
-            halves_of = [feature_ref[half, pl.ds(start, 32), :] for half, start in enumerate(starts)]
-            tiles.append(halves_of[0] + halves_of[1])
+            tiles.append(feature_ref[0, numbers[2 * tile]] + feature_ref[1, numbers[2 * tile + 1]])
         return jnp.concatenate(tiles, axis=1)
+
+    def targets_of(leaf, rows):
+        first = 2 * jnp.minimum(leaf, leaf_count - 1)
+        if rows <= PIECE:
+            return pack_ref[first, :rows][:, :32]
+        return jnp.concatenate([pack_ref[first][:, :32], pack_ref[first + 1, : rows - PIECE][:, :32]], axis=0)
 
     def run(rows, first, count):
         def blocks_step(step, carry):
             slot = jnp.bitwise_and(step, 1) * UNROLL
-            done = [item_of(step - 1, part) for part in range(UNROLL)]
-            items = [item_of(step, part) for part in range(UNROLL)]
-            features = [features_of(leaf, place) for leaf, place in items]
-            targets = []
-            for leaf, _ in items:
-                start = pl.multiple_of(jnp.minimum(leaf, leaf_count - 1) * p_width, p_width)
-                targets.append(pack_ref[pl.ds(start, rows), :][:, :32])
-            sources = [sources_of(leaf, place) for leaf, place in done]
+            done, items = items_of(step - 1), items_of(step)
+            features = [features_of(numbers) for _, numbers in items]
+            targets = [targets_of(leaf, rows) for leaf, _ in items]
+            sources = [sources_of(numbers) for _, numbers in done]
             values = [
                 jnp.concatenate([value_ref[UNROLL - slot + part, side, :rows] for side in range(2)], axis=1)
                 for part in range(UNROLL)
@@ -365,17 +372,22 @@
             for part, value in enumerate(following):
                 for side in range(2):
                     value_ref[slot + part, side, :rows] = value[:, side * 128 : (side + 1) * 128]
-            for (leaf, _), product in zip(done, products):
-                total_ref[leaf, :rows] += product
+            for first in range(0, UNROLL, TOTALS):
+                sums = [
+                    total_refs[part][done[first + part][0], :rows] + products[first + part] for part in range(TOTALS)
+                ]
+                for part, value in enumerate(sums):
+                    total_refs[part][done[first + part][0], :rows] = value
             return carry
 
         lax.fori_loop(first, first + count, blocks_step, 0)
 
     for number, rows in enumerate(CLASS_ROWS):
-        run(rows, plan_ref[PLAN_CLASS, 2 * number], plan_ref[PLAN_CLASS, 2 * number + 1])
+        run(rows, step_ref[0, 2 * number], step_ref[0, 2 * number + 1])
 
     def turn_step(step, carry):
-        turned = [total_ref[step * 8 + part].T for part in range(8)]
+        sums = [[total_ref[step * 8 + part] for total_ref in total_refs] for part in range(8)]
+        turned = [(a + b + (c + d)).T for a, b, c, d in sums]
         for part, value in enumerate(turned):
             out_ref[step * 8 + part] = value[32 : 32 + q_width] + value[32 + q_width : 32 + 2 * q_width]
         return carry
@@ -389,7 +401,7 @@
     return jnp.broadcast_to(wide, (128, 128)).T[:width, :width]
 
 
-def plan_of(ulist_ref, counts, plan_ref, item_ref):
+def plan_of(ulist_ref, counts, step_ref, piece_ref, item_ref):
     slot_count, leaf_count = ulist_ref.shape
     index = lax.axis_index("oct")
     shape = (leaf_count, leaf_count)
@@ -402,10 +414,10 @@
     rank_wide = jnp.broadcast_to(rank, shape).astype(jnp.int32)
 
     block_pieces = BLOCK // PIECE
-    zero_row = 3 * leaf_count * 64
-    place_shape = (PLAN_PLACES, leaf_count)
+    empty = 6 * leaf_count
+    place_shape = (PLACES, leaf_count)
     place_row = iota(place_shape, 0)
-    listed = jnp.full(place_shape, zero_row, jnp.int32)
+    listed = jnp.full(place_shape, empty, jnp.int32)
     offset = jnp.zeros((1, leaf_count), jnp.int32)
     for slot in range(slot_count):
         side = 1 if slot == 0 else (0 if slot < 9 else (1 if slot < 18 else 2))
@@ -414,12 +426,10 @@
         found = jnp.sum(jnp.where(row == place, tables[side], 0.0), axis=0, keepdims=True).astype(jnp.int32)
         length = lax.shift_right_logical(found + (PIECE - 1), PIECE.bit_length() - 1)
         length = jnp.where(ids >= 0, length, 0)
-        start = (place + (1, 0, 2)[side] * leaf_count) * 64
+        start = (place + (1, 0, 2)[side] * leaf_count) * 2
         inside = (place_row >= offset) & (place_row < offset + length)
-        listed = jnp.where(inside, start + (place_row - offset) * 32, listed)
+        listed = jnp.where(inside, start + place_row - offset, listed)
         offset = offset + length
-    plan_ref[:PLAN_PLACES, :leaf_count] = listed
-    plan_ref[:PLAN_PLACES, leaf_count:] = jnp.full((PLAN_PLACES, 128 - leaf_count), zero_row, jnp.int32)
 
     blocks = lax.shift_right_logical(offset + (block_pieces - 1), block_pieces.bit_length() - 1)
     blocks_column = as_column(blocks.astype(F32))
@@ -438,24 +448,35 @@
         first = first + jnp.where(own_class == number, start * UNROLL, 0)
         steps_line = jnp.where(lane == 2 * number, start, jnp.where(lane == 2 * number + 1, steps, steps_line))
         start = start + steps
-    plan_ref[PLAN_CLASS : PLAN_CLASS + 1, :] = steps_line
-
-    first_column = as_column(first.astype(F32))
-    wide = (leaf_count, 128)
-    first_wide = jnp.concatenate([first_column] * (128 // leaf_count), axis=1).astype(jnp.int32)
-    blocks_wide = jnp.concatenate([blocks_column] * (128 // leaf_count), axis=1).astype(jnp.int32)
+    step_ref[...] = steps_line
+
+    first_column = as_column(first.astype(F32))[:, :1].astype(jnp.int32)
+    blocks_column = blocks_column[:, :1].astype(jnp.int32)
+    high = lax.shift_right_logical(listed, 8).astype(F32)
+    low = jnp.bitwise_and(listed, 255).astype(F32)
+    parts = jnp.concatenate([high, low], axis=0).astype(BF16)
+    chunk = 1024
+    wide = (leaf_count, chunk)
+    column = iota(wide, 1)
     leaf_row = iota(wide, 0).astype(F32)
+    for number in range(block_pieces):
+        entry = column + chunk * number
+        after = lax.shift_right_logical(entry, block_pieces.bit_length() - 1) - first_column
+        inside = (after >= 0) & (after < blocks_column)
+        place = after * block_pieces + jnp.bitwise_and(entry, block_pieces - 1)
+        place = jnp.sum(jnp.where(inside, place.astype(F32), 0.0), axis=0, keepdims=True).astype(jnp.int32)
+        found = jnp.sum(jnp.where(inside, 1.0, 0.0), axis=0, keepdims=True)
+        both = dot(parts, jnp.where(inside, 1.0, 0.0).astype(BF16))
+        value = both[:PLACES] * 256.0 + both[PLACES:]
+        value = jnp.sum(jnp.where(iota((PLACES, chunk), 0) == place, value, 0.0), axis=0, keepdims=True)
+        value = jnp.where(found > 0.0, value, float(empty)).astype(jnp.int32)
+        for line in range(8):
+            piece_ref[8 * number + line : 8 * number + line + 1, :] = value[:, line * 128 : (line + 1) * 128]
+    after = column - first_column
+    inside = (after >= 0) & (after < blocks_column)
+    leaf = jnp.sum(jnp.where(inside, leaf_row - leaf_count, 0.0), axis=0, keepdims=True).astype(jnp.int32) + leaf_count
     for line in range(8):
-        after = iota(wide, 1) + 128 * line - first_wide
-        inside = (after >= 0) & (after < blocks_wide)
-        leaf = jnp.sum(jnp.where(inside, leaf_row - leaf_count, 0.0), axis=0, keepdims=True)
-        place = jnp.sum(jnp.where(inside, (after * block_pieces).astype(F32), 0.0), axis=0, keepdims=True)
-        item_ref[line : line + 1, :] = leaf.astype(jnp.int32) + leaf_count
-        item_ref[8 + line : 9 + line, :] = place.astype(jnp.int32)
-
-    order = jnp.sum(jnp.where(rank_column == column, row.astype(F32), 0.0), axis=0, keepdims=True)
-    plan_ref[PLAN_ORDER : PLAN_ORDER + 1, :leaf_count] = order.astype(jnp.int32)
-    plan_ref[PLAN_COUNT : PLAN_COUNT + 1, :leaf_count] = counts[1].astype(jnp.int32)
+        item_ref[line : line + 1, :] = leaf[:, line * 128 : (line + 1) * 128]
 
 
 def final_kernel(
@@ -481,13 +502,20 @@
         leaves = [node * 8 + child for child in range(8)]
         features = []
         for leaf in leaves:
-            starts = [pl.multiple_of((2 * leaf + half) * 32, 32) for half in range(2)]
-            features.append(feature_ref[0, pl.ds(starts[0], 32), :] + feature_ref[1, pl.ds(starts[1], 32), :])
-        turned = [turned_ref[leaf] for leaf in leaves]
+            features.append(feature_ref[0, 2 * leaf] + feature_ref[1, 2 * leaf + 1])
+        turned = [turned_ref[2 * node + number] for number in range(2)]
         node_rows = pl.ds(pl.multiple_of(node * q_width, q_width), q_width)
         downs = [weight_rows(down_leaf_ref[child, node_rows, :]) for child in range(8)]
         nears = [near_ref[leaf] for leaf in leaves]
-        exponents = [dot(left, right) for left, right in zip(turned, features)]
+        blank = jnp.zeros((32, p_width), BF16)
+        exponents = []
+        for first in range(0, 8, 2):
+            sides = []
+            for child in (first, first + 1):
+                lines = [features[child] if place == child % 4 else blank for place in range(4)]
+                sides.append(jnp.concatenate(lines, axis=0))
+            both = dot(turned[first // 4], jnp.concatenate(sides, axis=1))
+            exponents += [both[:, :p_width], both[:, p_width:]]
         values = [halves(jnp.exp2(value)) for value in exponents]
         lefts = [jnp.concatenate(down, axis=0).astype(BF16) for down in downs]
         products = [dot(left, jnp.concatenate(value, axis=1)) for left, value in zip(lefts, values)]
@@ -545,12 +573,12 @@
     pack, features, turned, message, send, slab = pl.pallas_call(
         lambda *refs: upward_kernel(level_count, *refs),
         out_shape=(
-            jax.ShapeDtypeStruct((leaf_count * p_width, 128), BF16),
-            jax.ShapeDtypeStruct((2, leaf_count * 64, p_width), BF16),
-            jax.ShapeDtypeStruct((leaf_count, eq_width, 32), BF16),
+            jax.ShapeDtypeStruct((2 * leaf_count, PIECE, 128), BF16),
+            jax.ShapeDtypeStruct((2, 2 * leaf_count, 32, p_width), BF16),
+            jax.ShapeDtypeStruct((leaf_count // 4, eq_width, 128), BF16),
             jax.ShapeDtypeStruct((leaf_count, q_width + 8, p_width), F32),
-            jax.ShapeDtypeStruct((node_rows + 3 * level_count * q_width + 16, eq_width), BF16),
-            jax.ShapeDtypeStruct((level_count * q_width, eq_width), F32),
+            jax.ShapeDtypeStruct((node_rows + 3 * level_rows + 16, eq_width), BF16),
+            jax.ShapeDtypeStruct((level_rows, eq_width), F32),
         ),
         in_specs=[vmem, vmem, vmem, smem, vmem, vmem, vmem],
         out_specs=(vmem,) * 6,
@@ -565,25 +593,33 @@
     total = slab + (partner[:level_rows] + partner[level_rows : 2 * level_rows] + partner[2 * level_rows :])
     message, total = lax.optimization_barrier((message, total))
     lower, upper = shifted(message, size)
+    exchanges = [(level, bit) for level in range(level_count) for bit in range(max(1, 3 * level), min(3 * level + 3, bits))]
     tops = []
-    for level in range(level_count):
-        if level:
+
+    def exchange(total, wanted):
+        level, bit = wanted
+        if level and bit == 3 * level:
             tops.append(total)
             total = total[q_width:]
-        for bit in range(max(1, 3 * level), min(3 * level + 3, bits)):
-            total = total + swapped(total, size, bit)
-    tops.append(total)
+        return total, swapped(total, size, bit)
+
+    early, late = exchanges[:2], exchanges[2:]
+    total, arrived = exchange(total, early[0])
+    total = total + arrived
+    total, arrived = exchange(total, early[1])
+    send_lower, total = lax.optimization_barrier((send_lower, total))
 
     table = table.reshape(eq_width * eq_width, type_count)
-    far_node, plan, items = pl.pallas_call(
+    far_node, steps, piece_table, items = pl.pallas_call(
         far_kernel,
         out_shape=(
             jax.ShapeDtypeStruct((node_rows, eq_width), F32),
-            jax.ShapeDtypeStruct((64, 128), jnp.int32),
-            jax.ShapeDtypeStruct((16, 128), jnp.int32),
+            jax.ShapeDtypeStruct((1, 128), jnp.int32),
+            jax.ShapeDtypeStruct((32, 128), jnp.int32),
+            jax.ShapeDtypeStruct((8, 128), jnp.int32),
         ),
         in_specs=[vmem, vmem, vmem, vmem, vmem, hbm],
-        out_specs=(vmem,) * 3,
+        out_specs=(vmem,) * 4,
         scratch_shapes=[
             pltpu.VMEM((type_count // 128, eq_width * eq_width, 128), BF16),
             pltpu.VMEM((eq_width * eq_width, type_count % 128), BF16),
@@ -598,25 +634,31 @@
     )(send_lower, send, send_upper, vlist, ulist, table)
     far_node, lower, upper = lax.optimization_barrier((far_node, lower, upper))
 
+    far_node, total, arrived = lax.optimization_barrier((far_node, total, arrived))
+    for wanted in late:
+        total = total + arrived
+        total, arrived = exchange(total, wanted)
+    steps, total = lax.optimization_barrier((steps, total))
     near = pl.pallas_call(
         near_kernel,
         out_shape=jax.ShapeDtypeStruct((leaf_count, q_width, p_width), F32),
-        in_specs=[smem, smem, hbm, hbm, vmem, vmem],
+        in_specs=[smem, smem, smem, hbm, hbm, vmem, vmem],
         out_specs=vmem,
         scratch_shapes=[
-            pltpu.VMEM((3 * leaf_count * p_width + PIECE, 128), BF16),
-            pltpu.VMEM((2, 3 * leaf_count * 64 + 32, 128), BF16),
+            pltpu.VMEM((6 * leaf_count + 1, PIECE, 128), BF16),
+            pltpu.VMEM((2, 6 * leaf_count + 1, 32, 128), BF16),
             pltpu.VMEM((2 * UNROLL, 2, p_width, 128), BF16),
-            pltpu.VMEM((leaf_count + 1, p_width, 128), F32),
+            *[pltpu.VMEM((leaf_count + 1, p_width, 128), F32)] * TOTALS,
             pltpu.SemaphoreType.DMA((2,)),
         ],
         compiler_params=params,
         cost_estimate=pl.CostEstimate(flops=3 * 10**10, bytes_accessed=10**7, transcendentals=0),
         name="near",
-    )(plan, items, pack, features, lower, upper)
-
+    )(steps, piece_table.reshape(-1), items.reshape(-1), pack, features, lower, upper)
+
+    tops.append(total + arrived)
     return pl.pallas_call(
-        lambda *refs: final_kernel(len(tops), *refs),
+        lambda *refs: final_kernel(level_count, *refs),
         out_shape=jax.ShapeDtypeStruct((leaf_count, q_width, p_width), F32),
         in_specs=[smem] + [vmem] * (7 + len(tops)),
         out_specs=vmem,

time: 135 us -> 117 us (0.87); the launches traced: 134 us -> 114 us
  Pallas kernels: 98.2 us -> 84.1 us
  waiting for transfers between devices: 13 us -> 9.87 us
  starting transfers between devices: 20.3 us -> 18.8 us
    pallas_call x1, Pallas kernels: 55.4 us -> 41.3 us  [local(): pl.pallas_call(near_kernel, out_shape=jax.ShapeDtypeStruct((leaf_count, q...]
    ppermute x4, waiting for transfers between devices: 3.54 us -> 1.48 us  [swapped(): lax.ppermute(value, 'oct', [(source, source ^ 1 << bit) for source in ran...]
  transfers between devices with their start and end apart: 8 -> 8, of which waited for: 6 -> 5; matrix products, arithmetic and copies ran while one was open for 0% -> 0% of each run, Pallas kernels for 16% -> 56%
where the time goes in v8:
time: 117 us; the launch traced here: 114 us
  Pallas kernels  84.1 us (72%)
  starting transfers between devices  18.8 us (16%)
  waiting for transfers between devices  9.87 us (8%)
  other arithmetic  1.6 us (1%)
    pallas_call x1, Pallas kernels, local(): pl.pallas_call(near_kernel, out_shape=jax.ShapeDtypeStruct((leaf_count, q...  41.3 us
    pallas_call x1, Pallas kernels, local(): pl.pallas_call(far_kernel, out_shape=(jax.ShapeDtypeStruct((node_rows, eq...  22.4 us
    ppermute x4, starting transfers between devices, shifted(): return (lax.ppermute(value, 'oct', up), lax.ppermute(value, 'oct', down))  10.8 us
    pallas_call x1, Pallas kernels, local(): pl.pallas_call(lambda *refs: upward_kernel(level_count, *refs), out_shape...  10.3 us
    pallas_call x1, Pallas kernels, local(): pl.pallas_call(lambda *refs: final_kernel(level_count, *refs), out_shape=...  10 us
    ppermute x4, waiting for transfers between devices, shifted(): return (lax.ppermute(value, 'oct', up), lax.ppermute(value, 'oct', down))  8.4 us
    ppermute x4, starting transfers between devices, swapped(): lax.ppermute(value, 'oct', [(source, source ^ 1 << bit) for source in ran...  7.97 us
  transfers between devices with their start and end apart: 8, of which 5 were waited for; matrix products, arithmetic and copies ran while one was open for 0% of the time, Pallas kernels for 56%

profile of v8, /device:TPU:1, one launch (start us, length us, event | category | flops | bytes accessed | tf_op | source)
XLA Modules:
  0.0 114.5 jit_solution(2521569801179353972)
XLA Ops:
  0.0 10.3 %upward.1 = (bf16[128,64,128]{2,1,0:T(8,128)(2,1)}, bf16[2,128,32,128]{3,2,1,0:T(8,128)(2,1)}, bf16[16,152,128]{2,1,0:T(8,128)(2,1)}, f32[64,40,128]{2,1,0:T(8,1...) custom-call(f32[3,64,128]{2,1,0:T(8,128)} %bitcast.10, f32[64,32,128]{2,1,0:T(8,128)} %refs_1_.1, ...), custom_call_target="tpu_custom_call" | custom-call | tf_op jit(solution)/shard_map/upward/pallas_call | solution.py:573
  10.3 4.5 %collective-permute-start = (bf16[464,152]{1,0:T(8,128)(2,1)}, bf16[464,152]{1,0:T(8,128)(2,1)S(1)}, u32[]{:S(2)}, u32[]{:S(2)}) collective-permute-start(bf16[464,152]{1,0:T(8,128)(2,1)} %get-tuple-element.29.own_ref), channel_id=1, source_target_pairs={{0,1},{1,2},{2,3},{3,4},{4,5},{5,6},{6,7},{7,8},{8,9},{9,10},{10,1... | collective-permute-start | bytes 423176 | tf_op jit(solution)/shard_map/ppermute | solution.py:534
  14.8 1.9 %collective-permute-start.1 = (bf16[464,152]{1,0:T(8,128)(2,1)}, bf16[464,152]{1,0:T(8,128)(2,1)S(1)}, u32[]{:S(2)}, u32[]{:S(2)}) collective-permute-start(bf16[464,152]{1,0:T(8,128)(2,1)} %get-tuple-element.29.own_ref), channel_id=1, source_target_pairs={{1,0},{2,1},{3,2},{4,3},{5,4},{6,5},{7,6},{8,7},{9,8},{10,9},{11,1... | collective-permute-start | bytes 423176 | tf_op jit(solution)/shard_map/ppermute | solution.py:534
  16.8 1.4 %collective-permute-done.lower_ref = bf16[464,152]{1,0:T(8,128)(2,1)S(1)} collective-permute-done((bf16[464,152]{1,0:T(8,128)(2,1)}, bf16[464,152]{1,0:T(8,128)(2,1)S(1)}, u32[]{:S(2)}, u32[]{:S(2)}) %collective-permute-start) | collective-permute-done | bytes 141088 | tf_op jit(solution)/shard_map/ppermute | solution.py:534
  18.2 0.0 copy-start.1
  18.2 4.3 %collective-permute-done.1.upper_ref = bf16[464,152]{1,0:T(8,128)(2,1)S(1)} collective-permute-done((bf16[464,152]{1,0:T(8,128)(2,1)}, bf16[464,152]{1,0:T(8,128)(2,1)S(1)}, u32[]{:S(2)}, u32[]{:S(2)}) %collective-permute-start.1) | collective-permute-done | bytes 141088 | tf_op jit(solution)/shard_map/ppermute | solution.py:534
  22.5 0.0 copy-start.2
  22.5 0.9 fusion.1
  23.4 2.2 %collective-permute-start.2 = (f32[64,152]{1,0:T(8,128)S(1)}, f32[64,152]{1,0:T(8,128)S(1)}, u32[]{:S(2)}, u32[]{:S(2)}) collective-permute-start(f32[64,152]{1,0:T(8,128)S(1)} %fusion.1), channel_id=1, source_target_pairs={{0,2},{1,3},{2,0},{3,1},{4,6},{5,7},{6,4},{7,5},{8,10},{9,11},{10,... | collective-permute-start | bytes 116744 | tf_op jit(solution)/shard_map/ppermute | solution.py:538
  25.6 1.9 %collective-permute-start.3 = (f32[64,40,128]{2,1,0:T(8,128)}, f32[64,40,128]{2,1,0:T(8,128)S(1)}, u32[]{:S(2)}, u32[]{:S(2)}) collective-permute-start(f32[64,40,128]{2,1,0:T(8,128)} %get-tuple-element.36), channel_id=1, source_target_pairs={{0,1},{1,2},{2,3},{3,4},{4,5},{5,6},{6,7},{7,8},{8,9},{9,10},{10,1... | collective-permute-start | bytes 3932168 | tf_op jit(solution)/shard_map/ppermute | solution.py:534
  27.5 2.5 %collective-permute-start.4 = (f32[64,40,128]{2,1,0:T(8,128)}, f32[64,40,128]{2,1,0:T(8,128)S(1)}, u32[]{:S(2)}, u32[]{:S(2)}) collective-permute-start(f32[64,40,128]{2,1,0:T(8,128)} %get-tuple-element.36), channel_id=1, source_target_pairs={{1,0},{2,1},{3,2},{4,3},{5,4},{6,5},{7,6},{8,7},{9,8},{10,9},{11,1... | collective-permute-start | bytes 3932168 | tf_op jit(solution)/shard_map/ppermute | solution.py:534
  30.0 0.0 collective-permute-done.2
  30.1 2.1 %collective-permute-start.5 = (f32[64,152]{1,0:T(8,128)S(1)}, f32[64,152]{1,0:T(8,128)S(1)}, u32[]{:S(2)}, u32[]{:S(2)}) collective-permute-start(f32[64,152]{1,0:T(8,128)S(1)} %add.24), channel_id=1, source_target_pairs={{0,4},{1,5},{2,6},{3,7},{4,0},{5,1},{6,2},{7,3},{8,12},{9,13},{10,... | collective-permute-start | bytes 116744 | tf_op jit(solution)/shard_map/ppermute | solution.py:538
  32.2 0.0 copy-done.1
  32.2 0.0 copy-done.2
  32.2 22.4 %far.1 = (f32[256,152]{1,0:T(8,128)}, s32[1,128]{1,0:T(1,128)}, s32[32,128]{1,0:T(8,128)}, s32[8,128]{1,0:T(8,128)}) custom-call(bf16[464,152]{1,0:T(8,128)(2,1)} %copy-done.1, bf16[464,152]{1,0:T(8,128)(2,1)} %get-tuple-element.29.own_ref, bf16[464,152]{1,0:T(8,128)(2,1)} %copy-done.2, s32[8,316]{1,0:T(8,128)} %vlist_ref.1, s32[27,64]{1,0:T(8,128)} %bitcast.13, ...), custom_call_target="tpu_custom_call" | custom-call | flops 20000000000 | bytes 18000000 | tf_op jit(solution)/shard_map/far/pallas_call | solution.py:613
  54.6 1.8 %collective-permute-done.3.lower_ref = f32[64,40,128]{2,1,0:T(8,128)S(1)} collective-permute-done((f32[64,40,128]{2,1,0:T(8,128)}, f32[64,40,128]{2,1,0:T(8,128)S(1)}, u32[]{:S(2)}, u32[]{:S(2)}) %collective-permute-start.3) | collective-permute-done | bytes 1310752 | tf_op jit(solution)/shard_map/ppermute | solution.py:534
  56.4 0.0 copy-start.3
  56.4 0.9 collective-permute-done.4.upper_ref
  57.3 0.0 copy-start.4
  57.3 0.0 collective-permute-done.5
  57.3 0.0 copy-start
  57.3 1.4 %collective-permute-start.6 = (f32[32,152]{1,0:T(8,128)S(1)}, f32[32,152]{1,0:T(8,128)S(1)}, u32[]{:S(2)}, u32[]{:S(2)}) collective-permute-start(f32[32,152]{1,0:T(8,128)S(1)} %slice.29), channel_id=1, source_target_pairs={{0,8},{1,9},{2,10},{3,11},{4,12},{5,13},{6,14},{7,15},{8,0},{9,1},... | collective-permute-start | bytes 58376 | tf_op jit(solution)/shard_map/ppermute | solution.py:538
  58.7 1.5 %collective-permute-done.6 = f32[32,152]{1,0:T(8,128)S(1)} collective-permute-done((f32[32,152]{1,0:T(8,128)S(1)}, f32[32,152]{1,0:T(8,128)S(1)}, u32[]{:S(2)}, u32[]{:S(2)}) %collective-permute-start.6) | collective-permute-done | bytes 19488 | tf_op jit(solution)/shard_map/ppermute | solution.py:538
  60.2 2.3 %collective-permute-start.7 = (f32[32,152]{1,0:T(8,128)S(1)}, f32[32,152]{1,0:T(8,128)S(1)}, u32[]{:S(2)}, u32[]{:S(2)}) collective-permute-start(f32[32,152]{1,0:T(8,128)S(1)} %slice_add_fusion.2), channel_id=1, source_target_pairs={{0,16},{1,17},{2,18},{3,19},{4,20},{5,21},{6,22},{7,23},{8,24},{9,... | collective-permute-start | bytes 58376 | tf_op jit(solution)/shard_map/ppermute | solution.py:538
  62.5 0.0 copy-done.3
  62.5 0.0 copy-done.4
  62.5 41.3 %near.1.refs_3_ = f32[64,32,128]{2,1,0:T(8,128)} custom-call(s32[1,128]{1,0:T(1,128)} %get-tuple-element.41.step_ref, s32[4096]{0:T(1024)} %bitcast.14, s32[1024]{0:T(1024)} %bitcast.15, bf16[128,64,128]{2,1,0:T(8,128)(2,1)} %get-tuple-element.44.own_hbm, bf16[2,128,32,128]{3,2,1,0:T(8,128)(2,1)} %get-tuple-element.27.own_feature_hbm.refs_1_, ...), custom_call_target="tpu_custom_call" | custom-call | flops 30000001024 | bytes 10000000 | tf_op jit(solution)/shard_map/near/pallas_call | solution.py:642
  103.8 0.0 copy-done
  103.8 0.0 collective-permute-done.7
  103.8 0.6 add.27.refs_9_
  104.5 10.0 %final.1 = f32[64,32,128]{2,1,0:T(8,128)} custom-call(s32[64]{0:T(128)} %refs_0_.1, bf16[2,128,32,128]{3,2,1,0:T(8,128)(2,1)} %get-tuple-element.27.own_feature_hbm.refs_1_, bf16[16,152,128]{2,1,0:T(8,128)(2,1)} %get-tuple-element.28.refs_2_, f32[64,32,128]{2,1,0:T(8,128)} %near.1.refs_3_, f32[256,152]{1,0:T(8,128)} %get-tuple-element.47.refs_4_, ...), custom_call_target="tpu_custom_call" | custom-call | tf_op jit(solution)/shard_map/final/pallas_call | solution.py:660
  (5 shorter events, 0.0 us)
Async XLA Ops:
  10.3 7.9 %collective-permute-start = (bf16[464,152]{1,0:T(8,128)(2,1)}, bf16[464,152]{1,0:T(8,128)(2,1)S(1)}, u32[]{:S(2)}, u32[]{:S(2)}) collective-permute-start(bf16[464,152]{1,0:T(8,128)(2,1)} %get-tuple-element.29.own_ref), channel_id=1, source_target_pairs={{0,1},{1,2},{2,3},{3,4},{4,5},{5,6},{6,7},{7,8},{8,9},{9,10},{10,1... | collective-permute-start | bytes 423176 | tf_op jit(solution)/shard_map/ppermute | solution.py:534
  14.8 7.6 %collective-permute-start.1 = (bf16[464,152]{1,0:T(8,128)(2,1)}, bf16[464,152]{1,0:T(8,128)(2,1)S(1)}, u32[]{:S(2)}, u32[]{:S(2)}) collective-permute-start(bf16[464,152]{1,0:T(8,128)(2,1)} %get-tuple-element.29.own_ref), channel_id=1, source_target_pairs={{1,0},{2,1},{3,2},{4,3},{5,4},{6,5},{7,6},{8,7},{9,8},{10,9},{11,1... | collective-permute-start | bytes 423176 | tf_op jit(solution)/shard_map/ppermute | solution.py:534
  18.2 14.0 %copy-start.1 = (bf16[464,152]{1,0:T(8,128)(2,1)}, bf16[464,152]{1,0:T(8,128)(2,1)S(1)}, u32[]{:S(2)}) copy-start(bf16[464,152]{1,0:T(8,128)(2,1)S(1)} %collective-permute-done.lower_ref) | copy-start | bytes 423172
  22.5 9.7 %copy-start.2 = (bf16[464,152]{1,0:T(8,128)(2,1)}, bf16[464,152]{1,0:T(8,128)(2,1)S(1)}, u32[]{:S(2)}) copy-start(bf16[464,152]{1,0:T(8,128)(2,1)S(1)} %collective-permute-done.1.upper_ref) | copy-start | bytes 423172
  23.4 6.6 %collective-permute-start.2 = (f32[64,152]{1,0:T(8,128)S(1)}, f32[64,152]{1,0:T(8,128)S(1)}, u32[]{:S(2)}, u32[]{:S(2)}) collective-permute-start(f32[64,152]{1,0:T(8,128)S(1)} %fusion.1), channel_id=1, source_target_pairs={{0,2},{1,3},{2,0},{3,1},{4,6},{5,7},{6,4},{7,5},{8,10},{9,11},{10,... | collective-permute-start | bytes 116744 | tf_op jit(solution)/shard_map/ppermute | solution.py:538
  25.6 30.8 %collective-permute-start.3 = (f32[64,40,128]{2,1,0:T(8,128)}, f32[64,40,128]{2,1,0:T(8,128)S(1)}, u32[]{:S(2)}, u32[]{:S(2)}) collective-permute-start(f32[64,40,128]{2,1,0:T(8,128)} %get-tuple-element.36), channel_id=1, source_target_pairs={{0,1},{1,2},{2,3},{3,4},{4,5},{5,6},{6,7},{7,8},{8,9},{9,10},{10,1... | collective-permute-start | bytes 3932168 | tf_op jit(solution)/shard_map/ppermute | solution.py:534
  27.5 29.7 %collective-permute-start.4 = (f32[64,40,128]{2,1,0:T(8,128)}, f32[64,40,128]{2,1,0:T(8,128)S(1)}, u32[]{:S(2)}, u32[]{:S(2)}) collective-permute-start(f32[64,40,128]{2,1,0:T(8,128)} %get-tuple-element.36), channel_id=1, source_target_pairs={{1,0},{2,1},{3,2},{4,3},{5,4},{6,5},{7,6},{8,7},{9,8},{10,9},{11,1... | collective-permute-start | bytes 3932168 | tf_op jit(solution)/shard_map/ppermute | solution.py:534
  30.1 27.2 %collective-permute-start.5 = (f32[64,152]{1,0:T(8,128)S(1)}, f32[64,152]{1,0:T(8,128)S(1)}, u32[]{:S(2)}, u32[]{:S(2)}) collective-permute-start(f32[64,152]{1,0:T(8,128)S(1)} %add.24), channel_id=1, source_target_pairs={{0,4},{1,5},{2,6},{3,7},{4,0},{5,1},{6,2},{7,3},{8,12},{9,13},{10,... | collective-permute-start | bytes 116744 | tf_op jit(solution)/shard_map/ppermute | solution.py:538
  56.4 6.0 %copy-start.3 = (f32[64,40,128]{2,1,0:T(8,128)}, f32[64,40,128]{2,1,0:T(8,128)S(1)}, u32[]{:S(2)}) copy-start(f32[64,40,128]{2,1,0:T(8,128)S(1)} %collective-permute-done.3.lower_ref) | copy-start | bytes 3932164
  57.3 5.2 %copy-start.4 = (f32[64,40,128]{2,1,0:T(8,128)}, f32[64,40,128]{2,1,0:T(8,128)S(1)}, u32[]{:S(2)}) copy-start(f32[64,40,128]{2,1,0:T(8,128)S(1)} %collective-permute-done.4.upper_ref) | copy-start | bytes 3932164
  57.3 46.5 %copy-start = (f32[64,152]{1,0:T(8,128)}, f32[64,152]{1,0:T(8,128)S(1)}, u32[]{:S(2)}) copy-start(f32[64,152]{1,0:T(8,128)S(1)} %add.25.refs_8_) | copy-start | bytes 116740
  57.3 2.8 %collective-permute-start.6 = (f32[32,152]{1,0:T(8,128)S(1)}, f32[32,152]{1,0:T(8,128)S(1)}, u32[]{:S(2)}, u32[]{:S(2)}) collective-permute-start(f32[32,152]{1,0:T(8,128)S(1)} %slice.29), channel_id=1, source_target_pairs={{0,8},{1,9},{2,10},{3,11},{4,12},{5,13},{6,14},{7,15},{8,0},{9,1},... | collective-permute-start | bytes 58376 | tf_op jit(solution)/shard_map/ppermute | solution.py:538
  60.2 43.7 %collective-permute-start.7 = (f32[32,152]{1,0:T(8,128)S(1)}, f32[32,152]{1,0:T(8,128)S(1)}, u32[]{:S(2)}, u32[]{:S(2)}) collective-permute-start(f32[32,152]{1,0:T(8,128)S(1)} %slice_add_fusion.2), channel_id=1, source_target_pairs={{0,16},{1,17},{2,18},{3,19},{4,20},{5,21},{6,22},{7,23},{8,24},{9,... | collective-permute-start | bytes 58376 | tf_op jit(solution)/shard_map/ppermute | solution.py:538

commit v9 on v8

--- a/solution.py
+++ b/solution.py
@@ -15,7 +15,7 @@
 TN = (((0,), (0,)), ((), ()))
 BLOCK = 256
 UNROLL = 8
-TOTALS = 4
+TOTALS = 2
 PIECE = 64
 CLASS_ROWS = (32, 64, 96, 128)
 PLACES = 56
@@ -181,11 +181,10 @@
         slab = dot3(slab, shift_ref[jnp.right_shift(index, 3 * level) & 7])
         slab_ref[level * q_width : (level + 1) * q_width, :] = slab
         high, rest = halves(slab)
-        low = (slab - high.astype(F32) - rest.astype(F32)).astype(BF16)
-        for place, part in enumerate((high, rest, low)):
+        for place, part in enumerate((high, rest)):
             first = start + (place * level_count + level) * q_width
             send_ref[first : first + q_width, :] = part
-    start = start + 3 * level_count * q_width
+    start = start + 2 * level_count * q_width
     line = jnp.concatenate([count_line_ref[...].astype(F32), jnp.zeros((1, eq_width - leaf_count), F32)], axis=1)
     send_ref[start : start + 16, :] = jnp.broadcast_to(line, (16, eq_width)).astype(BF16)
 
@@ -293,7 +292,7 @@
 
 
 def near_kernel(
-    step_ref, piece_ref, item_ref, own_hbm, own_feature_hbm, lower_ref, upper_ref, out_ref, pack_ref, feature_ref, value_ref,
+    step_ref, piece_ref, item_ref, own_hbm, own_feature_hbm, lower_ref, upper_ref, out_ref, pack_ref, feature_ref,
     *rest
 ):
     total_refs, sems = rest[:TOTALS], rest[TOTALS]
@@ -353,31 +352,23 @@
 
     def run(rows, first, count):
         def blocks_step(step, carry):
-            slot = jnp.bitwise_and(step, 1) * UNROLL
-            done, items = items_of(step - 1), items_of(step)
+            items = items_of(step)
             features = [features_of(numbers) for _, numbers in items]
             targets = [targets_of(leaf, rows) for leaf, _ in items]
-            sources = [sources_of(numbers) for _, numbers in done]
-            values = [
-                jnp.concatenate([value_ref[UNROLL - slot + part, side, :rows] for side in range(2)], axis=1)
-                for part in range(UNROLL)
-            ]
+            sources = [sources_of(numbers) for _, numbers in items]
             exponents = [dot(target, feature) for target, feature in zip(targets, features)]
+            values = [jnp.exp2(value).astype(BF16) for value in exponents]
             products = []
             for part in range(0, UNROLL, 2):
                 left = jnp.concatenate(values[part : part + 2], axis=0)
                 both = dot(left, jnp.concatenate(sources[part : part + 2], axis=1))
                 products += [both[:rows, :128], both[rows:, 128:]]
-            following = [jnp.exp2(value).astype(BF16) for value in exponents]
-            for part, value in enumerate(following):
-                for side in range(2):
-                    value_ref[slot + part, side, :rows] = value[:, side * 128 : (side + 1) * 128]
             for first in range(0, UNROLL, TOTALS):
                 sums = [
-                    total_refs[part][done[first + part][0], :rows] + products[first + part] for part in range(TOTALS)
+                    total_refs[part][items[first + part][0], :rows] + products[first + part] for part in range(TOTALS)
                 ]
                 for part, value in enumerate(sums):
-                    total_refs[part][done[first + part][0], :rows] = value
+                    total_refs[part][items[first + part][0], :rows] = value
             return carry
 
         lax.fori_loop(first, first + count, blocks_step, 0)
@@ -387,7 +378,7 @@
 
     def turn_step(step, carry):
         sums = [[total_ref[step * 8 + part] for total_ref in total_refs] for part in range(8)]
-        turned = [(a + b + (c + d)).T for a, b, c, d in sums]
+        turned = [sum(values[1:], values[0]).T for values in sums]
         for part, value in enumerate(turned):
             out_ref[step * 8 + part] = value[32 : 32 + q_width] + value[32 + q_width : 32 + 2 * q_width]
         return carry
@@ -443,8 +434,7 @@
     for number in range(len(CLASS_ROWS)):
         inside = jnp.where(own_class == number, blocks.astype(F32), 0.0)
         items = jnp.sum(inside, axis=1, keepdims=True).astype(jnp.int32)
-        steps = lax.shift_right_logical(items + (2 * UNROLL - 1), UNROLL.bit_length() - 1)
-        steps = jnp.where(items > 0, steps, 0)
+        steps = lax.shift_right_logical(items + (UNROLL - 1), UNROLL.bit_length() - 1)
         first = first + jnp.where(own_class == number, start * UNROLL, 0)
         steps_line = jnp.where(lane == 2 * number, start, jnp.where(lane == 2 * number + 1, steps, steps_line))
         start = start + steps
@@ -577,7 +567,7 @@
             jax.ShapeDtypeStruct((2, 2 * leaf_count, 32, p_width), BF16),
             jax.ShapeDtypeStruct((leaf_count // 4, eq_width, 128), BF16),
             jax.ShapeDtypeStruct((leaf_count, q_width + 8, p_width), F32),
-            jax.ShapeDtypeStruct((node_rows + 3 * level_rows + 16, eq_width), BF16),
+            jax.ShapeDtypeStruct((node_rows + 2 * level_rows + 16, eq_width), BF16),
             jax.ShapeDtypeStruct((level_rows, eq_width), F32),
         ),
         in_specs=[vmem, vmem, vmem, smem, vmem, vmem, vmem],
@@ -588,9 +578,9 @@
     )(points, dens, surface, counts, counts.reshape(1, leaf_count), up_inverse, shift_up)
 
     send_lower, send_upper = shifted(send, size)
-    ends = slice(node_rows, node_rows + 3 * level_rows)
+    ends = slice(node_rows, node_rows + 2 * level_rows)
     partner = jnp.where(index & 1 == 1, send_lower[ends], send_upper[ends]).astype(F32)
-    total = slab + (partner[:level_rows] + partner[level_rows : 2 * level_rows] + partner[2 * level_rows :])
+    total = slab + (partner[:level_rows] + partner[level_rows:])
     message, total = lax.optimization_barrier((message, total))
     lower, upper = shifted(message, size)
     exchanges = [(level, bit) for level in range(level_count) for bit in range(max(1, 3 * level), min(3 * level + 3, bits))]
@@ -647,7 +637,6 @@
         scratch_shapes=[
             pltpu.VMEM((6 * leaf_count + 1, PIECE, 128), BF16),
             pltpu.VMEM((2, 6 * leaf_count + 1, 32, 128), BF16),
-            pltpu.VMEM((2 * UNROLL, 2, p_width, 128), BF16),
             *[pltpu.VMEM((leaf_count + 1, p_width, 128), F32)] * TOTALS,
             pltpu.SemaphoreType.DMA((2,)),
         ],

time: 117 us -> 108 us (0.923); the launches traced: 114 us -> 107 us
  Pallas kernels: 84.1 us -> 77.2 us
    pallas_call x1, Pallas kernels: 41.3 us -> 34.5 us  [local(): pl.pallas_call(near_kernel, out_shape=jax.ShapeDtypeStruct((leaf_count, q...]
  transfers between devices with their start and end apart: 8 -> 8, of which waited for: 5 -> 5; matrix products, arithmetic and copies ran while one was open for 0% -> 0% of each run, Pallas kernels for 56% -> 53%
where the time goes in v9:
time: 108 us; the launch traced here: 107 us
  Pallas kernels  77.2 us (71%)
  starting transfers between devices  18.8 us (17%)
  waiting for transfers between devices  9.56 us (9%)
  other arithmetic  1.59 us (1%)
    pallas_call x1, Pallas kernels, local(): pl.pallas_call(near_kernel, out_shape=jax.ShapeDtypeStruct((leaf_count, q...  34.5 us
    pallas_call x1, Pallas kernels, local(): pl.pallas_call(far_kernel, out_shape=(jax.ShapeDtypeStruct((node_rows, eq...  22.4 us
    ppermute x4, starting transfers between devices, shifted(): return (lax.ppermute(value, 'oct', up), lax.ppermute(value, 'oct', down))  10.8 us
    pallas_call x1, Pallas kernels, local(): pl.pallas_call(lambda *refs: upward_kernel(level_count, *refs), out_shape...  10.3 us
    pallas_call x1, Pallas kernels, local(): pl.pallas_call(lambda *refs: final_kernel(level_count, *refs), out_shape=...  9.99 us
    ppermute x4, waiting for transfers between devices, shifted(): return (lax.ppermute(value, 'oct', up), lax.ppermute(value, 'oct', down))  8.08 us
    ppermute x4, starting transfers between devices, swapped(): lax.ppermute(value, 'oct', [(source, source ^ 1 << bit) for source in ran...  7.97 us
  transfers between devices with their start and end apart: 8, of which 5 were waited for; matrix products, arithmetic and copies ran while one was open for 0% of the time, Pallas kernels for 53%

profile of v9, /device:TPU:1, one launch (start us, length us, event | category | flops | bytes accessed | tf_op | source)
XLA Modules:
  0.0 107.3 jit_solution(14697343852702205613)
XLA Ops:
  0.0 10.3 %upward.1 = (bf16[128,64,128]{2,1,0:T(8,128)(2,1)}, bf16[2,128,32,128]{3,2,1,0:T(8,128)(2,1)}, bf16[16,152,128]{2,1,0:T(8,128)(2,1)}, f32[64,40,128]{2,1,0:T(8,1...) custom-call(f32[3,64,128]{2,1,0:T(8,128)} %bitcast.10, f32[64,32,128]{2,1,0:T(8,128)} %refs_1_.1, ...), custom_call_target="tpu_custom_call" | custom-call | tf_op jit(solution)/shard_map/upward/pallas_call | solution.py:563
  10.3 4.5 %collective-permute-start = (bf16[400,152]{1,0:T(8,128)(2,1)}, bf16[400,152]{1,0:T(8,128)(2,1)S(1)}, u32[]{:S(2)}, u32[]{:S(2)}) collective-permute-start(bf16[400,152]{1,0:T(8,128)(2,1)} %get-tuple-element.29.own_ref), channel_id=1, source_target_pairs={{0,1},{1,2},{2,3},{3,4},{4,5},{5,6},{6,7},{7,8},{8,9},{9,10},{10,1... | collective-permute-start | bytes 364808 | tf_op jit(solution)/shard_map/ppermute | solution.py:524
  14.8 1.9 %collective-permute-start.1 = (bf16[400,152]{1,0:T(8,128)(2,1)}, bf16[400,152]{1,0:T(8,128)(2,1)S(1)}, u32[]{:S(2)}, u32[]{:S(2)}) collective-permute-start(bf16[400,152]{1,0:T(8,128)(2,1)} %get-tuple-element.29.own_ref), channel_id=1, source_target_pairs={{1,0},{2,1},{3,2},{4,3},{5,4},{6,5},{7,6},{8,7},{9,8},{10,9},{11,1... | collective-permute-start | bytes 364808 | tf_op jit(solution)/shard_map/ppermute | solution.py:524
  16.8 1.1 collective-permute-done.lower_ref
  17.8 0.0 copy-start.1
  17.8 4.3 %collective-permute-done.1.upper_ref = bf16[400,152]{1,0:T(8,128)(2,1)S(1)} collective-permute-done((bf16[400,152]{1,0:T(8,128)(2,1)}, bf16[400,152]{1,0:T(8,128)(2,1)S(1)}, u32[]{:S(2)}, u32[]{:S(2)}) %collective-permute-start.1) | collective-permute-done | bytes 121632 | tf_op jit(solution)/shard_map/ppermute | solution.py:524
  22.1 0.0 copy-start.2
  22.1 0.9 fusion
  23.1 2.2 %collective-permute-start.2 = (f32[64,152]{1,0:T(8,128)S(1)}, f32[64,152]{1,0:T(8,128)S(1)}, u32[]{:S(2)}, u32[]{:S(2)}) collective-permute-start(f32[64,152]{1,0:T(8,128)S(1)} %fusion), channel_id=1, source_target_pairs={{0,2},{1,3},{2,0},{3,1},{4,6},{5,7},{6,4},{7,5},{8,10},{9,11},{10,... | collective-permute-start | bytes 116744 | tf_op jit(solution)/shard_map/ppermute | solution.py:528
  25.2 1.9 %collective-permute-start.3 = (f32[64,40,128]{2,1,0:T(8,128)}, f32[64,40,128]{2,1,0:T(8,128)S(1)}, u32[]{:S(2)}, u32[]{:S(2)}) collective-permute-start(f32[64,40,128]{2,1,0:T(8,128)} %get-tuple-element.36), channel_id=1, source_target_pairs={{0,1},{1,2},{2,3},{3,4},{4,5},{5,6},{6,7},{7,8},{8,9},{9,10},{10,1... | collective-permute-start | bytes 3932168 | tf_op jit(solution)/shard_map/ppermute | solution.py:524
  27.2 2.5 %collective-permute-start.4 = (f32[64,40,128]{2,1,0:T(8,128)}, f32[64,40,128]{2,1,0:T(8,128)S(1)}, u32[]{:S(2)}, u32[]{:S(2)}) collective-permute-start(f32[64,40,128]{2,1,0:T(8,128)} %get-tuple-element.36), channel_id=1, source_target_pairs={{1,0},{2,1},{3,2},{4,3},{5,4},{6,5},{7,6},{8,7},{9,8},{10,9},{11,1... | collective-permute-start | bytes 3932168 | tf_op jit(solution)/shard_map/ppermute | solution.py:524
  29.7 0.0 collective-permute-done.2
  29.7 2.1 %collective-permute-start.5 = (f32[64,152]{1,0:T(8,128)S(1)}, f32[64,152]{1,0:T(8,128)S(1)}, u32[]{:S(2)}, u32[]{:S(2)}) collective-permute-start(f32[64,152]{1,0:T(8,128)S(1)} %add.20), channel_id=1, source_target_pairs={{0,4},{1,5},{2,6},{3,7},{4,0},{5,1},{6,2},{7,3},{8,12},{9,13},{10,... | collective-permute-start | bytes 116744 | tf_op jit(solution)/shard_map/ppermute | solution.py:528
  31.8 0.0 copy-done.1
  31.8 0.0 copy-done.2
  31.8 22.4 %far.1 = (f32[256,152]{1,0:T(8,128)}, s32[1,128]{1,0:T(1,128)}, s32[32,128]{1,0:T(8,128)}, s32[8,128]{1,0:T(8,128)}) custom-call(bf16[400,152]{1,0:T(8,128)(2,1)} %copy-done.1, bf16[400,152]{1,0:T(8,128)(2,1)} %get-tuple-element.29.own_ref, bf16[400,152]{1,0:T(8,128)(2,1)} %copy-done.2, s32[8,316]{1,0:T(8,128)} %vlist_ref.1, s32[27,64]{1,0:T(8,128)} %bitcast.13, ...), custom_call_target="tpu_custom_call" | custom-call | flops 20000000000 | bytes 18000000 | tf_op jit(solution)/shard_map/far/pallas_call | solution.py:603
  54.2 1.9 %collective-permute-done.3.lower_ref = f32[64,40,128]{2,1,0:T(8,128)S(1)} collective-permute-done((f32[64,40,128]{2,1,0:T(8,128)}, f32[64,40,128]{2,1,0:T(8,128)S(1)}, u32[]{:S(2)}, u32[]{:S(2)}) %collective-permute-start.3) | collective-permute-done | bytes 1310752 | tf_op jit(solution)/shard_map/ppermute | solution.py:524
  56.1 0.0 copy-start.3
  56.1 0.9 collective-permute-done.4.upper_ref
  56.9 0.0 copy-start.4
  56.9 0.0 collective-permute-done.5
  56.9 0.0 copy-start
  56.9 1.4 %collective-permute-start.6 = (f32[32,152]{1,0:T(8,128)S(1)}, f32[32,152]{1,0:T(8,128)S(1)}, u32[]{:S(2)}, u32[]{:S(2)}) collective-permute-start(f32[32,152]{1,0:T(8,128)S(1)} %slice.24), channel_id=1, source_target_pairs={{0,8},{1,9},{2,10},{3,11},{4,12},{5,13},{6,14},{7,15},{8,0},{9,1},... | collective-permute-start | bytes 58376 | tf_op jit(solution)/shard_map/ppermute | solution.py:528
  58.3 1.5 %collective-permute-done.6 = f32[32,152]{1,0:T(8,128)S(1)} collective-permute-done((f32[32,152]{1,0:T(8,128)S(1)}, f32[32,152]{1,0:T(8,128)S(1)}, u32[]{:S(2)}, u32[]{:S(2)}) %collective-permute-start.6) | collective-permute-done | bytes 19488 | tf_op jit(solution)/shard_map/ppermute | solution.py:528
  59.8 2.3 %collective-permute-start.7 = (f32[32,152]{1,0:T(8,128)S(1)}, f32[32,152]{1,0:T(8,128)S(1)}, u32[]{:S(2)}, u32[]{:S(2)}) collective-permute-start(f32[32,152]{1,0:T(8,128)S(1)} %slice_add_fusion.1), channel_id=1, source_target_pairs={{0,16},{1,17},{2,18},{3,19},{4,20},{5,21},{6,22},{7,23},{8,24},{9,... | collective-permute-start | bytes 58376 | tf_op jit(solution)/shard_map/ppermute | solution.py:528
  62.1 0.0 copy-done.3
  62.1 0.0 copy-done.4
  62.1 34.5 %near.1.refs_3_ = f32[64,32,128]{2,1,0:T(8,128)} custom-call(s32[1,128]{1,0:T(1,128)} %get-tuple-element.41.step_ref, s32[4096]{0:T(1024)} %bitcast.14, s32[1024]{0:T(1024)} %bitcast.15, bf16[128,64,128]{2,1,0:T(8,128)(2,1)} %get-tuple-element.44.own_hbm, bf16[2,128,32,128]{3,2,1,0:T(8,128)(2,1)} %get-tuple-element.27.own_feature_hbm.refs_1_, ...), custom_call_target="tpu_custom_call" | custom-call | flops 30000001024 | bytes 10000000 | tf_op jit(solution)/shard_map/near/pallas_call | solution.py:632
  96.6 0.0 copy-done
  96.7 0.0 collective-permute-done.7
  96.7 0.6 add.23.refs_9_
  97.3 10.0 %final.1 = f32[64,32,128]{2,1,0:T(8,128)} custom-call(s32[64]{0:T(128)} %refs_0_.1, bf16[2,128,32,128]{3,2,1,0:T(8,128)(2,1)} %get-tuple-element.27.own_feature_hbm.refs_1_, bf16[16,152,128]{2,1,0:T(8,128)(2,1)} %get-tuple-element.28.refs_2_, f32[64,32,128]{2,1,0:T(8,128)} %near.1.refs_3_, f32[256,152]{1,0:T(8,128)} %get-tuple-element.47.refs_4_, ...), custom_call_target="tpu_custom_call" | custom-call | tf_op jit(solution)/shard_map/final/pallas_call | solution.py:649
  (5 shorter events, 0.0 us)
Async XLA Ops:
  10.3 7.5 %collective-permute-start = (bf16[400,152]{1,0:T(8,128)(2,1)}, bf16[400,152]{1,0:T(8,128)(2,1)S(1)}, u32[]{:S(2)}, u32[]{:S(2)}) collective-permute-start(bf16[400,152]{1,0:T(8,128)(2,1)} %get-tuple-element.29.own_ref), channel_id=1, source_target_pairs={{0,1},{1,2},{2,3},{3,4},{4,5},{5,6},{6,7},{7,8},{8,9},{9,10},{10,1... | collective-permute-start | bytes 364808 | tf_op jit(solution)/shard_map/ppermute | solution.py:524
  14.8 7.3 %collective-permute-start.1 = (bf16[400,152]{1,0:T(8,128)(2,1)}, bf16[400,152]{1,0:T(8,128)(2,1)S(1)}, u32[]{:S(2)}, u32[]{:S(2)}) collective-permute-start(bf16[400,152]{1,0:T(8,128)(2,1)} %get-tuple-element.29.own_ref), channel_id=1, source_target_pairs={{1,0},{2,1},{3,2},{4,3},{5,4},{6,5},{7,6},{8,7},{9,8},{10,9},{11,1... | collective-permute-start | bytes 364808 | tf_op jit(solution)/shard_map/ppermute | solution.py:524
  17.8 14.0 %copy-start.1 = (bf16[400,152]{1,0:T(8,128)(2,1)}, bf16[400,152]{1,0:T(8,128)(2,1)S(1)}, u32[]{:S(2)}) copy-start(bf16[400,152]{1,0:T(8,128)(2,1)S(1)} %collective-permute-done.lower_ref) | copy-start | bytes 364804
  22.1 9.7 %copy-start.2 = (bf16[400,152]{1,0:T(8,128)(2,1)}, bf16[400,152]{1,0:T(8,128)(2,1)S(1)}, u32[]{:S(2)}) copy-start(bf16[400,152]{1,0:T(8,128)(2,1)S(1)} %collective-permute-done.1.upper_ref) | copy-start | bytes 364804
  23.1 6.6 %collective-permute-start.2 = (f32[64,152]{1,0:T(8,128)S(1)}, f32[64,152]{1,0:T(8,128)S(1)}, u32[]{:S(2)}, u32[]{:S(2)}) collective-permute-start(f32[64,152]{1,0:T(8,128)S(1)} %fusion), channel_id=1, source_target_pairs={{0,2},{1,3},{2,0},{3,1},{4,6},{5,7},{6,4},{7,5},{8,10},{9,11},{10,... | collective-permute-start | bytes 116744 | tf_op jit(solution)/shard_map/ppermute | solution.py:528
  25.2 30.8 %collective-permute-start.3 = (f32[64,40,128]{2,1,0:T(8,128)}, f32[64,40,128]{2,1,0:T(8,128)S(1)}, u32[]{:S(2)}, u32[]{:S(2)}) collective-permute-start(f32[64,40,128]{2,1,0:T(8,128)} %get-tuple-element.36), channel_id=1, source_target_pairs={{0,1},{1,2},{2,3},{3,4},{4,5},{5,6},{6,7},{7,8},{8,9},{9,10},{10,1... | collective-permute-start | bytes 3932168 | tf_op jit(solution)/shard_map/ppermute | solution.py:524
  27.2 29.7 %collective-permute-start.4 = (f32[64,40,128]{2,1,0:T(8,128)}, f32[64,40,128]{2,1,0:T(8,128)S(1)}, u32[]{:S(2)}, u32[]{:S(2)}) collective-permute-start(f32[64,40,128]{2,1,0:T(8,128)} %get-tuple-element.36), channel_id=1, source_target_pairs={{1,0},{2,1},{3,2},{4,3},{5,4},{6,5},{7,6},{8,7},{9,8},{10,9},{11,1... | collective-permute-start | bytes 3932168 | tf_op jit(solution)/shard_map/ppermute | solution.py:524
  29.7 27.2 %collective-permute-start.5 = (f32[64,152]{1,0:T(8,128)S(1)}, f32[64,152]{1,0:T(8,128)S(1)}, u32[]{:S(2)}, u32[]{:S(2)}) collective-permute-start(f32[64,152]{1,0:T(8,128)S(1)} %add.20), channel_id=1, source_target_pairs={{0,4},{1,5},{2,6},{3,7},{4,0},{5,1},{6,2},{7,3},{8,12},{9,13},{10,... | collective-permute-start | bytes 116744 | tf_op jit(solution)/shard_map/ppermute | solution.py:528
  56.1 6.0 %copy-start.3 = (f32[64,40,128]{2,1,0:T(8,128)}, f32[64,40,128]{2,1,0:T(8,128)S(1)}, u32[]{:S(2)}) copy-start(f32[64,40,128]{2,1,0:T(8,128)S(1)} %collective-permute-done.3.lower_ref) | copy-start | bytes 3932164
  56.9 5.2 %copy-start.4 = (f32[64,40,128]{2,1,0:T(8,128)}, f32[64,40,128]{2,1,0:T(8,128)S(1)}, u32[]{:S(2)}) copy-start(f32[64,40,128]{2,1,0:T(8,128)S(1)} %collective-permute-done.4.upper_ref) | copy-start | bytes 3932164
  56.9 39.7 %copy-start = (f32[64,152]{1,0:T(8,128)}, f32[64,152]{1,0:T(8,128)S(1)}, u32[]{:S(2)}) copy-start(f32[64,152]{1,0:T(8,128)S(1)} %add.21.refs_8_) | copy-start | bytes 116740
  56.9 2.8 %collective-permute-start.6 = (f32[32,152]{1,0:T(8,128)S(1)}, f32[32,152]{1,0:T(8,128)S(1)}, u32[]{:S(2)}, u32[]{:S(2)}) collective-permute-start(f32[32,152]{1,0:T(8,128)S(1)} %slice.24), channel_id=1, source_target_pairs={{0,8},{1,9},{2,10},{3,11},{4,12},{5,13},{6,14},{7,15},{8,0},{9,1},... | collective-permute-start | bytes 58376 | tf_op jit(solution)/shard_map/ppermute | solution.py:528
  59.8 36.9 %collective-permute-start.7 = (f32[32,152]{1,0:T(8,128)S(1)}, f32[32,152]{1,0:T(8,128)S(1)}, u32[]{:S(2)}, u32[]{:S(2)}) collective-permute-start(f32[32,152]{1,0:T(8,128)S(1)} %slice_add_fusion.1), channel_id=1, source_target_pairs={{0,16},{1,17},{2,18},{3,19},{4,20},{5,21},{6,22},{7,23},{8,24},{9,... | collective-permute-start | bytes 58376 | tf_op jit(solution)/shard_map/ppermute | solution.py:528

commit v10 on v9

--- a/solution.py
+++ b/solution.py
@@ -21,6 +21,7 @@
 PLACES = 56
 SOURCES = 32
 CHUNK = 4
+FIRST, SECOND = 16, 8
 
 
 def dot(left, right):
@@ -123,14 +124,24 @@
 
 
 def upward_kernel(
-    level_count, points_ref, dens_ref, surface_ref, counts_ref, count_line_ref, up_ref, shift_ref, pack_ref, feature_ref, turned_ref,
-    message_ref, send_ref, slab_ref, check_ref
+    level_count, points_ref, dens_ref, surface_ref, counts_ref, count_line_ref, up_ref, shift_ref, pack_hbm, feature_hbm, turned_hbm,
+    message_hbm, send_ref, slab_ref, check_ref, pack_ref, feature_ref, turned_ref, message_ref, sems
 ):
     leaf_count, q_width, p_width = dens_ref.shape
     eq_width = surface_ref.shape[2]
     node_count = leaf_count // 8
     lane = iota((q_width, p_width), 1)
     row = iota((8, p_width), 0)
+
+    def copies_of(node):
+        leaves, pairs, fours = pl.ds(8 * node, 8), pl.ds(16 * node, 16), pl.ds(2 * node, 2)
+        ends = [
+            (pack_ref.at[pairs], pack_hbm.at[pairs]),
+            (feature_ref.at[:, pairs], feature_hbm.at[:, pairs]),
+            (turned_ref.at[fours], turned_hbm.at[fours]),
+            (message_ref.at[leaves], message_hbm.at[leaves]),
+        ]
+        return [pltpu.make_async_copy(*end, sems.at[node, number]) for number, end in enumerate(ends)]
 
     def node_step(node, carry):
         leaves = [node * 8 + child for child in range(8)]
@@ -163,6 +174,8 @@
             put_features(feature_ref, leaf, versions[child])
             check = firsts[child][:q_width] + firsts[child][q_width:] + seconds[child]
             check_ref[child, pl.ds(pl.multiple_of(node * q_width, q_width), q_width), :] = check
+        for copy in copies_of(node):
+            copy.start()
         return carry
 
     lax.fori_loop(0, node_count, node_step, 0)
@@ -188,6 +201,13 @@
     line = jnp.concatenate([count_line_ref[...].astype(F32), jnp.zeros((1, eq_width - leaf_count), F32)], axis=1)
     send_ref[start : start + 16, :] = jnp.broadcast_to(line, (16, eq_width)).astype(BF16)
 
+    def wait_step(node, carry):
+        for copy in copies_of(node):
+            copy.wait()
+        return carry
+
+    lax.fori_loop(0, node_count, wait_step, 0)
+
 
 def far_kernel(
     lower_ref, own_ref, upper_ref, vlist_ref, ulist_ref, table_hbm, out_ref, step_ref, piece_ref, item_ref, table_ref,
@@ -228,13 +248,17 @@
 
     ids = vlist_ref[...]
     places = jnp.where(ids >= 0, ids - (index - 1) * node_count, -1).astype(F32).astype(BF16)
-    spread = (iota((node_count, lanes), 1) // SOURCES == iota((node_count, lanes), 0)).astype(BF16)
+    lane = iota((1, lanes), 1)
+    second_half = jnp.bitwise_and(lane, 63)
+    node_of = jnp.where(lane < 128, lane // FIRST, second_half // SECOND)
+    source_of = jnp.where(lane < 128, lane % FIRST, FIRST + second_half % SECOND)
+    spread = (jnp.broadcast_to(node_of, (node_count, lanes)) == iota((node_count, lanes), 0)).astype(BF16)
     wanted = dot_tn(places, spread)
-    chosen = (wanted == (iota((type_count, lanes), 1) % SOURCES).astype(F32)).astype(F32)
+    chosen = (wanted == source_of.astype(F32)).astype(F32)
     chosen_full = chosen[: full * 128].astype(BF16)
     chosen_tail = chosen[full * 128 :].astype(BF16)
     lane_node = iota((SOURCES, 128), 1) // q_width
-    nothing = jnp.zeros((SOURCES, 128), F32)
+    lower_lanes = iota((eq_width, 128), 1) < 64
     total_ref[...] = jnp.zeros_like(total_ref)
 
     leaf_count = ulist_ref.shape[1]
@@ -250,18 +274,30 @@
     def first_product(left, tail):
         return dot(left, chosen_full) + dot(tail, chosen_tail)
 
+    def block_rows(sents, first, count):
+        lines = []
+        for sent in sents:
+            blank = jnp.zeros((count, 128), F32)
+            for node in range(node_count):
+                own = sent[node % tile][first : first + count]
+                line = [own if place == node // tile else blank for place in range(node_count // tile)]
+                lines.append(jnp.concatenate(line, axis=1))
+        return lines
+
     def second_product(number, summed):
         lefts, rights = [], []
-        for step in range(chunk):
-            value = summed[step * eq_width : (step + 1) * eq_width]
-            high = value.astype(BF16).astype(F32)
-            lefts.append(jnp.concatenate([high, value - high], axis=0).astype(BF16))
-            row = number * chunk + step
-            sent = wide_ref[pl.ds(pl.multiple_of(row * SOURCES, SOURCES), SOURCES), :]
-            parts = [jnp.where(lane_node == place, sent, 0.0) for place in range(tile)]
-            for node in range(node_count):
-                line = [parts[node % tile] if place == node // tile else nothing for place in range(node_count // tile)]
-                rights.append(jnp.concatenate(line, axis=1))
+        for step in range(0, chunk, 2):
+            sents = []
+            for place in (step, step + 1):
+                row = number * chunk + place
+                sent = wide_ref[pl.ds(pl.multiple_of(row * SOURCES, SOURCES), SOURCES), :]
+                sents.append([jnp.where(lane_node == part, sent, 0.0) for part in range(tile)])
+            pair = [summed[place * eq_width : (place + 1) * eq_width] for place in (step, step + 1)]
+            tiles = [pair[0][:, :128], pair[1][:, :128], jnp.where(lower_lanes, pair[0][:, 128:], pair[1][:, 128:])]
+            for value in tiles:
+                high = value.astype(BF16).astype(F32)
+                lefts.append(jnp.concatenate([high, value - high], axis=0).astype(BF16))
+            rights += block_rows(sents, 0, FIRST) + block_rows(sents, FIRST, SECOND)
         product = dot(jnp.concatenate(lefts, axis=1), jnp.concatenate(rights, axis=0).astype(BF16))
         return product[:eq_width] + product[eq_width:]
 
@@ -571,8 +607,15 @@
             jax.ShapeDtypeStruct((level_rows, eq_width), F32),
         ),
         in_specs=[vmem, vmem, vmem, smem, vmem, vmem, vmem],
-        out_specs=(vmem,) * 6,
-        scratch_shapes=[pltpu.VMEM((8, node_rows, eq_width), F32)],
+        out_specs=(hbm,) * 4 + (vmem,) * 2,
+        scratch_shapes=[
+            pltpu.VMEM((8, node_rows, eq_width), F32),
+            pltpu.VMEM((2 * leaf_count, PIECE, 128), BF16),
+            pltpu.VMEM((2, 2 * leaf_count, 32, p_width), BF16),
+            pltpu.VMEM((leaf_count // 4, eq_width, 128), BF16),
+            pltpu.VMEM((leaf_count, q_width + 8, p_width), F32),
+            pltpu.SemaphoreType.DMA((node_count, 4)),
+        ],
         compiler_params=params,
         name="upward",
     )(points, dens, surface, counts, counts.reshape(1, leaf_count), up_inverse, shift_up)

time: 108 us -> 109 us (level)
  waiting for transfers between devices: 9.56 us -> 11 us
    ppermute x4, waiting for transfers between devices: 8.08 us -> 9.47 us  [shifted(): return (lax.ppermute(value, 'oct', up), lax.ppermute(value, 'oct', down))]
    pallas_call x1, Pallas kernels: 22.4 us -> 21 us  [local(): pl.pallas_call(far_kernel, out_shape=(jax.ShapeDtypeStruct((node_rows, eq...]
  transfers between devices with their start and end apart: 8 -> 8, of which waited for: 5 -> 5; matrix products, arithmetic and copies ran while one was open for 0% -> 0% of each run, Pallas kernels for 53% -> 52%
where the time goes in v10:
time: 109 us; the launch traced here: 108 us
  Pallas kernels  76.3 us (70%)
  starting transfers between devices  18.8 us (17%)
  waiting for transfers between devices  11 us (10%)
  other arithmetic  1.59 us (1%)
    pallas_call x1, Pallas kernels, local(): pl.pallas_call(near_kernel, out_shape=jax.ShapeDtypeStruct((leaf_count, q...  34.7 us
    pallas_call x1, Pallas kernels, local(): pl.pallas_call(far_kernel, out_shape=(jax.ShapeDtypeStruct((node_rows, eq...  21 us
    ppermute x4, starting transfers between devices, shifted(): return (lax.ppermute(value, 'oct', up), lax.ppermute(value, 'oct', down))  10.8 us
    pallas_call x1, Pallas kernels, local(): pl.pallas_call(lambda *refs: upward_kernel(level_count, *refs), out_shape...  10.7 us
    pallas_call x1, Pallas kernels, local(): pl.pallas_call(lambda *refs: final_kernel(level_count, *refs), out_shape=...  9.98 us
    ppermute x4, waiting for transfers between devices, shifted(): return (lax.ppermute(value, 'oct', up), lax.ppermute(value, 'oct', down))  9.47 us
    ppermute x4, starting transfers between devices, swapped(): lax.ppermute(value, 'oct', [(source, source ^ 1 << bit) for source in ran...  7.97 us
  transfers between devices with their start and end apart: 8, of which 5 were waited for; matrix products, arithmetic and copies ran while one was open for 0% of the time, Pallas kernels for 52%

profile of v10, /device:TPU:1, one launch (start us, length us, event | category | flops | bytes accessed | tf_op | source)
XLA Modules:
  0.0 107.8 jit_solution(11713475794086194288)
XLA Ops:
  0.0 10.7 %upward.1 = (bf16[128,64,128]{2,1,0:T(8,128)(2,1)}, bf16[2,128,32,128]{3,2,1,0:T(8,128)(2,1)}, bf16[16,152,128]{2,1,0:T(8,128)(2,1)}, f32[64,40,128]{2,1,0:T(8,1...) custom-call(f32[3,64,128]{2,1,0:T(8,128)} %bitcast.10, f32[64,32,128]{2,1,0:T(8,128)} %refs_1_.1, ...), custom_call_target="tpu_custom_call" | custom-call | tf_op jit(solution)/shard_map/upward/pallas_call | solution.py:599
  10.7 4.5 %collective-permute-start = (bf16[400,152]{1,0:T(8,128)(2,1)}, bf16[400,152]{1,0:T(8,128)(2,1)S(1)}, u32[]{:S(2)}, u32[]{:S(2)}) collective-permute-start(bf16[400,152]{1,0:T(8,128)(2,1)} %get-tuple-element.29.own_ref), channel_id=1, source_target_pairs={{0,1},{1,2},{2,3},{3,4},{4,5},{5,6},{6,7},{7,8},{8,9},{9,10},{10,1... | collective-permute-start | bytes 364808 | tf_op jit(solution)/shard_map/ppermute | solution.py:560
  15.2 1.9 %collective-permute-start.1 = (bf16[400,152]{1,0:T(8,128)(2,1)}, bf16[400,152]{1,0:T(8,128)(2,1)S(1)}, u32[]{:S(2)}, u32[]{:S(2)}) collective-permute-start(bf16[400,152]{1,0:T(8,128)(2,1)} %get-tuple-element.29.own_ref), channel_id=1, source_target_pairs={{1,0},{2,1},{3,2},{4,3},{5,4},{6,5},{7,6},{8,7},{9,8},{10,9},{11,1... | collective-permute-start | bytes 364808 | tf_op jit(solution)/shard_map/ppermute | solution.py:560
  17.1 1.1 collective-permute-done.lower_ref
  18.2 0.0 copy-start.1
  18.2 4.3 %collective-permute-done.1.upper_ref = bf16[400,152]{1,0:T(8,128)(2,1)S(1)} collective-permute-done((bf16[400,152]{1,0:T(8,128)(2,1)}, bf16[400,152]{1,0:T(8,128)(2,1)S(1)}, u32[]{:S(2)}, u32[]{:S(2)}) %collective-permute-start.1) | collective-permute-done | bytes 121632 | tf_op jit(solution)/shard_map/ppermute | solution.py:560
  22.5 0.0 copy-start.2
  22.5 0.9 fusion
  23.4 2.2 %collective-permute-start.2 = (f32[64,152]{1,0:T(8,128)S(1)}, f32[64,152]{1,0:T(8,128)S(1)}, u32[]{:S(2)}, u32[]{:S(2)}) collective-permute-start(f32[64,152]{1,0:T(8,128)S(1)} %fusion), channel_id=1, source_target_pairs={{0,2},{1,3},{2,0},{3,1},{4,6},{5,7},{6,4},{7,5},{8,10},{9,11},{10,... | collective-permute-start | bytes 116744 | tf_op jit(solution)/shard_map/ppermute | solution.py:564
  25.6 1.9 %collective-permute-start.3 = (f32[64,40,128]{2,1,0:T(8,128)}, f32[64,40,128]{2,1,0:T(8,128)S(1)}, u32[]{:S(2)}, u32[]{:S(2)}) collective-permute-start(f32[64,40,128]{2,1,0:T(8,128)} %get-tuple-element.36), channel_id=1, source_target_pairs={{0,1},{1,2},{2,3},{3,4},{4,5},{5,6},{6,7},{7,8},{8,9},{9,10},{10,1... | collective-permute-start | bytes 3932168 | tf_op jit(solution)/shard_map/ppermute | solution.py:560
  27.5 2.5 %collective-permute-start.4 = (f32[64,40,128]{2,1,0:T(8,128)}, f32[64,40,128]{2,1,0:T(8,128)S(1)}, u32[]{:S(2)}, u32[]{:S(2)}) collective-permute-start(f32[64,40,128]{2,1,0:T(8,128)} %get-tuple-element.36), channel_id=1, source_target_pairs={{1,0},{2,1},{3,2},{4,3},{5,4},{6,5},{7,6},{8,7},{9,8},{10,9},{11,1... | collective-permute-start | bytes 3932168 | tf_op jit(solution)/shard_map/ppermute | solution.py:560
  30.0 0.0 collective-permute-done.2
  30.1 2.1 %collective-permute-start.5 = (f32[64,152]{1,0:T(8,128)S(1)}, f32[64,152]{1,0:T(8,128)S(1)}, u32[]{:S(2)}, u32[]{:S(2)}) collective-permute-start(f32[64,152]{1,0:T(8,128)S(1)} %add.20), channel_id=1, source_target_pairs={{0,4},{1,5},{2,6},{3,7},{4,0},{5,1},{6,2},{7,3},{8,12},{9,13},{10,... | collective-permute-start | bytes 116744 | tf_op jit(solution)/shard_map/ppermute | solution.py:564
  32.2 0.0 copy-done.1
  32.2 0.0 copy-done.2
  32.2 21.0 %far.1 = (f32[256,152]{1,0:T(8,128)}, s32[1,128]{1,0:T(1,128)}, s32[32,128]{1,0:T(8,128)}, s32[8,128]{1,0:T(8,128)}) custom-call(bf16[400,152]{1,0:T(8,128)(2,1)} %copy-done.1, bf16[400,152]{1,0:T(8,128)(2,1)} %get-tuple-element.29.own_ref, bf16[400,152]{1,0:T(8,128)(2,1)} %copy-done.2, s32[8,316]{1,0:T(8,128)} %vlist_ref.1, s32[27,64]{1,0:T(8,128)} %bitcast.13, ...), custom_call_target="tpu_custom_call" | custom-call | flops 20000000000 | bytes 18000000 | tf_op jit(solution)/shard_map/far/pallas_call | solution.py:646
  53.2 3.3 %collective-permute-done.3.lower_ref = f32[64,40,128]{2,1,0:T(8,128)S(1)} collective-permute-done((f32[64,40,128]{2,1,0:T(8,128)}, f32[64,40,128]{2,1,0:T(8,128)S(1)}, u32[]{:S(2)}, u32[]{:S(2)}) %collective-permute-start.3) | collective-permute-done | bytes 1310752 | tf_op jit(solution)/shard_map/ppermute | solution.py:560
  56.4 0.0 copy-start.3
  56.4 0.9 collective-permute-done.4.upper_ref
  57.3 0.0 copy-start.4
  57.3 0.0 collective-permute-done.5
  57.3 0.0 copy-start
  57.3 1.4 %collective-permute-start.6 = (f32[32,152]{1,0:T(8,128)S(1)}, f32[32,152]{1,0:T(8,128)S(1)}, u32[]{:S(2)}, u32[]{:S(2)}) collective-permute-start(f32[32,152]{1,0:T(8,128)S(1)} %slice.24), channel_id=1, source_target_pairs={{0,8},{1,9},{2,10},{3,11},{4,12},{5,13},{6,14},{7,15},{8,0},{9,1},... | collective-permute-start | bytes 58376 | tf_op jit(solution)/shard_map/ppermute | solution.py:564
  58.7 1.5 %collective-permute-done.6 = f32[32,152]{1,0:T(8,128)S(1)} collective-permute-done((f32[32,152]{1,0:T(8,128)S(1)}, f32[32,152]{1,0:T(8,128)S(1)}, u32[]{:S(2)}, u32[]{:S(2)}) %collective-permute-start.6) | collective-permute-done | bytes 19488 | tf_op jit(solution)/shard_map/ppermute | solution.py:564
  60.2 2.3 %collective-permute-start.7 = (f32[32,152]{1,0:T(8,128)S(1)}, f32[32,152]{1,0:T(8,128)S(1)}, u32[]{:S(2)}, u32[]{:S(2)}) collective-permute-start(f32[32,152]{1,0:T(8,128)S(1)} %slice_add_fusion.1), channel_id=1, source_target_pairs={{0,16},{1,17},{2,18},{3,19},{4,20},{5,21},{6,22},{7,23},{8,24},{9,... | collective-permute-start | bytes 58376 | tf_op jit(solution)/shard_map/ppermute | solution.py:564
  62.5 0.0 copy-done.3
  62.5 0.0 copy-done.4
  62.5 34.7 %near.1.refs_3_ = f32[64,32,128]{2,1,0:T(8,128)} custom-call(s32[1,128]{1,0:T(1,128)} %get-tuple-element.41.step_ref, s32[4096]{0:T(1024)} %bitcast.14, s32[1024]{0:T(1024)} %bitcast.15, bf16[128,64,128]{2,1,0:T(8,128)(2,1)} %get-tuple-element.44.own_hbm, bf16[2,128,32,128]{3,2,1,0:T(8,128)(2,1)} %get-tuple-element.27.own_feature_hbm.refs_1_, ...), custom_call_target="tpu_custom_call" | custom-call | flops 30000001024 | bytes 10000000 | tf_op jit(solution)/shard_map/near/pallas_call | solution.py:675
  97.2 0.0 copy-done
  97.2 0.0 collective-permute-done.7
  97.2 0.6 add.23.refs_9_
  97.8 10.0 %final.1 = f32[64,32,128]{2,1,0:T(8,128)} custom-call(s32[64]{0:T(128)} %refs_0_.1, bf16[2,128,32,128]{3,2,1,0:T(8,128)(2,1)} %get-tuple-element.27.own_feature_hbm.refs_1_, bf16[16,152,128]{2,1,0:T(8,128)(2,1)} %get-tuple-element.28.refs_2_, f32[64,32,128]{2,1,0:T(8,128)} %near.1.refs_3_, f32[256,152]{1,0:T(8,128)} %get-tuple-element.47.refs_4_, ...), custom_call_target="tpu_custom_call" | custom-call | tf_op jit(solution)/shard_map/final/pallas_call | solution.py:692
  (5 shorter events, 0.0 us)
Async XLA Ops:
  10.7 7.5 %collective-permute-start = (bf16[400,152]{1,0:T(8,128)(2,1)}, bf16[400,152]{1,0:T(8,128)(2,1)S(1)}, u32[]{:S(2)}, u32[]{:S(2)}) collective-permute-start(bf16[400,152]{1,0:T(8,128)(2,1)} %get-tuple-element.29.own_ref), channel_id=1, source_target_pairs={{0,1},{1,2},{2,3},{3,4},{4,5},{5,6},{6,7},{7,8},{8,9},{9,10},{10,1... | collective-permute-start | bytes 364808 | tf_op jit(solution)/shard_map/ppermute | solution.py:560
  15.2 7.3 %collective-permute-start.1 = (bf16[400,152]{1,0:T(8,128)(2,1)}, bf16[400,152]{1,0:T(8,128)(2,1)S(1)}, u32[]{:S(2)}, u32[]{:S(2)}) collective-permute-start(bf16[400,152]{1,0:T(8,128)(2,1)} %get-tuple-element.29.own_ref), channel_id=1, source_target_pairs={{1,0},{2,1},{3,2},{4,3},{5,4},{6,5},{7,6},{8,7},{9,8},{10,9},{11,1... | collective-permute-start | bytes 364808 | tf_op jit(solution)/shard_map/ppermute | solution.py:560
  18.2 14.0 %copy-start.1 = (bf16[400,152]{1,0:T(8,128)(2,1)}, bf16[400,152]{1,0:T(8,128)(2,1)S(1)}, u32[]{:S(2)}) copy-start(bf16[400,152]{1,0:T(8,128)(2,1)S(1)} %collective-permute-done.lower_ref) | copy-start | bytes 364804
  22.5 9.7 %copy-start.2 = (bf16[400,152]{1,0:T(8,128)(2,1)}, bf16[400,152]{1,0:T(8,128)(2,1)S(1)}, u32[]{:S(2)}) copy-start(bf16[400,152]{1,0:T(8,128)(2,1)S(1)} %collective-permute-done.1.upper_ref) | copy-start | bytes 364804
  23.4 6.6 %collective-permute-start.2 = (f32[64,152]{1,0:T(8,128)S(1)}, f32[64,152]{1,0:T(8,128)S(1)}, u32[]{:S(2)}, u32[]{:S(2)}) collective-permute-start(f32[64,152]{1,0:T(8,128)S(1)} %fusion), channel_id=1, source_target_pairs={{0,2},{1,3},{2,0},{3,1},{4,6},{5,7},{6,4},{7,5},{8,10},{9,11},{10,... | collective-permute-start | bytes 116744 | tf_op jit(solution)/shard_map/ppermute | solution.py:564
  25.6 30.8 %collective-permute-start.3 = (f32[64,40,128]{2,1,0:T(8,128)}, f32[64,40,128]{2,1,0:T(8,128)S(1)}, u32[]{:S(2)}, u32[]{:S(2)}) collective-permute-start(f32[64,40,128]{2,1,0:T(8,128)} %get-tuple-element.36), channel_id=1, source_target_pairs={{0,1},{1,2},{2,3},{3,4},{4,5},{5,6},{6,7},{7,8},{8,9},{9,10},{10,1... | collective-permute-start | bytes 3932168 | tf_op jit(solution)/shard_map/ppermute | solution.py:560
  27.5 29.8 %collective-permute-start.4 = (f32[64,40,128]{2,1,0:T(8,128)}, f32[64,40,128]{2,1,0:T(8,128)S(1)}, u32[]{:S(2)}, u32[]{:S(2)}) collective-permute-start(f32[64,40,128]{2,1,0:T(8,128)} %get-tuple-element.36), channel_id=1, source_target_pairs={{1,0},{2,1},{3,2},{4,3},{5,4},{6,5},{7,6},{8,7},{9,8},{10,9},{11,1... | collective-permute-start | bytes 3932168 | tf_op jit(solution)/shard_map/ppermute | solution.py:560
  30.1 27.2 %collective-permute-start.5 = (f32[64,152]{1,0:T(8,128)S(1)}, f32[64,152]{1,0:T(8,128)S(1)}, u32[]{:S(2)}, u32[]{:S(2)}) collective-permute-start(f32[64,152]{1,0:T(8,128)S(1)} %add.20), channel_id=1, source_target_pairs={{0,4},{1,5},{2,6},{3,7},{4,0},{5,1},{6,2},{7,3},{8,12},{9,13},{10,... | collective-permute-start | bytes 116744 | tf_op jit(solution)/shard_map/ppermute | solution.py:564
  56.4 6.0 %copy-start.3 = (f32[64,40,128]{2,1,0:T(8,128)}, f32[64,40,128]{2,1,0:T(8,128)S(1)}, u32[]{:S(2)}) copy-start(f32[64,40,128]{2,1,0:T(8,128)S(1)} %collective-permute-done.3.lower_ref) | copy-start | bytes 3932164
  57.3 5.2 %copy-start.4 = (f32[64,40,128]{2,1,0:T(8,128)}, f32[64,40,128]{2,1,0:T(8,128)S(1)}, u32[]{:S(2)}) copy-start(f32[64,40,128]{2,1,0:T(8,128)S(1)} %collective-permute-done.4.upper_ref) | copy-start | bytes 3932164
  57.3 39.9 %copy-start = (f32[64,152]{1,0:T(8,128)}, f32[64,152]{1,0:T(8,128)S(1)}, u32[]{:S(2)}) copy-start(f32[64,152]{1,0:T(8,128)S(1)} %add.21.refs_8_) | copy-start | bytes 116740
  57.3 2.8 %collective-permute-start.6 = (f32[32,152]{1,0:T(8,128)S(1)}, f32[32,152]{1,0:T(8,128)S(1)}, u32[]{:S(2)}, u32[]{:S(2)}) collective-permute-start(f32[32,152]{1,0:T(8,128)S(1)} %slice.24), channel_id=1, source_target_pairs={{0,8},{1,9},{2,10},{3,11},{4,12},{5,13},{6,14},{7,15},{8,0},{9,1},... | collective-permute-start | bytes 58376 | tf_op jit(solution)/shard_map/ppermute | solution.py:564
  60.2 37.0 %collective-permute-start.7 = (f32[32,152]{1,0:T(8,128)S(1)}, f32[32,152]{1,0:T(8,128)S(1)}, u32[]{:S(2)}, u32[]{:S(2)}) collective-permute-start(f32[32,152]{1,0:T(8,128)S(1)} %slice_add_fusion.1), channel_id=1, source_target_pairs={{0,16},{1,17},{2,18},{3,19},{4,20},{5,21},{6,22},{7,23},{8,24},{9,... | collective-permute-start | bytes 58376 | tf_op jit(solution)/shard_map/ppermute | solution.py:564

commit v11 on v10

--- a/solution.py
+++ b/solution.py
@@ -124,24 +124,13 @@
 
 
 def upward_kernel(
-    level_count, points_ref, dens_ref, surface_ref, counts_ref, count_line_ref, up_ref, shift_ref, pack_hbm, feature_hbm, turned_hbm,
-    message_hbm, send_ref, slab_ref, check_ref, pack_ref, feature_ref, turned_ref, message_ref, sems
+    level_count, points_ref, dens_ref, surface_ref, counts_ref, count_line_ref, up_ref, shift_ref, pack_ref, send_ref,
+    slab_ref, check_ref
 ):
     leaf_count, q_width, p_width = dens_ref.shape
     eq_width = surface_ref.shape[2]
     node_count = leaf_count // 8
     lane = iota((q_width, p_width), 1)
-    row = iota((8, p_width), 0)
-
-    def copies_of(node):
-        leaves, pairs, fours = pl.ds(8 * node, 8), pl.ds(16 * node, 16), pl.ds(2 * node, 2)
-        ends = [
-            (pack_ref.at[pairs], pack_hbm.at[pairs]),
-            (feature_ref.at[:, pairs], feature_hbm.at[:, pairs]),
-            (turned_ref.at[fours], turned_hbm.at[fours]),
-            (message_ref.at[leaves], message_hbm.at[leaves]),
-        ]
-        return [pltpu.make_async_copy(*end, sems.at[node, number]) for number, end in enumerate(ends)]
 
     def node_step(node, carry):
         leaves = [node * 8 + child for child in range(8)]
@@ -163,19 +152,10 @@
         rows = [jnp.concatenate(split, axis=0).astype(BF16) for split in lists]
         firsts = [dot(row, value[0]) for row, value in zip(rows, values)]
         seconds = [dot(row[:q_width], value[1]) for row, value in zip(rows, values)]
-        fours = [jnp.concatenate(surfaces[first : first + 4], axis=0).astype(BF16).T for first in range(0, 8, 4)]
-        versions = [feature_versions(right) for right in rights]
-        for number, four in enumerate(fours):
-            turned_ref[2 * node + number] = four
         for child, leaf in enumerate(leaves):
-            message_ref[leaf, :q_width, :] = weights[child]
-            message_ref[leaf, q_width:, :] = jnp.where(row == 3, counts[child].astype(F32), coords[child])
             put_pack(pack_ref, leaf, packs[child])
-            put_features(feature_ref, leaf, versions[child])
             check = firsts[child][:q_width] + firsts[child][q_width:] + seconds[child]
             check_ref[child, pl.ds(pl.multiple_of(node * q_width, q_width), q_width), :] = check
-        for copy in copies_of(node):
-            copy.start()
         return carry
 
     lax.fori_loop(0, node_count, node_step, 0)
@@ -201,12 +181,31 @@
     line = jnp.concatenate([count_line_ref[...].astype(F32), jnp.zeros((1, eq_width - leaf_count), F32)], axis=1)
     send_ref[start : start + 16, :] = jnp.broadcast_to(line, (16, eq_width)).astype(BF16)
 
-    def wait_step(node, carry):
-        for copy in copies_of(node):
-            copy.wait()
+
+def outline_kernel(
+    points_ref, dens_ref, surface_ref, counts_ref, order_ref, feature_ref, turned_ref, message_ref
+):
+    leaf_count, q_width, p_width = dens_ref.shape
+    lane = iota((q_width, p_width), 1)
+    row = iota((8, p_width), 0)
+
+    def node_step(node, carry):
+        leaves = [node * 8 + child for child in range(8)]
+        counts = [counts_ref[leaf] for leaf in leaves]
+        weights = [jnp.where(lane < count, dens_ref[leaf], 0.0) for leaf, count in zip(leaves, counts)]
+        coords = [coords_of(points_ref, leaf) for leaf in leaves]
+        surfaces = [left_rows(pieces(coords_of(surface_ref, leaf))) for leaf in leaves]
+        versions = [feature_versions(right_rows(pieces(value))) for value in coords]
+        fours = [jnp.concatenate(surfaces[first : first + 4], axis=0).astype(BF16).T for first in range(0, 8, 4)]
+        for number, four in enumerate(fours):
+            turned_ref[2 * node + number] = four
+        for child, leaf in enumerate(leaves):
+            message_ref[leaf, :q_width, :] = weights[child]
+            message_ref[leaf, q_width:, :] = jnp.where(row == 3, counts[child].astype(F32), coords[child])
+            put_features(feature_ref, leaf, versions[child])
         return carry
 
-    lax.fori_loop(0, node_count, wait_step, 0)
+    lax.fori_loop(0, leaf_count // 8, node_step, 0)
 
 
 def far_kernel(
@@ -343,14 +342,16 @@
         feature_ref[half, 6 * leaf_count] = jnp.zeros((32, 128), BF16)
     for total_ref in total_refs:
         total_ref[...] = jnp.zeros_like(total_ref)
-    blank = jnp.zeros((32, p_width), F32)
-
     def pack_step(step, carry):
-        chosen = [(step * 4 + part, side) for part in range(4) for side in range(2)]
+        chosen = [(step * 4 + part, side) for side in range(2) for part in range(4)]
         sources = (lower_ref, upper_ref)
         weights = [weight_rows(sources[side][leaf, :q_width, :]) for leaf, side in chosen]
         versions = [feature_versions(right_rows(pieces(sources[side][leaf, q_width:, :]))) for leaf, side in chosen]
-        packs = [jnp.concatenate([blank] + value + [blank], axis=0).astype(BF16).T for value in weights]
+        packs = []
+        for part in range(0, len(chosen), 2):
+            (high, low), (next_high, next_low) = weights[part : part + 2]
+            both = jnp.concatenate([next_low, high, low, next_high], axis=0).astype(BF16).T
+            packs += [both, pltpu.roll(both.astype(F32), 64, 1).astype(BF16)]
         for (leaf, side), pack, version in zip(chosen, packs, versions):
             place = (1 + side) * leaf_count + leaf
             put_pack(pack_ref, place, pack)
@@ -414,9 +415,12 @@
 
     def turn_step(step, carry):
         sums = [[total_ref[step * 8 + part] for total_ref in total_refs] for part in range(8)]
-        turned = [sum(values[1:], values[0]).T for values in sums]
-        for part, value in enumerate(turned):
-            out_ref[step * 8 + part] = value[32 : 32 + q_width] + value[32 + q_width : 32 + 2 * q_width]
+        sums = [sum(values[1:], values[0]) for values in sums]
+        inner = (iota((p_width, 128), 1) >= 32) & (iota((p_width, 128), 1) < 96)
+        for part in range(0, 8, 2):
+            turned = jnp.where(inner, sums[part], pltpu.roll(sums[part + 1], 64, 1)).T
+            out_ref[step * 8 + part] = turned[32 : 32 + q_width] + turned[32 + q_width : 32 + 2 * q_width]
+            out_ref[step * 8 + part + 1] = turned[96 : 96 + q_width] + turned[:q_width]
         return carry
 
     lax.fori_loop(0, leaf_count // 8, turn_step, 0)
@@ -596,31 +600,34 @@
     ulist = ulist.T
     table = jnp.transpose(translate, (1, 2, 0))
 
-    pack, features, turned, message, send, slab = pl.pallas_call(
+    pack, send, slab = pl.pallas_call(
         lambda *refs: upward_kernel(level_count, *refs),
         out_shape=(
             jax.ShapeDtypeStruct((2 * leaf_count, PIECE, 128), BF16),
-            jax.ShapeDtypeStruct((2, 2 * leaf_count, 32, p_width), BF16),
-            jax.ShapeDtypeStruct((leaf_count // 4, eq_width, 128), BF16),
-            jax.ShapeDtypeStruct((leaf_count, q_width + 8, p_width), F32),
             jax.ShapeDtypeStruct((node_rows + 2 * level_rows + 16, eq_width), BF16),
             jax.ShapeDtypeStruct((level_rows, eq_width), F32),
         ),
         in_specs=[vmem, vmem, vmem, smem, vmem, vmem, vmem],
-        out_specs=(hbm,) * 4 + (vmem,) * 2,
-        scratch_shapes=[
-            pltpu.VMEM((8, node_rows, eq_width), F32),
-            pltpu.VMEM((2 * leaf_count, PIECE, 128), BF16),
-            pltpu.VMEM((2, 2 * leaf_count, 32, p_width), BF16),
-            pltpu.VMEM((leaf_count // 4, eq_width, 128), BF16),
-            pltpu.VMEM((leaf_count, q_width + 8, p_width), F32),
-            pltpu.SemaphoreType.DMA((node_count, 4)),
-        ],
+        out_specs=(vmem,) * 3,
+        scratch_shapes=[pltpu.VMEM((8, node_rows, eq_width), F32)],
         compiler_params=params,
         name="upward",
     )(points, dens, surface, counts, counts.reshape(1, leaf_count), up_inverse, shift_up)
 
     send_lower, send_upper = shifted(send, size)
+    features, turned, message = pl.pallas_call(
+        outline_kernel,
+        out_shape=(
+            jax.ShapeDtypeStruct((2, 2 * leaf_count, 32, p_width), BF16),
+            jax.ShapeDtypeStruct((leaf_count // 4, eq_width, 128), BF16),
+            jax.ShapeDtypeStruct((leaf_count, q_width + 8, p_width), F32),
+        ),
+        in_specs=[vmem, vmem, vmem, smem, hbm],
+        out_specs=(vmem,) * 3,
+        compiler_params=params,
+        cost_estimate=pl.CostEstimate(flops=4 * 10**9, bytes_accessed=10**7, transcendentals=0),
+        name="outline",
+    )(points, dens, surface, counts, slab)
     ends = slice(node_rows, node_rows + 2 * level_rows)
     partner = jnp.where(index & 1 == 1, send_lower[ends], send_upper[ends]).astype(F32)
     total = slab + (partner[:level_rows] + partner[level_rows:])

time: 109 us -> 110 us (level)
  Pallas kernels: 76.3 us -> 80.9 us
  waiting for transfers between devices: 11 us -> 7.41 us
    pallas_call x0 -> x1, Pallas kernels: none -> 4.91 us  [local(): pl.pallas_call(outline_kernel, out_shape=(jax.ShapeDtypeStruct((2, 2 * le...]
    ppermute x4, waiting for transfers between devices: 9.47 us -> 5.93 us  [shifted(): return (lax.ppermute(value, 'oct', up), lax.ppermute(value, 'oct', down))]
  transfers between devices with their start and end apart: 8 -> 8, of which waited for: 5 -> 4; matrix products, arithmetic and copies ran while one was open for 0% -> 0% of each run, Pallas kernels for 52% -> 56%
where the time goes in v11:
time: 110 us; the launch traced here: 108 us
  Pallas kernels  80.9 us (74%)
  starting transfers between devices  19.1 us (17%)
  waiting for transfers between devices  7.41 us (7%)
    pallas_call x1, Pallas kernels, local(): pl.pallas_call(near_kernel, out_shape=jax.ShapeDtypeStruct((leaf_count, q...  34.8 us
    pallas_call x1, Pallas kernels, local(): pl.pallas_call(far_kernel, out_shape=(jax.ShapeDtypeStruct((node_rows, eq...  21 us
    ppermute x4, starting transfers between devices, shifted(): return (lax.ppermute(value, 'oct', up), lax.ppermute(value, 'oct', down))  10.8 us
    pallas_call x1, Pallas kernels, local(): pl.pallas_call(lambda *refs: upward_kernel(level_count, *refs), out_shape...  10.2 us
    pallas_call x1, Pallas kernels, local(): pl.pallas_call(lambda *refs: final_kernel(level_count, *refs), out_shape=...  10 us
    ppermute x4, starting transfers between devices, swapped(): lax.ppermute(value, 'oct', [(source, source ^ 1 << bit) for source in ran...  8.26 us
    ppermute x4, waiting for transfers between devices, shifted(): return (lax.ppermute(value, 'oct', up), lax.ppermute(value, 'oct', down))  5.93 us
    pallas_call x1, Pallas kernels, local(): pl.pallas_call(outline_kernel, out_shape=(jax.ShapeDtypeStruct((2, 2 * le...  4.91 us
  transfers between devices with their start and end apart: 8, of which 4 were waited for; matrix products, arithmetic and copies ran while one was open for 0% of the time, Pallas kernels for 56%

profile of v11, /device:TPU:1, one launch (start us, length us, event | category | flops | bytes accessed | tf_op | source)
XLA Modules:
  0.0 108.2 jit_solution(8730729200605685221)
XLA Ops:
  0.0 10.2 %upward.1 = (bf16[128,64,128]{2,1,0:T(8,128)(2,1)}, bf16[400,152]{1,0:T(8,128)(2,1)}, f32[64,152]{1,0:T(8,128)}) custom-call(f32[3,64,128]{2,1,0:T(8,128)} %bitcast.11, f32[64,32,128]{2,1,0:T(8,128)} %dens_ref.1, f32[3,64,152]{2,1,0:T(8,128)} %bitcast.9, s32[64]{0:T(128)} %refs_0_.1, s32[1,64]{1,0:T(1,128)} %bitcast.13, f32[152,152]{1,0:T(8,128)} %refs_5_.2, ...), custom_call_target="tpu_custom_call" | custom-call | tf_op jit(solution)/shard_map/upward/pallas_call | solution.py:603
  10.2 4.5 %collective-permute-start = (bf16[400,152]{1,0:T(8,128)(2,1)}, bf16[400,152]{1,0:T(8,128)(2,1)S(1)}, u32[]{:S(2)}, u32[]{:S(2)}) collective-permute-start(bf16[400,152]{1,0:T(8,128)(2,1)} %get-tuple-element.30.own_ref), channel_id=1, source_target_pairs={{0,1},{1,2},{2,3},{3,4},{4,5},{5,6},{6,7},{7,8},{8,9},{9,10},{10,1... | collective-permute-start | bytes 364808 | tf_op jit(solution)/shard_map/ppermute | solution.py:564
  14.7 1.9 %collective-permute-start.1 = (bf16[400,152]{1,0:T(8,128)(2,1)}, bf16[400,152]{1,0:T(8,128)(2,1)S(1)}, u32[]{:S(2)}, u32[]{:S(2)}) collective-permute-start(bf16[400,152]{1,0:T(8,128)(2,1)} %get-tuple-element.30.own_ref), channel_id=1, source_target_pairs={{1,0},{2,1},{3,2},{4,3},{5,4},{6,5},{7,6},{8,7},{9,8},{10,9},{11,1... | collective-permute-start | bytes 364808 | tf_op jit(solution)/shard_map/ppermute | solution.py:564
  16.7 0.0 copy-start.1
  16.7 4.9 %outline.1 = (bf16[2,128,32,128]{3,2,1,0:T(8,128)(2,1)}, bf16[16,152,128]{2,1,0:T(8,128)(2,1)}, f32[64,40,128]{2,1,0:T(8,128)}) custom-call(f32[3,64,128]{2,1,0:T(8,128)} %bitcast.12, f32[64,32,128]{2,1,0:T(8,128)} %dens_ref.1, f32[3,64,152]{2,1,0:T(8,128)} %bitcast.10, s32[64]{0:T(128)} %refs_0_.1, f32[64,152]{1,0:T(8,128)} %get-tuple-element.27.order_ref), custom_call_target="tpu_custom_call" | custom-call | flops 4000000000 | bytes 10000000 | tf_op jit(solution)/shard_map/outline/pallas_call | solution.py:618
  21.6 0.0 collective-permute-done.lower_ref
  21.6 0.0 copy-start.2
  21.6 0.4 collective-permute-done.1.upper_ref
  22.0 0.0 copy-start.3
  22.1 0.0 copy-done.1
  22.1 2.2 %collective-permute-start.2 = (f32[64,152]{1,0:T(8,128)S(1)}, f32[64,152]{1,0:T(8,128)S(1)}, u32[]{:S(2)}, u32[]{:S(2)}) collective-permute-start(f32[64,152]{1,0:T(8,128)S(1)} %fusion), channel_id=1, source_target_pairs={{0,2},{1,3},{2,0},{3,1},{4,6},{5,7},{6,4},{7,5},{8,10},{9,11},{10,... | collective-permute-start | bytes 116744 | tf_op jit(solution)/shard_map/ppermute | solution.py:568
  24.3 1.9 %collective-permute-start.3 = (f32[64,40,128]{2,1,0:T(8,128)}, f32[64,40,128]{2,1,0:T(8,128)S(1)}, u32[]{:S(2)}, u32[]{:S(2)}) collective-permute-start(f32[64,40,128]{2,1,0:T(8,128)} %get-tuple-element.36), channel_id=1, source_target_pairs={{0,1},{1,2},{2,3},{3,4},{4,5},{5,6},{6,7},{7,8},{8,9},{9,10},{10,1... | collective-permute-start | bytes 3932168 | tf_op jit(solution)/shard_map/ppermute | solution.py:564
  26.2 2.5 %collective-permute-start.4 = (f32[64,40,128]{2,1,0:T(8,128)}, f32[64,40,128]{2,1,0:T(8,128)S(1)}, u32[]{:S(2)}, u32[]{:S(2)}) collective-permute-start(f32[64,40,128]{2,1,0:T(8,128)} %get-tuple-element.36), channel_id=1, source_target_pairs={{1,0},{2,1},{3,2},{4,3},{5,4},{6,5},{7,6},{8,7},{9,8},{10,9},{11,1... | collective-permute-start | bytes 3932168 | tf_op jit(solution)/shard_map/ppermute | solution.py:564
  28.7 0.0 collective-permute-done.2
  28.7 2.1 %collective-permute-start.5 = (f32[64,152]{1,0:T(8,128)S(1)}, f32[64,152]{1,0:T(8,128)S(1)}, u32[]{:S(2)}, u32[]{:S(2)}) collective-permute-start(f32[64,152]{1,0:T(8,128)S(1)} %add.20), channel_id=1, source_target_pairs={{0,4},{1,5},{2,6},{3,7},{4,0},{5,1},{6,2},{7,3},{8,12},{9,13},{10,... | collective-permute-start | bytes 116744 | tf_op jit(solution)/shard_map/ppermute | solution.py:568
  30.8 0.0 copy-done.2
  30.8 0.0 copy-done.3
  30.8 21.0 %far.1 = (f32[256,152]{1,0:T(8,128)}, s32[1,128]{1,0:T(1,128)}, s32[32,128]{1,0:T(8,128)}, s32[8,128]{1,0:T(8,128)}) custom-call(bf16[400,152]{1,0:T(8,128)(2,1)} %copy-done.2, bf16[400,152]{1,0:T(8,128)(2,1)} %get-tuple-element.30.own_ref, bf16[400,152]{1,0:T(8,128)(2,1)} %copy-done.3, s32[8,316]{1,0:T(8,128)} %vlist_ref.1, s32[27,64]{1,0:T(8,128)} %bitcast.15, ...), custom_call_target="tpu_custom_call" | custom-call | flops 20000000000 | bytes 18000000 | tf_op jit(solution)/shard_map/far/pallas_call | solution.py:653
  51.8 3.3 %collective-permute-done.3.lower_ref = f32[64,40,128]{2,1,0:T(8,128)S(1)} collective-permute-done((f32[64,40,128]{2,1,0:T(8,128)}, f32[64,40,128]{2,1,0:T(8,128)S(1)}, u32[]{:S(2)}, u32[]{:S(2)}) %collective-permute-start.3) | collective-permute-done | bytes 1310752 | tf_op jit(solution)/shard_map/ppermute | solution.py:564
  55.1 2.2 %collective-permute-done.4.upper_ref = f32[64,40,128]{2,1,0:T(8,128)S(1)} collective-permute-done((f32[64,40,128]{2,1,0:T(8,128)}, f32[64,40,128]{2,1,0:T(8,128)S(1)}, u32[]{:S(2)}, u32[]{:S(2)}) %collective-permute-start.4) | collective-permute-done | bytes 1310752 | tf_op jit(solution)/shard_map/ppermute | solution.py:564
  57.3 0.0 collective-permute-done.5
  57.3 0.0 copy-start
  57.3 1.4 %collective-permute-start.6 = (f32[32,152]{1,0:T(8,128)S(1)}, f32[32,152]{1,0:T(8,128)S(1)}, u32[]{:S(2)}, u32[]{:S(2)}) collective-permute-start(f32[32,152]{1,0:T(8,128)S(1)} %slice.24), channel_id=1, source_target_pairs={{0,8},{1,9},{2,10},{3,11},{4,12},{5,13},{6,14},{7,15},{8,0},{9,1},... | collective-permute-start | bytes 58376 | tf_op jit(solution)/shard_map/ppermute | solution.py:568
  58.7 1.5 %collective-permute-done.6 = f32[32,152]{1,0:T(8,128)S(1)} collective-permute-done((f32[32,152]{1,0:T(8,128)S(1)}, f32[32,152]{1,0:T(8,128)S(1)}, u32[]{:S(2)}, u32[]{:S(2)}) %collective-permute-start.6) | collective-permute-done | bytes 19488 | tf_op jit(solution)/shard_map/ppermute | solution.py:568
  60.2 2.6 %collective-permute-start.7 = (f32[32,152]{1,0:T(8,128)S(1)}, f32[32,152]{1,0:T(8,128)S(1)}, u32[]{:S(2)}, u32[]{:S(2)}) collective-permute-start(f32[32,152]{1,0:T(8,128)S(1)} %slice_add_fusion.1), channel_id=1, source_target_pairs={{0,16},{1,17},{2,18},{3,19},{4,20},{5,21},{6,22},{7,23},{8,24},{9,... | collective-permute-start | bytes 58376 | tf_op jit(solution)/shard_map/ppermute | solution.py:568
  62.8 0.0 copy-done.4
  62.8 0.0 copy-done.5
  62.8 34.8 %near.1.refs_3_ = f32[64,32,128]{2,1,0:T(8,128)} custom-call(s32[1,128]{1,0:T(1,128)} %get-tuple-element.41.step_ref, s32[4096]{0:T(1024)} %bitcast.16, s32[1024]{0:T(1024)} %bitcast.17, bf16[128,64,128]{2,1,0:T(8,128)(2,1)} %get-tuple-element.44.own_hbm, bf16[2,128,32,128]{3,2,1,0:T(8,128)(2,1)} %get-tuple-element.28.own_feature_hbm.refs_1_, ...), custom_call_target="tpu_custom_call" | custom-call | flops 30000001024 | bytes 10000000 | tf_op jit(solution)/shard_map/near/pallas_call | solution.py:682
  97.6 0.0 copy-done
  97.6 0.0 collective-permute-done.7
  97.6 0.6 add.23.refs_9_
  98.2 10.0 %final.1 = f32[64,32,128]{2,1,0:T(8,128)} custom-call(s32[64]{0:T(128)} %refs_0_.1, bf16[2,128,32,128]{3,2,1,0:T(8,128)(2,1)} %get-tuple-element.28.own_feature_hbm.refs_1_, bf16[16,152,128]{2,1,0:T(8,128)(2,1)} %get-tuple-element.29.refs_2_, f32[64,32,128]{2,1,0:T(8,128)} %near.1.refs_3_, f32[256,152]{1,0:T(8,128)} %get-tuple-element.47.refs_4_, ...), custom_call_target="tpu_custom_call" | custom-call | tf_op jit(solution)/shard_map/final/pallas_call | solution.py:699
  (8 shorter events, 0.1 us)
Async XLA Ops:
  10.2 11.4 %collective-permute-start = (bf16[400,152]{1,0:T(8,128)(2,1)}, bf16[400,152]{1,0:T(8,128)(2,1)S(1)}, u32[]{:S(2)}, u32[]{:S(2)}) collective-permute-start(bf16[400,152]{1,0:T(8,128)(2,1)} %get-tuple-element.30.own_ref), channel_id=1, source_target_pairs={{0,1},{1,2},{2,3},{3,4},{4,5},{5,6},{6,7},{7,8},{8,9},{9,10},{10,1... | collective-permute-start | bytes 364808 | tf_op jit(solution)/shard_map/ppermute | solution.py:564
  14.7 7.3 %collective-permute-start.1 = (bf16[400,152]{1,0:T(8,128)(2,1)}, bf16[400,152]{1,0:T(8,128)(2,1)S(1)}, u32[]{:S(2)}, u32[]{:S(2)}) collective-permute-start(bf16[400,152]{1,0:T(8,128)(2,1)} %get-tuple-element.30.own_ref), channel_id=1, source_target_pairs={{1,0},{2,1},{3,2},{4,3},{5,4},{6,5},{7,6},{8,7},{9,8},{10,9},{11,1... | collective-permute-start | bytes 364808 | tf_op jit(solution)/shard_map/ppermute | solution.py:564
  16.7 5.4 %copy-start.1 = (f32[64,152]{1,0:T(8,128)S(1)}, f32[64,152]{1,0:T(8,128)}, u32[]{:S(2)}) copy-start(f32[64,152]{1,0:T(8,128)} %get-tuple-element.27.order_ref) | copy-start | bytes 116740
  21.6 9.2 %copy-start.2 = (bf16[400,152]{1,0:T(8,128)(2,1)}, bf16[400,152]{1,0:T(8,128)(2,1)S(1)}, u32[]{:S(2)}) copy-start(bf16[400,152]{1,0:T(8,128)(2,1)S(1)} %collective-permute-done.lower_ref) | copy-start | bytes 364804
  22.0 8.8 %copy-start.3 = (bf16[400,152]{1,0:T(8,128)(2,1)}, bf16[400,152]{1,0:T(8,128)(2,1)S(1)}, u32[]{:S(2)}) copy-start(bf16[400,152]{1,0:T(8,128)(2,1)S(1)} %collective-permute-done.1.upper_ref) | copy-start | bytes 364804
  22.1 6.6 %collective-permute-start.2 = (f32[64,152]{1,0:T(8,128)S(1)}, f32[64,152]{1,0:T(8,128)S(1)}, u32[]{:S(2)}, u32[]{:S(2)}) collective-permute-start(f32[64,152]{1,0:T(8,128)S(1)} %fusion), channel_id=1, source_target_pairs={{0,2},{1,3},{2,0},{3,1},{4,6},{5,7},{6,4},{7,5},{8,10},{9,11},{10,... | collective-permute-start | bytes 116744 | tf_op jit(solution)/shard_map/ppermute | solution.py:568
  24.3 30.8 %collective-permute-start.3 = (f32[64,40,128]{2,1,0:T(8,128)}, f32[64,40,128]{2,1,0:T(8,128)S(1)}, u32[]{:S(2)}, u32[]{:S(2)}) collective-permute-start(f32[64,40,128]{2,1,0:T(8,128)} %get-tuple-element.36), channel_id=1, source_target_pairs={{0,1},{1,2},{2,3},{3,4},{4,5},{5,6},{6,7},{7,8},{8,9},{9,10},{10,1... | collective-permute-start | bytes 3932168 | tf_op jit(solution)/shard_map/ppermute | solution.py:564
  26.2 31.1 %collective-permute-start.4 = (f32[64,40,128]{2,1,0:T(8,128)}, f32[64,40,128]{2,1,0:T(8,128)S(1)}, u32[]{:S(2)}, u32[]{:S(2)}) collective-permute-start(f32[64,40,128]{2,1,0:T(8,128)} %get-tuple-element.36), channel_id=1, source_target_pairs={{1,0},{2,1},{3,2},{4,3},{5,4},{6,5},{7,6},{8,7},{9,8},{10,9},{11,1... | collective-permute-start | bytes 3932168 | tf_op jit(solution)/shard_map/ppermute | solution.py:564
  28.7 28.6 %collective-permute-start.5 = (f32[64,152]{1,0:T(8,128)S(1)}, f32[64,152]{1,0:T(8,128)S(1)}, u32[]{:S(2)}, u32[]{:S(2)}) collective-permute-start(f32[64,152]{1,0:T(8,128)S(1)} %add.20), channel_id=1, source_target_pairs={{0,4},{1,5},{2,6},{3,7},{4,0},{5,1},{6,2},{7,3},{8,12},{9,13},{10,... | collective-permute-start | bytes 116744 | tf_op jit(solution)/shard_map/ppermute | solution.py:568
  55.1 7.7 %copy-start.4 = (f32[64,40,128]{2,1,0:T(8,128)}, f32[64,40,128]{2,1,0:T(8,128)S(1)}, u32[]{:S(2)}) copy-start(f32[64,40,128]{2,1,0:T(8,128)S(1)} %collective-permute-done.3.lower_ref) | copy-start | bytes 3932164
  57.3 5.5 %copy-start.5 = (f32[64,40,128]{2,1,0:T(8,128)}, f32[64,40,128]{2,1,0:T(8,128)S(1)}, u32[]{:S(2)}) copy-start(f32[64,40,128]{2,1,0:T(8,128)S(1)} %collective-permute-done.4.upper_ref) | copy-start | bytes 3932164
  57.3 40.3 %copy-start = (f32[64,152]{1,0:T(8,128)}, f32[64,152]{1,0:T(8,128)S(1)}, u32[]{:S(2)}) copy-start(f32[64,152]{1,0:T(8,128)S(1)} %add.21.refs_8_) | copy-start | bytes 116740
  57.3 2.8 %collective-permute-start.6 = (f32[32,152]{1,0:T(8,128)S(1)}, f32[32,152]{1,0:T(8,128)S(1)}, u32[]{:S(2)}, u32[]{:S(2)}) collective-permute-start(f32[32,152]{1,0:T(8,128)S(1)} %slice.24), channel_id=1, source_target_pairs={{0,8},{1,9},{2,10},{3,11},{4,12},{5,13},{6,14},{7,15},{8,0},{9,1},... | collective-permute-start | bytes 58376 | tf_op jit(solution)/shard_map/ppermute | solution.py:568
  60.2 37.4 %collective-permute-start.7 = (f32[32,152]{1,0:T(8,128)S(1)}, f32[32,152]{1,0:T(8,128)S(1)}, u32[]{:S(2)}, u32[]{:S(2)}) collective-permute-start(f32[32,152]{1,0:T(8,128)S(1)} %slice_add_fusion.1), channel_id=1, source_target_pairs={{0,16},{1,17},{2,18},{3,19},{4,20},{5,21},{6,22},{7,23},{8,24},{9,... | collective-permute-start | bytes 58376 | tf_op jit(solution)/shard_map/ppermute | solution.py:568

commit v12 on v11

--- a/solution.py
+++ b/solution.py
@@ -187,7 +187,6 @@
 ):
     leaf_count, q_width, p_width = dens_ref.shape
     lane = iota((q_width, p_width), 1)
-    row = iota((8, p_width), 0)
 
     def node_step(node, carry):
         leaves = [node * 8 + child for child in range(8)]
@@ -200,9 +199,11 @@
         for number, four in enumerate(fours):
             turned_ref[2 * node + number] = four
         for child, leaf in enumerate(leaves):
-            message_ref[leaf, :q_width, :] = weights[child]
-            message_ref[leaf, q_width:, :] = jnp.where(row == 3, counts[child].astype(F32), coords[child])
+            pair, side = node * 4 + child // 2, child % 2
+            message_ref[pair, side * q_width : (side + 1) * q_width, :] = weights[child]
             put_features(feature_ref, leaf, versions[child])
+        for number in range(4):
+            message_ref[node * 4 + number, 2 * q_width :, :] = paired(coords[2 * number], coords[2 * number + 1])
         return carry
 
     lax.fori_loop(0, leaf_count // 8, node_step, 0)
@@ -343,17 +344,22 @@
     for total_ref in total_refs:
         total_ref[...] = jnp.zeros_like(total_ref)
     def pack_step(step, carry):
-        chosen = [(step * 4 + part, side) for side in range(2) for part in range(4)]
+        chosen = [(part, side) for side in range(2) for part in range(4)]
         sources = (lower_ref, upper_ref)
-        weights = [weight_rows(sources[side][leaf, :q_width, :]) for leaf, side in chosen]
-        versions = [feature_versions(right_rows(pieces(sources[side][leaf, q_width:, :]))) for leaf, side in chosen]
+        weights, versions = [], []
+        for part, side in chosen:
+            place, half = step * 2 + part // 2, part % 2
+            weights.append(weight_rows(sources[side][place, half * q_width : (half + 1) * q_width, :]))
+            tail = sources[side][place, 2 * q_width :, :]
+            tail = pltpu.roll(tail, 4, 0) if half else tail
+            versions.append(feature_versions(right_rows(pieces(tail))))
         packs = []
         for part in range(0, len(chosen), 2):
             (high, low), (next_high, next_low) = weights[part : part + 2]
             both = jnp.concatenate([next_low, high, low, next_high], axis=0).astype(BF16).T
             packs += [both, pltpu.roll(both.astype(F32), 64, 1).astype(BF16)]
-        for (leaf, side), pack, version in zip(chosen, packs, versions):
-            place = (1 + side) * leaf_count + leaf
+        for (part, side), pack, version in zip(chosen, packs, versions):
+            place = (1 + side) * leaf_count + step * 4 + part
             put_pack(pack_ref, place, pack)
             put_features(feature_ref, place, version)
         return carry
@@ -564,8 +570,8 @@
     return lax.ppermute(value, "oct", up), lax.ppermute(value, "oct", down)
 
 
-def swapped(value, size, bit):
-    return lax.ppermute(value, "oct", [(source, source ^ (1 << bit)) for source in range(size)])
+def swapped(value, size, mask):
+    return lax.ppermute(value, "oct", [(source, source ^ mask) for source in range(size)])
 
 
 def local(
@@ -620,7 +626,7 @@
         out_shape=(
             jax.ShapeDtypeStruct((2, 2 * leaf_count, 32, p_width), BF16),
             jax.ShapeDtypeStruct((leaf_count // 4, eq_width, 128), BF16),
-            jax.ShapeDtypeStruct((leaf_count, q_width + 8, p_width), F32),
+            jax.ShapeDtypeStruct((leaf_count // 2, 2 * q_width + 8, p_width), F32),
         ),
         in_specs=[vmem, vmem, vmem, smem, hbm],
         out_specs=(vmem,) * 3,
@@ -628,25 +634,13 @@
         cost_estimate=pl.CostEstimate(flops=4 * 10**9, bytes_accessed=10**7, transcendentals=0),
         name="outline",
     )(points, dens, surface, counts, slab)
+    lower, upper = shifted(message, size)
+    send_lower, send_upper, features = lax.optimization_barrier((send_lower, send_upper, features))
     ends = slice(node_rows, node_rows + 2 * level_rows)
     partner = jnp.where(index & 1 == 1, send_lower[ends], send_upper[ends]).astype(F32)
     total = slab + (partner[:level_rows] + partner[level_rows:])
-    message, total = lax.optimization_barrier((message, total))
-    lower, upper = shifted(message, size)
-    exchanges = [(level, bit) for level in range(level_count) for bit in range(max(1, 3 * level), min(3 * level + 3, bits))]
-    tops = []
-
-    def exchange(total, wanted):
-        level, bit = wanted
-        if level and bit == 3 * level:
-            tops.append(total)
-            total = total[q_width:]
-        return total, swapped(total, size, bit)
-
-    early, late = exchanges[:2], exchanges[2:]
-    total, arrived = exchange(total, early[0])
-    total = total + arrived
-    total, arrived = exchange(total, early[1])
+    total = total + swapped(total, size, 2)
+    arrived = swapped(total, size, 4)
     send_lower, total = lax.optimization_barrier((send_lower, total))
 
     table = table.reshape(eq_width * eq_width, type_count)
@@ -675,10 +669,10 @@
     far_node, lower, upper = lax.optimization_barrier((far_node, lower, upper))
 
     far_node, total, arrived = lax.optimization_barrier((far_node, total, arrived))
-    for wanted in late:
-        total = total + arrived
-        total, arrived = exchange(total, wanted)
-    steps, total = lax.optimization_barrier((steps, total))
+    total = total + arrived
+    shares = total[q_width:]
+    others = [swapped(shares, size, mask << 3) for mask in range(1, size >> 3)]
+    steps, shares = lax.optimization_barrier((steps, shares))
     near = pl.pallas_call(
         near_kernel,
         out_shape=jax.ShapeDtypeStruct((leaf_count, q_width, p_width), F32),
@@ -695,7 +689,11 @@
         name="near",
     )(steps, piece_table.reshape(-1), items.reshape(-1), pack, features, lower, upper)
 
-    tops.append(total + arrived)
+    tops = [total]
+    for level in range(1, level_count):
+        rows = slice((level - 1) * q_width, level * q_width)
+        group = 1 << (min(3 * level + 3, bits) - 3)
+        tops.append(sum([other[rows] for other in others[: group - 1]], shares[rows]))
     return pl.pallas_call(
         lambda *refs: final_kernel(level_count, *refs),
         out_shape=jax.ShapeDtypeStruct((leaf_count, q_width, p_width), F32),

time: 110 us -> 104 us (0.945)
  waiting for transfers between devices: 7.41 us -> 3.13 us
    ppermute x4, waiting for transfers between devices: 5.93 us -> 3.11 us  [shifted(): return (lax.ppermute(value, 'oct', up), lax.ppermute(value, 'oct', down))]
    ppermute x4 -> x5, waiting for transfers between devices: 1.48 us -> 0.01 us  [swapped(): lax.ppermute(value, 'oct', [(source, source ^ mask) for source in range(s...]
    ppermute x4 -> x5, starting transfers between devices: 8.26 us -> 8.07 us  [swapped(): lax.ppermute(value, 'oct', [(source, source ^ mask) for source in range(s...]
  transfers between devices with their start and end apart: 8 -> 9, of which waited for: 4 -> 3; matrix products, arithmetic and copies ran while one was open for 0% -> 0% of each run, Pallas kernels for 56% -> 58%
where the time goes in v12:
time: 104 us; the launch traced here: 103 us
  Pallas kernels  80 us (77%)
  starting transfers between devices  18.9 us (18%)
  waiting for transfers between devices  3.13 us (3%)
    pallas_call x1, Pallas kernels, local(): pl.pallas_call(near_kernel, out_shape=jax.ShapeDtypeStruct((leaf_count, q...  33.9 us
    pallas_call x1, Pallas kernels, local(): pl.pallas_call(far_kernel, out_shape=(jax.ShapeDtypeStruct((node_rows, eq...  21 us
    ppermute x4, starting transfers between devices, shifted(): return (lax.ppermute(value, 'oct', up), lax.ppermute(value, 'oct', down))  10.8 us
    pallas_call x1, Pallas kernels, local(): pl.pallas_call(lambda *refs: upward_kernel(level_count, *refs), out_shape...  10.2 us
    pallas_call x1, Pallas kernels, local(): pl.pallas_call(lambda *refs: final_kernel(level_count, *refs), out_shape=...  9.99 us
    ppermute x5, starting transfers between devices, swapped(): lax.ppermute(value, 'oct', [(source, source ^ mask) for source in range(s...  8.07 us
    pallas_call x1, Pallas kernels, local(): pl.pallas_call(outline_kernel, out_shape=(jax.ShapeDtypeStruct((2, 2 * le...  4.85 us
    ppermute x4, waiting for transfers between devices, shifted(): return (lax.ppermute(value, 'oct', up), lax.ppermute(value, 'oct', down))  3.11 us
  transfers between devices with their start and end apart: 9, of which 3 were waited for; matrix products, arithmetic and copies ran while one was open for 0% of the time, Pallas kernels for 58%

profile of v12, /device:TPU:1, one launch (start us, length us, event | category | flops | bytes accessed | tf_op | source)
XLA Modules:
  0.0 102.8 jit_solution(7981936519538935380)
XLA Ops:
  0.0 10.2 %upward.1 = (bf16[128,64,128]{2,1,0:T(8,128)(2,1)}, bf16[400,152]{1,0:T(8,128)(2,1)}, f32[64,152]{1,0:T(8,128)}) custom-call(f32[3,64,128]{2,1,0:T(8,128)} %bitcast.11, f32[64,32,128]{2,1,0:T(8,128)} %dens_ref.1, f32[3,64,152]{2,1,0:T(8,128)} %bitcast.9, s32[64]{0:T(128)} %refs_0_.1, s32[1,64]{1,0:T(1,128)} %bitcast.13, f32[152,152]{1,0:T(8,128)} %refs_5_.2, ...), custom_call_target="tpu_custom_call" | custom-call | tf_op jit(solution)/shard_map/upward/pallas_call | solution.py:609
  10.2 4.5 %collective-permute-start = (bf16[400,152]{1,0:T(8,128)(2,1)}, bf16[400,152]{1,0:T(8,128)(2,1)S(1)}, u32[]{:S(2)}, u32[]{:S(2)}) collective-permute-start(bf16[400,152]{1,0:T(8,128)(2,1)} %get-tuple-element.28.own_ref), channel_id=1, source_target_pairs={{0,1},{1,2},{2,3},{3,4},{4,5},{5,6},{6,7},{7,8},{8,9},{9,10},{10,1... | collective-permute-start | bytes 364808 | tf_op jit(solution)/shard_map/ppermute | solution.py:570
  14.7 1.9 %collective-permute-start.1 = (bf16[400,152]{1,0:T(8,128)(2,1)}, bf16[400,152]{1,0:T(8,128)(2,1)S(1)}, u32[]{:S(2)}, u32[]{:S(2)}) collective-permute-start(bf16[400,152]{1,0:T(8,128)(2,1)} %get-tuple-element.28.own_ref), channel_id=1, source_target_pairs={{1,0},{2,1},{3,2},{4,3},{5,4},{6,5},{7,6},{8,7},{9,8},{10,9},{11,1... | collective-permute-start | bytes 364808 | tf_op jit(solution)/shard_map/ppermute | solution.py:570
  16.7 0.0 copy-start.1
  16.7 4.8 %outline.1 = (bf16[2,128,32,128]{3,2,1,0:T(8,128)(2,1)}, bf16[16,152,128]{2,1,0:T(8,128)(2,1)}, f32[32,72,128]{2,1,0:T(8,128)}) custom-call(f32[3,64,128]{2,1,0:T(8,128)} %bitcast.12, f32[64,32,128]{2,1,0:T(8,128)} %dens_ref.1, f32[3,64,152]{2,1,0:T(8,128)} %bitcast.10, s32[64]{0:T(128)} %refs_0_.1, f32[64,152]{1,0:T(8,128)} %get-tuple-element.29.order_ref), custom_call_target="tpu_custom_call" | custom-call | flops 4000000000 | bytes 10000000 | tf_op jit(solution)/shard_map/outline/pallas_call | solution.py:624
  21.5 0.0 collective-permute-done.lower_ref
  21.5 0.5 collective-permute-done.1.upper_ref
  22.0 0.0 copy-done.1
  22.1 2.2 %collective-permute-start.2 = (f32[64,152]{1,0:T(8,128)S(1)}, f32[64,152]{1,0:T(8,128)S(1)}, u32[]{:S(2)}, u32[]{:S(2)}) collective-permute-start(f32[64,152]{1,0:T(8,128)S(1)} %fusion), channel_id=1, source_target_pairs={{0,2},{1,3},{2,0},{3,1},{4,6},{5,7},{6,4},{7,5},{8,10},{9,11},{10,... | collective-permute-start | bytes 116744 | tf_op jit(solution)/shard_map/ppermute | solution.py:574
  24.2 1.9 %collective-permute-start.3 = (f32[32,72,128]{2,1,0:T(8,128)}, f32[32,72,128]{2,1,0:T(8,128)S(1)}, u32[]{:S(2)}, u32[]{:S(2)}) collective-permute-start(f32[32,72,128]{2,1,0:T(8,128)} %get-tuple-element.38), channel_id=1, source_target_pairs={{0,1},{1,2},{2,3},{3,4},{4,5},{5,6},{6,7},{7,8},{8,9},{9,10},{10,1... | collective-permute-start | bytes 3538952 | tf_op jit(solution)/shard_map/ppermute | solution.py:570
  26.2 2.5 %collective-permute-start.4 = (f32[32,72,128]{2,1,0:T(8,128)}, f32[32,72,128]{2,1,0:T(8,128)S(1)}, u32[]{:S(2)}, u32[]{:S(2)}) collective-permute-start(f32[32,72,128]{2,1,0:T(8,128)} %get-tuple-element.38), channel_id=1, source_target_pairs={{1,0},{2,1},{3,2},{4,3},{5,4},{6,5},{7,6},{8,7},{9,8},{10,9},{11,1... | collective-permute-start | bytes 3538952 | tf_op jit(solution)/shard_map/ppermute | solution.py:570
  28.6 0.0 collective-permute-done.2
  28.7 2.1 %collective-permute-start.5 = (f32[64,152]{1,0:T(8,128)S(1)}, f32[64,152]{1,0:T(8,128)S(1)}, u32[]{:S(2)}, u32[]{:S(2)}) collective-permute-start(f32[64,152]{1,0:T(8,128)S(1)} %add.23), channel_id=1, source_target_pairs={{0,4},{1,5},{2,6},{3,7},{4,0},{5,1},{6,2},{7,3},{8,12},{9,13},{10,... | collective-permute-start | bytes 116744 | tf_op jit(solution)/shard_map/ppermute | solution.py:574
  30.8 0.0 copy-done.2
  30.8 0.0 copy-done.3
  30.8 21.0 %far.1 = (f32[256,152]{1,0:T(8,128)}, s32[1,128]{1,0:T(1,128)}, s32[32,128]{1,0:T(8,128)}, s32[8,128]{1,0:T(8,128)}) custom-call(bf16[400,152]{1,0:T(8,128)(2,1)} %copy-done.2, bf16[400,152]{1,0:T(8,128)(2,1)} %get-tuple-element.28.own_ref, bf16[400,152]{1,0:T(8,128)(2,1)} %copy-done.3, s32[8,316]{1,0:T(8,128)} %vlist_ref.1, s32[27,64]{1,0:T(8,128)} %bitcast.15, ...), custom_call_target="tpu_custom_call" | custom-call | flops 20000000000 | bytes 18000000 | tf_op jit(solution)/shard_map/far/pallas_call | solution.py:647
  51.8 0.4 collective-permute-done.3.lower_ref
  52.2 2.2 %collective-permute-done.4.upper_ref = f32[32,72,128]{2,1,0:T(8,128)S(1)} collective-permute-done((f32[32,72,128]{2,1,0:T(8,128)}, f32[32,72,128]{2,1,0:T(8,128)S(1)}, u32[]{:S(2)}, u32[]{:S(2)}) %collective-permute-start.4) | collective-permute-done | bytes 1179680 | tf_op jit(solution)/shard_map/ppermute | solution.py:570
  54.4 0.0 collective-permute-done.5
  54.4 0.0 copy-start
  54.5 3.4 %collective-permute-start.8 = (f32[32,152]{1,0:T(8,128)S(1)}, f32[32,152]{1,0:T(8,128)S(1)}, u32[]{:S(2)}, u32[]{:S(2)}) collective-permute-start(f32[32,152]{1,0:T(8,128)S(1)} %slice.22), channel_id=1, source_target_pairs={{0,24},{1,25},{2,26},{3,27},{4,28},{5,29},{6,30},{7,31},{8,16},{9,... | collective-permute-start | bytes 58376 | tf_op jit(solution)/shard_map/ppermute | solution.py:574
  57.9 0.0 collective-permute-start.7
  57.9 0.4 collective-permute-start.6
  58.2 0.0 copy-done.4
  58.2 0.0 copy-done.5
  58.2 33.9 %near.1.refs_3_ = f32[64,32,128]{2,1,0:T(8,128)} custom-call(s32[1,128]{1,0:T(1,128)} %get-tuple-element.43.step_ref, s32[4096]{0:T(1024)} %bitcast.16, s32[1024]{0:T(1024)} %bitcast.17, bf16[128,64,128]{2,1,0:T(8,128)(2,1)} %get-tuple-element.46.own_hbm, bf16[2,128,32,128]{3,2,1,0:T(8,128)(2,1)} %get-tuple-element.31.own_feature_hbm.refs_1_, ...), custom_call_target="tpu_custom_call" | custom-call | flops 30000001024 | bytes 10000000 | tf_op jit(solution)/shard_map/near/pallas_call | solution.py:676
  92.2 0.0 copy-done
  92.2 0.0 collective-permute-done.8
  92.2 0.0 collective-permute-done.7
  92.2 0.0 collective-permute-done.6
  92.2 0.6 add_add_fusion.refs_9_
  92.8 10.0 %final.1 = f32[64,32,128]{2,1,0:T(8,128)} custom-call(s32[64]{0:T(128)} %refs_0_.1, bf16[2,128,32,128]{3,2,1,0:T(8,128)(2,1)} %get-tuple-element.31.own_feature_hbm.refs_1_, bf16[16,152,128]{2,1,0:T(8,128)(2,1)} %get-tuple-element.32.refs_2_, f32[64,32,128]{2,1,0:T(8,128)} %near.1.refs_3_, f32[256,152]{1,0:T(8,128)} %get-tuple-element.49.refs_4_, ...), custom_call_target="tpu_custom_call" | custom-call | tf_op jit(solution)/shard_map/final/pallas_call | solution.py:697
  (9 shorter events, 0.1 us)
Async XLA Ops:
  10.2 11.3 %collective-permute-start = (bf16[400,152]{1,0:T(8,128)(2,1)}, bf16[400,152]{1,0:T(8,128)(2,1)S(1)}, u32[]{:S(2)}, u32[]{:S(2)}) collective-permute-start(bf16[400,152]{1,0:T(8,128)(2,1)} %get-tuple-element.28.own_ref), channel_id=1, source_target_pairs={{0,1},{1,2},{2,3},{3,4},{4,5},{5,6},{6,7},{7,8},{8,9},{9,10},{10,1... | collective-permute-start | bytes 364808 | tf_op jit(solution)/shard_map/ppermute | solution.py:570
  14.7 7.3 %collective-permute-start.1 = (bf16[400,152]{1,0:T(8,128)(2,1)}, bf16[400,152]{1,0:T(8,128)(2,1)S(1)}, u32[]{:S(2)}, u32[]{:S(2)}) collective-permute-start(bf16[400,152]{1,0:T(8,128)(2,1)} %get-tuple-element.28.own_ref), channel_id=1, source_target_pairs={{1,0},{2,1},{3,2},{4,3},{5,4},{6,5},{7,6},{8,7},{9,8},{10,9},{11,1... | collective-permute-start | bytes 364808 | tf_op jit(solution)/shard_map/ppermute | solution.py:570
  16.7 5.4 %copy-start.1 = (f32[64,152]{1,0:T(8,128)S(1)}, f32[64,152]{1,0:T(8,128)}, u32[]{:S(2)}) copy-start(f32[64,152]{1,0:T(8,128)} %get-tuple-element.29.order_ref) | copy-start | bytes 116740
  21.5 9.3 %copy-start.2 = (bf16[400,152]{1,0:T(8,128)(2,1)}, bf16[400,152]{1,0:T(8,128)(2,1)S(1)}, u32[]{:S(2)}) copy-start(bf16[400,152]{1,0:T(8,128)(2,1)S(1)} %collective-permute-done.lower_ref) | copy-start | bytes 364804
  22.0 8.8 %copy-start.3 = (bf16[400,152]{1,0:T(8,128)(2,1)}, bf16[400,152]{1,0:T(8,128)(2,1)S(1)}, u32[]{:S(2)}) copy-start(bf16[400,152]{1,0:T(8,128)(2,1)S(1)} %collective-permute-done.1.upper_ref) | copy-start | bytes 364804
  22.1 6.6 %collective-permute-start.2 = (f32[64,152]{1,0:T(8,128)S(1)}, f32[64,152]{1,0:T(8,128)S(1)}, u32[]{:S(2)}, u32[]{:S(2)}) collective-permute-start(f32[64,152]{1,0:T(8,128)S(1)} %fusion), channel_id=1, source_target_pairs={{0,2},{1,3},{2,0},{3,1},{4,6},{5,7},{6,4},{7,5},{8,10},{9,11},{10,... | collective-permute-start | bytes 116744 | tf_op jit(solution)/shard_map/ppermute | solution.py:574
  24.2 28.0 %collective-permute-start.3 = (f32[32,72,128]{2,1,0:T(8,128)}, f32[32,72,128]{2,1,0:T(8,128)S(1)}, u32[]{:S(2)}, u32[]{:S(2)}) collective-permute-start(f32[32,72,128]{2,1,0:T(8,128)} %get-tuple-element.38), channel_id=1, source_target_pairs={{0,1},{1,2},{2,3},{3,4},{4,5},{5,6},{6,7},{7,8},{8,9},{9,10},{10,1... | collective-permute-start | bytes 3538952 | tf_op jit(solution)/shard_map/ppermute | solution.py:570
  26.2 28.3 %collective-permute-start.4 = (f32[32,72,128]{2,1,0:T(8,128)}, f32[32,72,128]{2,1,0:T(8,128)S(1)}, u32[]{:S(2)}, u32[]{:S(2)}) collective-permute-start(f32[32,72,128]{2,1,0:T(8,128)} %get-tuple-element.38), channel_id=1, source_target_pairs={{1,0},{2,1},{3,2},{4,3},{5,4},{6,5},{7,6},{8,7},{9,8},{10,9},{11,1... | collective-permute-start | bytes 3538952 | tf_op jit(solution)/shard_map/ppermute | solution.py:570
  28.7 25.7 %collective-permute-start.5 = (f32[64,152]{1,0:T(8,128)S(1)}, f32[64,152]{1,0:T(8,128)S(1)}, u32[]{:S(2)}, u32[]{:S(2)}) collective-permute-start(f32[64,152]{1,0:T(8,128)S(1)} %add.23), channel_id=1, source_target_pairs={{0,4},{1,5},{2,6},{3,7},{4,0},{5,1},{6,2},{7,3},{8,12},{9,13},{10,... | collective-permute-start | bytes 116744 | tf_op jit(solution)/shard_map/ppermute | solution.py:574
  52.2 6.0 %copy-start.4 = (f32[32,72,128]{2,1,0:T(8,128)}, f32[32,72,128]{2,1,0:T(8,128)S(1)}, u32[]{:S(2)}) copy-start(f32[32,72,128]{2,1,0:T(8,128)S(1)} %collective-permute-done.3.lower_ref) | copy-start | bytes 3538948
  54.4 3.8 %copy-start.5 = (f32[32,72,128]{2,1,0:T(8,128)}, f32[32,72,128]{2,1,0:T(8,128)S(1)}, u32[]{:S(2)}) copy-start(f32[32,72,128]{2,1,0:T(8,128)S(1)} %collective-permute-done.4.upper_ref) | copy-start | bytes 3538948
  54.4 37.7 %copy-start = (f32[64,152]{1,0:T(8,128)}, f32[64,152]{1,0:T(8,128)S(1)}, u32[]{:S(2)}) copy-start(f32[64,152]{1,0:T(8,128)S(1)} %add.24.refs_8_) | copy-start | bytes 116740
  54.5 37.7 %collective-permute-start.8 = (f32[32,152]{1,0:T(8,128)S(1)}, f32[32,152]{1,0:T(8,128)S(1)}, u32[]{:S(2)}, u32[]{:S(2)}) collective-permute-start(f32[32,152]{1,0:T(8,128)S(1)} %slice.22), channel_id=1, source_target_pairs={{0,24},{1,25},{2,26},{3,27},{4,28},{5,29},{6,30},{7,31},{8,16},{9,... | collective-permute-start | bytes 58376 | tf_op jit(solution)/shard_map/ppermute | solution.py:574
  57.9 34.3 %collective-permute-start.7 = (f32[32,152]{1,0:T(8,128)S(1)}, f32[32,152]{1,0:T(8,128)S(1)}, u32[]{:S(2)}, u32[]{:S(2)}) collective-permute-start(f32[32,152]{1,0:T(8,128)S(1)} %slice.22), channel_id=1, source_target_pairs={{0,16},{1,17},{2,18},{3,19},{4,20},{5,21},{6,22},{7,23},{8,24},{9,... | collective-permute-start | bytes 58376 | tf_op jit(solution)/shard_map/ppermute | solution.py:574
  57.9 34.3 %collective-permute-start.6 = (f32[32,152]{1,0:T(8,128)S(1)}, f32[32,152]{1,0:T(8,128)S(1)}, u32[]{:S(2)}, u32[]{:S(2)}) collective-permute-start(f32[32,152]{1,0:T(8,128)S(1)} %slice.22), channel_id=1, source_target_pairs={{0,8},{1,9},{2,10},{3,11},{4,12},{5,13},{6,14},{7,15},{8,0},{9,1},... | collective-permute-start | bytes 58376 | tf_op jit(solution)/shard_map/ppermute | solution.py:574

commit v13 on v12

--- a/solution.py
+++ b/solution.py
@@ -17,7 +17,7 @@
 UNROLL = 8
 TOTALS = 2
 PIECE = 64
-CLASS_ROWS = (32, 64, 96, 128)
+CLASS_ROWS = tuple(range(16, 129, 16))
 PLACES = 56
 SOURCES = 32
 CHUNK = 4
@@ -470,7 +470,7 @@
 
     blocks = lax.shift_right_logical(offset + (block_pieces - 1), block_pieces.bit_length() - 1)
     blocks_column = as_column(blocks.astype(F32))
-    own_class = lax.shift_right_logical(counts[1].astype(jnp.int32) - 1, 5)
+    own_class = lax.shift_right_logical(counts[1].astype(jnp.int32) - 1, 4)
     class_column = as_column(own_class.astype(F32)).astype(jnp.int32)
     earlier = (class_column == jnp.broadcast_to(own_class, shape)) & (rank_column < rank_wide)
     first = jnp.sum(jnp.where(earlier, blocks_column, 0.0), axis=0, keepdims=True).astype(jnp.int32)
@@ -516,29 +516,40 @@
 
 
 def final_kernel(
-    level_count, counts_ref, feature_ref, turned_ref, near_ref, far_ref, coarse_ref, shift_ref, down_ref, *rest
+    level_count, counts_ref, feature_hbm, turned_hbm, near_hbm, far_ref, coarse_hbm, shift_ref, down_ref, *rest
 ):
-    top_refs, (out_ref, node_ref, down_leaf_ref) = rest[:level_count], rest[level_count:]
+    top_refs, rest = rest[:level_count], rest[level_count:]
+    out_ref, node_ref, down_leaf_ref, lower_ref, upper_ref, turned_ref, near_ref, coarse_ref, sems = rest
     leaf_count, q_width, p_width = out_ref.shape
     eq_width = far_ref.shape[1]
     node_count = leaf_count // 8
     index = lax.axis_index("oct")
+    ends = [(coarse_hbm.at[jnp.right_shift(index, 3 * level) & 7], coarse_ref.at[level]) for level in range(level_count)]
+    ends += [(feature_hbm.at[0, :, 0], lower_ref), (feature_hbm.at[1, :, 1], upper_ref)]
+    ends += [(turned_hbm, turned_ref), (near_hbm, near_ref)]
+    copies = [pltpu.make_async_copy(*end, sems.at[number]) for number, end in enumerate(ends)]
+    for copy in copies:
+        copy.start()
+    for copy in copies[:level_count]:
+        copy.wait()
     slab_local = jnp.zeros((q_width, eq_width), F32)
     for level, top_ref in enumerate(top_refs):
-        slab_local = slab_local + dot3(top_ref[:q_width, :], coarse_ref[jnp.right_shift(index, 3 * level) & 7])
+        slab_local = slab_local + dot3(top_ref[:q_width, :], coarse_ref[level])
     for node in range(node_count):
         rows = slice(node * q_width, (node + 1) * q_width)
         node_ref[rows, :] = far_ref[rows, :] + dot3(slab_local, shift_ref[node])
 
     for child in range(8):
         down_leaf_ref[child] = dot3(dot3(node_ref[...], shift_ref[child]), down_ref[...])
+    for copy in copies[level_count:]:
+        copy.wait()
     lane = iota((q_width, p_width), 1)
 
     def node_step(node, carry):
         leaves = [node * 8 + child for child in range(8)]
         features = []
         for leaf in leaves:
-            features.append(feature_ref[0, 2 * leaf] + feature_ref[1, 2 * leaf + 1])
+            features.append(lower_ref[leaf] + upper_ref[leaf])
         turned = [turned_ref[2 * node + number] for number in range(2)]
         node_rows = pl.ds(pl.multiple_of(node * q_width, q_width), q_width)
         downs = [weight_rows(down_leaf_ref[child, node_rows, :]) for child in range(8)]
@@ -697,15 +708,21 @@
     return pl.pallas_call(
         lambda *refs: final_kernel(level_count, *refs),
         out_shape=jax.ShapeDtypeStruct((leaf_count, q_width, p_width), F32),
-        in_specs=[smem] + [vmem] * (7 + len(tops)),
+        in_specs=[smem, hbm, hbm, hbm, vmem, hbm] + [vmem] * (2 + len(tops)),
         out_specs=vmem,
         scratch_shapes=[
             pltpu.VMEM((node_rows, eq_width), F32),
             pltpu.VMEM((8, node_rows, eq_width), F32),
+            pltpu.VMEM((leaf_count, 32, p_width), BF16),
+            pltpu.VMEM((leaf_count, 32, p_width), BF16),
+            pltpu.VMEM((leaf_count // 4, eq_width, 128), BF16),
+            pltpu.VMEM((leaf_count, q_width, p_width), F32),
+            pltpu.VMEM((level_count, eq_width, eq_width), F32),
+            pltpu.SemaphoreType.DMA((level_count + 4,)),
         ],
         compiler_params=params,
         name="final",
-    )(counts, features, turned, near, far_node, coarse, shift_down, down_inverse, *tops)
+    )(counts, features.reshape(2, leaf_count, 2, 32, p_width), turned, near, far_node, coarse, shift_down, down_inverse, *tops)
 
 
 def solution(mesh):

time: 104 us -> 104 us (level)
  transfers between devices with their start and end apart: 9 -> 9, of which waited for: 3 -> 3; matrix products, arithmetic and copies ran while one was open for 0% -> 0% of each run, Pallas kernels for 58% -> 59%
where the time goes in v13:
time: 104 us; the launch traced here: 103 us
  Pallas kernels  79.9 us (77%)
  starting transfers between devices  18.9 us (18%)
  waiting for transfers between devices  2.98 us (3%)
    pallas_call x1, Pallas kernels, local(): pl.pallas_call(near_kernel, out_shape=jax.ShapeDtypeStruct((leaf_count, q...  34.2 us
    pallas_call x1, Pallas kernels, local(): pl.pallas_call(far_kernel, out_shape=(jax.ShapeDtypeStruct((node_rows, eq...  21.1 us
    ppermute x4, starting transfers between devices, shifted(): return (lax.ppermute(value, 'oct', up), lax.ppermute(value, 'oct', down))  10.8 us
    pallas_call x1, Pallas kernels, local(): pl.pallas_call(lambda *refs: upward_kernel(level_count, *refs), out_shape...  10.2 us
    pallas_call x1, Pallas kernels, local(): pl.pallas_call(lambda *refs: final_kernel(level_count, *refs), out_shape=...  9.51 us
    ppermute x5, starting transfers between devices, swapped(): lax.ppermute(value, 'oct', [(source, source ^ mask) for source in range(s...  8.07 us
    pallas_call x1, Pallas kernels, local(): pl.pallas_call(outline_kernel, out_shape=(jax.ShapeDtypeStruct((2, 2 * le...  4.85 us
    ppermute x4, waiting for transfers between devices, shifted(): return (lax.ppermute(value, 'oct', up), lax.ppermute(value, 'oct', down))  2.97 us
  transfers between devices with their start and end apart: 9, of which 3 were waited for; matrix products, arithmetic and copies ran while one was open for 0% of the time, Pallas kernels for 59%

profile of v13, /device:TPU:1, one launch (start us, length us, event | category | flops | bytes accessed | tf_op | source)
XLA Modules:
  0.0 102.8 jit_solution(16626155607603334770)
XLA Ops:
  0.0 10.2 %upward.1 = (bf16[128,64,128]{2,1,0:T(8,128)(2,1)}, bf16[400,152]{1,0:T(8,128)(2,1)}, f32[64,152]{1,0:T(8,128)}) custom-call(f32[3,64,128]{2,1,0:T(8,128)} %bitcast.13, f32[64,32,128]{2,1,0:T(8,128)} %dens_ref.1, f32[3,64,152]{2,1,0:T(8,128)} %bitcast.11, s32[64]{0:T(128)} %refs_0_.1, s32[1,64]{1,0:T(1,128)} %bitcast.15, f32[152,152]{1,0:T(8,128)} %refs_5_.2, ...), custom_call_target="tpu_custom_call" | custom-call | tf_op jit(solution)/shard_map/upward/pallas_call | solution.py:620
  10.2 4.5 %collective-permute-start = (bf16[400,152]{1,0:T(8,128)(2,1)}, bf16[400,152]{1,0:T(8,128)(2,1)S(1)}, u32[]{:S(2)}, u32[]{:S(2)}) collective-permute-start(bf16[400,152]{1,0:T(8,128)(2,1)} %get-tuple-element.28.own_ref), channel_id=1, source_target_pairs={{0,1},{1,2},{2,3},{3,4},{4,5},{5,6},{6,7},{7,8},{8,9},{9,10},{10,1... | collective-permute-start | bytes 364808 | tf_op jit(solution)/shard_map/ppermute | solution.py:581
  14.7 1.9 %collective-permute-start.1 = (bf16[400,152]{1,0:T(8,128)(2,1)}, bf16[400,152]{1,0:T(8,128)(2,1)S(1)}, u32[]{:S(2)}, u32[]{:S(2)}) collective-permute-start(bf16[400,152]{1,0:T(8,128)(2,1)} %get-tuple-element.28.own_ref), channel_id=1, source_target_pairs={{1,0},{2,1},{3,2},{4,3},{5,4},{6,5},{7,6},{8,7},{9,8},{10,9},{11,1... | collective-permute-start | bytes 364808 | tf_op jit(solution)/shard_map/ppermute | solution.py:581
  16.7 0.0 copy-start.1
  16.7 4.8 %outline.1 = (bf16[2,128,32,128]{3,2,1,0:T(8,128)(2,1)}, bf16[16,152,128]{2,1,0:T(8,128)(2,1)}, f32[32,72,128]{2,1,0:T(8,128)}) custom-call(f32[3,64,128]{2,1,0:T(8,128)} %bitcast.14, f32[64,32,128]{2,1,0:T(8,128)} %dens_ref.1, f32[3,64,152]{2,1,0:T(8,128)} %bitcast.12, s32[64]{0:T(128)} %refs_0_.1, f32[64,152]{1,0:T(8,128)} %get-tuple-element.29.order_ref), custom_call_target="tpu_custom_call" | custom-call | flops 4000000000 | bytes 10000000 | tf_op jit(solution)/shard_map/outline/pallas_call | solution.py:635
  21.5 0.0 collective-permute-done.lower_ref
  21.5 0.5 collective-permute-done.1.upper_ref
  22.0 0.0 copy-done.1
  22.1 2.2 %collective-permute-start.2 = (f32[64,152]{1,0:T(8,128)S(1)}, f32[64,152]{1,0:T(8,128)S(1)}, u32[]{:S(2)}, u32[]{:S(2)}) collective-permute-start(f32[64,152]{1,0:T(8,128)S(1)} %fusion), channel_id=1, source_target_pairs={{0,2},{1,3},{2,0},{3,1},{4,6},{5,7},{6,4},{7,5},{8,10},{9,11},{10,... | collective-permute-start | bytes 116744 | tf_op jit(solution)/shard_map/ppermute | solution.py:585
  24.2 1.9 %collective-permute-start.3 = (f32[32,72,128]{2,1,0:T(8,128)}, f32[32,72,128]{2,1,0:T(8,128)S(1)}, u32[]{:S(2)}, u32[]{:S(2)}) collective-permute-start(f32[32,72,128]{2,1,0:T(8,128)} %get-tuple-element.38), channel_id=1, source_target_pairs={{0,1},{1,2},{2,3},{3,4},{4,5},{5,6},{6,7},{7,8},{8,9},{9,10},{10,1... | collective-permute-start | bytes 3538952 | tf_op jit(solution)/shard_map/ppermute | solution.py:581
  26.2 2.5 %collective-permute-start.4 = (f32[32,72,128]{2,1,0:T(8,128)}, f32[32,72,128]{2,1,0:T(8,128)S(1)}, u32[]{:S(2)}, u32[]{:S(2)}) collective-permute-start(f32[32,72,128]{2,1,0:T(8,128)} %get-tuple-element.38), channel_id=1, source_target_pairs={{1,0},{2,1},{3,2},{4,3},{5,4},{6,5},{7,6},{8,7},{9,8},{10,9},{11,1... | collective-permute-start | bytes 3538952 | tf_op jit(solution)/shard_map/ppermute | solution.py:581
  28.6 0.0 collective-permute-done.2
  28.7 2.1 %collective-permute-start.5 = (f32[64,152]{1,0:T(8,128)S(1)}, f32[64,152]{1,0:T(8,128)S(1)}, u32[]{:S(2)}, u32[]{:S(2)}) collective-permute-start(f32[64,152]{1,0:T(8,128)S(1)} %add.23), channel_id=1, source_target_pairs={{0,4},{1,5},{2,6},{3,7},{4,0},{5,1},{6,2},{7,3},{8,12},{9,13},{10,... | collective-permute-start | bytes 116744 | tf_op jit(solution)/shard_map/ppermute | solution.py:585
  30.8 0.0 copy-done.2
  30.8 0.0 copy-done.3
  30.8 21.1 %far.1 = (f32[256,152]{1,0:T(8,128)}, s32[1,128]{1,0:T(1,128)}, s32[32,128]{1,0:T(8,128)}, s32[8,128]{1,0:T(8,128)}) custom-call(bf16[400,152]{1,0:T(8,128)(2,1)} %copy-done.2, bf16[400,152]{1,0:T(8,128)(2,1)} %get-tuple-element.28.own_ref, bf16[400,152]{1,0:T(8,128)(2,1)} %copy-done.3, s32[8,316]{1,0:T(8,128)} %vlist_ref.1, s32[27,64]{1,0:T(8,128)} %bitcast.17, ...), custom_call_target="tpu_custom_call" | custom-call | flops 20000000000 | bytes 18000000 | tf_op jit(solution)/shard_map/far/pallas_call | solution.py:658
  51.9 0.3 collective-permute-done.3.lower_ref
  52.2 2.2 %collective-permute-done.4.upper_ref = f32[32,72,128]{2,1,0:T(8,128)S(1)} collective-permute-done((f32[32,72,128]{2,1,0:T(8,128)}, f32[32,72,128]{2,1,0:T(8,128)S(1)}, u32[]{:S(2)}, u32[]{:S(2)}) %collective-permute-start.4) | collective-permute-done | bytes 1179680 | tf_op jit(solution)/shard_map/ppermute | solution.py:581
  54.4 0.0 collective-permute-done.5
  54.4 0.0 copy-start
  54.5 3.4 %collective-permute-start.8 = (f32[32,152]{1,0:T(8,128)S(1)}, f32[32,152]{1,0:T(8,128)S(1)}, u32[]{:S(2)}, u32[]{:S(2)}) collective-permute-start(f32[32,152]{1,0:T(8,128)S(1)} %slice.22), channel_id=1, source_target_pairs={{0,24},{1,25},{2,26},{3,27},{4,28},{5,29},{6,30},{7,31},{8,16},{9,... | collective-permute-start | bytes 58376 | tf_op jit(solution)/shard_map/ppermute | solution.py:585
  57.9 0.0 collective-permute-start.7
  57.9 0.4 collective-permute-start.6
  58.2 0.0 copy-done.4
  58.2 0.0 copy-done.5
  58.2 34.2 %near.1.refs_3_ = f32[64,32,128]{2,1,0:T(8,128)} custom-call(s32[1,128]{1,0:T(1,128)} %get-tuple-element.43.step_ref, s32[4096]{0:T(1024)} %bitcast.18, s32[1024]{0:T(1024)} %bitcast.19, bf16[128,64,128]{2,1,0:T(8,128)(2,1)} %get-tuple-element.46.own_hbm, bf16[2,128,32,128]{3,2,1,0:T(8,128)(2,1)} %get-tuple-element.31.own_feature_hbm, ...), custom_call_target="tpu_custom_call" | custom-call | flops 30000001024 | bytes 10000000 | tf_op jit(solution)/shard_map/near/pallas_call | solution.py:687
  92.5 0.0 copy-done
  92.5 0.0 collective-permute-done.8
  92.5 0.0 collective-permute-done.7
  92.5 0.0 collective-permute-done.6
  92.5 0.6 add_add_fusion.refs_9_
  93.1 9.5 %final.1 = f32[64,32,128]{2,1,0:T(8,128)} custom-call(s32[64]{0:T(128)} %refs_0_.1, bf16[2,64,2,32,128]{4,3,2,1,0:T(8,128)(2,1)} %bitcast.10, bf16[16,152,128]{2,1,0:T(8,128)(2,1)} %get-tuple-element.32.refs_2_, f32[64,32,128]{2,1,0:T(8,128)} %near.1.refs_3_, f32[256,152]{1,0:T(8,128)} %get-tuple-element.49.refs_4_, f32[8,152,152]{2,1,0:T(8,128)} %refs_5_.3, ...), custom_call_target="tpu_custom_call" | custom-call | tf_op jit(solution)/shard_map/final/pallas_call | solution.py:708
  (9 shorter events, 0.1 us)
Async XLA Ops:
  10.2 11.3 %collective-permute-start = (bf16[400,152]{1,0:T(8,128)(2,1)}, bf16[400,152]{1,0:T(8,128)(2,1)S(1)}, u32[]{:S(2)}, u32[]{:S(2)}) collective-permute-start(bf16[400,152]{1,0:T(8,128)(2,1)} %get-tuple-element.28.own_ref), channel_id=1, source_target_pairs={{0,1},{1,2},{2,3},{3,4},{4,5},{5,6},{6,7},{7,8},{8,9},{9,10},{10,1... | collective-permute-start | bytes 364808 | tf_op jit(solution)/shard_map/ppermute | solution.py:581
  14.7 7.3 %collective-permute-start.1 = (bf16[400,152]{1,0:T(8,128)(2,1)}, bf16[400,152]{1,0:T(8,128)(2,1)S(1)}, u32[]{:S(2)}, u32[]{:S(2)}) collective-permute-start(bf16[400,152]{1,0:T(8,128)(2,1)} %get-tuple-element.28.own_ref), channel_id=1, source_target_pairs={{1,0},{2,1},{3,2},{4,3},{5,4},{6,5},{7,6},{8,7},{9,8},{10,9},{11,1... | collective-permute-start | bytes 364808 | tf_op jit(solution)/shard_map/ppermute | solution.py:581
  16.7 5.4 %copy-start.1 = (f32[64,152]{1,0:T(8,128)S(1)}, f32[64,152]{1,0:T(8,128)}, u32[]{:S(2)}) copy-start(f32[64,152]{1,0:T(8,128)} %get-tuple-element.29.order_ref) | copy-start | bytes 116740
  21.5 9.3 %copy-start.2 = (bf16[400,152]{1,0:T(8,128)(2,1)}, bf16[400,152]{1,0:T(8,128)(2,1)S(1)}, u32[]{:S(2)}) copy-start(bf16[400,152]{1,0:T(8,128)(2,1)S(1)} %collective-permute-done.lower_ref) | copy-start | bytes 364804
  22.0 8.8 %copy-start.3 = (bf16[400,152]{1,0:T(8,128)(2,1)}, bf16[400,152]{1,0:T(8,128)(2,1)S(1)}, u32[]{:S(2)}) copy-start(bf16[400,152]{1,0:T(8,128)(2,1)S(1)} %collective-permute-done.1.upper_ref) | copy-start | bytes 364804
  22.1 6.6 %collective-permute-start.2 = (f32[64,152]{1,0:T(8,128)S(1)}, f32[64,152]{1,0:T(8,128)S(1)}, u32[]{:S(2)}, u32[]{:S(2)}) collective-permute-start(f32[64,152]{1,0:T(8,128)S(1)} %fusion), channel_id=1, source_target_pairs={{0,2},{1,3},{2,0},{3,1},{4,6},{5,7},{6,4},{7,5},{8,10},{9,11},{10,... | collective-permute-start | bytes 116744 | tf_op jit(solution)/shard_map/ppermute | solution.py:585
  24.2 28.0 %collective-permute-start.3 = (f32[32,72,128]{2,1,0:T(8,128)}, f32[32,72,128]{2,1,0:T(8,128)S(1)}, u32[]{:S(2)}, u32[]{:S(2)}) collective-permute-start(f32[32,72,128]{2,1,0:T(8,128)} %get-tuple-element.38), channel_id=1, source_target_pairs={{0,1},{1,2},{2,3},{3,4},{4,5},{5,6},{6,7},{7,8},{8,9},{9,10},{10,1... | collective-permute-start | bytes 3538952 | tf_op jit(solution)/shard_map/ppermute | solution.py:581
  26.2 28.3 %collective-permute-start.4 = (f32[32,72,128]{2,1,0:T(8,128)}, f32[32,72,128]{2,1,0:T(8,128)S(1)}, u32[]{:S(2)}, u32[]{:S(2)}) collective-permute-start(f32[32,72,128]{2,1,0:T(8,128)} %get-tuple-element.38), channel_id=1, source_target_pairs={{1,0},{2,1},{3,2},{4,3},{5,4},{6,5},{7,6},{8,7},{9,8},{10,9},{11,1... | collective-permute-start | bytes 3538952 | tf_op jit(solution)/shard_map/ppermute | solution.py:581
  28.7 25.7 %collective-permute-start.5 = (f32[64,152]{1,0:T(8,128)S(1)}, f32[64,152]{1,0:T(8,128)S(1)}, u32[]{:S(2)}, u32[]{:S(2)}) collective-permute-start(f32[64,152]{1,0:T(8,128)S(1)} %add.23), channel_id=1, source_target_pairs={{0,4},{1,5},{2,6},{3,7},{4,0},{5,1},{6,2},{7,3},{8,12},{9,13},{10,... | collective-permute-start | bytes 116744 | tf_op jit(solution)/shard_map/ppermute | solution.py:585
  52.2 6.0 %copy-start.4 = (f32[32,72,128]{2,1,0:T(8,128)}, f32[32,72,128]{2,1,0:T(8,128)S(1)}, u32[]{:S(2)}) copy-start(f32[32,72,128]{2,1,0:T(8,128)S(1)} %collective-permute-done.3.lower_ref) | copy-start | bytes 3538948
  54.4 3.8 %copy-start.5 = (f32[32,72,128]{2,1,0:T(8,128)}, f32[32,72,128]{2,1,0:T(8,128)S(1)}, u32[]{:S(2)}) copy-start(f32[32,72,128]{2,1,0:T(8,128)S(1)} %collective-permute-done.4.upper_ref) | copy-start | bytes 3538948
  54.4 38.0 %copy-start = (f32[64,152]{1,0:T(8,128)}, f32[64,152]{1,0:T(8,128)S(1)}, u32[]{:S(2)}) copy-start(f32[64,152]{1,0:T(8,128)S(1)} %add.24.refs_8_) | copy-start | bytes 116740
  54.5 38.0 %collective-permute-start.8 = (f32[32,152]{1,0:T(8,128)S(1)}, f32[32,152]{1,0:T(8,128)S(1)}, u32[]{:S(2)}, u32[]{:S(2)}) collective-permute-start(f32[32,152]{1,0:T(8,128)S(1)} %slice.22), channel_id=1, source_target_pairs={{0,24},{1,25},{2,26},{3,27},{4,28},{5,29},{6,30},{7,31},{8,16},{9,... | collective-permute-start | bytes 58376 | tf_op jit(solution)/shard_map/ppermute | solution.py:585
  57.9 34.6 %collective-permute-start.7 = (f32[32,152]{1,0:T(8,128)S(1)}, f32[32,152]{1,0:T(8,128)S(1)}, u32[]{:S(2)}, u32[]{:S(2)}) collective-permute-start(f32[32,152]{1,0:T(8,128)S(1)} %slice.22), channel_id=1, source_target_pairs={{0,16},{1,17},{2,18},{3,19},{4,20},{5,21},{6,22},{7,23},{8,24},{9,... | collective-permute-start | bytes 58376 | tf_op jit(solution)/shard_map/ppermute | solution.py:585
  57.9 34.6 %collective-permute-start.6 = (f32[32,152]{1,0:T(8,128)S(1)}, f32[32,152]{1,0:T(8,128)S(1)}, u32[]{:S(2)}, u32[]{:S(2)}) collective-permute-start(f32[32,152]{1,0:T(8,128)S(1)} %slice.22), channel_id=1, source_target_pairs={{0,8},{1,9},{2,10},{3,11},{4,12},{5,13},{6,14},{7,15},{8,0},{9,1},... | collective-permute-start | bytes 58376 | tf_op jit(solution)/shard_map/ppermute | solution.py:585

commit v14 on v13

--- a/solution.py
+++ b/solution.py
@@ -109,8 +109,8 @@
     versions = []
     for half in range(2):
         alone = jnp.where(lower == (half == 0), rows, 0.0)
-        versions.append((half, half, alone.astype(BF16)))
-        versions.append((half, 1 - half, pltpu.roll(alone, PIECE, 1).astype(BF16)))
+        versions.append((half, half, alone))
+        versions.append((half, 1 - half, pltpu.roll(alone, PIECE, 1)))
     return versions
 
 
@@ -153,7 +153,7 @@
         firsts = [dot(row, value[0]) for row, value in zip(rows, values)]
         seconds = [dot(row[:q_width], value[1]) for row, value in zip(rows, values)]
         for child, leaf in enumerate(leaves):
-            put_pack(pack_ref, leaf, packs[child])
+            put_pack(pack_ref, leaf, packs[child].astype(F32))
             check = firsts[child][:q_width] + firsts[child][q_width:] + seconds[child]
             check_ref[child, pl.ds(pl.multiple_of(node * q_width, q_width), q_width), :] = check
         return carry
@@ -338,9 +338,9 @@
     feature_copy = pltpu.make_async_copy(own_feature_hbm, feature_ref.at[:, own], sems.at[1])
     own_copy.start()
     feature_copy.start()
-    pack_ref[6 * leaf_count] = jnp.zeros((PIECE, 128), BF16)
+    pack_ref[6 * leaf_count] = jnp.zeros((PIECE, 128), F32)
     for half in range(2):
-        feature_ref[half, 6 * leaf_count] = jnp.zeros((32, 128), BF16)
+        feature_ref[half, 6 * leaf_count] = jnp.zeros((32, 128), F32)
     for total_ref in total_refs:
         total_ref[...] = jnp.zeros_like(total_ref)
     def pack_step(step, carry):
@@ -357,7 +357,8 @@
         for part in range(0, len(chosen), 2):
             (high, low), (next_high, next_low) = weights[part : part + 2]
             both = jnp.concatenate([next_low, high, low, next_high], axis=0).astype(BF16).T
-            packs += [both, pltpu.roll(both.astype(F32), 64, 1).astype(BF16)]
+            both = both.astype(F32)
+            packs += [both, pltpu.roll(both, 64, 1)]
         for (part, side), pack, version in zip(chosen, packs, versions):
             place = (1 + side) * leaf_count + step * 4 + part
             put_pack(pack_ref, place, pack)
@@ -379,19 +380,20 @@
         return list(zip(leaves, pieces_of))
 
     def sources_of(numbers):
-        return jnp.concatenate([pack_ref[number] for number in numbers], axis=0)
+        return jnp.concatenate([pack_ref[number] for number in numbers], axis=0).astype(BF16)
 
     def features_of(numbers):
         tiles = []
         for tile in range(BLOCK // 128):
             tiles.append(feature_ref[0, numbers[2 * tile]] + feature_ref[1, numbers[2 * tile + 1]])
-        return jnp.concatenate(tiles, axis=1)
+        return jnp.concatenate(tiles, axis=1).astype(BF16)
 
     def targets_of(leaf, rows):
         first = 2 * jnp.minimum(leaf, leaf_count - 1)
-        if rows <= PIECE:
-            return pack_ref[first, :rows][:, :32]
-        return jnp.concatenate([pack_ref[first][:, :32], pack_ref[first + 1, : rows - PIECE][:, :32]], axis=0)
+        value = pack_ref[first, : min(rows, PIECE)]
+        if rows > PIECE:
+            value = jnp.concatenate([value, pack_ref[first + 1, : rows - PIECE]], axis=0)
+        return value.astype(BF16)[:, :32]
 
     def run(rows, first, count):
         def blocks_step(step, carry):
@@ -549,7 +551,7 @@
         leaves = [node * 8 + child for child in range(8)]
         features = []
         for leaf in leaves:
-            features.append(lower_ref[leaf] + upper_ref[leaf])
+            features.append((lower_ref[leaf] + upper_ref[leaf]).astype(BF16))
         turned = [turned_ref[2 * node + number] for number in range(2)]
         node_rows = pl.ds(pl.multiple_of(node * q_width, q_width), q_width)
         downs = [weight_rows(down_leaf_ref[child, node_rows, :]) for child in range(8)]
@@ -620,7 +622,7 @@
     pack, send, slab = pl.pallas_call(
         lambda *refs: upward_kernel(level_count, *refs),
         out_shape=(
-            jax.ShapeDtypeStruct((2 * leaf_count, PIECE, 128), BF16),
+            jax.ShapeDtypeStruct((2 * leaf_count, PIECE, 128), F32),
             jax.ShapeDtypeStruct((node_rows + 2 * level_rows + 16, eq_width), BF16),
             jax.ShapeDtypeStruct((level_rows, eq_width), F32),
         ),
@@ -635,7 +637,7 @@
     features, turned, message = pl.pallas_call(
         outline_kernel,
         out_shape=(
-            jax.ShapeDtypeStruct((2, 2 * leaf_count, 32, p_width), BF16),
+            jax.ShapeDtypeStruct((2, 2 * leaf_count, 32, p_width), F32),
             jax.ShapeDtypeStruct((leaf_count // 4, eq_width, 128), BF16),
             jax.ShapeDtypeStruct((leaf_count // 2, 2 * q_width + 8, p_width), F32),
         ),
@@ -690,8 +692,8 @@
         in_specs=[smem, smem, smem, hbm, hbm, vmem, vmem],
         out_specs=vmem,
         scratch_shapes=[
-            pltpu.VMEM((6 * leaf_count + 1, PIECE, 128), BF16),
-            pltpu.VMEM((2, 6 * leaf_count + 1, 32, 128), BF16),
+            pltpu.VMEM((6 * leaf_count + 1, PIECE, 128), F32),
+            pltpu.VMEM((2, 6 * leaf_count + 1, 32, 128), F32),
             *[pltpu.VMEM((leaf_count + 1, p_width, 128), F32)] * TOTALS,
             pltpu.SemaphoreType.DMA((2,)),
         ],
@@ -713,8 +715,8 @@
         scratch_shapes=[
             pltpu.VMEM((node_rows, eq_width), F32),
             pltpu.VMEM((8, node_rows, eq_width), F32),
-            pltpu.VMEM((leaf_count, 32, p_width), BF16),
-            pltpu.VMEM((leaf_count, 32, p_width), BF16),
+            pltpu.VMEM((leaf_count, 32, p_width), F32),
+            pltpu.VMEM((leaf_count, 32, p_width), F32),
             pltpu.VMEM((leaf_count // 4, eq_width, 128), BF16),
             pltpu.VMEM((leaf_count, q_width, p_width), F32),
             pltpu.VMEM((level_count, eq_width, eq_width), F32),

time: 104 us -> 106 us (1.019)
  Pallas kernels: 79.9 us -> 81 us
  transfers between devices with their start and end apart: 9 -> 9, of which waited for: 3 -> 2; matrix products, arithmetic and copies ran while one was open for 0% -> 0% of each run, Pallas kernels for 59% -> 59%
where the time goes in v14:
time: 106 us; the launch traced here: 104 us
  Pallas kernels  81 us (76%)
  starting transfers between devices  18.8 us (18%)
  waiting for transfers between devices  3.03 us (3%)
    pallas_call x1, Pallas kernels, local(): pl.pallas_call(near_kernel, out_shape=jax.ShapeDtypeStruct((leaf_count, q...  34.8 us
    pallas_call x1, Pallas kernels, local(): pl.pallas_call(far_kernel, out_shape=(jax.ShapeDtypeStruct((node_rows, eq...  21.1 us
    ppermute x4, starting transfers between devices, shifted(): return (lax.ppermute(value, 'oct', up), lax.ppermute(value, 'oct', down))  10.8 us
    pallas_call x1, Pallas kernels, local(): pl.pallas_call(lambda *refs: upward_kernel(level_count, *refs), out_shape...  10.2 us
    pallas_call x1, Pallas kernels, local(): pl.pallas_call(lambda *refs: final_kernel(level_count, *refs), out_shape=...  9.49 us
    ppermute x5, starting transfers between devices, swapped(): lax.ppermute(value, 'oct', [(source, source ^ mask) for source in range(s...  8.03 us
    pallas_call x1, Pallas kernels, local(): pl.pallas_call(outline_kernel, out_shape=(jax.ShapeDtypeStruct((2, 2 * le...  5.37 us
    ppermute x4, waiting for transfers between devices, shifted(): return (lax.ppermute(value, 'oct', up), lax.ppermute(value, 'oct', down))  3.02 us
  transfers between devices with their start and end apart: 9, of which 2 were waited for; matrix products, arithmetic and copies ran while one was open for 0% of the time, Pallas kernels for 59%

profile of v14, /device:TPU:1, one launch (start us, length us, event | category | flops | bytes accessed | tf_op | source)
XLA Modules:
  0.0 103.8 jit_solution(3359875325154676712)
XLA Ops:
  0.0 10.2 %upward.1 = (f32[128,64,128]{2,1,0:T(8,128)}, bf16[400,152]{1,0:T(8,128)(2,1)}, f32[64,152]{1,0:T(8,128)}) custom-call(f32[3,64,128]{2,1,0:T(8,128)} %bitcast.13, f32[64,32,128]{2,1,0:T(8,128)} %dens_ref.1, f32[3,64,152]{2,1,0:T(8,128)} %bitcast.11, s32[64]{0:T(128)} %refs_0_.1, s32[1,64]{1,0:T(1,128)} %bitcast.15, f32[152,152]{1,0:T(8,128)} %refs_5_.2, ...), custom_call_target="tpu_custom_call" | custom-call | tf_op jit(solution)/shard_map/upward/pallas_call | solution.py:622
  10.2 4.5 %collective-permute-start = (bf16[400,152]{1,0:T(8,128)(2,1)}, bf16[400,152]{1,0:T(8,128)(2,1)S(1)}, u32[]{:S(2)}, u32[]{:S(2)}) collective-permute-start(bf16[400,152]{1,0:T(8,128)(2,1)} %get-tuple-element.28.own_ref), channel_id=1, source_target_pairs={{0,1},{1,2},{2,3},{3,4},{4,5},{5,6},{6,7},{7,8},{8,9},{9,10},{10,1... | collective-permute-start | bytes 364808 | tf_op jit(solution)/shard_map/ppermute | solution.py:583
  14.7 1.9 %collective-permute-start.1 = (bf16[400,152]{1,0:T(8,128)(2,1)}, bf16[400,152]{1,0:T(8,128)(2,1)S(1)}, u32[]{:S(2)}, u32[]{:S(2)}) collective-permute-start(bf16[400,152]{1,0:T(8,128)(2,1)} %get-tuple-element.28.own_ref), channel_id=1, source_target_pairs={{1,0},{2,1},{3,2},{4,3},{5,4},{6,5},{7,6},{8,7},{9,8},{10,9},{11,1... | collective-permute-start | bytes 364808 | tf_op jit(solution)/shard_map/ppermute | solution.py:583
  16.7 0.0 copy-start.1
  16.7 5.4 %outline.1 = (f32[2,128,32,128]{3,2,1,0:T(8,128)}, bf16[16,152,128]{2,1,0:T(8,128)(2,1)}, f32[32,72,128]{2,1,0:T(8,128)}) custom-call(f32[3,64,128]{2,1,0:T(8,128)} %bitcast.14, f32[64,32,128]{2,1,0:T(8,128)} %dens_ref.1, f32[3,64,152]{2,1,0:T(8,128)} %bitcast.12, s32[64]{0:T(128)} %refs_0_.1, f32[64,152]{1,0:T(8,128)} %get-tuple-element.29.order_ref), custom_call_target="tpu_custom_call" | custom-call | flops 4000000000 | bytes 10000000 | tf_op jit(solution)/shard_map/outline/pallas_call | solution.py:637
  22.0 0.0 collective-permute-done.lower_ref
  22.0 0.0 collective-permute-done.1.upper_ref
  22.0 0.0 copy-start.3
  22.1 0.0 copy-done.1
  22.1 2.1 %collective-permute-start.2 = (f32[64,152]{1,0:T(8,128)S(1)}, f32[64,152]{1,0:T(8,128)S(1)}, u32[]{:S(2)}, u32[]{:S(2)}) collective-permute-start(f32[64,152]{1,0:T(8,128)S(1)} %fusion), channel_id=1, source_target_pairs={{0,2},{1,3},{2,0},{3,1},{4,6},{5,7},{6,4},{7,5},{8,10},{9,11},{10,... | collective-permute-start | bytes 116744 | tf_op jit(solution)/shard_map/ppermute | solution.py:587
  24.2 1.9 %collective-permute-start.3 = (f32[32,72,128]{2,1,0:T(8,128)}, f32[32,72,128]{2,1,0:T(8,128)S(1)}, u32[]{:S(2)}, u32[]{:S(2)}) collective-permute-start(f32[32,72,128]{2,1,0:T(8,128)} %get-tuple-element.38), channel_id=1, source_target_pairs={{0,1},{1,2},{2,3},{3,4},{4,5},{5,6},{6,7},{7,8},{8,9},{9,10},{10,1... | collective-permute-start | bytes 3538952 | tf_op jit(solution)/shard_map/ppermute | solution.py:583
  26.2 2.5 %collective-permute-start.4 = (f32[32,72,128]{2,1,0:T(8,128)}, f32[32,72,128]{2,1,0:T(8,128)S(1)}, u32[]{:S(2)}, u32[]{:S(2)}) collective-permute-start(f32[32,72,128]{2,1,0:T(8,128)} %get-tuple-element.38), channel_id=1, source_target_pairs={{1,0},{2,1},{3,2},{4,3},{5,4},{6,5},{7,6},{8,7},{9,8},{10,9},{11,1... | collective-permute-start | bytes 3538952 | tf_op jit(solution)/shard_map/ppermute | solution.py:583
  28.6 0.0 collective-permute-done.2
  28.7 2.1 %collective-permute-start.5 = (f32[64,152]{1,0:T(8,128)S(1)}, f32[64,152]{1,0:T(8,128)S(1)}, u32[]{:S(2)}, u32[]{:S(2)}) collective-permute-start(f32[64,152]{1,0:T(8,128)S(1)} %add.23), channel_id=1, source_target_pairs={{0,4},{1,5},{2,6},{3,7},{4,0},{5,1},{6,2},{7,3},{8,12},{9,13},{10,... | collective-permute-start | bytes 116744 | tf_op jit(solution)/shard_map/ppermute | solution.py:587
  30.8 0.0 copy-done.2
  30.8 0.0 copy-done.3
  30.8 21.1 %far.1 = (f32[256,152]{1,0:T(8,128)}, s32[1,128]{1,0:T(1,128)}, s32[32,128]{1,0:T(8,128)}, s32[8,128]{1,0:T(8,128)}) custom-call(bf16[400,152]{1,0:T(8,128)(2,1)} %copy-done.2, bf16[400,152]{1,0:T(8,128)(2,1)} %get-tuple-element.28.own_ref, bf16[400,152]{1,0:T(8,128)(2,1)} %copy-done.3, s32[8,316]{1,0:T(8,128)} %vlist_ref.1, s32[27,64]{1,0:T(8,128)} %bitcast.17, ...), custom_call_target="tpu_custom_call" | custom-call | flops 20000000000 | bytes 18000000 | tf_op jit(solution)/shard_map/far/pallas_call | solution.py:660
  51.9 0.3 collective-permute-done.3.lower_ref
  52.2 2.7 %collective-permute-done.4.upper_ref = f32[32,72,128]{2,1,0:T(8,128)S(1)} collective-permute-done((f32[32,72,128]{2,1,0:T(8,128)}, f32[32,72,128]{2,1,0:T(8,128)S(1)}, u32[]{:S(2)}, u32[]{:S(2)}) %collective-permute-start.4) | collective-permute-done | bytes 1179680 | tf_op jit(solution)/shard_map/ppermute | solution.py:583
  54.9 0.0 collective-permute-done.5
  55.0 0.0 copy-start
  55.0 3.4 %collective-permute-start.8 = (f32[32,152]{1,0:T(8,128)S(1)}, f32[32,152]{1,0:T(8,128)S(1)}, u32[]{:S(2)}, u32[]{:S(2)}) collective-permute-start(f32[32,152]{1,0:T(8,128)S(1)} %slice.22), channel_id=1, source_target_pairs={{0,24},{1,25},{2,26},{3,27},{4,28},{5,29},{6,30},{7,31},{8,16},{9,... | collective-permute-start | bytes 58376 | tf_op jit(solution)/shard_map/ppermute | solution.py:587
  58.4 0.0 collective-permute-start.7
  58.4 0.4 collective-permute-start.6
  58.7 0.0 copy-done.4
  58.7 0.0 copy-done.5
  58.7 34.8 %near.1.refs_3_ = f32[64,32,128]{2,1,0:T(8,128)} custom-call(s32[1,128]{1,0:T(1,128)} %get-tuple-element.43.step_ref, s32[4096]{0:T(1024)} %bitcast.18, s32[1024]{0:T(1024)} %bitcast.19, f32[128,64,128]{2,1,0:T(8,128)} %get-tuple-element.46.own_hbm, f32[2,128,32,128]{3,2,1,0:T(8,128)} %get-tuple-element.31.own_feature_hbm, f32[32,72,128]{2,1,0:T(8,128)} %copy-done.4, ...), custom_call_target="tpu_custom_call" | custom-call | flops 30000001024 | bytes 10000000 | tf_op jit(solution)/shard_map/near/pallas_call | solution.py:689
  93.5 0.0 collective-permute-done.8
  93.5 0.0 collective-permute-done.7
  93.6 0.0 collective-permute-done.6
  93.6 0.6 add_add_fusion.refs_9_
  94.2 9.5 %final.1 = f32[64,32,128]{2,1,0:T(8,128)} custom-call(s32[64]{0:T(128)} %refs_0_.1, f32[2,64,2,32,128]{4,3,2,1,0:T(8,128)} %bitcast.10, bf16[16,152,128]{2,1,0:T(8,128)(2,1)} %get-tuple-element.32.refs_2_, f32[64,32,128]{2,1,0:T(8,128)} %near.1.refs_3_, f32[256,152]{1,0:T(8,128)} %get-tuple-element.49.refs_4_, f32[8,152,152]{2,1,0:T(8,128)} %refs_5_.3, ...), custom_call_target="tpu_custom_call" | custom-call | tf_op jit(solution)/shard_map/final/pallas_call | solution.py:710
  (9 shorter events, 0.1 us)
Async XLA Ops:
  10.2 11.8 %collective-permute-start = (bf16[400,152]{1,0:T(8,128)(2,1)}, bf16[400,152]{1,0:T(8,128)(2,1)S(1)}, u32[]{:S(2)}, u32[]{:S(2)}) collective-permute-start(bf16[400,152]{1,0:T(8,128)(2,1)} %get-tuple-element.28.own_ref), channel_id=1, source_target_pairs={{0,1},{1,2},{2,3},{3,4},{4,5},{5,6},{6,7},{7,8},{8,9},{9,10},{10,1... | collective-permute-start | bytes 364808 | tf_op jit(solution)/shard_map/ppermute | solution.py:583
  14.7 7.3 %collective-permute-start.1 = (bf16[400,152]{1,0:T(8,128)(2,1)}, bf16[400,152]{1,0:T(8,128)(2,1)S(1)}, u32[]{:S(2)}, u32[]{:S(2)}) collective-permute-start(bf16[400,152]{1,0:T(8,128)(2,1)} %get-tuple-element.28.own_ref), channel_id=1, source_target_pairs={{1,0},{2,1},{3,2},{4,3},{5,4},{6,5},{7,6},{8,7},{9,8},{10,9},{11,1... | collective-permute-start | bytes 364808 | tf_op jit(solution)/shard_map/ppermute | solution.py:583
  16.7 5.4 %copy-start.1 = (f32[64,152]{1,0:T(8,128)S(1)}, f32[64,152]{1,0:T(8,128)}, u32[]{:S(2)}) copy-start(f32[64,152]{1,0:T(8,128)} %get-tuple-element.29.order_ref) | copy-start | bytes 116740
  22.0 8.8 %copy-start.2 = (bf16[400,152]{1,0:T(8,128)(2,1)}, bf16[400,152]{1,0:T(8,128)(2,1)S(1)}, u32[]{:S(2)}) copy-start(bf16[400,152]{1,0:T(8,128)(2,1)S(1)} %collective-permute-done.lower_ref) | copy-start | bytes 364804
  22.0 8.8 %copy-start.3 = (bf16[400,152]{1,0:T(8,128)(2,1)}, bf16[400,152]{1,0:T(8,128)(2,1)S(1)}, u32[]{:S(2)}) copy-start(bf16[400,152]{1,0:T(8,128)(2,1)S(1)} %collective-permute-done.1.upper_ref) | copy-start | bytes 364804
  22.1 6.5 %collective-permute-start.2 = (f32[64,152]{1,0:T(8,128)S(1)}, f32[64,152]{1,0:T(8,128)S(1)}, u32[]{:S(2)}, u32[]{:S(2)}) collective-permute-start(f32[64,152]{1,0:T(8,128)S(1)} %fusion), channel_id=1, source_target_pairs={{0,2},{1,3},{2,0},{3,1},{4,6},{5,7},{6,4},{7,5},{8,10},{9,11},{10,... | collective-permute-start | bytes 116744 | tf_op jit(solution)/shard_map/ppermute | solution.py:587
  24.2 28.0 %collective-permute-start.3 = (f32[32,72,128]{2,1,0:T(8,128)}, f32[32,72,128]{2,1,0:T(8,128)S(1)}, u32[]{:S(2)}, u32[]{:S(2)}) collective-permute-start(f32[32,72,128]{2,1,0:T(8,128)} %get-tuple-element.38), channel_id=1, source_target_pairs={{0,1},{1,2},{2,3},{3,4},{4,5},{5,6},{6,7},{7,8},{8,9},{9,10},{10,1... | collective-permute-start | bytes 3538952 | tf_op jit(solution)/shard_map/ppermute | solution.py:583
  26.2 28.8 %collective-permute-start.4 = (f32[32,72,128]{2,1,0:T(8,128)}, f32[32,72,128]{2,1,0:T(8,128)S(1)}, u32[]{:S(2)}, u32[]{:S(2)}) collective-permute-start(f32[32,72,128]{2,1,0:T(8,128)} %get-tuple-element.38), channel_id=1, source_target_pairs={{1,0},{2,1},{3,2},{4,3},{5,4},{6,5},{7,6},{8,7},{9,8},{10,9},{11,1... | collective-permute-start | bytes 3538952 | tf_op jit(solution)/shard_map/ppermute | solution.py:583
  28.7 26.3 %collective-permute-start.5 = (f32[64,152]{1,0:T(8,128)S(1)}, f32[64,152]{1,0:T(8,128)S(1)}, u32[]{:S(2)}, u32[]{:S(2)}) collective-permute-start(f32[64,152]{1,0:T(8,128)S(1)} %add.23), channel_id=1, source_target_pairs={{0,4},{1,5},{2,6},{3,7},{4,0},{5,1},{6,2},{7,3},{8,12},{9,13},{10,... | collective-permute-start | bytes 116744 | tf_op jit(solution)/shard_map/ppermute | solution.py:587
  52.2 6.5 %copy-start.4 = (f32[32,72,128]{2,1,0:T(8,128)}, f32[32,72,128]{2,1,0:T(8,128)S(1)}, u32[]{:S(2)}) copy-start(f32[32,72,128]{2,1,0:T(8,128)S(1)} %collective-permute-done.3.lower_ref) | copy-start | bytes 3538948
  54.9 3.8 %copy-start.5 = (f32[32,72,128]{2,1,0:T(8,128)}, f32[32,72,128]{2,1,0:T(8,128)S(1)}, u32[]{:S(2)}) copy-start(f32[32,72,128]{2,1,0:T(8,128)S(1)} %collective-permute-done.4.upper_ref) | copy-start | bytes 3538948
  55.0 38.6 %copy-start = (f32[64,152]{1,0:T(8,128)}, f32[64,152]{1,0:T(8,128)S(1)}, u32[]{:S(2)}) copy-start(f32[64,152]{1,0:T(8,128)S(1)} %add.24.refs_8_) | copy-start | bytes 116740
  55.0 38.6 %collective-permute-start.8 = (f32[32,152]{1,0:T(8,128)S(1)}, f32[32,152]{1,0:T(8,128)S(1)}, u32[]{:S(2)}, u32[]{:S(2)}) collective-permute-start(f32[32,152]{1,0:T(8,128)S(1)} %slice.22), channel_id=1, source_target_pairs={{0,24},{1,25},{2,26},{3,27},{4,28},{5,29},{6,30},{7,31},{8,16},{9,... | collective-permute-start | bytes 58376 | tf_op jit(solution)/shard_map/ppermute | solution.py:587
  58.4 35.2 %collective-permute-start.7 = (f32[32,152]{1,0:T(8,128)S(1)}, f32[32,152]{1,0:T(8,128)S(1)}, u32[]{:S(2)}, u32[]{:S(2)}) collective-permute-start(f32[32,152]{1,0:T(8,128)S(1)} %slice.22), channel_id=1, source_target_pairs={{0,16},{1,17},{2,18},{3,19},{4,20},{5,21},{6,22},{7,23},{8,24},{9,... | collective-permute-start | bytes 58376 | tf_op jit(solution)/shard_map/ppermute | solution.py:587
  58.4 35.2 %collective-permute-start.6 = (f32[32,152]{1,0:T(8,128)S(1)}, f32[32,152]{1,0:T(8,128)S(1)}, u32[]{:S(2)}, u32[]{:S(2)}) collective-permute-start(f32[32,152]{1,0:T(8,128)S(1)} %slice.22), channel_id=1, source_target_pairs={{0,8},{1,9},{2,10},{3,11},{4,12},{5,13},{6,14},{7,15},{8,0},{9,1},... | collective-permute-start | bytes 58376 | tf_op jit(solution)/shard_map/ppermute | solution.py:587

commit v15 on v13

--- a/solution.py
+++ b/solution.py
@@ -328,19 +328,17 @@
 
 
 def near_kernel(
-    step_ref, piece_ref, item_ref, own_hbm, own_feature_hbm, lower_ref, upper_ref, out_ref, pack_ref, feature_ref,
-    *rest
+    step_ref, piece_ref, item_ref, own_hbm, own_feature_hbm, lower_ref, upper_ref, out_ref, pack_ref, *rest
 ):
     total_refs, sems = rest[:TOTALS], rest[TOTALS]
     leaf_count, q_width, p_width = out_ref.shape
     own = pl.ds(0, 2 * leaf_count)
-    own_copy = pltpu.make_async_copy(own_hbm, pack_ref.at[own], sems.at[0])
-    feature_copy = pltpu.make_async_copy(own_feature_hbm, feature_ref.at[:, own], sems.at[1])
-    own_copy.start()
-    feature_copy.start()
-    pack_ref[6 * leaf_count] = jnp.zeros((PIECE, 128), BF16)
-    for half in range(2):
-        feature_ref[half, 6 * leaf_count] = jnp.zeros((32, 128), BF16)
+    ends = [(own_hbm, pack_ref.at[own, pl.ds(0, PIECE)])]
+    ends += [(own_feature_hbm.at[half], pack_ref.at[own, pl.ds(PIECE + 32 * half, 32)]) for half in range(2)]
+    copies = [pltpu.make_async_copy(*end, sems.at[number]) for number, end in enumerate(ends)]
+    for copy in copies:
+        copy.start()
+    pack_ref[6 * leaf_count] = jnp.zeros((2 * PIECE, 128), BF16)
     for total_ref in total_refs:
         total_ref[...] = jnp.zeros_like(total_ref)
     def pack_step(step, carry):
@@ -360,13 +358,14 @@
             packs += [both, pltpu.roll(both.astype(F32), 64, 1).astype(BF16)]
         for (part, side), pack, version in zip(chosen, packs, versions):
             place = (1 + side) * leaf_count + step * 4 + part
-            put_pack(pack_ref, place, pack)
-            put_features(feature_ref, place, version)
+            pack_ref[pl.ds(2 * place, 2), :PIECE] = pack.reshape(2, PIECE, 128)
+            for half, number, value in version:
+                pack_ref[2 * place + half, PIECE + 32 * number : PIECE + 32 * (number + 1)] = value
         return carry
 
     lax.fori_loop(0, leaf_count // 4, pack_step, 0)
-    own_copy.wait()
-    feature_copy.wait()
+    for copy in copies:
+        copy.wait()
     block_pieces = BLOCK // PIECE
 
     def items_of(step):
@@ -379,19 +378,20 @@
         return list(zip(leaves, pieces_of))
 
     def sources_of(numbers):
-        return jnp.concatenate([pack_ref[number] for number in numbers], axis=0)
+        return jnp.concatenate([pack_ref[number, :PIECE] for number in numbers], axis=0)
 
     def features_of(numbers):
         tiles = []
         for tile in range(BLOCK // 128):
-            tiles.append(feature_ref[0, numbers[2 * tile]] + feature_ref[1, numbers[2 * tile + 1]])
+            lower = pack_ref[numbers[2 * tile], PIECE : PIECE + 32]
+            tiles.append(lower + pack_ref[numbers[2 * tile + 1], PIECE + 32 :])
         return jnp.concatenate(tiles, axis=1)
 
     def targets_of(leaf, rows):
-        first = 2 * jnp.minimum(leaf, leaf_count - 1)
+        first = 2 * leaf
         if rows <= PIECE:
             return pack_ref[first, :rows][:, :32]
-        return jnp.concatenate([pack_ref[first][:, :32], pack_ref[first + 1, : rows - PIECE][:, :32]], axis=0)
+        return jnp.concatenate([pack_ref[first, :PIECE][:, :32], pack_ref[first + 1, : rows - PIECE][:, :32]], axis=0)
 
     def run(rows, first, count):
         def blocks_step(step, carry):
@@ -690,10 +690,9 @@
         in_specs=[smem, smem, smem, hbm, hbm, vmem, vmem],
         out_specs=vmem,
         scratch_shapes=[
-            pltpu.VMEM((6 * leaf_count + 1, PIECE, 128), BF16),
-            pltpu.VMEM((2, 6 * leaf_count + 1, 32, 128), BF16),
+            pltpu.VMEM((6 * leaf_count + 1, 2 * PIECE, 128), BF16),
             *[pltpu.VMEM((leaf_count + 1, p_width, 128), F32)] * TOTALS,
-            pltpu.SemaphoreType.DMA((2,)),
+            pltpu.SemaphoreType.DMA((3,)),
         ],
         compiler_params=params,
         cost_estimate=pl.CostEstimate(flops=3 * 10**10, bytes_accessed=10**7, transcendentals=0),

time: 104 us -> 104 us (level)
  no operation moved by 1% of the time
where the time goes in v15:
time: 104 us; the launch traced here: 103 us
  Pallas kernels  80.6 us (77%)
  starting transfers between devices  18.9 us (18%)
  waiting for transfers between devices  2.98 us (3%)
    pallas_call x1, Pallas kernels, local(): pl.pallas_call(near_kernel, out_shape=jax.ShapeDtypeStruct((leaf_count, q...  34.9 us
    pallas_call x1, Pallas kernels, local(): pl.pallas_call(far_kernel, out_shape=(jax.ShapeDtypeStruct((node_rows, eq...  21.1 us
    ppermute x4, starting transfers between devices, shifted(): return (lax.ppermute(value, 'oct', up), lax.ppermute(value, 'oct', down))  10.8 us
    pallas_call x1, Pallas kernels, local(): pl.pallas_call(lambda *refs: upward_kernel(level_count, *refs), out_shape...  10.2 us
    pallas_call x1, Pallas kernels, local(): pl.pallas_call(lambda *refs: final_kernel(level_count, *refs), out_shape=...  9.51 us
    ppermute x5, starting transfers between devices, swapped(): lax.ppermute(value, 'oct', [(source, source ^ mask) for source in range(s...  8.07 us
    pallas_call x1, Pallas kernels, local(): pl.pallas_call(outline_kernel, out_shape=(jax.ShapeDtypeStruct((2, 2 * le...  4.85 us
    ppermute x4, waiting for transfers between devices, shifted(): return (lax.ppermute(value, 'oct', up), lax.ppermute(value, 'oct', down))  2.97 us
  transfers between devices with their start and end apart: 9, of which 3 were waited for; matrix products, arithmetic and copies ran while one was open for 0% of the time, Pallas kernels for 59%

profile of v15, /device:TPU:1, one launch (start us, length us, event | category | flops | bytes accessed | tf_op | source)
XLA Modules:
  0.0 103.5 jit_solution(11478099666054278805)
XLA Ops:
  0.0 10.2 %upward.1 = (bf16[128,64,128]{2,1,0:T(8,128)(2,1)}, bf16[400,152]{1,0:T(8,128)(2,1)}, f32[64,152]{1,0:T(8,128)}) custom-call(f32[3,64,128]{2,1,0:T(8,128)} %bitcast.13, f32[64,32,128]{2,1,0:T(8,128)} %dens_ref.1, f32[3,64,152]{2,1,0:T(8,128)} %bitcast.11, s32[64]{0:T(128)} %refs_0_.1, s32[1,64]{1,0:T(1,128)} %bitcast.15, f32[152,152]{1,0:T(8,128)} %refs_5_.2, ...), custom_call_target="tpu_custom_call" | custom-call | tf_op jit(solution)/shard_map/upward/pallas_call | solution.py:620
  10.2 4.5 %collective-permute-start = (bf16[400,152]{1,0:T(8,128)(2,1)}, bf16[400,152]{1,0:T(8,128)(2,1)S(1)}, u32[]{:S(2)}, u32[]{:S(2)}) collective-permute-start(bf16[400,152]{1,0:T(8,128)(2,1)} %get-tuple-element.28.own_ref), channel_id=1, source_target_pairs={{0,1},{1,2},{2,3},{3,4},{4,5},{5,6},{6,7},{7,8},{8,9},{9,10},{10,1... | collective-permute-start | bytes 364808 | tf_op jit(solution)/shard_map/ppermute | solution.py:581
  14.7 1.9 %collective-permute-start.1 = (bf16[400,152]{1,0:T(8,128)(2,1)}, bf16[400,152]{1,0:T(8,128)(2,1)S(1)}, u32[]{:S(2)}, u32[]{:S(2)}) collective-permute-start(bf16[400,152]{1,0:T(8,128)(2,1)} %get-tuple-element.28.own_ref), channel_id=1, source_target_pairs={{1,0},{2,1},{3,2},{4,3},{5,4},{6,5},{7,6},{8,7},{9,8},{10,9},{11,1... | collective-permute-start | bytes 364808 | tf_op jit(solution)/shard_map/ppermute | solution.py:581
  16.7 0.0 copy-start.1
  16.7 4.8 %outline.1 = (bf16[2,128,32,128]{3,2,1,0:T(8,128)(2,1)}, bf16[16,152,128]{2,1,0:T(8,128)(2,1)}, f32[32,72,128]{2,1,0:T(8,128)}) custom-call(f32[3,64,128]{2,1,0:T(8,128)} %bitcast.14, f32[64,32,128]{2,1,0:T(8,128)} %dens_ref.1, f32[3,64,152]{2,1,0:T(8,128)} %bitcast.12, s32[64]{0:T(128)} %refs_0_.1, f32[64,152]{1,0:T(8,128)} %get-tuple-element.29.order_ref), custom_call_target="tpu_custom_call" | custom-call | flops 4000000000 | bytes 10000000 | tf_op jit(solution)/shard_map/outline/pallas_call | solution.py:635
  21.5 0.0 collective-permute-done.lower_ref
  21.5 0.5 collective-permute-done.1.upper_ref
  22.0 0.0 copy-done.1
  22.1 2.2 %collective-permute-start.2 = (f32[64,152]{1,0:T(8,128)S(1)}, f32[64,152]{1,0:T(8,128)S(1)}, u32[]{:S(2)}, u32[]{:S(2)}) collective-permute-start(f32[64,152]{1,0:T(8,128)S(1)} %fusion), channel_id=1, source_target_pairs={{0,2},{1,3},{2,0},{3,1},{4,6},{5,7},{6,4},{7,5},{8,10},{9,11},{10,... | collective-permute-start | bytes 116744 | tf_op jit(solution)/shard_map/ppermute | solution.py:585
  24.2 1.9 %collective-permute-start.3 = (f32[32,72,128]{2,1,0:T(8,128)}, f32[32,72,128]{2,1,0:T(8,128)S(1)}, u32[]{:S(2)}, u32[]{:S(2)}) collective-permute-start(f32[32,72,128]{2,1,0:T(8,128)} %get-tuple-element.38), channel_id=1, source_target_pairs={{0,1},{1,2},{2,3},{3,4},{4,5},{5,6},{6,7},{7,8},{8,9},{9,10},{10,1... | collective-permute-start | bytes 3538952 | tf_op jit(solution)/shard_map/ppermute | solution.py:581
  26.2 2.5 %collective-permute-start.4 = (f32[32,72,128]{2,1,0:T(8,128)}, f32[32,72,128]{2,1,0:T(8,128)S(1)}, u32[]{:S(2)}, u32[]{:S(2)}) collective-permute-start(f32[32,72,128]{2,1,0:T(8,128)} %get-tuple-element.38), channel_id=1, source_target_pairs={{1,0},{2,1},{3,2},{4,3},{5,4},{6,5},{7,6},{8,7},{9,8},{10,9},{11,1... | collective-permute-start | bytes 3538952 | tf_op jit(solution)/shard_map/ppermute | solution.py:581
  28.6 0.0 collective-permute-done.2
  28.7 2.1 %collective-permute-start.5 = (f32[64,152]{1,0:T(8,128)S(1)}, f32[64,152]{1,0:T(8,128)S(1)}, u32[]{:S(2)}, u32[]{:S(2)}) collective-permute-start(f32[64,152]{1,0:T(8,128)S(1)} %add.23), channel_id=1, source_target_pairs={{0,4},{1,5},{2,6},{3,7},{4,0},{5,1},{6,2},{7,3},{8,12},{9,13},{10,... | collective-permute-start | bytes 116744 | tf_op jit(solution)/shard_map/ppermute | solution.py:585
  30.8 0.0 copy-done.2
  30.8 0.0 copy-done.3
  30.8 21.1 %far.1 = (f32[256,152]{1,0:T(8,128)}, s32[1,128]{1,0:T(1,128)}, s32[32,128]{1,0:T(8,128)}, s32[8,128]{1,0:T(8,128)}) custom-call(bf16[400,152]{1,0:T(8,128)(2,1)} %copy-done.2, bf16[400,152]{1,0:T(8,128)(2,1)} %get-tuple-element.28.own_ref, bf16[400,152]{1,0:T(8,128)(2,1)} %copy-done.3, s32[8,316]{1,0:T(8,128)} %vlist_ref.1, s32[27,64]{1,0:T(8,128)} %bitcast.17, ...), custom_call_target="tpu_custom_call" | custom-call | flops 20000000000 | bytes 18000000 | tf_op jit(solution)/shard_map/far/pallas_call | solution.py:658
  51.9 0.3 collective-permute-done.3.lower_ref
  52.2 2.2 %collective-permute-done.4.upper_ref = f32[32,72,128]{2,1,0:T(8,128)S(1)} collective-permute-done((f32[32,72,128]{2,1,0:T(8,128)}, f32[32,72,128]{2,1,0:T(8,128)S(1)}, u32[]{:S(2)}, u32[]{:S(2)}) %collective-permute-start.4) | collective-permute-done | bytes 1179680 | tf_op jit(solution)/shard_map/ppermute | solution.py:581
  54.4 0.0 collective-permute-done.5
  54.4 0.0 copy-start
  54.5 3.4 %collective-permute-start.8 = (f32[32,152]{1,0:T(8,128)S(1)}, f32[32,152]{1,0:T(8,128)S(1)}, u32[]{:S(2)}, u32[]{:S(2)}) collective-permute-start(f32[32,152]{1,0:T(8,128)S(1)} %slice.22), channel_id=1, source_target_pairs={{0,24},{1,25},{2,26},{3,27},{4,28},{5,29},{6,30},{7,31},{8,16},{9,... | collective-permute-start | bytes 58376 | tf_op jit(solution)/shard_map/ppermute | solution.py:585
  57.9 0.0 collective-permute-start.7
  57.9 0.4 collective-permute-start.6
  58.2 0.0 copy-done.4
  58.2 0.0 copy-done.5
  58.2 34.9 %near.1.refs_3_ = f32[64,32,128]{2,1,0:T(8,128)} custom-call(s32[1,128]{1,0:T(1,128)} %get-tuple-element.43.step_ref, s32[4096]{0:T(1024)} %bitcast.18, s32[1024]{0:T(1024)} %bitcast.19, bf16[128,64,128]{2,1,0:T(8,128)(2,1)} %get-tuple-element.46.own_hbm, bf16[2,128,32,128]{3,2,1,0:T(8,128)(2,1)} %get-tuple-element.31.own_feature_hbm, ...), custom_call_target="tpu_custom_call" | custom-call | flops 30000001024 | bytes 10000000 | tf_op jit(solution)/shard_map/near/pallas_call | solution.py:687
  93.2 0.0 copy-done
  93.2 0.0 collective-permute-done.8
  93.2 0.0 collective-permute-done.7
  93.2 0.0 collective-permute-done.6
  93.2 0.6 add_add_fusion.refs_9_
  93.8 9.5 %final.1 = f32[64,32,128]{2,1,0:T(8,128)} custom-call(s32[64]{0:T(128)} %refs_0_.1, bf16[2,64,2,32,128]{4,3,2,1,0:T(8,128)(2,1)} %bitcast.10, bf16[16,152,128]{2,1,0:T(8,128)(2,1)} %get-tuple-element.32.refs_2_, f32[64,32,128]{2,1,0:T(8,128)} %near.1.refs_3_, f32[256,152]{1,0:T(8,128)} %get-tuple-element.49.refs_4_, f32[8,152,152]{2,1,0:T(8,128)} %refs_5_.3, ...), custom_call_target="tpu_custom_call" | custom-call | tf_op jit(solution)/shard_map/final/pallas_call | solution.py:707
  (9 shorter events, 0.1 us)
Async XLA Ops:
  10.2 11.3 %collective-permute-start = (bf16[400,152]{1,0:T(8,128)(2,1)}, bf16[400,152]{1,0:T(8,128)(2,1)S(1)}, u32[]{:S(2)}, u32[]{:S(2)}) collective-permute-start(bf16[400,152]{1,0:T(8,128)(2,1)} %get-tuple-element.28.own_ref), channel_id=1, source_target_pairs={{0,1},{1,2},{2,3},{3,4},{4,5},{5,6},{6,7},{7,8},{8,9},{9,10},{10,1... | collective-permute-start | bytes 364808 | tf_op jit(solution)/shard_map/ppermute | solution.py:581
  14.7 7.3 %collective-permute-start.1 = (bf16[400,152]{1,0:T(8,128)(2,1)}, bf16[400,152]{1,0:T(8,128)(2,1)S(1)}, u32[]{:S(2)}, u32[]{:S(2)}) collective-permute-start(bf16[400,152]{1,0:T(8,128)(2,1)} %get-tuple-element.28.own_ref), channel_id=1, source_target_pairs={{1,0},{2,1},{3,2},{4,3},{5,4},{6,5},{7,6},{8,7},{9,8},{10,9},{11,1... | collective-permute-start | bytes 364808 | tf_op jit(solution)/shard_map/ppermute | solution.py:581
  16.7 5.4 %copy-start.1 = (f32[64,152]{1,0:T(8,128)S(1)}, f32[64,152]{1,0:T(8,128)}, u32[]{:S(2)}) copy-start(f32[64,152]{1,0:T(8,128)} %get-tuple-element.29.order_ref) | copy-start | bytes 116740
  21.5 9.3 %copy-start.2 = (bf16[400,152]{1,0:T(8,128)(2,1)}, bf16[400,152]{1,0:T(8,128)(2,1)S(1)}, u32[]{:S(2)}) copy-start(bf16[400,152]{1,0:T(8,128)(2,1)S(1)} %collective-permute-done.lower_ref) | copy-start | bytes 364804
  22.0 8.8 %copy-start.3 = (bf16[400,152]{1,0:T(8,128)(2,1)}, bf16[400,152]{1,0:T(8,128)(2,1)S(1)}, u32[]{:S(2)}) copy-start(bf16[400,152]{1,0:T(8,128)(2,1)S(1)} %collective-permute-done.1.upper_ref) | copy-start | bytes 364804
  22.1 6.6 %collective-permute-start.2 = (f32[64,152]{1,0:T(8,128)S(1)}, f32[64,152]{1,0:T(8,128)S(1)}, u32[]{:S(2)}, u32[]{:S(2)}) collective-permute-start(f32[64,152]{1,0:T(8,128)S(1)} %fusion), channel_id=1, source_target_pairs={{0,2},{1,3},{2,0},{3,1},{4,6},{5,7},{6,4},{7,5},{8,10},{9,11},{10,... | collective-permute-start | bytes 116744 | tf_op jit(solution)/shard_map/ppermute | solution.py:585
  24.2 28.0 %collective-permute-start.3 = (f32[32,72,128]{2,1,0:T(8,128)}, f32[32,72,128]{2,1,0:T(8,128)S(1)}, u32[]{:S(2)}, u32[]{:S(2)}) collective-permute-start(f32[32,72,128]{2,1,0:T(8,128)} %get-tuple-element.38), channel_id=1, source_target_pairs={{0,1},{1,2},{2,3},{3,4},{4,5},{5,6},{6,7},{7,8},{8,9},{9,10},{10,1... | collective-permute-start | bytes 3538952 | tf_op jit(solution)/shard_map/ppermute | solution.py:581
  26.2 28.3 %collective-permute-start.4 = (f32[32,72,128]{2,1,0:T(8,128)}, f32[32,72,128]{2,1,0:T(8,128)S(1)}, u32[]{:S(2)}, u32[]{:S(2)}) collective-permute-start(f32[32,72,128]{2,1,0:T(8,128)} %get-tuple-element.38), channel_id=1, source_target_pairs={{1,0},{2,1},{3,2},{4,3},{5,4},{6,5},{7,6},{8,7},{9,8},{10,9},{11,1... | collective-permute-start | bytes 3538952 | tf_op jit(solution)/shard_map/ppermute | solution.py:581
  28.7 25.7 %collective-permute-start.5 = (f32[64,152]{1,0:T(8,128)S(1)}, f32[64,152]{1,0:T(8,128)S(1)}, u32[]{:S(2)}, u32[]{:S(2)}) collective-permute-start(f32[64,152]{1,0:T(8,128)S(1)} %add.23), channel_id=1, source_target_pairs={{0,4},{1,5},{2,6},{3,7},{4,0},{5,1},{6,2},{7,3},{8,12},{9,13},{10,... | collective-permute-start | bytes 116744 | tf_op jit(solution)/shard_map/ppermute | solution.py:585
  52.2 6.0 %copy-start.4 = (f32[32,72,128]{2,1,0:T(8,128)}, f32[32,72,128]{2,1,0:T(8,128)S(1)}, u32[]{:S(2)}) copy-start(f32[32,72,128]{2,1,0:T(8,128)S(1)} %collective-permute-done.3.lower_ref) | copy-start | bytes 3538948
  54.4 3.8 %copy-start.5 = (f32[32,72,128]{2,1,0:T(8,128)}, f32[32,72,128]{2,1,0:T(8,128)S(1)}, u32[]{:S(2)}) copy-start(f32[32,72,128]{2,1,0:T(8,128)S(1)} %collective-permute-done.4.upper_ref) | copy-start | bytes 3538948
  54.4 38.7 %copy-start = (f32[64,152]{1,0:T(8,128)}, f32[64,152]{1,0:T(8,128)S(1)}, u32[]{:S(2)}) copy-start(f32[64,152]{1,0:T(8,128)S(1)} %add.24.refs_8_) | copy-start | bytes 116740
  54.5 38.7 %collective-permute-start.8 = (f32[32,152]{1,0:T(8,128)S(1)}, f32[32,152]{1,0:T(8,128)S(1)}, u32[]{:S(2)}, u32[]{:S(2)}) collective-permute-start(f32[32,152]{1,0:T(8,128)S(1)} %slice.22), channel_id=1, source_target_pairs={{0,24},{1,25},{2,26},{3,27},{4,28},{5,29},{6,30},{7,31},{8,16},{9,... | collective-permute-start | bytes 58376 | tf_op jit(solution)/shard_map/ppermute | solution.py:585
  57.9 35.3 %collective-permute-start.7 = (f32[32,152]{1,0:T(8,128)S(1)}, f32[32,152]{1,0:T(8,128)S(1)}, u32[]{:S(2)}, u32[]{:S(2)}) collective-permute-start(f32[32,152]{1,0:T(8,128)S(1)} %slice.22), channel_id=1, source_target_pairs={{0,16},{1,17},{2,18},{3,19},{4,20},{5,21},{6,22},{7,23},{8,24},{9,... | collective-permute-start | bytes 58376 | tf_op jit(solution)/shard_map/ppermute | solution.py:585
  57.9 35.3 %collective-permute-start.6 = (f32[32,152]{1,0:T(8,128)S(1)}, f32[32,152]{1,0:T(8,128)S(1)}, u32[]{:S(2)}, u32[]{:S(2)}) collective-permute-start(f32[32,152]{1,0:T(8,128)S(1)} %slice.22), channel_id=1, source_target_pairs={{0,8},{1,9},{2,10},{3,11},{4,12},{5,13},{6,14},{7,15},{8,0},{9,1},... | collective-permute-start | bytes 58376 | tf_op jit(solution)/shard_map/ppermute | solution.py:585

commit v16 on v15

--- a/solution.py
+++ b/solution.py
@@ -14,10 +14,10 @@
 NT = (((1,), (1,)), ((), ()))
 TN = (((0,), (0,)), ((), ()))
 BLOCK = 256
-UNROLL = 8
+UNROLL = 16
 TOTALS = 2
 PIECE = 64
-CLASS_ROWS = tuple(range(16, 129, 16))
+CLASS_ROWS = (32, 64, 96, 128)
 PLACES = 56
 SOURCES = 32
 CHUNK = 4
@@ -470,7 +470,7 @@
 
     blocks = lax.shift_right_logical(offset + (block_pieces - 1), block_pieces.bit_length() - 1)
     blocks_column = as_column(blocks.astype(F32))
-    own_class = lax.shift_right_logical(counts[1].astype(jnp.int32) - 1, 4)
+    own_class = lax.shift_right_logical(counts[1].astype(jnp.int32) - 1, 5)
     class_column = as_column(own_class.astype(F32)).astype(jnp.int32)
     earlier = (class_column == jnp.broadcast_to(own_class, shape)) & (rank_column < rank_wide)
     first = jnp.sum(jnp.where(earlier, blocks_column, 0.0), axis=0, keepdims=True).astype(jnp.int32)

time: 104 us -> 97.2 us (0.935); the launches traced: 103 us -> 95.5 us
  Pallas kernels: 80.6 us -> 72.5 us
    pallas_call x1, Pallas kernels: 34.9 us -> 26.9 us  [local(): pl.pallas_call(near_kernel, out_shape=jax.ShapeDtypeStruct((leaf_count, q...]
  transfers between devices with their start and end apart: 9 -> 9, of which waited for: 3 -> 3; matrix products, arithmetic and copies ran while one was open for 0% -> 0% of each run, Pallas kernels for 59% -> 55%
where the time goes in v16:
time: 97.2 us; the launch traced here: 95.5 us
  Pallas kernels  72.5 us (75%)
  starting transfers between devices  18.9 us (19%)
  waiting for transfers between devices  3.13 us (3%)
    pallas_call x1, Pallas kernels, local(): pl.pallas_call(near_kernel, out_shape=jax.ShapeDtypeStruct((leaf_count, q...  26.9 us
    pallas_call x1, Pallas kernels, local(): pl.pallas_call(far_kernel, out_shape=(jax.ShapeDtypeStruct((node_rows, eq...  21 us
    ppermute x4, starting transfers between devices, shifted(): return (lax.ppermute(value, 'oct', up), lax.ppermute(value, 'oct', down))  10.8 us
    pallas_call x1, Pallas kernels, local(): pl.pallas_call(lambda *refs: upward_kernel(level_count, *refs), out_shape...  10.2 us
    pallas_call x1, Pallas kernels, local(): pl.pallas_call(lambda *refs: final_kernel(level_count, *refs), out_shape=...  9.51 us
    ppermute x5, starting transfers between devices, swapped(): lax.ppermute(value, 'oct', [(source, source ^ mask) for source in range(s...  8.07 us
    pallas_call x1, Pallas kernels, local(): pl.pallas_call(outline_kernel, out_shape=(jax.ShapeDtypeStruct((2, 2 * le...  4.85 us
    ppermute x4, waiting for transfers between devices, shifted(): return (lax.ppermute(value, 'oct', up), lax.ppermute(value, 'oct', down))  3.11 us
  transfers between devices with their start and end apart: 9, of which 3 were waited for; matrix products, arithmetic and copies ran while one was open for 0% of the time, Pallas kernels for 55%

profile of v16, /device:TPU:1, one launch (start us, length us, event | category | flops | bytes accessed | tf_op | source)
XLA Modules:
  0.0 95.5 jit_solution(11470673777666176467)
XLA Ops:
  0.0 10.2 %upward.1 = (bf16[128,64,128]{2,1,0:T(8,128)(2,1)}, bf16[400,152]{1,0:T(8,128)(2,1)}, f32[64,152]{1,0:T(8,128)}) custom-call(f32[3,64,128]{2,1,0:T(8,128)} %bitcast.13, f32[64,32,128]{2,1,0:T(8,128)} %dens_ref.1, f32[3,64,152]{2,1,0:T(8,128)} %bitcast.11, s32[64]{0:T(128)} %refs_0_.1, s32[1,64]{1,0:T(1,128)} %bitcast.15, f32[152,152]{1,0:T(8,128)} %refs_5_.2, ...), custom_call_target="tpu_custom_call" | custom-call | tf_op jit(solution)/shard_map/upward/pallas_call | solution.py:620
  10.2 4.5 %collective-permute-start = (bf16[400,152]{1,0:T(8,128)(2,1)}, bf16[400,152]{1,0:T(8,128)(2,1)S(1)}, u32[]{:S(2)}, u32[]{:S(2)}) collective-permute-start(bf16[400,152]{1,0:T(8,128)(2,1)} %get-tuple-element.28.own_ref), channel_id=1, source_target_pairs={{0,1},{1,2},{2,3},{3,4},{4,5},{5,6},{6,7},{7,8},{8,9},{9,10},{10,1... | collective-permute-start | bytes 364808 | tf_op jit(solution)/shard_map/ppermute | solution.py:581
  14.7 1.9 %collective-permute-start.1 = (bf16[400,152]{1,0:T(8,128)(2,1)}, bf16[400,152]{1,0:T(8,128)(2,1)S(1)}, u32[]{:S(2)}, u32[]{:S(2)}) collective-permute-start(bf16[400,152]{1,0:T(8,128)(2,1)} %get-tuple-element.28.own_ref), channel_id=1, source_target_pairs={{1,0},{2,1},{3,2},{4,3},{5,4},{6,5},{7,6},{8,7},{9,8},{10,9},{11,1... | collective-permute-start | bytes 364808 | tf_op jit(solution)/shard_map/ppermute | solution.py:581
  16.7 0.0 copy-start.1
  16.7 4.8 %outline.1 = (bf16[2,128,32,128]{3,2,1,0:T(8,128)(2,1)}, bf16[16,152,128]{2,1,0:T(8,128)(2,1)}, f32[32,72,128]{2,1,0:T(8,128)}) custom-call(f32[3,64,128]{2,1,0:T(8,128)} %bitcast.14, f32[64,32,128]{2,1,0:T(8,128)} %dens_ref.1, f32[3,64,152]{2,1,0:T(8,128)} %bitcast.12, s32[64]{0:T(128)} %refs_0_.1, f32[64,152]{1,0:T(8,128)} %get-tuple-element.29.order_ref), custom_call_target="tpu_custom_call" | custom-call | flops 4000000000 | bytes 10000000 | tf_op jit(solution)/shard_map/outline/pallas_call | solution.py:635
  21.5 0.0 collective-permute-done.lower_ref
  21.5 0.5 collective-permute-done.1.upper_ref
  22.0 0.0 copy-done.1
  22.1 2.2 %collective-permute-start.2 = (f32[64,152]{1,0:T(8,128)S(1)}, f32[64,152]{1,0:T(8,128)S(1)}, u32[]{:S(2)}, u32[]{:S(2)}) collective-permute-start(f32[64,152]{1,0:T(8,128)S(1)} %fusion), channel_id=1, source_target_pairs={{0,2},{1,3},{2,0},{3,1},{4,6},{5,7},{6,4},{7,5},{8,10},{9,11},{10,... | collective-permute-start | bytes 116744 | tf_op jit(solution)/shard_map/ppermute | solution.py:585
  24.2 1.9 %collective-permute-start.3 = (f32[32,72,128]{2,1,0:T(8,128)}, f32[32,72,128]{2,1,0:T(8,128)S(1)}, u32[]{:S(2)}, u32[]{:S(2)}) collective-permute-start(f32[32,72,128]{2,1,0:T(8,128)} %get-tuple-element.38), channel_id=1, source_target_pairs={{0,1},{1,2},{2,3},{3,4},{4,5},{5,6},{6,7},{7,8},{8,9},{9,10},{10,1... | collective-permute-start | bytes 3538952 | tf_op jit(solution)/shard_map/ppermute | solution.py:581
  26.2 2.5 %collective-permute-start.4 = (f32[32,72,128]{2,1,0:T(8,128)}, f32[32,72,128]{2,1,0:T(8,128)S(1)}, u32[]{:S(2)}, u32[]{:S(2)}) collective-permute-start(f32[32,72,128]{2,1,0:T(8,128)} %get-tuple-element.38), channel_id=1, source_target_pairs={{1,0},{2,1},{3,2},{4,3},{5,4},{6,5},{7,6},{8,7},{9,8},{10,9},{11,1... | collective-permute-start | bytes 3538952 | tf_op jit(solution)/shard_map/ppermute | solution.py:581
  28.6 0.0 collective-permute-done.2
  28.7 2.1 %collective-permute-start.5 = (f32[64,152]{1,0:T(8,128)S(1)}, f32[64,152]{1,0:T(8,128)S(1)}, u32[]{:S(2)}, u32[]{:S(2)}) collective-permute-start(f32[64,152]{1,0:T(8,128)S(1)} %add.23), channel_id=1, source_target_pairs={{0,4},{1,5},{2,6},{3,7},{4,0},{5,1},{6,2},{7,3},{8,12},{9,13},{10,... | collective-permute-start | bytes 116744 | tf_op jit(solution)/shard_map/ppermute | solution.py:585
  30.8 0.0 copy-done.2
  30.8 0.0 copy-done.3
  30.8 21.0 %far.1 = (f32[256,152]{1,0:T(8,128)}, s32[1,128]{1,0:T(1,128)}, s32[32,128]{1,0:T(8,128)}, s32[8,128]{1,0:T(8,128)}) custom-call(bf16[400,152]{1,0:T(8,128)(2,1)} %copy-done.2, bf16[400,152]{1,0:T(8,128)(2,1)} %get-tuple-element.28.own_ref, bf16[400,152]{1,0:T(8,128)(2,1)} %copy-done.3, s32[8,316]{1,0:T(8,128)} %vlist_ref.1, s32[27,64]{1,0:T(8,128)} %bitcast.17, ...), custom_call_target="tpu_custom_call" | custom-call | flops 20000000000 | bytes 18000000 | tf_op jit(solution)/shard_map/far/pallas_call | solution.py:658
  51.8 0.4 collective-permute-done.3.lower_ref
  52.2 2.2 %collective-permute-done.4.upper_ref = f32[32,72,128]{2,1,0:T(8,128)S(1)} collective-permute-done((f32[32,72,128]{2,1,0:T(8,128)}, f32[32,72,128]{2,1,0:T(8,128)S(1)}, u32[]{:S(2)}, u32[]{:S(2)}) %collective-permute-start.4) | collective-permute-done | bytes 1179680 | tf_op jit(solution)/shard_map/ppermute | solution.py:581
  54.4 0.0 collective-permute-done.5
  54.4 0.0 copy-start
  54.5 3.4 %collective-permute-start.8 = (f32[32,152]{1,0:T(8,128)S(1)}, f32[32,152]{1,0:T(8,128)S(1)}, u32[]{:S(2)}, u32[]{:S(2)}) collective-permute-start(f32[32,152]{1,0:T(8,128)S(1)} %slice.22), channel_id=1, source_target_pairs={{0,24},{1,25},{2,26},{3,27},{4,28},{5,29},{6,30},{7,31},{8,16},{9,... | collective-permute-start | bytes 58376 | tf_op jit(solution)/shard_map/ppermute | solution.py:585
  57.9 0.0 collective-permute-start.7
  57.9 0.4 collective-permute-start.6
  58.2 0.0 copy-done.4
  58.2 0.0 copy-done.5
  58.2 26.9 %near.1.refs_3_ = f32[64,32,128]{2,1,0:T(8,128)} custom-call(s32[1,128]{1,0:T(1,128)} %get-tuple-element.43.step_ref, s32[4096]{0:T(1024)} %bitcast.18, s32[1024]{0:T(1024)} %bitcast.19, bf16[128,64,128]{2,1,0:T(8,128)(2,1)} %get-tuple-element.46.own_hbm, bf16[2,128,32,128]{3,2,1,0:T(8,128)(2,1)} %get-tuple-element.31.own_feature_hbm, ...), custom_call_target="tpu_custom_call" | custom-call | flops 30000001024 | bytes 10000000 | tf_op jit(solution)/shard_map/near/pallas_call | solution.py:687
  85.2 0.0 copy-done
  85.2 0.0 collective-permute-done.8
  85.2 0.0 collective-permute-done.7
  85.2 0.0 collective-permute-done.6
  85.2 0.6 add_add_fusion.refs_9_
  85.8 9.5 %final.1 = f32[64,32,128]{2,1,0:T(8,128)} custom-call(s32[64]{0:T(128)} %refs_0_.1, bf16[2,64,2,32,128]{4,3,2,1,0:T(8,128)(2,1)} %bitcast.10, bf16[16,152,128]{2,1,0:T(8,128)(2,1)} %get-tuple-element.32.refs_2_, f32[64,32,128]{2,1,0:T(8,128)} %near.1.refs_3_, f32[256,152]{1,0:T(8,128)} %get-tuple-element.49.refs_4_, f32[8,152,152]{2,1,0:T(8,128)} %refs_5_.3, ...), custom_call_target="tpu_custom_call" | custom-call | tf_op jit(solution)/shard_map/final/pallas_call | solution.py:707
  (9 shorter events, 0.1 us)
Async XLA Ops:
  10.2 11.3 %collective-permute-start = (bf16[400,152]{1,0:T(8,128)(2,1)}, bf16[400,152]{1,0:T(8,128)(2,1)S(1)}, u32[]{:S(2)}, u32[]{:S(2)}) collective-permute-start(bf16[400,152]{1,0:T(8,128)(2,1)} %get-tuple-element.28.own_ref), channel_id=1, source_target_pairs={{0,1},{1,2},{2,3},{3,4},{4,5},{5,6},{6,7},{7,8},{8,9},{9,10},{10,1... | collective-permute-start | bytes 364808 | tf_op jit(solution)/shard_map/ppermute | solution.py:581
  14.7 7.3 %collective-permute-start.1 = (bf16[400,152]{1,0:T(8,128)(2,1)}, bf16[400,152]{1,0:T(8,128)(2,1)S(1)}, u32[]{:S(2)}, u32[]{:S(2)}) collective-permute-start(bf16[400,152]{1,0:T(8,128)(2,1)} %get-tuple-element.28.own_ref), channel_id=1, source_target_pairs={{1,0},{2,1},{3,2},{4,3},{5,4},{6,5},{7,6},{8,7},{9,8},{10,9},{11,1... | collective-permute-start | bytes 364808 | tf_op jit(solution)/shard_map/ppermute | solution.py:581
  16.7 5.4 %copy-start.1 = (f32[64,152]{1,0:T(8,128)S(1)}, f32[64,152]{1,0:T(8,128)}, u32[]{:S(2)}) copy-start(f32[64,152]{1,0:T(8,128)} %get-tuple-element.29.order_ref) | copy-start | bytes 116740
  21.5 9.3 %copy-start.2 = (bf16[400,152]{1,0:T(8,128)(2,1)}, bf16[400,152]{1,0:T(8,128)(2,1)S(1)}, u32[]{:S(2)}) copy-start(bf16[400,152]{1,0:T(8,128)(2,1)S(1)} %collective-permute-done.lower_ref) | copy-start | bytes 364804
  22.0 8.8 %copy-start.3 = (bf16[400,152]{1,0:T(8,128)(2,1)}, bf16[400,152]{1,0:T(8,128)(2,1)S(1)}, u32[]{:S(2)}) copy-start(bf16[400,152]{1,0:T(8,128)(2,1)S(1)} %collective-permute-done.1.upper_ref) | copy-start | bytes 364804
  22.1 6.6 %collective-permute-start.2 = (f32[64,152]{1,0:T(8,128)S(1)}, f32[64,152]{1,0:T(8,128)S(1)}, u32[]{:S(2)}, u32[]{:S(2)}) collective-permute-start(f32[64,152]{1,0:T(8,128)S(1)} %fusion), channel_id=1, source_target_pairs={{0,2},{1,3},{2,0},{3,1},{4,6},{5,7},{6,4},{7,5},{8,10},{9,11},{10,... | collective-permute-start | bytes 116744 | tf_op jit(solution)/shard_map/ppermute | solution.py:585
  24.2 28.0 %collective-permute-start.3 = (f32[32,72,128]{2,1,0:T(8,128)}, f32[32,72,128]{2,1,0:T(8,128)S(1)}, u32[]{:S(2)}, u32[]{:S(2)}) collective-permute-start(f32[32,72,128]{2,1,0:T(8,128)} %get-tuple-element.38), channel_id=1, source_target_pairs={{0,1},{1,2},{2,3},{3,4},{4,5},{5,6},{6,7},{7,8},{8,9},{9,10},{10,1... | collective-permute-start | bytes 3538952 | tf_op jit(solution)/shard_map/ppermute | solution.py:581
  26.2 28.3 %collective-permute-start.4 = (f32[32,72,128]{2,1,0:T(8,128)}, f32[32,72,128]{2,1,0:T(8,128)S(1)}, u32[]{:S(2)}, u32[]{:S(2)}) collective-permute-start(f32[32,72,128]{2,1,0:T(8,128)} %get-tuple-element.38), channel_id=1, source_target_pairs={{1,0},{2,1},{3,2},{4,3},{5,4},{6,5},{7,6},{8,7},{9,8},{10,9},{11,1... | collective-permute-start | bytes 3538952 | tf_op jit(solution)/shard_map/ppermute | solution.py:581
  28.7 25.7 %collective-permute-start.5 = (f32[64,152]{1,0:T(8,128)S(1)}, f32[64,152]{1,0:T(8,128)S(1)}, u32[]{:S(2)}, u32[]{:S(2)}) collective-permute-start(f32[64,152]{1,0:T(8,128)S(1)} %add.23), channel_id=1, source_target_pairs={{0,4},{1,5},{2,6},{3,7},{4,0},{5,1},{6,2},{7,3},{8,12},{9,13},{10,... | collective-permute-start | bytes 116744 | tf_op jit(solution)/shard_map/ppermute | solution.py:585
  52.2 6.0 %copy-start.4 = (f32[32,72,128]{2,1,0:T(8,128)}, f32[32,72,128]{2,1,0:T(8,128)S(1)}, u32[]{:S(2)}) copy-start(f32[32,72,128]{2,1,0:T(8,128)S(1)} %collective-permute-done.3.lower_ref) | copy-start | bytes 3538948
  54.4 3.8 %copy-start.5 = (f32[32,72,128]{2,1,0:T(8,128)}, f32[32,72,128]{2,1,0:T(8,128)S(1)}, u32[]{:S(2)}) copy-start(f32[32,72,128]{2,1,0:T(8,128)S(1)} %collective-permute-done.4.upper_ref) | copy-start | bytes 3538948
  54.4 30.7 %copy-start = (f32[64,152]{1,0:T(8,128)}, f32[64,152]{1,0:T(8,128)S(1)}, u32[]{:S(2)}) copy-start(f32[64,152]{1,0:T(8,128)S(1)} %add.24.refs_8_) | copy-start | bytes 116740
  54.5 30.7 %collective-permute-start.8 = (f32[32,152]{1,0:T(8,128)S(1)}, f32[32,152]{1,0:T(8,128)S(1)}, u32[]{:S(2)}, u32[]{:S(2)}) collective-permute-start(f32[32,152]{1,0:T(8,128)S(1)} %slice.22), channel_id=1, source_target_pairs={{0,24},{1,25},{2,26},{3,27},{4,28},{5,29},{6,30},{7,31},{8,16},{9,... | collective-permute-start | bytes 58376 | tf_op jit(solution)/shard_map/ppermute | solution.py:585
  57.9 27.3 %collective-permute-start.7 = (f32[32,152]{1,0:T(8,128)S(1)}, f32[32,152]{1,0:T(8,128)S(1)}, u32[]{:S(2)}, u32[]{:S(2)}) collective-permute-start(f32[32,152]{1,0:T(8,128)S(1)} %slice.22), channel_id=1, source_target_pairs={{0,16},{1,17},{2,18},{3,19},{4,20},{5,21},{6,22},{7,23},{8,24},{9,... | collective-permute-start | bytes 58376 | tf_op jit(solution)/shard_map/ppermute | solution.py:585
  57.9 27.3 %collective-permute-start.6 = (f32[32,152]{1,0:T(8,128)S(1)}, f32[32,152]{1,0:T(8,128)S(1)}, u32[]{:S(2)}, u32[]{:S(2)}) collective-permute-start(f32[32,152]{1,0:T(8,128)S(1)} %slice.22), channel_id=1, source_target_pairs={{0,8},{1,9},{2,10},{3,11},{4,12},{5,13},{6,14},{7,15},{8,0},{9,1},... | collective-permute-start | bytes 58376 | tf_op jit(solution)/shard_map/ppermute | solution.py:585
